TPU v7x, 256 devices: a whole 4x4x8 slice. The times are simulated.
256 devices in a mesh: tm: 32 (over z, x), rep: 8 (over y, core).
Axes of the slice: x: 4, y: 4, z: 8, core: 2. Of those that a mesh axis runs over, the one named last changes fastest.
Arguments:
- video: bfloat16 [8, 32, 32, 16, 256], P('rep', 'tm'), may hold values from -6 to 6
- cotangent: bfloat16 [8, 32, 32, 16, 256], P('rep', 'tm'), may hold values from -24 to 24
- w_spat1: bfloat16 [3, 3, 256, 256], replicated, may hold values from -0.125 to 0.125
- w_spat2: bfloat16 [3, 3, 256, 256], replicated, may hold values from -0.125 to 0.125
- w_time1: bfloat16 [3, 256, 256], replicated, may hold values from -0.21875 to 0.21875
- w_time2: bfloat16 [3, 256, 256], replicated, may hold values from -0.21875 to 0.21875
Outputs:
- grad_input: bfloat16 [8, 32, 32, 16, 256], P('rep', 'tm')
- grad_spat1: float32 [3, 3, 256, 256], replicated
- grad_spat2: float32 [3, 3, 256, 256], replicated
- grad_time1: float32 [3, 256, 256], replicated
- grad_time2: float32 [3, 256, 256], replicated
All inputs are finite; a program needn't handle non-finite values.
Results may differ from a plain program's by a relative error of at most 0.02.
Values may be sent and summed in bfloat16 or wider, within the bound.
No kernel may reach another device: no remote copies, remote signals or barrier semaphores. Data moves between devices by JAX's collectives and lax.ppermute only.
A program may use at most 64 MiB of HBM per device.

v0:
```python
import math

import jax
import jax.numpy as jnp
from jax import lax
from jax.sharding import PartitionSpec as P


def matmul(left, right):
    return jnp.dot(left, right, preferred_element_type=jnp.float32)


def matmul_nt(left, right):
    return lax.dot_general(
        left, right, (((1,), (1,)), ((), ())), preferred_element_type=jnp.float32
    )


def matmul_tn(left, right):
    return lax.dot_general(
        left, right, (((0,), (0,)), ((), ())), preferred_element_type=jnp.float32
    )


def padded_slab(values):
    return jnp.pad(values, ((0, 0), (1, 1), (1, 1), (0, 0)))


def spatial_conv(values, weight):
    frames, rows, cols, channels = values.shape
    padded = padded_slab(values)
    total = jnp.zeros((frames * rows * cols, channels), jnp.float32)
    for row_tap in range(3):
        for col_tap in range(3):
            window = padded[:, row_tap : row_tap + rows, col_tap : col_tap + cols, :].reshape(
                -1, channels
            )
            total = total + matmul(window, weight[row_tap, col_tap])
    return total.reshape(values.shape)


def spatial_back(grads, weight):
    frames, rows, cols, channels = grads.shape
    padded = padded_slab(grads)
    total = jnp.zeros((frames * rows * cols, channels), jnp.float32)
    for row_tap in range(3):
        for col_tap in range(3):
            window = padded[
                :, 2 - row_tap : 2 - row_tap + rows, 2 - col_tap : 2 - col_tap + cols, :
            ].reshape(-1, channels)
            total = total + matmul_nt(window, weight[row_tap, col_tap])
    return total.reshape(grads.shape)


def spatial_grad(values, grads):
    frames, rows, cols, channels = values.shape
    padded = padded_slab(values)
    grad_rows = grads.reshape(-1, channels)
    taps = []
    for row_tap in range(3):
        for col_tap in range(3):
            window = padded[:, row_tap : row_tap + rows, col_tap : col_tap + cols, :].reshape(
                -1, channels
            )
            taps.append(matmul_tn(window, grad_rows))
    return jnp.stack(taps).reshape(3, 3, channels, channels)


def frames_behind(values):
    count = values.shape[0]
    padded = jnp.pad(values, ((2, 0), (0, 0), (0, 0), (0, 0)))
    return [values, padded[1 : 1 + count], padded[0:count]]


def frames_ahead(values):
    count = values.shape[0]
    padded = jnp.pad(values, ((0, 2), (0, 0), (0, 0), (0, 0)))
    return [values, padded[1 : 1 + count], padded[2 : 2 + count]]


def silu_slope(pre):
    sigma = jax.nn.sigmoid(pre)
    return sigma * (1.0 + pre * (1.0 - sigma))


def time_block(behind, cot_ahead, w_time1, w_time2, ahead_fn):
    shape = behind[0].shape
    channels = shape[-1]
    time_pre = jnp.zeros((behind[0].size // channels, channels), jnp.float32)
    time_back = jnp.zeros_like(time_pre)
    for offset in range(3):
        time_pre = time_pre + matmul(behind[offset].reshape(-1, channels), w_time1[offset])
        time_back = time_back + matmul_nt(cot_ahead[offset].reshape(-1, channels), w_time2[offset])
    time_act = jax.nn.silu(time_pre).astype(jnp.bfloat16)
    time_grad = (time_back * silu_slope(time_pre)).astype(jnp.bfloat16)
    grad_second = jnp.stack(
        [matmul_tn(time_act, cot_ahead[offset].reshape(-1, channels)) for offset in range(3)]
    )
    grad_first = jnp.stack(
        [matmul_tn(behind[offset].reshape(-1, channels), time_grad) for offset in range(3)]
    )
    grad_ahead = ahead_fn(time_grad.reshape(shape))
    act_back = jnp.zeros_like(time_pre)
    for offset in range(3):
        act_back = act_back + matmul_nt(grad_ahead[offset].reshape(-1, channels), w_time1[offset])
    return (act_back.astype(jnp.bfloat16).reshape(shape), grad_first, grad_second)


def body(video, cotangent, w_spat1, w_spat2, w_time1, w_time2):
    frame_block = video[0]
    cot_block = cotangent[0]
    cot_ahead = frames_ahead(
        lax.all_to_all(cot_block, "tm", split_axis=1, concat_axis=0, tiled=True)
    )
    first_pre = spatial_conv(frame_block, w_spat1)
    first_act = jax.nn.silu(first_pre).astype(jnp.bfloat16)
    second_pre = spatial_conv(first_act, w_spat2)
    second_act = jax.nn.silu(second_pre).astype(jnp.bfloat16)
    tall_act = lax.all_to_all(second_act, "tm", split_axis=1, concat_axis=0, tiled=True)
    tall_back, grad_first, grad_second = time_block(
        frames_behind(tall_act), cot_ahead, w_time1, w_time2, frames_ahead
    )
    act_back = lax.all_to_all(tall_back, "tm", split_axis=0, concat_axis=1, tiled=True)
    second_grad = (act_back.astype(jnp.float32) * silu_slope(second_pre)).astype(jnp.bfloat16)
    first_back = spatial_back(second_grad, w_spat2)
    first_grad = (first_back * silu_slope(first_pre)).astype(jnp.bfloat16)
    grad_input = spatial_back(first_grad, w_spat1).astype(jnp.bfloat16)
    spat_one = spatial_grad(frame_block, first_grad)
    spat_two = spatial_grad(first_act, second_grad)
    spat_one, spat_two, time_one, time_two = lax.psum(
        (spat_one, spat_two, grad_first, grad_second), ("tm", "rep")
    )
    pixels = (
        lax.axis_size("rep")
        * lax.axis_size("tm")
        * frame_block.shape[0]
        * frame_block.shape[1]
        * frame_block.shape[2]
    )
    scale = 1.0 / math.sqrt(pixels)
    return (
        grad_input[None],
        spat_one * scale,
        spat_two * scale,
        time_one * scale,
        time_two * scale,
    )


def solution(mesh):
    return jax.shard_map(
        body,
        mesh=mesh,
        in_specs=(
            P("rep", "tm", None, None, None),
            P("rep", "tm", None, None, None),
            P(),
            P(),
            P(),
            P(),
        ),
        out_specs=(P("rep", "tm", None, None, None), P(), P(), P(), P()),
        check_vma=False,
    )
```

profile of v0, /device:TPU:1, one launch (start us, length us, event | category | flops | bytes accessed | tf_op | source)
XLA Modules:
  0.0 380.4 jit_solution(9328778707974425586)
XLA Ops:
  7.2 11.9 %all-to-all-start = ((bf16[1,32,16,256]{3,2,0,1:T(8,128)(2,1)}), bf16[1,32,16,256]{3,2,0,1:T(8,128)(2,1)S(1)}, u32[]{:S(2)}, u32[]{:S(2)}) async-start(bf16[1,32,16,256]{3,2,0,1:T(8,128)(2,1)} %bitcast.483), calls=%async_computation | async-start | bytes 524288 | tf_op jit(solution)/shard_map/all_to_all | solution.py:113
  19.0 1.0 copy.181
  30.8 0.9 copy.111
  31.6 9.2 %all-to-all-start.1 = ((bf16[1,32,16,256]{3,2,0,1:T(8,128)(2,1)}), bf16[1,32,16,256]{3,2,0,1:T(8,128)(2,1)S(1)}, u32[]{:S(2)}, u32[]{:S(2)}) async-start(bf16[1,32,16,256]{3,2,0,1:T(8,128)(2,1)} %copy.111), calls=%async_computation.1 | async-start | bytes 524288 | tf_op jit(solution)/shard_map/all_to_all | solution.py:119
  40.9 0.8 pad_slice_fusion.36
  41.7 9.7 %all-to-all-done.1 = bf16[1,32,16,256]{3,2,0,1:T(8,128)(2,1)S(1)} async-done(((bf16[1,32,16,256]{3,2,0,1:T(8,128)(2,1)}), bf16[1,32,16,256]{3,2,0,1:T(8,128)(2,1)S(1)}, u32[]{:S(2)}, u32[]{:S(2)}) %all-to-all-start.1) | async-done | bytes 262176 | tf_op jit(solution)/shard_map/all_to_all | solution.py:119
  51.5 1.2 fusion.93
  54.8 1.0 convolution_bitcast_fusion.3
  55.8 1.0 convolution_bitcast_fusion.4
  56.7 1.0 convolution_bitcast_fusion.5
  58.0 1.0 convolution_bitcast_fusion
  59.3 1.0 fusion.2
  60.2 5.1 %all-to-all-start.2 = ((bf16[32,1,16,256]{3,2,1,0:T(8,128)(2,1)}), bf16[32,1,16,256]{3,2,1,0:T(8,128)(2,1)S(1)}, u32[]{:S(2)}, u32[]{:S(2)}) async-start(bf16[32,1,16,256]{3,2,1,0:T(8,128)(2,1)} %bitcast.468), calls=%async_computation.2 | async-start | bytes 524288 | tf_op jit(solution)/shard_map/all_to_all | solution.py:123
  65.6 2.1 pad_maximum_fusion
  68.7 0.9 pad_maximum_fusion.1
  69.6 6.2 %all-to-all-done.2 = bf16[32,1,16,256]{3,2,1,0:T(8,128)(2,1)S(1)} async-done(((bf16[32,1,16,256]{3,2,1,0:T(8,128)(2,1)}), bf16[32,1,16,256]{3,2,1,0:T(8,128)(2,1)S(1)}, u32[]{:S(2)}, u32[]{:S(2)}) %all-to-all-start.2) | async-done | bytes 262176 | tf_op jit(solution)/shard_map/all_to_all | solution.py:123
  81.1 1.1 multiply_convert_fusion.2
  86.3 1.0 fusion.12
  87.2 1.0 fusion.11
  88.2 1.0 fusion.10
  89.2 1.0 fusion.9
  90.2 1.1 fusion.8
  91.2 1.0 fusion.7
  92.2 1.0 fusion.6
  93.2 1.0 fusion.5
  94.1 1.0 fusion.4
  95.2 1.0 copy-done.11
  96.3 0.7 fusion.24
  101.1 1.0 fusion.3
  102.1 264.9 %all-reduce.10.cloned.1.call-done = (f32[3,3,256,256]{3,2,1,0:T(8,128)}, f32[3,3,256,256]{3,2,1,0:T(8,128)}, f32[3,256,256]{2,1,0:T(8,128)}, f32[3,256,256]{2,1,0:T(8,128)}) async-done(((f32[3,3,256,256]{3,2,1,0:T(8,128)}, f32[3,3,256,256]{3,2,1,0:T(8,128)}, f32[3,256,256]{2,1,0:T(8,128)}, f32[3,256,256]{2,1,0:T(8,128)}), (f32[3,3,256,256]{3,2,1,0:T(8,128)}, f32[3,3,256,256]{3,2,1,0:T(8,128)}, ...) | async-done | bytes 6291472 | tf_op jit(solution)/shard_map/psum | solution.py:130
  367.0 5.2 %broadcast_multiply_fusion = (f32[3,3,256,256]{3,2,1,0:T(8,128)}, f32[3,3,256,256]{3,2,1,0:T(8,128)}) fusion(f32[3,3,256,256]{3,2,1,0:T(8,128)} %get-tuple-element.6, f32[3,3,256,256]{3,2,1,0:T(8,128)} %get-tuple-element.5), kind=kLoop, calls=%fused_computation.42 | loop fusion | flops 1179648 | bytes 9437184 | tf_op jit(solution)/shard_map/mul | solution.py:144
  372.3 1.3 broadcast_multiply_fusion.2
  (153 shorter events, 27.5 us)
Async XLA Ops:
  7.2 24.5 %all-to-all-start = ((bf16[1,32,16,256]{3,2,0,1:T(8,128)(2,1)}), bf16[1,32,16,256]{3,2,0,1:T(8,128)(2,1)S(1)}, u32[]{:S(2)}, u32[]{:S(2)}) async-start(bf16[1,32,16,256]{3,2,0,1:T(8,128)(2,1)} %bitcast.483), calls=%async_computation | async-start | bytes 524288 | tf_op jit(solution)/shard_map/all_to_all | solution.py:113
  20.1 0.7 copy-start.16
  21.4 1.3 copy-start
  23.1 1.0 copy-start.7
  25.3 0.8 copy-start.9
  25.4 3.7 copy-start.24
  25.7 0.7 copy-start.13
  26.9 1.3 copy-start.1
  31.6 19.8 %all-to-all-start.1 = ((bf16[1,32,16,256]{3,2,0,1:T(8,128)(2,1)}), bf16[1,32,16,256]{3,2,0,1:T(8,128)(2,1)S(1)}, u32[]{:S(2)}, u32[]{:S(2)}) async-start(bf16[1,32,16,256]{3,2,0,1:T(8,128)(2,1)} %copy.111), calls=%async_computation.1 | async-start | bytes 524288 | tf_op jit(solution)/shard_map/all_to_all | solution.py:119
  51.4 1.3 copy-start.5
  51.4 1.3 copy-start.26
  51.5 1.5 copy-start.12
  53.5 1.0 copy-start.15
  53.8 4.2 %copy-start.3 = (bf16[512,256]{1,0:T(8,128)(2,1)}, bf16[512,256]{1,0:T(8,128)(2,1)S(1)}, u32[]{:S(2)}) copy-start(bf16[512,256]{1,0:T(8,128)(2,1)S(1)} %get-tuple-element.51) | copy-start | bytes 786436
  60.2 15.5 %all-to-all-start.2 = ((bf16[32,1,16,256]{3,2,1,0:T(8,128)(2,1)}), bf16[32,1,16,256]{3,2,1,0:T(8,128)(2,1)S(1)}, u32[]{:S(2)}, u32[]{:S(2)}) async-start(bf16[32,1,16,256]{3,2,1,0:T(8,128)(2,1)} %bitcast.468), calls=%async_computation.2 | async-start | bytes 524288 | tf_op jit(solution)/shard_map/all_to_all | solution.py:123
  65.4 301.6 %all-reduce.10.cloned.1.call-start = ((), (), s32[]{:S(2)}) async-start(), calls=%async_computation.3 | async-start | bytes 12582912 | tf_op jit(solution)/shard_map/psum | solution.py:130
  65.6 2.1 copy-start.4
  65.6 2.1 copy-start.6
  67.7 1.0 copy-start.20
  80.0 1.0 copy-start.10
  81.1 1.1 copy-start.17
  82.2 3.1 copy-start.18
  83.1 1.0 copy-start.8
  85.3 1.0 copy-start.14
  85.7 1.6 copy-start.2
  89.2 1.0 copy-start.25
  95.1 1.0 copy-start.11
  95.1 1.2 copy-start.23
  99.1 1.0 copy-start.19
  367.0 5.2 %copy-start.21 = (f32[3,256,256]{2,1,0:T(8,128)S(1)}, f32[3,256,256]{2,1,0:T(8,128)}, u32[]{:S(2)}) copy-start(f32[3,256,256]{2,1,0:T(8,128)} %get-tuple-element.7) | copy-start | bytes 2359300
  367.0 5.2 %copy-start.22 = (f32[3,256,256]{2,1,0:T(8,128)S(1)}, f32[3,256,256]{2,1,0:T(8,128)}, u32[]{:S(2)}) copy-start(f32[3,256,256]{2,1,0:T(8,128)} %get-tuple-element.8) | copy-start | bytes 2359300
Sparse Core Ops, SparseCore 0:
  95.3 271.7 all-reduce.9
where the time goes:
time: 382 us; the launch traced here: 380 us
  waiting for transfers between devices  281 us (74%)
  matrix products  30.5 us (8%)
  starting transfers between devices  26.4 us (7%)
  local copies, waits for them, and re-layouts  15.6 us (4%)
  between operations  14.9 us (4%)
  other arithmetic  12.1 us (3%)
    psum x1, waiting for transfers between devices, body(): lax.psum((spat_one, spat_two, grad_first, grad_second), ('tm', 'rep'))  265 us
    dot_general x24, matrix products, matmul_tn(): lax.dot_general(left, right, (((0,), (0,)), ((), ())), preferred_element_...  16.1 us
    all_to_all x1, starting transfers between devices, body(): lax.all_to_all(cot_block, 'tm', split_axis=1, concat_axis=0, tiled=True)  11.9 us
    all_to_all x1, waiting for transfers between devices, body(): lax.all_to_all(second_act, 'tm', split_axis=1, concat_axis=0, tiled=True)  9.73 us
    dot_general x24, matrix products, matmul_nt(): lax.dot_general(left, right, (((1,), (1,)), ((), ())), preferred_element_...  9.52 us
    all_to_all x1, starting transfers between devices, body(): lax.all_to_all(second_act, 'tm', split_axis=1, concat_axis=0, tiled=True)  9.22 us
  transfers between devices with their start and end apart: 4, of which 3 were waited for; matrix products, arithmetic and copies ran while one was open for 5% of the time, Pallas kernels for 0%

commit v1 on v0

--- a/solution.py
+++ b/solution.py
@@ -3,6 +3,7 @@
 import jax
 import jax.numpy as jnp
 from jax import lax
+from jax.sharding import Mesh
 from jax.sharding import PartitionSpec as P
 
 
@@ -106,59 +107,72 @@
     return (act_back.astype(jnp.bfloat16).reshape(shape), grad_first, grad_second)
 
 
+def scatter_sum(values, axes, count):
+    parts = values.reshape(count, -1, values.shape[-1])
+    arrived = lax.all_to_all(parts, axes, 0, 0, tiled=True)
+    return jnp.sum(arrived.astype(jnp.float32), axis=0).astype(jnp.bfloat16)
+
+
+def gather_all(values, axes, count):
+    copies = jnp.broadcast_to(values[None], (count,) + values.shape)
+    arrived = lax.all_to_all(copies, axes, 0, 0, tiled=True)
+    return arrived.reshape(-1, values.shape[-1])
+
+
+def total_over_devices(values):
+    values = scatter_sum(values, "core", 2)
+    values = scatter_sum(values, ("x", "y"), 16)
+    values = scatter_sum(values, "z", 8)
+    values = gather_all(values, "z", 8)
+    values = gather_all(values, ("x", "y"), 16)
+    return gather_all(values, "core", 2)
+
+
 def body(video, cotangent, w_spat1, w_spat2, w_time1, w_time2):
     frame_block = video[0]
     cot_block = cotangent[0]
     cot_ahead = frames_ahead(
-        lax.all_to_all(cot_block, "tm", split_axis=1, concat_axis=0, tiled=True)
+        lax.all_to_all(cot_block, ("z", "x"), split_axis=1, concat_axis=0, tiled=True)
     )
     first_pre = spatial_conv(frame_block, w_spat1)
     first_act = jax.nn.silu(first_pre).astype(jnp.bfloat16)
     second_pre = spatial_conv(first_act, w_spat2)
     second_act = jax.nn.silu(second_pre).astype(jnp.bfloat16)
-    tall_act = lax.all_to_all(second_act, "tm", split_axis=1, concat_axis=0, tiled=True)
+    tall_act = lax.all_to_all(second_act, ("z", "x"), split_axis=1, concat_axis=0, tiled=True)
     tall_back, grad_first, grad_second = time_block(
         frames_behind(tall_act), cot_ahead, w_time1, w_time2, frames_ahead
     )
-    act_back = lax.all_to_all(tall_back, "tm", split_axis=0, concat_axis=1, tiled=True)
+    act_back = lax.all_to_all(tall_back, ("z", "x"), split_axis=0, concat_axis=1, tiled=True)
     second_grad = (act_back.astype(jnp.float32) * silu_slope(second_pre)).astype(jnp.bfloat16)
     first_back = spatial_back(second_grad, w_spat2)
     first_grad = (first_back * silu_slope(first_pre)).astype(jnp.bfloat16)
     grad_input = spatial_back(first_grad, w_spat1).astype(jnp.bfloat16)
     spat_one = spatial_grad(frame_block, first_grad)
     spat_two = spatial_grad(first_act, second_grad)
-    spat_one, spat_two, time_one, time_two = lax.psum(
-        (spat_one, spat_two, grad_first, grad_second), ("tm", "rep")
+    scale = 1.0 / math.sqrt(256 * 512)
+    channels = grad_first.shape[-1]
+    stacked = jnp.concatenate(
+        [part.reshape(-1, channels) for part in (spat_one, spat_two, grad_first, grad_second)]
     )
-    pixels = (
-        lax.axis_size("rep")
-        * lax.axis_size("tm")
-        * frame_block.shape[0]
-        * frame_block.shape[1]
-        * frame_block.shape[2]
-    )
-    scale = 1.0 / math.sqrt(pixels)
+    summed = total_over_devices((stacked * scale).astype(jnp.bfloat16)).astype(jnp.float32)
+    taps = summed.reshape(-1, channels, channels)
+    spat_shape = spat_one.shape
     return (
         grad_input[None],
-        spat_one * scale,
-        spat_two * scale,
-        time_one * scale,
-        time_two * scale,
+        taps[0:9].reshape(spat_shape),
+        taps[9:18].reshape(spat_shape),
+        taps[18:21],
+        taps[21:24],
     )
 
 
 def solution(mesh):
+    fine = Mesh(mesh.devices.reshape(8, 4, 4, 2), ("z", "x", "y", "core"))
+    frames = P(("y", "core"), ("z", "x"), None, None, None)
     return jax.shard_map(
         body,
-        mesh=mesh,
-        in_specs=(
-            P("rep", "tm", None, None, None),
-            P("rep", "tm", None, None, None),
-            P(),
-            P(),
-            P(),
-            P(),
-        ),
-        out_specs=(P("rep", "tm", None, None, None), P(), P(), P(), P()),
+        mesh=fine,
+        in_specs=(frames, frames, P(), P(), P(), P()),
+        out_specs=(frames, P(), P(), P(), P()),
         check_vma=False,
     )

time: 382 us -> 187 us (0.49)
  waiting for transfers between devices: 281 us -> 59.7 us
  blocking collectives: 0 us -> 21.6 us
  starting transfers between devices: 26.4 us -> 42.6 us
  between operations: 14.9 us -> 1.65 us
  local copies, waits for them, and re-layouts: 15.6 us -> 20.9 us
    psum x1 -> x0, waiting for transfers between devices: 265 us -> none  [body(): lax.psum((spat_one, spat_two, grad_first, grad_second), ('tm', 'rep'))]
    all_to_all x3 -> x7, waiting for transfers between devices: 15.9 us -> 59.7 us  [the longest x2 21.4 us: gather_all(): arrived = lax.all_to_all(copies, axes, 0, 0, tiled=True)]
    all_to_all x0 -> x2, blocking collectives: none -> 21.6 us  [the longest x1 12 us: gather_all(): arrived = lax.all_to_all(copies, axes, 0, 0, tiled=True)]
    all_to_all x3 -> x7, starting transfers between devices: 26.2 us -> 42.6 us  [the longest x1 11.9 us: body(): lax.all_to_all(cot_block, ('z', 'x'), split_axis=1, concat_axis=0, tiled=...]
    mul x2 -> x0, other arithmetic: 6.53 us -> none  [the longest x1 5.23 us: body(): spat_two * scale]
    dot_general x24, matrix products: 16.1 us -> 9.73 us  [matmul_tn(): lax.dot_general(left, right, (((0,), (0,)), ((), ())), preferred_element_...]
    slice x18, local copies, waits for them, and re-layouts: 3.01 us -> 7.85 us  [spatial_back(): padded[:, 2 - row_tap:2 - row_tap + rows, 2 - col_tap:2 - col_tap + cols, :]]
    unnamed x55 -> x45, local copies, waits for them, and re-layouts: 7.55 us -> 2.92 us
  transfers between devices with their start and end apart: 4 -> 7, of which waited for: 3 -> 6; matrix products, arithmetic and copies ran while one was open for 5% -> 14% of each run, Pallas kernels for 0% -> 0%
where the time goes in v1:
time: 187 us; the launch traced here: 186 us
  waiting for transfers between devices  59.7 us (32%)
  starting transfers between devices  42.6 us (23%)
  matrix products  29.7 us (16%)
  blocking collectives  21.6 us (12%)
  local copies, waits for them, and re-layouts  20.9 us (11%)
  other arithmetic  10.1 us (5%)
    all_to_all x2, waiting for transfers between devices, gather_all(): arrived = lax.all_to_all(copies, axes, 0, 0, tiled=True)  21.4 us
    all_to_all x2, waiting for transfers between devices, scatter_sum(): arrived = lax.all_to_all(parts, axes, 0, 0, tiled=True)  21.2 us
    dot_general x24, matrix products, matmul_nt(): lax.dot_general(left, right, (((1,), (1,)), ((), ())), preferred_element_...  12.3 us
    all_to_all x1, blocking collectives, gather_all(): arrived = lax.all_to_all(copies, axes, 0, 0, tiled=True)  12 us
    all_to_all x1, starting transfers between devices, body(): lax.all_to_all(cot_block, ('z', 'x'), split_axis=1, concat_axis=0, tiled=...  11.9 us
    all_to_all x1, waiting for transfers between devices, body(): lax.all_to_all(second_act, ('z', 'x'), split_axis=1, concat_axis=0, tiled...  10.5 us
    dot_general x24, matrix products, matmul_tn(): lax.dot_general(left, right, (((0,), (0,)), ((), ())), preferred_element_...  9.73 us
    all_to_all x1, blocking collectives, scatter_sum(): arrived = lax.all_to_all(parts, axes, 0, 0, tiled=True)  9.66 us
  transfers between devices with their start and end apart: 7, of which 6 were waited for; matrix products, arithmetic and copies ran while one was open for 14% of the time, Pallas kernels for 0%

profile of v1, /device:TPU:1, one launch (start us, length us, event | category | flops | bytes accessed | tf_op | source)
XLA Modules:
  0.0 186.3 jit_solution(12199614394481347934)
XLA Ops:
  0.6 11.9 %all-to-all-start = ((bf16[1,32,16,256]{3,2,0,1:T(8,128)(2,1)}), bf16[1,32,16,256]{3,2,0,1:T(8,128)(2,1)S(1)}, u32[]{:S(2)}, u32[]{:S(2)}) async-start(bf16[1,32,16,256]{3,2,0,1:T(8,128)(2,1)} %bitcast.508), calls=%async_computation | async-start | bytes 524288 | tf_op jit(solution)/shard_map/all_to_all | solution.py:135
  12.5 1.0 copy.232
  23.9 9.2 %all-to-all-start.1 = ((bf16[1,32,16,256]{3,2,0,1:T(8,128)(2,1)}), bf16[1,32,16,256]{3,2,0,1:T(8,128)(2,1)S(1)}, u32[]{:S(2)}, u32[]{:S(2)}) async-start(bf16[1,32,16,256]{3,2,0,1:T(8,128)(2,1)} %copy.164), calls=%async_computation.1 | async-start | bytes 524288 | tf_op jit(solution)/shard_map/all_to_all | solution.py:141
  33.1 10.5 %all-to-all-done.1 = bf16[1,32,16,256]{3,2,0,1:T(8,128)(2,1)S(1)} async-done(((bf16[1,32,16,256]{3,2,0,1:T(8,128)(2,1)}), bf16[1,32,16,256]{3,2,0,1:T(8,128)(2,1)S(1)}, u32[]{:S(2)}, u32[]{:S(2)}) %all-to-all-start.1) | async-done | bytes 262176 | tf_op jit(solution)/shard_map/all_to_all | solution.py:141
  43.7 1.2 fusion.94
  44.8 1.1 fusion.50
  45.9 1.1 convolution_add_fusion.19
  47.1 1.3 multiply_convert_fusion
  49.3 1.0 convolution_bitcast_fusion.1
  50.6 1.0 convolution_bitcast_fusion
  54.4 5.4 %all-to-all-start.2 = ((bf16[32,1,16,256]{3,2,1,0:T(8,128)(2,1)}), bf16[32,1,16,256]{3,2,1,0:T(8,128)(2,1)S(1)}, u32[]{:S(2)}, u32[]{:S(2)}) async-start(bf16[32,1,16,256]{3,2,1,0:T(8,128)(2,1)} %bitcast.57), calls=%async_computation.2 | async-start | bytes 524288 | tf_op jit(solution)/shard_map/all_to_all | solution.py:145
  59.8 1.2 pad_maximum_fusion.1
  61.5 1.9 %pad_maximum_fusion = f32[3,256,256]{2,1,0:T(8,128)} fusion(f32[1,256,256]{2,1,0:T(8,128)} %convolution_bitcast_fusion.3, f32[1,256,256]{2,1,0:T(8,128)S(1)} %convolution_bitcast_fusion.4, f32[1,256,256]{2,1,0:T(8,128)S(1)} %convolution_bitcast_fusion.5), kind=kLoop, calls=%fused_computation.87 | loop fusion | flops 393216 | bytes 1572864 | tf_op jit(solution)/shard_map/stack | solution.py:100
  63.4 6.6 %all-to-all-done.2 = bf16[32,1,16,256]{3,2,1,0:T(8,128)(2,1)S(1)} async-done(((bf16[32,1,16,256]{3,2,1,0:T(8,128)(2,1)}), bf16[32,1,16,256]{3,2,1,0:T(8,128)(2,1)S(1)}, u32[]{:S(2)}, u32[]{:S(2)}) %all-to-all-start.2) | async-done | bytes 262176 | tf_op jit(solution)/shard_map/all_to_all | solution.py:145
  78.2 1.1 multiply_convert_fusion.2
  83.0 9.7 %all_to_all.63 = bf16[2,3072,256]{2,1,0:T(8,128)(2,1)S(1)} all-to-all(bf16[2,3072,256]{2,1,0:T(8,128)(2,1)S(1)} %bitcast.426), channel_id=1, replica_groups=mesh['z'=8,'x'=4,'y'=4,'core'=2] {'core'}, dimensions={0} | all-to-all | bytes 6291456 | tf_op jit(solution)/shard_map/all_to_all | solution.py:112
  92.7 2.2 %reduce_sum.36 = bf16[3072,256]{1,0:T(8,128)(2,1)} reduce(bf16[2,3072,256]{2,1,0:T(8,128)(2,1)S(1)} %all_to_all.63, bf16[]{:T(256)} %constant.14.clone.1), dimensions={0}, to_apply=%region_0.1 | reduce | flops 786432 | bytes 4718594 | tf_op jit(solution)/shard_map/reduce_sum | solution.py:113
  94.8 5.1 %all-to-all-start.4 = ((bf16[16,192,256]{2,1,0:T(8,128)(2,1)}), bf16[16,192,256]{2,1,0:T(8,128)(2,1)S(1)}, u32[]{:S(2)}, u32[]{:S(2)}) async-start(bf16[16,192,256]{2,1,0:T(8,128)(2,1)} %bitcast.428), calls=%async_computation.4 | async-start | bytes 3145728 | tf_op jit(solution)/shard_map/all_to_all | solution.py:112
  107.4 14.8 %all-to-all-done.4 = bf16[16,192,256]{2,1,0:T(8,128)(2,1)S(1)} async-done(((bf16[16,192,256]{2,1,0:T(8,128)(2,1)}), bf16[16,192,256]{2,1,0:T(8,128)(2,1)S(1)}, u32[]{:S(2)}, u32[]{:S(2)}) %all-to-all-start.4) | async-done | bytes 1572896 | tf_op jit(solution)/shard_map/all_to_all | solution.py:112
  123.1 3.4 %all-to-all-start.5 = ((bf16[8,24,256]{2,1,0:T(8,128)(2,1)}), bf16[8,24,256]{2,1,0:T(8,128)(2,1)S(1)}, u32[]{:S(2)}, u32[]{:S(2)}) async-start(bf16[8,24,256]{2,1,0:T(8,128)(2,1)} %bitcast.507), calls=%async_computation.5 | async-start | bytes 196608 | tf_op jit(solution)/shard_map/all_to_all | solution.py:112
  126.4 1.2 convolution_add_fusion.7
  127.6 6.4 %all-to-all-done.5 = bf16[8,24,256]{2,1,0:T(8,128)(2,1)S(1)} async-done(((bf16[8,24,256]{2,1,0:T(8,128)(2,1)}), bf16[8,24,256]{2,1,0:T(8,128)(2,1)S(1)}, u32[]{:S(2)}, u32[]{:S(2)}) %all-to-all-start.5) | async-done | bytes 98336 | tf_op jit(solution)/shard_map/all_to_all | solution.py:112
  134.7 3.4 %all-to-all-start.6 = ((bf16[8,24,256]{2,1,0:T(8,128)(2,1)}), bf16[8,24,256]{2,1,0:T(8,128)(2,1)S(1)}, u32[]{:S(2)}, u32[]{:S(2)}) async-start(bf16[8,24,256]{2,1,0:T(8,128)(2,1)} %broadcast_in_dim.10), calls=%async_computation.6 | async-start | bytes 196608 | tf_op jit(solution)/shard_map/all_to_all | solution.py:118
  138.0 1.2 convolution_add_fusion.6
  139.3 6.3 %all-to-all-done.6 = bf16[8,24,256]{2,1,0:T(8,128)(2,1)S(1)} async-done(((bf16[8,24,256]{2,1,0:T(8,128)(2,1)}), bf16[8,24,256]{2,1,0:T(8,128)(2,1)S(1)}, u32[]{:S(2)}, u32[]{:S(2)}) %all-to-all-start.6) | async-done | bytes 98336 | tf_op jit(solution)/shard_map/all_to_all | solution.py:118
  145.5 1.3 broadcast_in_dim.23
  146.8 4.2 %all-to-all-start.7 = ((bf16[16,192,256]{2,1,0:T(8,128)(2,1)}), bf16[16,192,256]{2,1,0:T(8,128)(2,1)S(1)}, u32[]{:S(2)}, u32[]{:S(2)}) async-start(bf16[16,192,256]{2,1,0:T(8,128)(2,1)} %broadcast_in_dim.23), calls=%async_computation.7 | async-start | bytes 3145728 | tf_op jit(solution)/shard_map/all_to_all | solution.py:118
  151.1 1.3 convolution_add_fusion.5
  154.5 15.2 %all-to-all-done.7 = bf16[16,192,256]{2,1,0:T(8,128)(2,1)S(1)} async-done(((bf16[16,192,256]{2,1,0:T(8,128)(2,1)}), bf16[16,192,256]{2,1,0:T(8,128)(2,1)S(1)}, u32[]{:S(2)}, u32[]{:S(2)}) %all-to-all-start.7) | async-done | bytes 1572896 | tf_op jit(solution)/shard_map/all_to_all | solution.py:118
  169.9 12.0 %all_to_all.64 = bf16[2,3072,256]{2,1,0:T(8,128)(2,1)S(1)} all-to-all(bf16[2,3072,256]{2,1,0:T(8,128)(2,1)S(1)} %broadcast_in_dim.25), channel_id=1, replica_groups=mesh['z'=8,'x'=4,'y'=4,'core'=2] {'core'}, dimensions={0} | all-to-all | bytes 6291456 | tf_op jit(solution)/shard_map/all_to_all | solution.py:118
  182.6 2.5 %fusion.150 = (f32[2304,256]{1,0:T(8,128)}, f32[2304,256]{1,0:T(8,128)}) fusion(f32[6144,256]{1,0:T(8,128)S(1)} %bitcast_convert_fusion), kind=kLoop, calls=%fused_computation.269 | loop fusion | bytes 9437184 | tf_op jit(solution)/shard_map/slice | solution.py:163
  185.1 1.2 fusion.149
  (158 shorter events, 38.1 us)
Async XLA Ops:
  0.6 23.2 %all-to-all-start = ((bf16[1,32,16,256]{3,2,0,1:T(8,128)(2,1)}), bf16[1,32,16,256]{3,2,0,1:T(8,128)(2,1)S(1)}, u32[]{:S(2)}, u32[]{:S(2)}) async-start(bf16[1,32,16,256]{3,2,0,1:T(8,128)(2,1)} %bitcast.508), calls=%async_computation | async-start | bytes 524288 | tf_op jit(solution)/shard_map/all_to_all | solution.py:135
  13.5 1.1 copy-start.12
  13.9 1.3 copy-start
  15.4 1.0 copy-start.4
  17.6 0.8 copy-start.6
  17.6 3.7 %copy-start.19 = (bf16[512,256]{1,0:T(8,128)(2,1)}, bf16[512,256]{1,0:T(8,128)(2,1)S(1)}, u32[]{:S(2)}) copy-start(bf16[512,256]{1,0:T(8,128)(2,1)S(1)} %get-tuple-element.47) | copy-start | bytes 786436
  18.8 1.1 copy-start.10
  19.1 1.3 copy-start.2
  23.9 19.8 %all-to-all-start.1 = ((bf16[1,32,16,256]{3,2,0,1:T(8,128)(2,1)}), bf16[1,32,16,256]{3,2,0,1:T(8,128)(2,1)S(1)}, u32[]{:S(2)}, u32[]{:S(2)}) async-start(bf16[1,32,16,256]{3,2,0,1:T(8,128)(2,1)} %copy.164), calls=%async_computation.1 | async-start | bytes 524288 | tf_op jit(solution)/shard_map/all_to_all | solution.py:141
  47.1 3.2 %copy-start.21 = (bf16[3,256,256]{2,1,0:T(8,128)(2,1)S(1)}, bf16[3,256,256]{2,1,0:T(8,128)(2,1)}, u32[]{:S(2)}) copy-start(bf16[3,256,256]{2,1,0:T(8,128)(2,1)} %param.11) | copy-start | bytes 1179652
  50.6 1.3 copy-start.9
  54.4 15.6 %all-to-all-start.2 = ((bf16[32,1,16,256]{3,2,1,0:T(8,128)(2,1)}), bf16[32,1,16,256]{3,2,1,0:T(8,128)(2,1)S(1)}, u32[]{:S(2)}, u32[]{:S(2)}) async-start(bf16[32,1,16,256]{3,2,1,0:T(8,128)(2,1)} %bitcast.57), calls=%async_computation.2 | async-start | bytes 524288 | tf_op jit(solution)/shard_map/all_to_all | solution.py:145
  72.1 1.3 copy-start.11
  73.6 1.0 copy-start.20
  77.2 1.0 copy-start.7
  77.7 1.6 copy-start.13
  79.6 1.0 copy-start.5
  81.2 1.1 copy-start.3
  94.8 5.2 %copy-start.8 = (f32[512,256]{1,0:T(8,128)S(1)}, f32[512,256]{1,0:T(8,128)}, u32[]{:S(2)}) copy-start(f32[512,256]{1,0:T(8,128)} %copy-done.6) | copy-start | bytes 1572868
  94.8 5.2 %copy-start.18 = (f32[512,256]{1,0:T(8,128)S(1)}, f32[512,256]{1,0:T(8,128)}, u32[]{:S(2)}) copy-start(f32[512,256]{1,0:T(8,128)} %get-tuple-element.50) | copy-start | bytes 1572868
  94.8 27.3 %all-to-all-start.4 = ((bf16[16,192,256]{2,1,0:T(8,128)(2,1)}), bf16[16,192,256]{2,1,0:T(8,128)(2,1)S(1)}, u32[]{:S(2)}, u32[]{:S(2)}) async-start(bf16[16,192,256]{2,1,0:T(8,128)(2,1)} %bitcast.428), calls=%async_computation.4 | async-start | bytes 3145728 | tf_op jit(solution)/shard_map/all_to_all | solution.py:112
  101.0 6.1 %copy-start.1 = (bf16[3,3,256,256]{3,2,1,0:T(8,128)(2,1)S(1)}, bf16[3,3,256,256]{3,2,1,0:T(8,128)(2,1)}, u32[]{:S(2)}) copy-start(bf16[3,3,256,256]{3,2,1,0:T(8,128)(2,1)} %param.8) | copy-start | bytes 3538948
  123.1 10.9 %all-to-all-start.5 = ((bf16[8,24,256]{2,1,0:T(8,128)(2,1)}), bf16[8,24,256]{2,1,0:T(8,128)(2,1)S(1)}, u32[]{:S(2)}, u32[]{:S(2)}) async-start(bf16[8,24,256]{2,1,0:T(8,128)(2,1)} %bitcast.507), calls=%async_computation.5 | async-start | bytes 196608 | tf_op jit(solution)/shard_map/all_to_all | solution.py:112
  134.7 10.9 %all-to-all-start.6 = ((bf16[8,24,256]{2,1,0:T(8,128)(2,1)}), bf16[8,24,256]{2,1,0:T(8,128)(2,1)S(1)}, u32[]{:S(2)}, u32[]{:S(2)}) async-start(bf16[8,24,256]{2,1,0:T(8,128)(2,1)} %broadcast_in_dim.10), calls=%async_computation.6 | async-start | bytes 196608 | tf_op jit(solution)/shard_map/all_to_all | solution.py:118
  146.8 22.9 %all-to-all-start.7 = ((bf16[16,192,256]{2,1,0:T(8,128)(2,1)}), bf16[16,192,256]{2,1,0:T(8,128)(2,1)S(1)}, u32[]{:S(2)}, u32[]{:S(2)}) async-start(bf16[16,192,256]{2,1,0:T(8,128)(2,1)} %broadcast_in_dim.23), calls=%async_computation.7 | async-start | bytes 3145728 | tf_op jit(solution)/shard_map/all_to_all | solution.py:118
  151.0 1.6 copy-start.17
  151.1 1.8 copy-start.16
  152.3 1.0 copy-start.14
  152.6 1.0 copy-start.15

commit v2 on v1

v2 whole, which is shorter than its diff:
```python
import math

import jax
import jax.numpy as jnp
from jax import lax
from jax.experimental import pallas as pl
from jax.experimental.pallas import tpu as pltpu
from jax.sharding import Mesh
from jax.sharding import PartitionSpec as P

CH = 256
COLS = 16
PIX = 512
PAD = PIX + 2 * COLS
SCALE = 1.0 / math.sqrt(131072)
BF = jnp.bfloat16
F32 = jnp.float32
VMEM = pl.BlockSpec(memory_space=pltpu.VMEM)
SMEM = pl.BlockSpec(memory_space=pltpu.SMEM)


def dot_nn(left, right):
    return lax.dot_general(left, right, (((1,), (0,)), ((), ())), preferred_element_type=F32)


def dot_nt(left, right):
    return lax.dot_general(left, right, (((1,), (1,)), ((), ())), preferred_element_type=F32)


def dot_tn(left, right):
    return lax.dot_general(left, right, (((0,), (0,)), ((), ())), preferred_element_type=F32)


def call(kernel, outs, ins, scratch=(), flops=0):
    specs = [SMEM if value.dtype == jnp.int32 else VMEM for value in ins]
    moved = sum(value.size * value.dtype.itemsize for value in ins)
    return pl.pallas_call(
        kernel,
        out_shape=[jax.ShapeDtypeStruct(shape, kind) for shape, kind in outs],
        in_specs=specs,
        out_specs=[VMEM] * len(outs),
        scratch_shapes=list(scratch),
        cost_estimate=pl.CostEstimate(flops=flops, bytes_accessed=moved, transcendentals=0),
        compiler_params=pltpu.CompilerParams(vmem_limit_bytes=40 * 1024 * 1024),
    )(*ins)


def fill_windows(wide, values):
    edge = jnp.zeros((COLS, 3 * CH), BF)
    wide[0:COLS, :] = edge
    wide[COLS + PIX : PAD, :] = edge
    column = lax.broadcasted_iota(jnp.int32, (PIX, CH), 0) & (COLS - 1)
    full = values.astype(F32)
    before = jnp.where(column == 0, 0.0, pltpu.roll(full, 1, 0))
    after = jnp.where(column == COLS - 1, 0.0, pltpu.roll(full, PIX - 1, 0))
    wide[COLS : COLS + PIX, 0:CH] = before.astype(BF)
    wide[COLS : COLS + PIX, CH : 2 * CH] = values.astype(BF)
    wide[COLS : COLS + PIX, 2 * CH : 3 * CH] = after.astype(BF)


def conv_from(wide, weight):
    total = None
    for tap in range(3):
        term = dot_nn(
            wide[tap * COLS : tap * COLS + PIX, :], weight[tap * 3 * CH : (tap + 1) * 3 * CH, :]
        )
        total = term if total is None else total + term
    return total


def back_from(wide, weight):
    total = None
    for tap in range(3):
        for side in range(3):
            at = (tap * 3 + side) * CH
            term = dot_nt(
                wide[(2 - tap) * COLS : (2 - tap) * COLS + PIX, (2 - side) * CH : (3 - side) * CH],
                weight[at : at + CH, :],
            )
            total = term if total is None else total + term
    return total


def silu_pair(pre):
    sigma = jax.nn.sigmoid(pre)
    act = pre * sigma
    return act, sigma * (1.0 + pre * (1.0 - sigma))


def forward_kernel(core, video, w1, w2, act2, slope1, slope2, keep, send, wide):
    values = video[...]
    fill_windows(wide, values)
    act, slope = silu_pair(conv_from(wide, w1))
    slope1[...] = slope
    first = act.astype(BF)

    @pl.when(core[0] == 0)
    def _():
        keep[...] = first
        send[...] = values

    @pl.when(core[0] != 0)
    def _():
        keep[...] = values
        send[...] = first

    fill_windows(wide, first)
    act, slope = silu_pair(conv_from(wide, w2))
    slope2[...] = slope
    act2[...] = act.astype(BF)


def ahead_sum(padded, weight):
    total = None
    for step in range(3):
        term = dot_nt(padded[step * COLS : step * COLS + PIX, :], weight[step * CH : (step + 1) * CH, :])
        total = term if total is None else total + term
    return total


def time_back_kernel(cot, wt2, back, padded):
    padded[0:PIX, :] = cot[...]
    padded[PIX:PAD, :] = jnp.zeros((2 * COLS, CH), BF)
    back[...] = ahead_sum(padded, wt2)


def time_kernel(core, act, cot, back, wt1, act_back, keep, send, padded):
    padded[0 : 2 * COLS, :] = jnp.zeros((2 * COLS, CH), BF)
    padded[2 * COLS : PAD, :] = act[...]
    pre = None
    for step in range(3):
        at = (2 - step) * COLS
        term = dot_nn(padded[at : at + PIX, :], wt1[step * CH : (step + 1) * CH, :])
        pre = term if pre is None else pre + term
    value, slope = silu_pair(pre)
    time_act = value.astype(BF)
    time_grad = (back[...] * slope).astype(BF)

    @pl.when(core[0] == 0)
    def _():
        keep[0] = act[...]
        keep[1] = time_grad
        send[0] = time_act
        send[1] = cot[...]

    @pl.when(core[0] != 0)
    def _():
        keep[0] = time_act
        keep[1] = cot[...]
        send[0] = act[...]
        send[1] = time_grad

    padded[0:PIX, :] = time_grad
    padded[PIX:PAD, :] = jnp.zeros((2 * COLS, CH), BF)
    act_back[...] = ahead_sum(padded, wt1).astype(BF)


def time_weights_kernel(keep, recv, out):
    for step in range(3):
        rows = PIX - step * COLS
        total = dot_tn(keep[0, 0:rows, :], keep[1, step * COLS : PIX, :])
        total = total + dot_tn(recv[0, 0:rows, :], recv[1, step * COLS : PIX, :])
        out[step * CH : (step + 1) * CH, :] = (total * SCALE).astype(BF)


def backward_kernel(core, act_back, slope1, slope2, w2, first_grad, keep, send, wide):
    second = (act_back[...].astype(F32) * slope2[...]).astype(BF)
    fill_windows(wide, second)
    first = (back_from(wide, w2) * slope1[...]).astype(BF)
    first_grad[...] = first

    @pl.when(core[0] == 0)
    def _():
        keep[...] = second
        send[...] = first

    @pl.when(core[0] != 0)
    def _():
        keep[...] = first
        send[...] = second


def space_weights_kernel(keep_x, recv_x, keep_g, recv_g, time_part, out, wide, other):
    fill_windows(wide, keep_x[...])
    fill_windows(other, recv_x[...])
    for tap in range(3):
        for side in range(3):
            rows = slice(tap * COLS, tap * COLS + PIX)
            lanes = slice(side * CH, (side + 1) * CH)
            total = dot_tn(wide[rows, lanes], keep_g[...])
            total = total + dot_tn(other[rows, lanes], recv_g[...])
            at = (tap * 3 + side) * CH
            out[at : at + CH, :] = (total * SCALE).astype(BF)
    out[9 * CH : 12 * CH, :] = time_part[...]


def input_kernel(first_grad, w1, out, wide):
    fill_windows(wide, first_grad[...])
    out[...] = back_from(wide, w1).astype(BF)


def swap_cores(values):
    return lax.ppermute(values, "core", [(0, 1), (1, 0)])


def swap_frames(values):
    blocks = values.reshape(PIX // COLS, COLS, CH)
    return lax.all_to_all(blocks, ("z", "x"), 0, 0, tiled=True).reshape(PIX, CH)


def scatter_sum(values, axes, count):
    parts = values.reshape(count, -1, CH)
    arrived = lax.all_to_all(parts, axes, 0, 0, tiled=True)
    return jnp.sum(arrived.astype(F32), axis=0).astype(BF)


def gather_all(values, axes, count):
    copies = jnp.broadcast_to(values[None], (count,) + values.shape)
    return lax.all_to_all(copies, axes, 0, 0, tiled=True).reshape(-1, CH)


def body(video, cotangent, w_spat1, w_spat2, w_time1, w_time2):
    core = lax.axis_index("core").astype(jnp.int32).reshape(1)
    w1, w2, wt1, wt2 = (w.reshape(-1, CH) for w in (w_spat1, w_spat2, w_time1, w_time2))
    slab, slab32 = ((PIX, CH), BF), ((PIX, CH), F32)
    pair = ((2, PIX, CH), BF)
    wide, tall = pltpu.VMEM((PAD, 3 * CH), BF), pltpu.VMEM((PAD, CH), BF)
    conv_flops, time_flops = 2 * PIX * 9 * CH * CH, 2 * PIX * 3 * CH * CH

    cot = swap_frames(cotangent.reshape(PIX, CH))
    second_act, slope1, slope2, keep_x, send_x = call(
        forward_kernel,
        [slab, slab32, slab32, slab, slab],
        (core, video.reshape(PIX, CH), w1, w2),
        [wide],
        2 * conv_flops,
    )
    act = swap_frames(second_act)
    recv_x = swap_cores(send_x)
    (time_back,) = call(time_back_kernel, [slab32], (cot, wt2), [tall], time_flops)
    act_back, keep_t, send_t = call(
        time_kernel, [slab, pair, pair], (core, act, cot, time_back, wt1), [tall], 2 * time_flops
    )
    act_back = swap_frames(act_back)
    recv_t = swap_cores(send_t)
    (time_part,) = call(
        time_weights_kernel, [((3 * CH, CH), BF)], (keep_t, recv_t), (), 2 * time_flops
    )
    first_grad, keep_g, send_g = call(
        backward_kernel, [slab, slab, slab], (core, act_back, slope1, slope2, w2), [wide], conv_flops
    )
    recv_g = swap_cores(send_g)
    (part,) = call(
        space_weights_kernel,
        [((12 * CH, CH), BF)],
        (keep_x, recv_x, keep_g, recv_g, time_part),
        [wide, wide],
        2 * conv_flops,
    )
    (grad_input,) = call(input_kernel, [slab], (first_grad, w1), [wide], conv_flops)

    part = scatter_sum(part, ("x", "y"), 16)
    part = scatter_sum(part, "z", 8)
    part = gather_all(part, "z", 8)
    part = gather_all(part, ("x", "y"), 16)
    peer = swap_cores(part)
    low = jnp.where(core[0] == 0, part, peer).astype(F32).reshape(12, CH, CH)
    high = jnp.where(core[0] == 0, peer, part).astype(F32).reshape(12, CH, CH)
    return (
        grad_input.reshape(video.shape),
        high[0:9].reshape(w_spat1.shape),
        low[0:9].reshape(w_spat2.shape),
        low[9:12],
        high[9:12],
    )


def solution(mesh):
    fine = Mesh(mesh.devices.reshape(8, 4, 4, 2), ("z", "x", "y", "core"))
    frames = P(("y", "core"), ("z", "x"), None, None, None)
    return jax.shard_map(
        body,
        mesh=fine,
        in_specs=(frames, frames, P(), P(), P(), P()),
        out_specs=(frames, P(), P(), P(), P()),
        check_vma=False,
    )
```

time: 187 us -> 155 us (0.83)
  blocking collectives: 21.6 us -> 67.5 us
  waiting for transfers between devices: 59.7 us -> 23.2 us
  matrix products: 29.7 us -> 0 us
  Pallas kernels: 0 us -> 12.3 us
  local copies, waits for them, and re-layouts: 20.9 us -> 12.5 us
  other arithmetic: 10.1 us -> 2.05 us
  starting transfers between devices: 42.6 us -> 35.8 us
    all_to_all x7 -> x3, waiting for transfers between devices: 59.7 us -> 21 us  [swap_frames(): return lax.all_to_all(blocks, ('z', 'x'), 0, 0, tiled=True).reshape(PIX, CH)]
    dot_general x69 -> x0, matrix products: 29.7 us -> none  [the longest x24 12.3 us: matmul_nt(): lax.dot_general(left, right, (((1,), (1,)), ((), ())), preferred_element_...]
    all_to_all x1 -> x2, blocking collectives: 9.66 us -> 36.5 us  [scatter_sum(): arrived = lax.all_to_all(parts, axes, 0, 0, tiled=True)]
    all_to_all x1 -> x2, blocking collectives: 12 us -> 31 us  [gather_all(): return lax.all_to_all(copies, axes, 0, 0, tiled=True).reshape(-1, CH)]
    all_to_all x7 -> x3, starting transfers between devices: 42.6 us -> 23.6 us  [swap_frames(): return lax.all_to_all(blocks, ('z', 'x'), 0, 0, tiled=True).reshape(PIX, CH)]
    pallas_call x0 -> x7, Pallas kernels: none -> 12.3 us  [call(): pl.pallas_call(kernel, out_shape=[jax.ShapeDtypeStruct(shape, kind) for s...]
    ppermute x0 -> x4, starting transfers between devices: none -> 12.2 us  [swap_cores(): return lax.ppermute(values, 'core', [(0, 1), (1, 0)])]
    slice x41 -> x4, local copies, waits for them, and re-layouts: 14.7 us -> 4.97 us  [the longest x1 1.56 us: body(): low[0:9].reshape(w_spat2.shape)]
  transfers between devices with their start and end apart: 7 -> 7, of which waited for: 6 -> 5; matrix products, arithmetic and copies ran while one was open for 14% -> 0% of each run, Pallas kernels for 0% -> 4%
where the time goes in v2:
time: 155 us; the launch traced here: 154 us
  blocking collectives  67.5 us (44%)
  starting transfers between devices  35.8 us (23%)
  waiting for transfers between devices  23.2 us (15%)
  local copies, waits for them, and re-layouts  12.5 us (8%)
  Pallas kernels  12.3 us (8%)
  other arithmetic  2.05 us (1%)
    all_to_all x2, blocking collectives, scatter_sum(): arrived = lax.all_to_all(parts, axes, 0, 0, tiled=True)  36.5 us
    all_to_all x2, blocking collectives, gather_all(): return lax.all_to_all(copies, axes, 0, 0, tiled=True).reshape(-1, CH)  31 us
    all_to_all x3, starting transfers between devices, swap_frames(): return lax.all_to_all(blocks, ('z', 'x'), 0, 0, tiled=True).reshape(PIX, CH)  23.6 us
    all_to_all x3, waiting for transfers between devices, swap_frames(): return lax.all_to_all(blocks, ('z', 'x'), 0, 0, tiled=True).reshape(PIX, CH)  21 us
    pallas_call x7, Pallas kernels, call(): pl.pallas_call(kernel, out_shape=[jax.ShapeDtypeStruct(shape, kind) for s...  12.3 us
    ppermute x4, starting transfers between devices, swap_cores(): return lax.ppermute(values, 'core', [(0, 1), (1, 0)])  12.2 us
    unnamed x28, local copies, waits for them, and re-layouts  7.4 us
  transfers between devices with their start and end apart: 7, of which 5 were waited for; matrix products, arithmetic and copies ran while one was open for 0% of the time, Pallas kernels for 4%

profile of v2, /device:TPU:1, one launch (start us, length us, event | category | flops | bytes accessed | tf_op | source)
XLA Modules:
  0.0 154.1 jit_solution(8235376425829410843)
XLA Ops:
  0.6 11.9 %all-to-all-start.1 = ((bf16[32,16,256]{2,1,0:T(8,128)(2,1)}), bf16[32,16,256]{2,1,0:T(8,128)(2,1)S(1)}, u32[]{:S(2)}, u32[]{:S(2)}) async-start(bf16[32,16,256]{2,1,0:T(8,128)(2,1)} %bitcast.41), calls=%async_computation.1 | async-start | bytes 524288 | tf_op jit(solution)/shard_map/all_to_all | solution.py:208
  12.5 1.3 copy-done
  13.8 1.3 copy-done.3
  15.1 0.9 copy-done.6
  16.0 3.5 %shard_map.101 = (bf16[512,256]{1,0:T(8,128)(2,1)}, f32[512,256]{1,0:T(8,128)S(1)}, f32[512,256]{1,0:T(8,128)S(1)}, bf16[512,256]{1,0:T(8,128)(2,1)S(1)}, bf16[512,256]{1,0:T(8,128)(2,1)S(1)}) custom-call(s32[1]{0:T(128)} %bitcast.core, bf16[512,256]{1,0:T(8,128)(2,1)S(1)} %bitcast.33, bf16[2304,256]{1,0:T(8,128)(2,1)S(1)} %bitcast.30, ...), custom_call_target="tpu_custom_call" | custom-call | flops 1207959552 | bytes 2621444 | tf_op jit(solution)/shard_map/pallas_call | solution.py:37
  19.5 0.7 copy-done.7
  20.3 0.7 copy-done.12
  21.0 2.8 %all-to-all-done.1 = bf16[32,16,256]{2,1,0:T(8,128)(2,1)S(1)} async-done(((bf16[32,16,256]{2,1,0:T(8,128)(2,1)}), bf16[32,16,256]{2,1,0:T(8,128)(2,1)S(1)}, u32[]{:S(2)}, u32[]{:S(2)}) %all-to-all-start.1) | async-done | bytes 262176 | tf_op jit(solution)/shard_map/all_to_all | solution.py:208
  23.7 6.6 %all-to-all-start = ((bf16[32,16,256]{2,1,0:T(8,128)(2,1)}), bf16[32,16,256]{2,1,0:T(8,128)(2,1)}, u32[]{:S(2)}, u32[]{:S(2)}) async-start(bf16[32,16,256]{2,1,0:T(8,128)(2,1)} %bitcast.4), calls=%async_computation | async-start | bytes 524288 | tf_op jit(solution)/shard_map/all_to_all | solution.py:208
  30.7 10.1 %all-to-all-done = bf16[32,16,256]{2,1,0:T(8,128)(2,1)} async-done(((bf16[32,16,256]{2,1,0:T(8,128)(2,1)}), bf16[32,16,256]{2,1,0:T(8,128)(2,1)}, u32[]{:S(2)}, u32[]{:S(2)}) %all-to-all-start) | async-done | bytes 262176 | tf_op jit(solution)/shard_map/all_to_all | solution.py:208
  40.9 1.0 copy-done.5
  41.9 2.9 %shard_map.103 = (bf16[512,256]{1,0:T(8,128)(2,1)}, bf16[2,512,256]{2,1,0:T(8,128)(2,1)S(1)}, bf16[2,512,256]{2,1,0:T(8,128)(2,1)S(1)}) custom-call(s32[1]{0:T(128)} %bitcast.core, bf16[512,256]{1,0:T(8,128)(2,1)} %bitcast.5.act, bf16[512,256]{1,0:T(8,128)(2,1)S(1)} %bitcast.27, f32[512,256]{1,0:T(8,128)S(1)} %shard_map.102.back, bf16[768,256]{1,0:T(8,128)(2,1)S(1)} %bitcast.32), custom_call_target="tpu_custom_call" | custom-call | flops 402653184 | bytes 1441796 | tf_op jit(solution)/shard_map/pallas_call | solution.py:37
  44.7 0.8 copy-done.10
  45.5 5.1 %all-to-all-start.2 = ((bf16[32,16,256]{2,1,0:T(8,128)(2,1)}), bf16[32,16,256]{2,1,0:T(8,128)(2,1)S(1)}, u32[]{:S(2)}, u32[]{:S(2)}) async-start(bf16[32,16,256]{2,1,0:T(8,128)(2,1)} %bitcast.10), calls=%async_computation.2 | async-start | bytes 524288 | tf_op jit(solution)/shard_map/all_to_all | solution.py:208
  50.7 2.1 %collective-permute-start.2 = (bf16[2,512,256]{2,1,0:T(8,128)(2,1)S(1)}, bf16[2,512,256]{2,1,0:T(8,128)(2,1)S(1)}, u32[]{:S(2)}, u32[]{:S(2)}) collective-permute-start(bf16[2,512,256]{2,1,0:T(8,128)(2,1)S(1)} %get-tuple-element.26), channel_id=1, source_target_pairs={{0,1},{1,0},{2,3},{3,2},{4,5},{5,4},{6,7},{7,6},{8,9},{9,8},{10,11... | collective-permute-start | bytes 1572872 | tf_op jit(solution)/shard_map/ppermute | solution.py:203
  52.9 8.1 %all-to-all-done.2 = bf16[32,16,256]{2,1,0:T(8,128)(2,1)S(1)} async-done(((bf16[32,16,256]{2,1,0:T(8,128)(2,1)}), bf16[32,16,256]{2,1,0:T(8,128)(2,1)S(1)}, u32[]{:S(2)}, u32[]{:S(2)}) %all-to-all-start.2) | async-done | bytes 262176 | tf_op jit(solution)/shard_map/all_to_all | solution.py:208
  61.1 0.9 shard_map.104
  61.9 0.7 copy-done.8
  62.6 3.8 %collective-permute-start.1 = (bf16[512,256]{1,0:T(8,128)(2,1)S(1)}, bf16[512,256]{1,0:T(8,128)(2,1)S(1)}, u32[]{:S(2)}, u32[]{:S(2)}) collective-permute-start(bf16[512,256]{1,0:T(8,128)(2,1)S(1)} %get-tuple-element.24), channel_id=1, source_target_pairs={{0,1},{1,0},{2,3},{3,2},{4,5},{5,4},{6,7},{7,6},{8,9},{9,8},{10,11... | collective-permute-start | bytes 786440 | tf_op jit(solution)/shard_map/ppermute | solution.py:203
  67.5 2.4 %shard_map.107 = bf16[3072,256]{1,0:T(8,128)(2,1)S(1)} custom-call(bf16[512,256]{1,0:T(8,128)(2,1)S(1)} %copy-done.13, bf16[512,256]{1,0:T(8,128)(2,1)} %collective-permute-done.recv_x, bf16[512,256]{1,0:T(8,128)(2,1)S(1)} %get-tuple-element.23.keep_g, bf16[512,256]{1,0:T(8,128)(2,1)S(1)} %collective-permute-done.1.recv_g, ...), custom_call_target="tpu_custom_call" | custom-call | flops 1207959552 | bytes 1441792 | tf_op jit(solution)/shard_map/pallas_call | solution.py:37
  70.0 26.4 %all_to_all.35 = bf16[16,192,256]{2,1,0:T(8,128)(2,1)S(1)} all-to-all(bf16[16,192,256]{2,1,0:T(8,128)(2,1)S(1)} %bitcast.23), channel_id=1, replica_groups=mesh['z'=8,'x'=4,'y'=4,'core'=2] {'x','y'}, dimensions={0} | all-to-all | bytes 3145728 | tf_op jit(solution)/shard_map/all_to_all | solution.py:213
  96.6 10.1 %all_to_all.36 = bf16[8,24,256]{2,1,0:T(8,128)(2,1)S(1)} all-to-all(bf16[8,24,256]{2,1,0:T(8,128)(2,1)S(1)} %bitcast.39), channel_id=1, replica_groups=mesh['z'=8,'x'=4,'y'=4,'core'=2] {'z'}, dimensions={0} | all-to-all | bytes 196608 | tf_op jit(solution)/shard_map/all_to_all | solution.py:213
  106.7 10.1 %all_to_all.37 = bf16[8,24,256]{2,1,0:T(8,128)(2,1)S(1)} all-to-all(bf16[8,24,256]{2,1,0:T(8,128)(2,1)S(1)} %broadcast_in_dim.6), channel_id=1, replica_groups=mesh['z'=8,'x'=4,'y'=4,'core'=2] {'z'}, dimensions={0} | all-to-all | bytes 196608 | tf_op jit(solution)/shard_map/all_to_all | solution.py:219
  117.0 20.9 %all_to_all.38 = bf16[16,192,256]{2,1,0:T(8,128)(2,1)S(1)} all-to-all(bf16[16,192,256]{2,1,0:T(8,128)(2,1)S(1)} %broadcast_in_dim.15), channel_id=1, replica_groups=mesh['z'=8,'x'=4,'y'=4,'core'=2] {'x','y'}, dimensions={0} | all-to-all | bytes 3145728 | tf_op jit(solution)/shard_map/all_to_all | solution.py:219
  137.9 6.2 %collective-permute-start.3 = (bf16[3072,256]{1,0:T(8,128)(2,1)S(1)}, bf16[3072,256]{1,0:T(8,128)(2,1)}, u32[]{:S(2)}, u32[]{:S(2)}) collective-permute-start(bf16[3072,256]{1,0:T(8,128)(2,1)S(1)} %bitcast.34), channel_id=1, source_target_pairs={{0,1},{1,0},{2,3},{3,2},{4,5},{5,4},{6,7},{7,6},{8,9},{9,8},{10,11... | collective-permute-start | bytes 4718600 | tf_op jit(solution)/shard_map/ppermute | solution.py:203
  144.1 1.5 shard_map.105
  145.6 1.6 %collective-permute-done.3 = bf16[3072,256]{1,0:T(8,128)(2,1)} collective-permute-done((bf16[3072,256]{1,0:T(8,128)(2,1)S(1)}, bf16[3072,256]{1,0:T(8,128)(2,1)}, u32[]{:S(2)}, u32[]{:S(2)}) %collective-permute-start.3) | collective-permute-done | bytes 1572896 | tf_op jit(solution)/shard_map/ppermute | solution.py:203
  147.3 1.8 %select_convert_fusion = (f32[3072,256]{1,0:T(8,128)S(1)}, f32[3072,256]{1,0:T(8,128)S(1)}) fusion(bf16[3072,256]{1,0:T(8,128)(2,1)} %collective-permute-done.3, pred[]{:T(512)S(6)} %eq.4, bf16[16,192,256]{2,1,0:T(8,128)(2,1)S(1)} %all_to_all.38), kind=kLoop, calls=%fused_computation | loop fusion | flops 3145728 | bytes 9437185 | tf_op jit(solution)/shard_map/convert_element_type | solution.py:267
  149.1 0.9 slice.28
  150.0 1.6 %slice.27 = f32[2304,256]{1,0:T(8,128)} slice(f32[3072,256]{1,0:T(8,128)S(1)} %get-tuple-element.27), slice={[0:2304], [0:256]} | slice | bytes 4718592 | tf_op jit(solution)/shard_map/slice | solution.py:272
  151.6 0.9 slice.29
  152.5 1.6 %slice.26 = f32[2304,256]{1,0:T(8,128)} slice(f32[3072,256]{1,0:T(8,128)S(1)} %get-tuple-element.28), slice={[0:2304], [0:256]} | slice | bytes 4718592 | tf_op jit(solution)/shard_map/slice | solution.py:271
  (30 shorter events, 2.1 us)
Async XLA Ops:
  0.6 23.1 %all-to-all-start.1 = ((bf16[32,16,256]{2,1,0:T(8,128)(2,1)}), bf16[32,16,256]{2,1,0:T(8,128)(2,1)S(1)}, u32[]{:S(2)}, u32[]{:S(2)}) async-start(bf16[32,16,256]{2,1,0:T(8,128)(2,1)} %bitcast.41), calls=%async_computation.1 | async-start | bytes 524288 | tf_op jit(solution)/shard_map/all_to_all | solution.py:208
  12.5 1.3 copy-start
  13.8 1.3 copy-start.3
  15.1 0.9 copy-start.6
  16.0 14.3 %copy-start.2 = (bf16[3,256,256]{2,1,0:T(8,128)(2,1)S(1)}, bf16[3,256,256]{2,1,0:T(8,128)(2,1)}, u32[]{:S(2)}) copy-start(bf16[3,256,256]{2,1,0:T(8,128)(2,1)} %param.11) | copy-start | bytes 1179652
  19.5 0.7 copy-start.7
  20.2 0.7 copy-start.12
  23.7 17.2 %all-to-all-start = ((bf16[32,16,256]{2,1,0:T(8,128)(2,1)}), bf16[32,16,256]{2,1,0:T(8,128)(2,1)}, u32[]{:S(2)}, u32[]{:S(2)}) async-start(bf16[32,16,256]{2,1,0:T(8,128)(2,1)} %bitcast.4), calls=%async_computation | async-start | bytes 524288 | tf_op jit(solution)/shard_map/all_to_all | solution.py:208
  30.3 30.7 %copy-start.1 = (bf16[3,3,256,256]{3,2,1,0:T(8,128)(2,1)S(1)}, bf16[3,3,256,256]{3,2,1,0:T(8,128)(2,1)}, u32[]{:S(2)}) copy-start(bf16[3,3,256,256]{3,2,1,0:T(8,128)(2,1)} %param.9) | copy-start | bytes 3538948
  40.9 1.0 copy-start.5
  44.7 0.8 copy-start.10
  45.5 15.5 %all-to-all-start.2 = ((bf16[32,16,256]{2,1,0:T(8,128)(2,1)}), bf16[32,16,256]{2,1,0:T(8,128)(2,1)S(1)}, u32[]{:S(2)}, u32[]{:S(2)}) async-start(bf16[32,16,256]{2,1,0:T(8,128)(2,1)} %bitcast.10), calls=%async_computation.2 | async-start | bytes 524288 | tf_op jit(solution)/shard_map/all_to_all | solution.py:208
  50.7 15.7 %collective-permute-start.2 = (bf16[2,512,256]{2,1,0:T(8,128)(2,1)S(1)}, bf16[2,512,256]{2,1,0:T(8,128)(2,1)S(1)}, u32[]{:S(2)}, u32[]{:S(2)}) collective-permute-start(bf16[2,512,256]{2,1,0:T(8,128)(2,1)S(1)} %get-tuple-element.26), channel_id=1, source_target_pairs={{0,1},{1,0},{2,3},{3,2},{4,5},{5,4},{6,7},{7,6},{8,9},{9,8},{10,11... | collective-permute-start | bytes 1572872 | tf_op jit(solution)/shard_map/ppermute | solution.py:203
  52.8 14.2 %collective-permute-start = (bf16[512,256]{1,0:T(8,128)(2,1)}, bf16[512,256]{1,0:T(8,128)(2,1)}, u32[]{:S(2)}, u32[]{:S(2)}) collective-permute-start(bf16[512,256]{1,0:T(8,128)(2,1)} %copy-done.7), channel_id=1, source_target_pairs={{0,1},{1,0},{2,3},{3,2},{4,5},{5,4},{6,7},{7,6},{8,9},{9,8},{10,11... | collective-permute-start | bytes 786440 | tf_op jit(solution)/shard_map/ppermute | solution.py:203
  61.1 5.3 %copy-start.11 = (bf16[2,512,256]{2,1,0:T(8,128)(2,1)S(1)}, bf16[2,512,256]{2,1,0:T(8,128)(2,1)}, u32[]{:S(2)}) copy-start(bf16[2,512,256]{2,1,0:T(8,128)(2,1)} %copy-done.10) | copy-start | bytes 1572868
  61.1 6.5 %copy-start.13 = (bf16[512,256]{1,0:T(8,128)(2,1)S(1)}, bf16[512,256]{1,0:T(8,128)(2,1)}, u32[]{:S(2)}) copy-start(bf16[512,256]{1,0:T(8,128)(2,1)} %copy-done.12) | copy-start | bytes 786436
  61.9 0.7 copy-start.8
  62.6 4.9 %collective-permute-start.1 = (bf16[512,256]{1,0:T(8,128)(2,1)S(1)}, bf16[512,256]{1,0:T(8,128)(2,1)S(1)}, u32[]{:S(2)}, u32[]{:S(2)}) collective-permute-start(bf16[512,256]{1,0:T(8,128)(2,1)S(1)} %get-tuple-element.24), channel_id=1, source_target_pairs={{0,1},{1,0},{2,3},{3,2},{4,5},{5,4},{6,7},{7,6},{8,9},{9,8},{10,11... | collective-permute-start | bytes 786440 | tf_op jit(solution)/shard_map/ppermute | solution.py:203
  116.9 27.2 %copy-start.4 = (bf16[3,3,256,256]{3,2,1,0:T(8,128)(2,1)S(1)}, bf16[3,3,256,256]{3,2,1,0:T(8,128)(2,1)}, u32[]{:S(2)}) copy-start(bf16[3,3,256,256]{3,2,1,0:T(8,128)(2,1)} %param.8) | copy-start | bytes 3538948
  116.9 27.2 %copy-start.9 = (bf16[512,256]{1,0:T(8,128)(2,1)S(1)}, bf16[512,256]{1,0:T(8,128)(2,1)}, u32[]{:S(2)}) copy-start(bf16[512,256]{1,0:T(8,128)(2,1)} %copy-done.8) | copy-start | bytes 786436
  137.9 9.4 %collective-permute-start.3 = (bf16[3072,256]{1,0:T(8,128)(2,1)S(1)}, bf16[3072,256]{1,0:T(8,128)(2,1)}, u32[]{:S(2)}, u32[]{:S(2)}) collective-permute-start(bf16[3072,256]{1,0:T(8,128)(2,1)S(1)} %bitcast.34), channel_id=1, source_target_pairs={{0,1},{1,0},{2,3},{3,2},{4,5},{5,4},{6,7},{7,6},{8,9},{9,8},{10,11... | collective-permute-start | bytes 4718600 | tf_op jit(solution)/shard_map/ppermute | solution.py:203

commit v3 on v2

--- a/solution.py
+++ b/solution.py
@@ -1,3 +1,4 @@
+import functools
 import math
 
 import jax
@@ -17,6 +18,9 @@
 F32 = jnp.float32
 VMEM = pl.BlockSpec(memory_space=pltpu.VMEM)
 SMEM = pl.BlockSpec(memory_space=pltpu.SMEM)
+HBM = pl.BlockSpec(memory_space=pl.ANY)
+QUARTER = 384
+SIXTEENTH = 96
 
 
 def dot_nn(left, right):
@@ -31,14 +35,17 @@
     return lax.dot_general(left, right, (((0,), (0,)), ((), ())), preferred_element_type=F32)
 
 
-def call(kernel, outs, ins, scratch=(), flops=0):
+def call(kernel, outs, ins, scratch=(), flops=0, out_space=VMEM, aliases=None):
     specs = [SMEM if value.dtype == jnp.int32 else VMEM for value in ins]
+    for at in aliases or {}:
+        specs[at] = out_space
     moved = sum(value.size * value.dtype.itemsize for value in ins)
     return pl.pallas_call(
         kernel,
         out_shape=[jax.ShapeDtypeStruct(shape, kind) for shape, kind in outs],
         in_specs=specs,
-        out_specs=[VMEM] * len(outs),
+        out_specs=[out_space] * len(outs),
+        input_output_aliases=aliases or {},
         scratch_shapes=list(scratch),
         cost_estimate=pl.CostEstimate(flops=flops, bytes_accessed=moved, transcendentals=0),
         compiler_params=pltpu.CompilerParams(vmem_limit_bytes=40 * 1024 * 1024),
@@ -87,19 +94,19 @@
     return act, sigma * (1.0 + pre * (1.0 - sigma))
 
 
-def forward_kernel(core, video, w1, w2, act2, slope1, slope2, keep, send, wide):
+def forward_kernel(pos, video, w1, w2, act2, slope1, slope2, keep, send, wide):
     values = video[...]
     fill_windows(wide, values)
     act, slope = silu_pair(conv_from(wide, w1))
     slope1[...] = slope
     first = act.astype(BF)
 
-    @pl.when(core[0] == 0)
+    @pl.when(pos[0] == 0)
     def _():
         keep[...] = first
         send[...] = values
 
-    @pl.when(core[0] != 0)
+    @pl.when(pos[0] != 0)
     def _():
         keep[...] = values
         send[...] = first
@@ -124,7 +131,7 @@
     back[...] = ahead_sum(padded, wt2)
 
 
-def time_kernel(core, act, cot, back, wt1, act_back, keep, send, padded):
+def time_kernel(pos, act, cot, back, wt1, act_back, keep, send, padded):
     padded[0 : 2 * COLS, :] = jnp.zeros((2 * COLS, CH), BF)
     padded[2 * COLS : PAD, :] = act[...]
     pre = None
@@ -136,14 +143,14 @@
     time_act = value.astype(BF)
     time_grad = (back[...] * slope).astype(BF)
 
-    @pl.when(core[0] == 0)
+    @pl.when(pos[0] == 0)
     def _():
         keep[0] = act[...]
         keep[1] = time_grad
         send[0] = time_act
         send[1] = cot[...]
 
-    @pl.when(core[0] != 0)
+    @pl.when(pos[0] != 0)
     def _():
         keep[0] = time_act
         keep[1] = cot[...]
@@ -163,24 +170,30 @@
         out[step * CH : (step + 1) * CH, :] = (total * SCALE).astype(BF)
 
 
-def backward_kernel(core, act_back, slope1, slope2, w2, first_grad, keep, send, wide):
+def backward_kernel(pos, act_back, slope1, slope2, w2, first_grad, keep, send, wide):
     second = (act_back[...].astype(F32) * slope2[...]).astype(BF)
     fill_windows(wide, second)
     first = (back_from(wide, w2) * slope1[...]).astype(BF)
     first_grad[...] = first
 
-    @pl.when(core[0] == 0)
+    @pl.when(pos[0] == 0)
     def _():
         keep[...] = second
         send[...] = first
 
-    @pl.when(core[0] != 0)
+    @pl.when(pos[0] != 0)
     def _():
         keep[...] = first
         send[...] = second
 
 
-def space_weights_kernel(keep_x, recv_x, keep_g, recv_g, time_part, out, wide, other):
+def chunk(at, rows):
+    return pl.ds(pl.multiple_of(at * rows, rows), rows)
+
+
+def space_weights_kernel(pos, keep_x, recv_x, keep_g, recv_g, time_part, *rest):
+    first, second = rest[0:4], rest[4:8]
+    out, wide, other = rest[8:]
     fill_windows(wide, keep_x[...])
     fill_windows(other, recv_x[...])
     for tap in range(3):
@@ -192,6 +205,70 @@
             at = (tap * 3 + side) * CH
             out[at : at + CH, :] = (total * SCALE).astype(BF)
     out[9 * CH : 12 * CH, :] = time_part[...]
+    for step in range(4):
+        first[step][...] = out[chunk((pos[2] + step) & 3, QUARTER), :]
+        second[step][...] = out[chunk(4 + ((pos[1] + step) & 3), QUARTER), :]
+
+
+def add_up(parts):
+    total = parts[0][...].astype(F32)
+    for part in parts[1:]:
+        total = total + part[...].astype(F32)
+    return total.astype(BF)
+
+
+def add_quarters_kernel(pos, *refs):
+    first, second = refs[8:12], refs[12:16]
+    low, high = refs[16:]
+    low[...] = add_up(refs[0:4])
+    high[...] = add_up(refs[4:8])
+    for step in range(4):
+        first[step][...] = low[chunk((pos[1] + step) & 3, SIXTEENTH), :]
+        second[step][...] = high[chunk((pos[2] + step) & 3, SIXTEENTH), :]
+
+
+def add_sixteenths_kernel(*refs):
+    out = refs[8]
+    out[0:SIXTEENTH, :] = add_up(refs[0:4])
+    out[SIXTEENTH : 2 * SIXTEENTH, :] = add_up(refs[4:8])
+
+
+def join_sixteenths_kernel(pos, *refs):
+    low, high = refs[8:]
+    for step in range(4):
+        low[chunk((pos[1] - step) & 3, SIXTEENTH), :] = refs[step][...]
+        high[chunk((pos[2] - step) & 3, SIXTEENTH), :] = refs[4 + step][...]
+
+
+def join_quarters_kernel(pos, *refs):
+    out = refs[8]
+    for step in range(4):
+        out[chunk((pos[2] - step) & 3, QUARTER), :] = refs[step][...]
+        out[chunk(4 + ((pos[1] - step) & 3), QUARTER), :] = refs[4 + step][...]
+
+
+def spread_kernel(owner, pos, half, *refs):
+    spat1, spat2, time1, time2, stage, sems = refs[-6:]
+    targets = [(spat2, time1), (spat1, time2)]
+
+    def copies(at):
+        space, time = targets[at]
+        rows = 3 * CH
+        for piece in range(3):
+            part = pl.ds(piece * rows, rows)
+            yield pltpu.make_async_copy(stage.at[part], space.at[part], sems.at[piece])
+        yield pltpu.make_async_copy(stage.at[pl.ds(3 * rows, rows)], time, sems.at[3])
+
+    for at in range(2):
+
+        @pl.when((pos[0] ^ owner) == at)
+        def _():
+            for piece, copy in enumerate(copies(at)):
+                rows = slice(piece * 3 * CH, (piece + 1) * 3 * CH)
+                stage[rows, :] = half[rows, :].astype(F32)
+                copy.start()
+            for copy in copies(at):
+                copy.wait()
 
 
 def input_kernel(first_grad, w1, out, wide):
@@ -208,19 +285,21 @@
     return lax.all_to_all(blocks, ("z", "x"), 0, 0, tiled=True).reshape(PIX, CH)
 
 
-def scatter_sum(values, axes, count):
-    parts = values.reshape(count, -1, CH)
-    arrived = lax.all_to_all(parts, axes, 0, 0, tiled=True)
-    return jnp.sum(arrived.astype(F32), axis=0).astype(BF)
-
-
-def gather_all(values, axes, count):
-    copies = jnp.broadcast_to(values[None], (count,) + values.shape)
-    return lax.all_to_all(copies, axes, 0, 0, tiled=True).reshape(-1, CH)
+def ring(values, axis, step):
+    return lax.ppermute(values, axis, [(at, (at + step) % 4) for at in range(4)])
+
+
+def exchange(own, axis):
+    return [own[0]] + [ring(own[step], axis, step) for step in (1, 3, 2)]
+
+
+def ordered(parts):
+    return [parts[0], parts[1], parts[3], parts[2]]
 
 
 def body(video, cotangent, w_spat1, w_spat2, w_time1, w_time2):
-    core = lax.axis_index("core").astype(jnp.int32).reshape(1)
+    axes = ("core", "x", "y", "z")
+    pos = jnp.stack([lax.axis_index(axis) for axis in axes]).astype(jnp.int32)
     w1, w2, wt1, wt2 = (w.reshape(-1, CH) for w in (w_spat1, w_spat2, w_time1, w_time2))
     slab, slab32 = ((PIX, CH), BF), ((PIX, CH), F32)
     pair = ((2, PIX, CH), BF)
@@ -231,7 +310,7 @@
     second_act, slope1, slope2, keep_x, send_x = call(
         forward_kernel,
         [slab, slab32, slab32, slab, slab],
-        (core, video.reshape(PIX, CH), w1, w2),
+        (pos, video.reshape(PIX, CH), w1, w2),
         [wide],
         2 * conv_flops,
     )
@@ -239,7 +318,7 @@
     recv_x = swap_cores(send_x)
     (time_back,) = call(time_back_kernel, [slab32], (cot, wt2), [tall], time_flops)
     act_back, keep_t, send_t = call(
-        time_kernel, [slab, pair, pair], (core, act, cot, time_back, wt1), [tall], 2 * time_flops
+        time_kernel, [slab, pair, pair], (pos, act, cot, time_back, wt1), [tall], 2 * time_flops
     )
     act_back = swap_frames(act_back)
     recv_t = swap_cores(send_t)
@@ -247,31 +326,56 @@
         time_weights_kernel, [((3 * CH, CH), BF)], (keep_t, recv_t), (), 2 * time_flops
     )
     first_grad, keep_g, send_g = call(
-        backward_kernel, [slab, slab, slab], (core, act_back, slope1, slope2, w2), [wide], conv_flops
+        backward_kernel, [slab, slab, slab], (pos, act_back, slope1, slope2, w2), [wide], conv_flops
     )
     recv_g = swap_cores(send_g)
-    (part,) = call(
+    quarter, sixteenth = ((QUARTER, CH), BF), ((SIXTEENTH, CH), BF)
+    parts = call(
         space_weights_kernel,
-        [((12 * CH, CH), BF)],
-        (keep_x, recv_x, keep_g, recv_g, time_part),
-        [wide, wide],
+        [quarter] * 8,
+        (pos, keep_x, recv_x, keep_g, recv_g, time_part),
+        [pltpu.VMEM((12 * CH, CH), BF), wide, wide],
         2 * conv_flops,
     )
+    parts = ordered(exchange(parts[0:4], "y")) + ordered(exchange(parts[4:8], "x"))
     (grad_input,) = call(input_kernel, [slab], (first_grad, w1), [wide], conv_flops)
-
-    part = scatter_sum(part, ("x", "y"), 16)
-    part = scatter_sum(part, "z", 8)
-    part = gather_all(part, "z", 8)
-    part = gather_all(part, ("x", "y"), 16)
+    parts = call(
+        add_quarters_kernel,
+        [sixteenth] * 8,
+        (pos, *parts),
+        [pltpu.VMEM((QUARTER, CH), BF), pltpu.VMEM((QUARTER, CH), BF)],
+    )
+    parts = ordered(exchange(parts[0:4], "x")) + ordered(exchange(parts[4:8], "y"))
+    (part,) = call(add_sixteenths_kernel, [((2 * SIXTEENTH, CH), BF)], tuple(parts))
+    part = lax.all_to_all(part.reshape(8, -1, CH), "z", 0, 0, tiled=True)
+    part = jnp.sum(part.astype(F32), axis=0).astype(BF)
+    part = lax.all_to_all(jnp.broadcast_to(part[None], (8,) + part.shape), "z", 0, 0, tiled=True)
+    part = part.reshape(2 * SIXTEENTH, CH)
+    low, high = part[0:SIXTEENTH], part[SIXTEENTH:]
+    parts = ordered(exchange([low] * 4, "x")) + ordered(exchange([high] * 4, "y"))
+    low, high = call(join_sixteenths_kernel, [quarter] * 2, (pos, *parts))
+    parts = ordered(exchange([low] * 4, "y")) + ordered(exchange([high] * 4, "x"))
+    (part,) = call(join_quarters_kernel, [((12 * CH, CH), BF)], (pos, *parts))
     peer = swap_cores(part)
-    low = jnp.where(core[0] == 0, part, peer).astype(F32).reshape(12, CH, CH)
-    high = jnp.where(core[0] == 0, peer, part).astype(F32).reshape(12, CH, CH)
+    space, time = ((9 * CH, CH), F32), ((3 * CH, CH), F32)
+    grads = [space, space, time, time]
+    scratch = [pltpu.VMEM((12 * CH, CH), F32), pltpu.SemaphoreType.DMA((4,))]
+    outs = call(functools.partial(spread_kernel, 0), grads, (pos, part), scratch, 0, HBM)
+    outs = call(
+        functools.partial(spread_kernel, 1),
+        grads,
+        (pos, peer, *outs),
+        scratch,
+        0,
+        HBM,
+        {2: 0, 3: 1, 4: 2, 5: 3},
+    )
     return (
         grad_input.reshape(video.shape),
-        high[0:9].reshape(w_spat1.shape),
-        low[0:9].reshape(w_spat2.shape),
-        low[9:12],
-        high[9:12],
+        outs[0].reshape(w_spat1.shape),
+        outs[1].reshape(w_spat2.shape),
+        outs[2].reshape(w_time1.shape),
+        outs[3].reshape(w_time2.shape),
     )
 
 

time: 155 us -> 163 us (1.052)
  blocking collectives: 67.5 us -> 20.1 us
  starting transfers between devices: 35.8 us -> 67.5 us
  waiting for transfers between devices: 23.2 us -> 45.4 us
  Pallas kernels: 12.3 us -> 20.1 us
  local copies, waits for them, and re-layouts: 12.5 us -> 8.46 us
  other arithmetic: 2.05 us -> 0.1 us
    all_to_all x4 -> x2, blocking collectives: 67.5 us -> 20.1 us  [the longest x1 10.2 us: body(): part = lax.all_to_all(part.reshape(8, -1, CH), 'z', 0, 0, tiled=True)]
    ppermute x0 -> x24, starting transfers between devices: none -> 25.7 us  [ring(): lax.ppermute(values, axis, [(at, (at + step) % 4) for at in range(4)])]
    ppermute x0 -> x24, waiting for transfers between devices: none -> 24.5 us  [ring(): lax.ppermute(values, axis, [(at, (at + step) % 4) for at in range(4)])]
    pallas_call x7 -> x13, Pallas kernels: 12.3 us -> 20.1 us  [call(): pl.pallas_call(kernel, out_shape=[jax.ShapeDtypeStruct(shape, kind) for s...]
    ppermute x4, starting transfers between devices: 12.2 us -> 17.5 us  [swap_cores(): return lax.ppermute(values, 'core', [(0, 1), (1, 0)])]
    slice x4 -> x1, local copies, waits for them, and re-layouts: 4.97 us -> 0.01 us  [body(): low, high = (part[0:SIXTEENTH], part[SIXTEENTH:])]
    convert_element_type x1 -> x0, other arithmetic: 1.82 us -> none  [body(): low = jnp.where(core[0] == 0, part, peer).astype(F32).reshape(12, CH, CH)]
    unnamed x28 -> x26, local copies, waits for them, and re-layouts: 7.4 us -> 8.44 us
  transfers between devices with their start and end apart: 7 -> 31, of which waited for: 5 -> 20; matrix products, arithmetic and copies ran while one was open for 0% -> 0% of each run, Pallas kernels for 4% -> 6%
where the time goes in v3:
time: 163 us
  starting transfers between devices  67.5 us (41%)
  waiting for transfers between devices  45.4 us (28%)
  Pallas kernels  20.1 us (12%)
  blocking collectives  20.1 us (12%)
  local copies, waits for them, and re-layouts  8.46 us (5%)
    ppermute x24, starting transfers between devices, ring(): lax.ppermute(values, axis, [(at, (at + step) % 4) for at in range(4)])  25.7 us
    ppermute x24, waiting for transfers between devices, ring(): lax.ppermute(values, axis, [(at, (at + step) % 4) for at in range(4)])  24.5 us
    all_to_all x3, starting transfers between devices, swap_frames(): return lax.all_to_all(blocks, ('z', 'x'), 0, 0, tiled=True).reshape(PIX, CH)  24.4 us
    all_to_all x3, waiting for transfers between devices, swap_frames(): return lax.all_to_all(blocks, ('z', 'x'), 0, 0, tiled=True).reshape(PIX, CH)  20.4 us
    pallas_call x13, Pallas kernels, call(): pl.pallas_call(kernel, out_shape=[jax.ShapeDtypeStruct(shape, kind) for s...  20.1 us
    ppermute x4, starting transfers between devices, swap_cores(): return lax.ppermute(values, 'core', [(0, 1), (1, 0)])  17.5 us
    all_to_all x1, blocking collectives, body(): part = lax.all_to_all(part.reshape(8, -1, CH), 'z', 0, 0, tiled=True)  10.2 us
    all_to_all x1, blocking collectives, body(): lax.all_to_all(jnp.broadcast_to(part[None], (8,) + part.shape), 'z', 0, 0...  9.95 us
  transfers between devices with their start and end apart: 31, of which 20 were waited for; matrix products, arithmetic and copies ran while one was open for 0% of the time, Pallas kernels for 6%

profile of v3, /device:TPU:1, one launch (start us, length us, event | category | flops | bytes accessed | tf_op | source)
XLA Modules:
  0.0 162.7 jit_solution(6755349485044319915)
XLA Ops:
  0.6 11.9 %all-to-all-start.1 = ((bf16[32,16,256]{2,1,0:T(8,128)(2,1)}), bf16[32,16,256]{2,1,0:T(8,128)(2,1)S(1)}, u32[]{:S(2)}, u32[]{:S(2)}) async-start(bf16[32,16,256]{2,1,0:T(8,128)(2,1)} %bitcast.46), calls=%async_computation.1 | async-start | bytes 524288 | tf_op jit(solution)/shard_map/all_to_all | solution.py:285
  16.1 4.1 %shard_map.101 = (bf16[512,256]{1,0:T(8,128)(2,1)}, f32[512,256]{1,0:T(8,128)S(1)}, f32[512,256]{1,0:T(8,128)S(1)}, bf16[512,256]{1,0:T(8,128)(2,1)S(1)}, bf16[512,256]{1,0:T(8,128)(2,1)S(1)}) custom-call(s32[4]{0:T(128)S(1)} %pad_add_fusion.pos, bf16[512,256]{1,0:T(8,128)(2,1)S(1)} %bitcast.41, bf16[2304,256]{1,0:T(8,128)(2,1)S(1)} %bitcast.38, ...), custom_call_target="tpu_custom_call" | custom-call | flops 1207959552 | bytes 2621456 | tf_op jit(solution)/shard_map/pallas_call | solution.py:43
  21.6 2.1 %all-to-all-done.1 = bf16[32,16,256]{2,1,0:T(8,128)(2,1)S(1)} async-done(((bf16[32,16,256]{2,1,0:T(8,128)(2,1)}), bf16[32,16,256]{2,1,0:T(8,128)(2,1)S(1)}, u32[]{:S(2)}, u32[]{:S(2)}) %all-to-all-start.1) | async-done | bytes 262176 | tf_op jit(solution)/shard_map/all_to_all | solution.py:285
  23.7 7.4 %all-to-all-start = ((bf16[32,16,256]{2,1,0:T(8,128)(2,1)}), bf16[32,16,256]{2,1,0:T(8,128)(2,1)}, u32[]{:S(2)}, u32[]{:S(2)}) async-start(bf16[32,16,256]{2,1,0:T(8,128)(2,1)} %bitcast.7), calls=%async_computation | async-start | bytes 524288 | tf_op jit(solution)/shard_map/all_to_all | solution.py:285
  31.5 10.1 %all-to-all-done = bf16[32,16,256]{2,1,0:T(8,128)(2,1)} async-done(((bf16[32,16,256]{2,1,0:T(8,128)(2,1)}), bf16[32,16,256]{2,1,0:T(8,128)(2,1)}, u32[]{:S(2)}, u32[]{:S(2)}) %all-to-all-start) | async-done | bytes 262176 | tf_op jit(solution)/shard_map/all_to_all | solution.py:285
  42.6 2.9 %shard_map.103 = (bf16[512,256]{1,0:T(8,128)(2,1)}, bf16[2,512,256]{2,1,0:T(8,128)(2,1)S(1)}, bf16[2,512,256]{2,1,0:T(8,128)(2,1)S(1)}) custom-call(s32[4]{0:T(128)S(1)} %pad_add_fusion.pos, bf16[512,256]{1,0:T(8,128)(2,1)} %bitcast.8.act, bf16[512,256]{1,0:T(8,128)(2,1)S(1)} %bitcast.26, f32[512,256]{1,0:T(8,128)S(1)} %shard_map.102.back, ...), custom_call_target="tpu_custom_call" | custom-call | flops 402653184 | bytes 1441808 | tf_op jit(solution)/shard_map/pallas_call | solution.py:43
  47.1 5.1 %all-to-all-start.2 = ((bf16[32,16,256]{2,1,0:T(8,128)(2,1)}), bf16[32,16,256]{2,1,0:T(8,128)(2,1)S(1)}, u32[]{:S(2)}, u32[]{:S(2)}) async-start(bf16[32,16,256]{2,1,0:T(8,128)(2,1)} %bitcast.13), calls=%async_computation.2 | async-start | bytes 524288 | tf_op jit(solution)/shard_map/all_to_all | solution.py:285
  52.2 2.1 %collective-permute-start.2 = (bf16[2,512,256]{2,1,0:T(8,128)(2,1)}, bf16[2,512,256]{2,1,0:T(8,128)(2,1)S(1)}, u32[]{:S(2)}, u32[]{:S(2)}) collective-permute-start(bf16[2,512,256]{2,1,0:T(8,128)(2,1)} %copy-done.5), channel_id=1, source_target_pairs={{0,1},{1,0},{2,3},{3,2},{4,5},{5,4},{6,7},{7,6},{8,9},{9,8},{10,11... | collective-permute-start | bytes 1572872 | tf_op jit(solution)/shard_map/ppermute | solution.py:280
  54.5 8.2 %all-to-all-done.2 = bf16[32,16,256]{2,1,0:T(8,128)(2,1)S(1)} async-done(((bf16[32,16,256]{2,1,0:T(8,128)(2,1)}), bf16[32,16,256]{2,1,0:T(8,128)(2,1)S(1)}, u32[]{:S(2)}, u32[]{:S(2)}) %all-to-all-start.2) | async-done | bytes 262176 | tf_op jit(solution)/shard_map/all_to_all | solution.py:285
  62.6 1.4 shard_map.104
  64.0 3.8 %collective-permute-start.1 = (bf16[512,256]{1,0:T(8,128)(2,1)S(1)}, bf16[512,256]{1,0:T(8,128)(2,1)S(1)}, u32[]{:S(2)}, u32[]{:S(2)}) collective-permute-start(bf16[512,256]{1,0:T(8,128)(2,1)S(1)} %get-tuple-element.50), channel_id=1, source_target_pairs={{0,1},{1,0},{2,3},{3,2},{4,5},{5,4},{6,7},{7,6},{8,9},{9,8},{10,11... | collective-permute-start | bytes 786440 | tf_op jit(solution)/shard_map/ppermute | solution.py:280
  70.0 2.4 %shard_map.107 = (bf16[384,256]{1,0:T(8,128)(2,1)S(1)}, bf16[384,256]{1,0:T(8,128)(2,1)S(1)}, bf16[384,256]{1,0:T(8,128)(2,1)S(1)}, bf16[384,256]{1,0:T(8,128)(2...) custom-call(s32[4]{0:T(128)S(1)} %pad_add_fusion.pos, ...), custom_call_target="tpu_custom_call" | custom-call | flops 1207959552 | bytes 1441808 | tf_op jit(solution)/shard_map/pallas_call | solution.py:43
  73.8 2.6 %collective-permute-start.4 = (bf16[384,256]{1,0:T(8,128)(2,1)S(1)}, bf16[384,256]{1,0:T(8,128)(2,1)S(1)}, u32[]{:S(2)}, u32[]{:S(2)}) collective-permute-start(bf16[384,256]{1,0:T(8,128)(2,1)S(1)} %get-tuple-element.55), channel_id=1, source_target_pairs={{0,4},{2,6},{4,0},{6,2},{1,5},{3,7},{5,1},{7,3},{8,12},{10,14},{12... | collective-permute-start | bytes 589832 | tf_op jit(solution)/shard_map/ppermute | solution.py:289
  77.5 1.9 %collective-permute-start.7 = (bf16[384,256]{1,0:T(8,128)(2,1)S(1)}, bf16[384,256]{1,0:T(8,128)(2,1)S(1)}, u32[]{:S(2)}, u32[]{:S(2)}) collective-permute-start(bf16[384,256]{1,0:T(8,128)(2,1)S(1)} %get-tuple-element.59), channel_id=1, source_target_pairs={{0,16},{8,24},{16,0},{24,8},{1,17},{9,25},{17,1},{25,9},{2,18},{10... | collective-permute-start | bytes 589832 | tf_op jit(solution)/shard_map/ppermute | solution.py:289
  80.7 4.6 %collective-permute-done.4.refs_2_ = bf16[384,256]{1,0:T(8,128)(2,1)S(1)} collective-permute-done((bf16[384,256]{1,0:T(8,128)(2,1)S(1)}, bf16[384,256]{1,0:T(8,128)(2,1)S(1)}, u32[]{:S(2)}, u32[]{:S(2)}) %collective-permute-start.4) | collective-permute-done | bytes 196640 | tf_op jit(solution)/shard_map/ppermute | solution.py:289
  85.3 2.1 %collective-permute-done.7.refs_6_ = bf16[384,256]{1,0:T(8,128)(2,1)S(1)} collective-permute-done((bf16[384,256]{1,0:T(8,128)(2,1)S(1)}, bf16[384,256]{1,0:T(8,128)(2,1)S(1)}, u32[]{:S(2)}, u32[]{:S(2)}) %collective-permute-start.7) | collective-permute-done | bytes 196640 | tf_op jit(solution)/shard_map/ppermute | solution.py:289
  87.3 1.9 %collective-permute-done.8.refs_7_ = bf16[384,256]{1,0:T(8,128)(2,1)S(1)} collective-permute-done((bf16[384,256]{1,0:T(8,128)(2,1)S(1)}, bf16[384,256]{1,0:T(8,128)(2,1)S(1)}, u32[]{:S(2)}, u32[]{:S(2)}) %collective-permute-start.8) | collective-permute-done | bytes 196640 | tf_op jit(solution)/shard_map/ppermute | solution.py:289
  91.1 3.7 %collective-permute-start.10 = (bf16[96,256]{1,0:T(8,128)(2,1)S(1)}, bf16[96,256]{1,0:T(8,128)(2,1)S(1)}, u32[]{:S(2)}, u32[]{:S(2)}) collective-permute-start(bf16[96,256]{1,0:T(8,128)(2,1)S(1)} %get-tuple-element.63), channel_id=1, source_target_pairs={{0,16},{8,24},{16,0},{24,8},{1,17},{9,25},{17,1},{25,9},{2,18},{10... | collective-permute-start | bytes 147464 | tf_op jit(solution)/shard_map/ppermute | solution.py:289
  95.2 2.4 %collective-permute-start.14 = (bf16[96,256]{1,0:T(8,128)(2,1)S(1)}, bf16[96,256]{1,0:T(8,128)(2,1)S(1)}, u32[]{:S(2)}, u32[]{:S(2)}) collective-permute-start(bf16[96,256]{1,0:T(8,128)(2,1)S(1)} %get-tuple-element.68), channel_id=1, source_target_pairs={{0,6},{2,0},{4,2},{6,4},{1,7},{3,1},{5,3},{7,5},{8,14},{10,8},{12,... | collective-permute-start | bytes 147464 | tf_op jit(solution)/shard_map/ppermute | solution.py:289
  100.4 10.2 %all_to_all.25 = bf16[8,24,256]{2,1,0:T(8,128)(2,1)S(1)} all-to-all(bf16[8,24,256]{2,1,0:T(8,128)(2,1)S(1)} %bitcast.29), channel_id=1, replica_groups=mesh['z'=8,'x'=4,'y'=4,'core'=2] {'z'}, dimensions={0} | all-to-all | bytes 196608 | tf_op jit(solution)/shard_map/all_to_all | solution.py:350
  110.7 10.0 %all_to_all.26 = bf16[8,24,256]{2,1,0:T(8,128)(2,1)S(1)} all-to-all(bf16[8,24,256]{2,1,0:T(8,128)(2,1)S(1)} %broadcast_in_dim.2), channel_id=1, replica_groups=mesh['z'=8,'x'=4,'y'=4,'core'=2] {'z'}, dimensions={0} | all-to-all | bytes 196608 | tf_op jit(solution)/shard_map/all_to_all | solution.py:352
  120.9 2.7 %collective-permute-start.16 = (bf16[96,256]{1,0:T(8,128)(2,1)S(1)}, bf16[96,256]{1,0:T(8,128)(2,1)S(1)}, u32[]{:S(2)}, u32[]{:S(2)}) collective-permute-start(bf16[96,256]{1,0:T(8,128)(2,1)S(1)} %bitcast.35), channel_id=1, source_target_pairs={{0,16},{8,24},{16,0},{24,8},{1,17},{9,25},{17,1},{25,9},{2,18},{10... | collective-permute-start | bytes 147464 | tf_op jit(solution)/shard_map/ppermute | solution.py:289
  123.6 2.2 %collective-permute-start.20 = (bf16[96,256]{1,0:T(8,128)(2,1)S(1)}, bf16[96,256]{1,0:T(8,128)(2,1)S(1)}, u32[]{:S(2)}, u32[]{:S(2)}) collective-permute-start(bf16[96,256]{1,0:T(8,128)(2,1)S(1)} %bitcast.30), channel_id=1, source_target_pairs={{0,6},{2,0},{4,2},{6,4},{1,7},{3,1},{5,3},{7,5},{8,14},{10,8},{12,... | collective-permute-start | bytes 147464 | tf_op jit(solution)/shard_map/ppermute | solution.py:289
  127.7 2.8 %collective-permute-done.19.refs_6_ = bf16[96,256]{1,0:T(8,128)(2,1)S(1)} collective-permute-done((bf16[96,256]{1,0:T(8,128)(2,1)S(1)}, bf16[96,256]{1,0:T(8,128)(2,1)S(1)}, u32[]{:S(2)}, u32[]{:S(2)}) %collective-permute-start.19) | collective-permute-done | bytes 49184 | tf_op jit(solution)/shard_map/ppermute | solution.py:289
  133.5 2.7 %collective-permute-start.26 = (bf16[384,256]{1,0:T(8,128)(2,1)S(1)}, bf16[384,256]{1,0:T(8,128)(2,1)S(1)}, u32[]{:S(2)}, u32[]{:S(2)}) collective-permute-start(bf16[384,256]{1,0:T(8,128)(2,1)S(1)} %get-tuple-element.70.refs_4_), channel_id=1, source_target_pairs={{0,24},{8,0},{16,8},{24,16},{1,25},{9,1},{17,9},{25,17},{2,26},{10... | collective-permute-start | bytes 589832 | tf_op jit(solution)/shard_map/ppermute | solution.py:289
  136.8 2.4 %collective-permute-done.22.refs_2_ = bf16[384,256]{1,0:T(8,128)(2,1)S(1)} collective-permute-done((bf16[384,256]{1,0:T(8,128)(2,1)S(1)}, bf16[384,256]{1,0:T(8,128)(2,1)S(1)}, u32[]{:S(2)}, u32[]{:S(2)}) %collective-permute-start.22) | collective-permute-done | bytes 196640 | tf_op jit(solution)/shard_map/ppermute | solution.py:289
  139.1 2.1 %collective-permute-done.21.refs_1_ = bf16[384,256]{1,0:T(8,128)(2,1)S(1)} collective-permute-done((bf16[384,256]{1,0:T(8,128)(2,1)S(1)}, bf16[384,256]{1,0:T(8,128)(2,1)S(1)}, u32[]{:S(2)}, u32[]{:S(2)}) %collective-permute-start.21) | collective-permute-done | bytes 196640 | tf_op jit(solution)/shard_map/ppermute | solution.py:289
  142.3 2.0 %collective-permute-done.24.refs_5_ = bf16[384,256]{1,0:T(8,128)(2,1)S(1)} collective-permute-done((bf16[384,256]{1,0:T(8,128)(2,1)S(1)}, bf16[384,256]{1,0:T(8,128)(2,1)S(1)}, u32[]{:S(2)}, u32[]{:S(2)}) %collective-permute-start.24) | collective-permute-done | bytes 196640 | tf_op jit(solution)/shard_map/ppermute | solution.py:289
  145.0 11.4 %collective-permute-start.27 = (bf16[3072,256]{1,0:T(8,128)(2,1)S(1)}, bf16[3072,256]{1,0:T(8,128)(2,1)S(1)}, u32[]{:S(2)}, u32[]{:S(2)}) collective-permute-start(bf16[3072,256]{1,0:T(8,128)(2,1)S(1)} %shard_map.111.half), channel_id=1, source_target_pairs={{0,1},{1,0},{2,3},{3,2},{4,5},{5,4},{6,7},{7,6},{8,9},{9,8},{10,11... | collective-permute-start | bytes 4718600 | tf_op jit(solution)/shard_map/ppermute | solution.py:280
  156.4 1.5 shard_map.105
  157.9 2.3 %shard_map.112 = (f32[2304,256]{1,0:T(8,128)}, f32[2304,256]{1,0:T(8,128)}, f32[768,256]{1,0:T(8,128)}, f32[768,256]{1,0:T(8,128)}) custom-call(s32[4]{0:T(128)S(1)} %pad_add_fusion.pos, bf16[3072,256]{1,0:T(8,128)(2,1)S(1)} %shard_map.111.half), custom_call_target="tpu_custom_call" | custom-call | bytes 1572880 | tf_op jit(solution)/shard_map/pallas_call | solution.py:43
  160.2 2.3 %shard_map.113 = (f32[2304,256]{1,0:T(8,128)}, f32[2304,256]{1,0:T(8,128)}, f32[768,256]{1,0:T(8,128)}, f32[768,256]{1,0:T(8,128)}) custom-call(s32[4]{0:T(128)S(1)} %pad_add_fusion.pos, bf16[3072,256]{1,0:T(8,128)(2,1)S(1)} %collective-permute-done.27.half, ...), custom_call_target="tpu_custom_call", output_to_operand_aliasing={{0}: (2, {}), {1}: (3, {}), {2}: (4, {}), {3}: (5, {})} | custom-call | bytes 7864336 | tf_op jit(solution)/shard_map/pallas_call | solution.py:43
  (75 shorter events, 26.6 us)
Async XLA Ops:
  0.6 23.1 %all-to-all-start.1 = ((bf16[32,16,256]{2,1,0:T(8,128)(2,1)}), bf16[32,16,256]{2,1,0:T(8,128)(2,1)S(1)}, u32[]{:S(2)}, u32[]{:S(2)}) async-start(bf16[32,16,256]{2,1,0:T(8,128)(2,1)} %bitcast.46), calls=%async_computation.1 | async-start | bytes 524288 | tf_op jit(solution)/shard_map/all_to_all | solution.py:285
  23.7 17.9 %all-to-all-start = ((bf16[32,16,256]{2,1,0:T(8,128)(2,1)}), bf16[32,16,256]{2,1,0:T(8,128)(2,1)}, u32[]{:S(2)}, u32[]{:S(2)}) async-start(bf16[32,16,256]{2,1,0:T(8,128)(2,1)} %bitcast.7), calls=%async_computation | async-start | bytes 524288 | tf_op jit(solution)/shard_map/all_to_all | solution.py:285
  47.1 15.5 %all-to-all-start.2 = ((bf16[32,16,256]{2,1,0:T(8,128)(2,1)}), bf16[32,16,256]{2,1,0:T(8,128)(2,1)S(1)}, u32[]{:S(2)}, u32[]{:S(2)}) async-start(bf16[32,16,256]{2,1,0:T(8,128)(2,1)} %bitcast.13), calls=%async_computation.2 | async-start | bytes 524288 | tf_op jit(solution)/shard_map/all_to_all | solution.py:285
  52.2 15.7 %collective-permute-start.2 = (bf16[2,512,256]{2,1,0:T(8,128)(2,1)}, bf16[2,512,256]{2,1,0:T(8,128)(2,1)S(1)}, u32[]{:S(2)}, u32[]{:S(2)}) collective-permute-start(bf16[2,512,256]{2,1,0:T(8,128)(2,1)} %copy-done.5), channel_id=1, source_target_pairs={{0,1},{1,0},{2,3},{3,2},{4,5},{5,4},{6,7},{7,6},{8,9},{9,8},{10,11... | collective-permute-start | bytes 1572872 | tf_op jit(solution)/shard_map/ppermute | solution.py:280
  54.4 14.1 %collective-permute-start = (bf16[512,256]{1,0:T(8,128)(2,1)}, bf16[512,256]{1,0:T(8,128)(2,1)S(1)}, u32[]{:S(2)}, u32[]{:S(2)}) collective-permute-start(bf16[512,256]{1,0:T(8,128)(2,1)} %copy-done.8), channel_id=1, source_target_pairs={{0,1},{1,0},{2,3},{3,2},{4,5},{5,4},{6,7},{7,6},{8,9},{9,8},{10,11... | collective-permute-start | bytes 786440 | tf_op jit(solution)/shard_map/ppermute | solution.py:280
  64.0 5.0 %collective-permute-start.1 = (bf16[512,256]{1,0:T(8,128)(2,1)S(1)}, bf16[512,256]{1,0:T(8,128)(2,1)S(1)}, u32[]{:S(2)}, u32[]{:S(2)}) collective-permute-start(bf16[512,256]{1,0:T(8,128)(2,1)S(1)} %get-tuple-element.50), channel_id=1, source_target_pairs={{0,1},{1,0},{2,3},{3,2},{4,5},{5,4},{6,7},{7,6},{8,9},{9,8},{10,11... | collective-permute-start | bytes 786440 | tf_op jit(solution)/shard_map/ppermute | solution.py:280
  72.4 7.5 %collective-permute-start.3 = (bf16[384,256]{1,0:T(8,128)(2,1)S(1)}, bf16[384,256]{1,0:T(8,128)(2,1)S(1)}, u32[]{:S(2)}, u32[]{:S(2)}) collective-permute-start(bf16[384,256]{1,0:T(8,128)(2,1)S(1)} %get-tuple-element.54), channel_id=1, source_target_pairs={{0,2},{2,4},{4,6},{6,0},{1,3},{3,5},{5,7},{7,1},{8,10},{10,12},{12... | collective-permute-start | bytes 589832 | tf_op jit(solution)/shard_map/ppermute | solution.py:289
  73.8 11.5 %collective-permute-start.4 = (bf16[384,256]{1,0:T(8,128)(2,1)S(1)}, bf16[384,256]{1,0:T(8,128)(2,1)S(1)}, u32[]{:S(2)}, u32[]{:S(2)}) collective-permute-start(bf16[384,256]{1,0:T(8,128)(2,1)S(1)} %get-tuple-element.55), channel_id=1, source_target_pairs={{0,4},{2,6},{4,0},{6,2},{1,5},{3,7},{5,1},{7,3},{8,12},{10,14},{12... | collective-permute-start | bytes 589832 | tf_op jit(solution)/shard_map/ppermute | solution.py:289
  76.4 8.9 %collective-permute-start.5 = (bf16[384,256]{1,0:T(8,128)(2,1)S(1)}, bf16[384,256]{1,0:T(8,128)(2,1)S(1)}, u32[]{:S(2)}, u32[]{:S(2)}) collective-permute-start(bf16[384,256]{1,0:T(8,128)(2,1)S(1)} %get-tuple-element.56), channel_id=1, source_target_pairs={{0,6},{2,0},{4,2},{6,4},{1,7},{3,1},{5,3},{7,5},{8,14},{10,8},{12,... | collective-permute-start | bytes 589832 | tf_op jit(solution)/shard_map/ppermute | solution.py:289
  77.5 7.8 %collective-permute-start.6 = (bf16[384,256]{1,0:T(8,128)(2,1)S(1)}, bf16[384,256]{1,0:T(8,128)(2,1)S(1)}, u32[]{:S(2)}, u32[]{:S(2)}) collective-permute-start(bf16[384,256]{1,0:T(8,128)(2,1)S(1)} %get-tuple-element.58), channel_id=1, source_target_pairs={{0,8},{8,16},{16,24},{24,0},{1,9},{9,17},{17,25},{25,1},{2,10},{10... | collective-permute-start | bytes 589832 | tf_op jit(solution)/shard_map/ppermute | solution.py:289
  77.5 9.9 %collective-permute-start.7 = (bf16[384,256]{1,0:T(8,128)(2,1)S(1)}, bf16[384,256]{1,0:T(8,128)(2,1)S(1)}, u32[]{:S(2)}, u32[]{:S(2)}) collective-permute-start(bf16[384,256]{1,0:T(8,128)(2,1)S(1)} %get-tuple-element.59), channel_id=1, source_target_pairs={{0,16},{8,24},{16,0},{24,8},{1,17},{9,25},{17,1},{25,9},{2,18},{10... | collective-permute-start | bytes 589832 | tf_op jit(solution)/shard_map/ppermute | solution.py:289
  79.9 9.3 %collective-permute-start.8 = (bf16[384,256]{1,0:T(8,128)(2,1)S(1)}, bf16[384,256]{1,0:T(8,128)(2,1)S(1)}, u32[]{:S(2)}, u32[]{:S(2)}) collective-permute-start(bf16[384,256]{1,0:T(8,128)(2,1)S(1)} %get-tuple-element.60), channel_id=1, source_target_pairs={{0,24},{8,0},{16,8},{24,16},{1,25},{9,1},{17,9},{25,17},{2,26},{10... | collective-permute-start | bytes 589832 | tf_op jit(solution)/shard_map/ppermute | solution.py:289
  90.1 5.1 %collective-permute-start.9 = (bf16[96,256]{1,0:T(8,128)(2,1)S(1)}, bf16[96,256]{1,0:T(8,128)(2,1)S(1)}, u32[]{:S(2)}, u32[]{:S(2)}) collective-permute-start(bf16[96,256]{1,0:T(8,128)(2,1)S(1)} %get-tuple-element.62), channel_id=1, source_target_pairs={{0,8},{8,16},{16,24},{24,0},{1,9},{9,17},{17,25},{25,1},{2,10},{10... | collective-permute-start | bytes 147464 | tf_op jit(solution)/shard_map/ppermute | solution.py:289
  91.1 6.5 %collective-permute-start.10 = (bf16[96,256]{1,0:T(8,128)(2,1)S(1)}, bf16[96,256]{1,0:T(8,128)(2,1)S(1)}, u32[]{:S(2)}, u32[]{:S(2)}) collective-permute-start(bf16[96,256]{1,0:T(8,128)(2,1)S(1)} %get-tuple-element.63), channel_id=1, source_target_pairs={{0,16},{8,24},{16,0},{24,8},{1,17},{9,25},{17,1},{25,9},{2,18},{10... | collective-permute-start | bytes 147464 | tf_op jit(solution)/shard_map/ppermute | solution.py:289
  94.8 3.3 %collective-permute-start.11 = (bf16[96,256]{1,0:T(8,128)(2,1)S(1)}, bf16[96,256]{1,0:T(8,128)(2,1)S(1)}, u32[]{:S(2)}, u32[]{:S(2)}) collective-permute-start(bf16[96,256]{1,0:T(8,128)(2,1)S(1)} %get-tuple-element.64), channel_id=1, source_target_pairs={{0,24},{8,0},{16,8},{24,16},{1,25},{9,1},{17,9},{25,17},{2,26},{10... | collective-permute-start | bytes 147464 | tf_op jit(solution)/shard_map/ppermute | solution.py:289
  94.8 4.2 %collective-permute-start.12 = (bf16[96,256]{1,0:T(8,128)(2,1)S(1)}, bf16[96,256]{1,0:T(8,128)(2,1)S(1)}, u32[]{:S(2)}, u32[]{:S(2)}) collective-permute-start(bf16[96,256]{1,0:T(8,128)(2,1)S(1)} %get-tuple-element.66), channel_id=1, source_target_pairs={{0,2},{2,4},{4,6},{6,0},{1,3},{3,5},{5,7},{7,1},{8,10},{10,12},{12... | collective-permute-start | bytes 147464 | tf_op jit(solution)/shard_map/ppermute | solution.py:289
  95.2 4.4 %collective-permute-start.13 = (bf16[96,256]{1,0:T(8,128)(2,1)S(1)}, bf16[96,256]{1,0:T(8,128)(2,1)S(1)}, u32[]{:S(2)}, u32[]{:S(2)}) collective-permute-start(bf16[96,256]{1,0:T(8,128)(2,1)S(1)} %get-tuple-element.67), channel_id=1, source_target_pairs={{0,4},{2,6},{4,0},{6,2},{1,5},{3,7},{5,1},{7,3},{8,12},{10,14},{12... | collective-permute-start | bytes 147464 | tf_op jit(solution)/shard_map/ppermute | solution.py:289
  95.2 5.1 %collective-permute-start.14 = (bf16[96,256]{1,0:T(8,128)(2,1)S(1)}, bf16[96,256]{1,0:T(8,128)(2,1)S(1)}, u32[]{:S(2)}, u32[]{:S(2)}) collective-permute-start(bf16[96,256]{1,0:T(8,128)(2,1)S(1)} %get-tuple-element.68), channel_id=1, source_target_pairs={{0,6},{2,0},{4,2},{6,4},{1,7},{3,1},{5,3},{7,5},{8,14},{10,8},{12,... | collective-permute-start | bytes 147464 | tf_op jit(solution)/shard_map/ppermute | solution.py:289
  100.4 56.0 %copy-start.4 = (bf16[3,3,256,256]{3,2,1,0:T(8,128)(2,1)S(1)}, bf16[3,3,256,256]{3,2,1,0:T(8,128)(2,1)}, u32[]{:S(2)}) copy-start(bf16[3,3,256,256]{3,2,1,0:T(8,128)(2,1)} %param.8) | copy-start | bytes 3538948
  120.6 5.8 %collective-permute-start.17 = (bf16[96,256]{1,0:T(8,128)(2,1)S(1)}, bf16[96,256]{1,0:T(8,128)(2,1)S(1)}, u32[]{:S(2)}, u32[]{:S(2)}) collective-permute-start(bf16[96,256]{1,0:T(8,128)(2,1)S(1)} %bitcast.34), channel_id=1, source_target_pairs={{0,24},{8,0},{16,8},{24,16},{1,25},{9,1},{17,9},{25,17},{2,26},{10... | collective-permute-start | bytes 147464 | tf_op jit(solution)/shard_map/ppermute | solution.py:289
  120.9 5.5 %collective-permute-start.16 = (bf16[96,256]{1,0:T(8,128)(2,1)S(1)}, bf16[96,256]{1,0:T(8,128)(2,1)S(1)}, u32[]{:S(2)}, u32[]{:S(2)}) collective-permute-start(bf16[96,256]{1,0:T(8,128)(2,1)S(1)} %bitcast.35), channel_id=1, source_target_pairs={{0,16},{8,24},{16,0},{24,8},{1,17},{9,25},{17,1},{25,9},{2,18},{10... | collective-permute-start | bytes 147464 | tf_op jit(solution)/shard_map/ppermute | solution.py:289
  123.6 4.2 %collective-permute-start.15 = (bf16[96,256]{1,0:T(8,128)(2,1)S(1)}, bf16[96,256]{1,0:T(8,128)(2,1)S(1)}, u32[]{:S(2)}, u32[]{:S(2)}) collective-permute-start(bf16[96,256]{1,0:T(8,128)(2,1)S(1)} %bitcast.36), channel_id=1, source_target_pairs={{0,8},{8,16},{16,24},{24,0},{1,9},{9,17},{17,25},{25,1},{2,10},{10... | collective-permute-start | bytes 147464 | tf_op jit(solution)/shard_map/ppermute | solution.py:289
  123.6 4.2 %collective-permute-start.20 = (bf16[96,256]{1,0:T(8,128)(2,1)S(1)}, bf16[96,256]{1,0:T(8,128)(2,1)S(1)}, u32[]{:S(2)}, u32[]{:S(2)}) collective-permute-start(bf16[96,256]{1,0:T(8,128)(2,1)S(1)} %bitcast.30), channel_id=1, source_target_pairs={{0,6},{2,0},{4,2},{6,4},{1,7},{3,1},{5,3},{7,5},{8,14},{10,8},{12,... | collective-permute-start | bytes 147464 | tf_op jit(solution)/shard_map/ppermute | solution.py:289
  125.8 4.7 %collective-permute-start.19 = (bf16[96,256]{1,0:T(8,128)(2,1)S(1)}, bf16[96,256]{1,0:T(8,128)(2,1)S(1)}, u32[]{:S(2)}, u32[]{:S(2)}) collective-permute-start(bf16[96,256]{1,0:T(8,128)(2,1)S(1)} %bitcast.31), channel_id=1, source_target_pairs={{0,4},{2,6},{4,0},{6,2},{1,5},{3,7},{5,1},{7,3},{8,12},{10,14},{12... | collective-permute-start | bytes 147464 | tf_op jit(solution)/shard_map/ppermute | solution.py:289
  126.4 4.6 %collective-permute-start.18 = (bf16[96,256]{1,0:T(8,128)(2,1)S(1)}, bf16[96,256]{1,0:T(8,128)(2,1)S(1)}, u32[]{:S(2)}, u32[]{:S(2)}) collective-permute-start(bf16[96,256]{1,0:T(8,128)(2,1)S(1)} %bitcast.32), channel_id=1, source_target_pairs={{0,2},{2,4},{4,6},{6,0},{1,3},{3,5},{5,7},{7,1},{8,10},{10,12},{12... | collective-permute-start | bytes 147464 | tf_op jit(solution)/shard_map/ppermute | solution.py:289
  131.5 5.2 %collective-permute-start.23 = (bf16[384,256]{1,0:T(8,128)(2,1)S(1)}, bf16[384,256]{1,0:T(8,128)(2,1)S(1)}, u32[]{:S(2)}, u32[]{:S(2)}) collective-permute-start(bf16[384,256]{1,0:T(8,128)(2,1)S(1)} %get-tuple-element.69.refs_0_), channel_id=1, source_target_pairs={{0,6},{2,0},{4,2},{6,4},{1,7},{3,1},{5,3},{7,5},{8,14},{10,8},{12,... | collective-permute-start | bytes 589832 | tf_op jit(solution)/shard_map/ppermute | solution.py:289
  132.0 7.1 %collective-permute-start.22 = (bf16[384,256]{1,0:T(8,128)(2,1)S(1)}, bf16[384,256]{1,0:T(8,128)(2,1)S(1)}, u32[]{:S(2)}, u32[]{:S(2)}) collective-permute-start(bf16[384,256]{1,0:T(8,128)(2,1)S(1)} %get-tuple-element.69.refs_0_), channel_id=1, source_target_pairs={{0,4},{2,6},{4,0},{6,2},{1,5},{3,7},{5,1},{7,3},{8,12},{10,14},{12... | collective-permute-start | bytes 589832 | tf_op jit(solution)/shard_map/ppermute | solution.py:289
  132.7 8.4 %collective-permute-start.21 = (bf16[384,256]{1,0:T(8,128)(2,1)S(1)}, bf16[384,256]{1,0:T(8,128)(2,1)S(1)}, u32[]{:S(2)}, u32[]{:S(2)}) collective-permute-start(bf16[384,256]{1,0:T(8,128)(2,1)S(1)} %get-tuple-element.69.refs_0_), channel_id=1, source_target_pairs={{0,2},{2,4},{4,6},{6,0},{1,3},{3,5},{5,7},{7,1},{8,10},{10,12},{12... | collective-permute-start | bytes 589832 | tf_op jit(solution)/shard_map/ppermute | solution.py:289
  133.5 7.7 %collective-permute-start.26 = (bf16[384,256]{1,0:T(8,128)(2,1)S(1)}, bf16[384,256]{1,0:T(8,128)(2,1)S(1)}, u32[]{:S(2)}, u32[]{:S(2)}) collective-permute-start(bf16[384,256]{1,0:T(8,128)(2,1)S(1)} %get-tuple-element.70.refs_4_), channel_id=1, source_target_pairs={{0,24},{8,0},{16,8},{24,16},{1,25},{9,1},{17,9},{25,17},{2,26},{10... | collective-permute-start | bytes 589832 | tf_op jit(solution)/shard_map/ppermute | solution.py:289
  136.2 6.1 %collective-permute-start.25 = (bf16[384,256]{1,0:T(8,128)(2,1)S(1)}, bf16[384,256]{1,0:T(8,128)(2,1)S(1)}, u32[]{:S(2)}, u32[]{:S(2)}) collective-permute-start(bf16[384,256]{1,0:T(8,128)(2,1)S(1)} %get-tuple-element.70.refs_4_), channel_id=1, source_target_pairs={{0,16},{8,24},{16,0},{24,8},{1,17},{9,25},{17,1},{25,9},{2,18},{10... | collective-permute-start | bytes 589832 | tf_op jit(solution)/shard_map/ppermute | solution.py:289
  136.8 7.6 %collective-permute-start.24 = (bf16[384,256]{1,0:T(8,128)(2,1)S(1)}, bf16[384,256]{1,0:T(8,128)(2,1)S(1)}, u32[]{:S(2)}, u32[]{:S(2)}) collective-permute-start(bf16[384,256]{1,0:T(8,128)(2,1)S(1)} %get-tuple-element.70.refs_4_), channel_id=1, source_target_pairs={{0,8},{8,16},{16,24},{24,0},{1,9},{9,17},{17,25},{25,1},{2,10},{10... | collective-permute-start | bytes 589832 | tf_op jit(solution)/shard_map/ppermute | solution.py:289
  145.0 15.2 %collective-permute-start.27 = (bf16[3072,256]{1,0:T(8,128)(2,1)S(1)}, bf16[3072,256]{1,0:T(8,128)(2,1)S(1)}, u32[]{:S(2)}, u32[]{:S(2)}) collective-permute-start(bf16[3072,256]{1,0:T(8,128)(2,1)S(1)} %shard_map.111.half), channel_id=1, source_target_pairs={{0,1},{1,0},{2,3},{3,2},{4,5},{5,4},{6,7},{7,6},{8,9},{9,8},{10,11... | collective-permute-start | bytes 4718600 | tf_op jit(solution)/shard_map/ppermute | solution.py:280
  (12 other events, 69.7 us)

commit v4 on v2

--- a/solution.py
+++ b/solution.py
@@ -1,3 +1,4 @@
+import functools
 import math
 
 import jax
@@ -17,6 +18,7 @@
 F32 = jnp.float32
 VMEM = pl.BlockSpec(memory_space=pltpu.VMEM)
 SMEM = pl.BlockSpec(memory_space=pltpu.SMEM)
+HBM = pl.BlockSpec(memory_space=pltpu.HBM)
 
 
 def dot_nn(left, right):
@@ -31,18 +33,38 @@
     return lax.dot_general(left, right, (((0,), (0,)), ((), ())), preferred_element_type=F32)
 
 
-def call(kernel, outs, ins, scratch=(), flops=0):
+def call(kernel, outs, ins, scratch=(), flops=0, hbm_in=(), hbm_out=(), aliases=None, vmem=40):
     specs = [SMEM if value.dtype == jnp.int32 else VMEM for value in ins]
+    for at in hbm_in:
+        specs[at] = HBM
     moved = sum(value.size * value.dtype.itemsize for value in ins)
     return pl.pallas_call(
         kernel,
         out_shape=[jax.ShapeDtypeStruct(shape, kind) for shape, kind in outs],
         in_specs=specs,
-        out_specs=[VMEM] * len(outs),
+        out_specs=[HBM if at in hbm_out else VMEM for at in range(len(outs))],
         scratch_shapes=list(scratch),
+        input_output_aliases=aliases or {},
         cost_estimate=pl.CostEstimate(flops=flops, bytes_accessed=moved, transcendentals=0),
-        compiler_params=pltpu.CompilerParams(vmem_limit_bytes=40 * 1024 * 1024),
+        compiler_params=pltpu.CompilerParams(vmem_limit_bytes=vmem * 1024 * 1024),
     )(*ins)
+
+
+def start_by_core(pos, sems, first, pairs):
+    for at, (even, odd, target) in enumerate(pairs):
+
+        @pl.when(pos[0] == 0)
+        def _():
+            pltpu.make_async_copy(even, target, sems.at[first + at]).start()
+
+        @pl.when(pos[0] != 0)
+        def _():
+            pltpu.make_async_copy(odd, target, sems.at[first + at]).start()
+
+
+def wait_by_core(sems, first, pairs):
+    for at, (even, _, target) in enumerate(pairs):
+        pltpu.make_async_copy(even, target, sems.at[first + at]).wait()
 
 
 def fill_windows(wide, values):
@@ -87,27 +109,32 @@
     return act, sigma * (1.0 + pre * (1.0 - sigma))
 
 
-def forward_kernel(core, video, w1, w2, act2, slope1, slope2, keep, send, wide):
-    values = video[...]
-    fill_windows(wide, values)
+def forward_kernel(pos, video_at, cot_at, w1_at, w2_at, both, slope1, slope2, keep, send, *rest):
+    video, first, w1, w2, wide, sems = rest
+    rows = PIX // COLS
+    loads = [
+        pltpu.make_async_copy(source, target, sems.at[at])
+        for at, (source, target) in enumerate(
+            [(video_at, video), (w1_at, w1), (w2_at, w2), (cot_at, both.at[:, COLS : 2 * COLS, :])]
+        )
+    ]
+    for load in loads:
+        load.start()
+    loads[0].wait()
+    fill_windows(wide, video[...])
+    loads[1].wait()
     act, slope = silu_pair(conv_from(wide, w1))
+    first[...] = act.astype(BF)
+    stores = [(first, video, keep), (video, first, send)]
+    start_by_core(pos, sems, 4, stores)
     slope1[...] = slope
-    first = act.astype(BF)
-
-    @pl.when(core[0] == 0)
-    def _():
-        keep[...] = first
-        send[...] = values
-
-    @pl.when(core[0] != 0)
-    def _():
-        keep[...] = values
-        send[...] = first
-
-    fill_windows(wide, first)
+    fill_windows(wide, first[...])
+    loads[2].wait()
     act, slope = silu_pair(conv_from(wide, w2))
     slope2[...] = slope
-    act2[...] = act.astype(BF)
+    both[:, 0:COLS, :] = act.astype(BF).reshape(rows, COLS, CH)
+    loads[3].wait()
+    wait_by_core(sems, 4, stores)
 
 
 def ahead_sum(padded, weight):
@@ -118,41 +145,50 @@
     return total
 
 
-def time_back_kernel(cot, wt2, back, padded):
-    padded[0:PIX, :] = cot[...]
-    padded[PIX:PAD, :] = jnp.zeros((2 * COLS, CH), BF)
-    back[...] = ahead_sum(padded, wt2)
-
-
-def time_kernel(core, act, cot, back, wt1, act_back, keep, send, padded):
-    padded[0 : 2 * COLS, :] = jnp.zeros((2 * COLS, CH), BF)
-    padded[2 * COLS : PAD, :] = act[...]
+def time_kernel(pos, both_at, wt1_at, wt2_at, act_back, keep, send, *rest):
+    act, cot, wt1, wt2, time_act, time_grad, behind, ahead, sems = rest
+    loads = [
+        pltpu.make_async_copy(source, target, sems.at[at])
+        for at, (source, target) in enumerate(
+            [
+                (both_at.at[:, COLS : 2 * COLS, :], cot),
+                (wt2_at, wt2),
+                (both_at.at[:, 0:COLS, :], act),
+                (wt1_at, wt1),
+            ]
+        )
+    ]
+    for load in loads:
+        load.start()
+    edge = jnp.zeros((2 * COLS, CH), BF)
+    loads[0].wait()
+    ahead[0:PIX, :] = cot[...].reshape(PIX, CH)
+    ahead[PIX:PAD, :] = edge
+    loads[1].wait()
+    back = ahead_sum(ahead, wt2)
+    loads[2].wait()
+    behind[0 : 2 * COLS, :] = edge
+    behind[2 * COLS : PAD, :] = act[...].reshape(PIX, CH)
+    loads[3].wait()
     pre = None
     for step in range(3):
         at = (2 - step) * COLS
-        term = dot_nn(padded[at : at + PIX, :], wt1[step * CH : (step + 1) * CH, :])
+        term = dot_nn(behind[at : at + PIX, :], wt1[step * CH : (step + 1) * CH, :])
         pre = term if pre is None else pre + term
     value, slope = silu_pair(pre)
-    time_act = value.astype(BF)
-    time_grad = (back[...] * slope).astype(BF)
-
-    @pl.when(core[0] == 0)
-    def _():
-        keep[0] = act[...]
-        keep[1] = time_grad
-        send[0] = time_act
-        send[1] = cot[...]
-
-    @pl.when(core[0] != 0)
-    def _():
-        keep[0] = time_act
-        keep[1] = cot[...]
-        send[0] = act[...]
-        send[1] = time_grad
-
-    padded[0:PIX, :] = time_grad
-    padded[PIX:PAD, :] = jnp.zeros((2 * COLS, CH), BF)
-    act_back[...] = ahead_sum(padded, wt1).astype(BF)
+    grad = (back * slope).astype(BF)
+    time_act[...] = value.astype(BF).reshape(PIX // COLS, COLS, CH)
+    time_grad[...] = grad.reshape(PIX // COLS, COLS, CH)
+    stores = [
+        (act, time_act, keep.at[0]),
+        (time_grad, cot, keep.at[1]),
+        (time_act, act, send.at[0]),
+        (cot, time_grad, send.at[1]),
+    ]
+    start_by_core(pos, sems, 4, stores)
+    ahead[0:PIX, :] = grad
+    act_back[...] = ahead_sum(ahead, wt1).astype(BF)
+    wait_by_core(sems, 4, stores)
 
 
 def time_weights_kernel(keep, recv, out):
@@ -163,18 +199,18 @@
         out[step * CH : (step + 1) * CH, :] = (total * SCALE).astype(BF)
 
 
-def backward_kernel(core, act_back, slope1, slope2, w2, first_grad, keep, send, wide):
+def backward_kernel(pos, act_back, slope1, slope2, w2, first_grad, keep, send, wide):
     second = (act_back[...].astype(F32) * slope2[...]).astype(BF)
     fill_windows(wide, second)
     first = (back_from(wide, w2) * slope1[...]).astype(BF)
     first_grad[...] = first
 
-    @pl.when(core[0] == 0)
+    @pl.when(pos[0] == 0)
     def _():
         keep[...] = second
         send[...] = first
 
-    @pl.when(core[0] != 0)
+    @pl.when(pos[0] != 0)
     def _():
         keep[...] = first
         send[...] = second
@@ -194,6 +230,30 @@
     out[9 * CH : 12 * CH, :] = time_part[...]
 
 
+def spread_kernel(owner, pos, half, *refs):
+    spat1, spat2, time1, time2, stage, sems = refs[-6:]
+    targets = [(spat2, time1), (spat1, time2)]
+
+    def copies(at):
+        space, time = targets[at]
+        rows = 3 * CH
+        for piece in range(3):
+            part = pl.ds(piece * rows, rows)
+            yield pltpu.make_async_copy(stage.at[part], space.at[part], sems.at[piece])
+        yield pltpu.make_async_copy(stage.at[pl.ds(3 * rows, rows)], time, sems.at[3])
+
+    for at in range(2):
+
+        @pl.when((pos[0] ^ owner) == at)
+        def _():
+            for piece, copy in enumerate(copies(at)):
+                rows = slice(piece * 3 * CH, (piece + 1) * 3 * CH)
+                stage[rows, :] = half[rows, :].astype(F32)
+                copy.start()
+            for copy in copies(at):
+                copy.wait()
+
+
 def input_kernel(first_grad, w1, out, wide):
     fill_windows(wide, first_grad[...])
     out[...] = back_from(wide, w1).astype(BF)
@@ -220,34 +280,46 @@
 
 
 def body(video, cotangent, w_spat1, w_spat2, w_time1, w_time2):
-    core = lax.axis_index("core").astype(jnp.int32).reshape(1)
+    pos = lax.axis_index("core").astype(jnp.int32).reshape(1)
     w1, w2, wt1, wt2 = (w.reshape(-1, CH) for w in (w_spat1, w_spat2, w_time1, w_time2))
+    rows = PIX // COLS
     slab, slab32 = ((PIX, CH), BF), ((PIX, CH), F32)
-    pair = ((2, PIX, CH), BF)
+    pair = ((2, rows, COLS, CH), BF)
     wide, tall = pltpu.VMEM((PAD, 3 * CH), BF), pltpu.VMEM((PAD, CH), BF)
+    frame, lines = pltpu.VMEM((PIX, CH), BF), pltpu.VMEM((rows, COLS, CH), BF)
+    space, time = pltpu.VMEM((9 * CH, CH), BF), pltpu.VMEM((3 * CH, CH), BF)
     conv_flops, time_flops = 2 * PIX * 9 * CH * CH, 2 * PIX * 3 * CH * CH
 
-    cot = swap_frames(cotangent.reshape(PIX, CH))
-    second_act, slope1, slope2, keep_x, send_x = call(
+    both, slope1, slope2, keep_x, send_x = call(
         forward_kernel,
-        [slab, slab32, slab32, slab, slab],
-        (core, video.reshape(PIX, CH), w1, w2),
-        [wide],
+        [((rows, 2 * COLS, CH), BF), slab32, slab32, slab, slab],
+        (pos, video.reshape(PIX, CH), cotangent.reshape(rows, COLS, CH), w1, w2),
+        [frame, frame, space, space, wide, pltpu.SemaphoreType.DMA((6,))],
         2 * conv_flops,
-    )
-    act = swap_frames(second_act)
+        (1, 2, 3, 4),
+        (3, 4),
+        vmem=62,
+    )
+    both = lax.all_to_all(both, ("z", "x"), 0, 0, tiled=True)
     recv_x = swap_cores(send_x)
-    (time_back,) = call(time_back_kernel, [slab32], (cot, wt2), [tall], time_flops)
     act_back, keep_t, send_t = call(
-        time_kernel, [slab, pair, pair], (core, act, cot, time_back, wt1), [tall], 2 * time_flops
+        time_kernel,
+        [slab, pair, pair],
+        (pos, both, wt1, wt2),
+        [lines, lines, time, time, lines, lines, tall, tall, pltpu.SemaphoreType.DMA((8,))],
+        3 * time_flops,
+        (1, 2, 3),
+        (1, 2),
+        vmem=62,
     )
     act_back = swap_frames(act_back)
     recv_t = swap_cores(send_t)
+    keep_t, recv_t = keep_t.reshape(2, PIX, CH), recv_t.reshape(2, PIX, CH)
     (time_part,) = call(
         time_weights_kernel, [((3 * CH, CH), BF)], (keep_t, recv_t), (), 2 * time_flops
     )
     first_grad, keep_g, send_g = call(
-        backward_kernel, [slab, slab, slab], (core, act_back, slope1, slope2, w2), [wide], conv_flops
+        backward_kernel, [slab, slab, slab], (pos, act_back, slope1, slope2, w2), [wide], conv_flops
     )
     recv_g = swap_cores(send_g)
     (part,) = call(
@@ -257,21 +329,36 @@
         [wide, wide],
         2 * conv_flops,
     )
-    (grad_input,) = call(input_kernel, [slab], (first_grad, w1), [wide], conv_flops)
-
-    part = scatter_sum(part, ("x", "y"), 16)
+
+    part = lax.all_to_all(part.reshape(16, -1, CH), ("x", "y"), 0, 0, tiled=True)
+    part = jnp.sum(part.astype(F32), axis=0).astype(BF)
     part = scatter_sum(part, "z", 8)
     part = gather_all(part, "z", 8)
     part = gather_all(part, ("x", "y"), 16)
     peer = swap_cores(part)
-    low = jnp.where(core[0] == 0, part, peer).astype(F32).reshape(12, CH, CH)
-    high = jnp.where(core[0] == 0, peer, part).astype(F32).reshape(12, CH, CH)
+    part, first_grad = lax.optimization_barrier((part, first_grad))
+    (grad_input,) = call(input_kernel, [slab], (first_grad, w1), [wide], conv_flops)
+    grads = [((9 * CH, CH), F32)] * 2 + [((3 * CH, CH), F32)] * 2
+    scratch = [pltpu.VMEM((12 * CH, CH), F32), pltpu.SemaphoreType.DMA((4,))]
+    outs = call(
+        functools.partial(spread_kernel, 0), grads, (pos, part), scratch, 0, (), (0, 1, 2, 3)
+    )
+    outs = call(
+        functools.partial(spread_kernel, 1),
+        grads,
+        (pos, peer, *outs),
+        scratch,
+        0,
+        (2, 3, 4, 5),
+        (0, 1, 2, 3),
+        {2: 0, 3: 1, 4: 2, 5: 3},
+    )
     return (
         grad_input.reshape(video.shape),
-        high[0:9].reshape(w_spat1.shape),
-        low[0:9].reshape(w_spat2.shape),
-        low[9:12],
-        high[9:12],
+        outs[0].reshape(w_spat1.shape),
+        outs[1].reshape(w_spat2.shape),
+        outs[2].reshape(w_time1.shape),
+        outs[3].reshape(w_time2.shape),
     )
 
 

time: 155 us -> 143 us (0.923)
  blocking collectives: 67.5 us -> 95.6 us
  starting transfers between devices: 35.8 us -> 17.3 us
  waiting for transfers between devices: 23.2 us -> 8.96 us
  local copies, waits for them, and re-layouts: 12.5 us -> 1.22 us
  Pallas kernels: 12.3 us -> 18.4 us
  other arithmetic: 2.05 us -> 0.24 us
    all_to_all x0 -> x2, blocking collectives: none -> 54.7 us  [the longest x1 28.3 us: body(): both = lax.all_to_all(both, ('z', 'x'), 0, 0, tiled=True)]
    all_to_all x2 -> x1, blocking collectives: 36.5 us -> 10.1 us  [scatter_sum(): arrived = lax.all_to_all(parts, axes, 0, 0, tiled=True)]
    all_to_all x3 -> x1, starting transfers between devices: 23.6 us -> 5.22 us  [swap_frames(): return lax.all_to_all(blocks, ('z', 'x'), 0, 0, tiled=True).reshape(PIX, CH)]
    all_to_all x3 -> x1, waiting for transfers between devices: 21 us -> 8.43 us  [swap_frames(): return lax.all_to_all(blocks, ('z', 'x'), 0, 0, tiled=True).reshape(PIX, CH)]
    unnamed x28 -> x12, local copies, waits for them, and re-layouts: 7.4 us -> 1.06 us
    pallas_call x7 -> x8, Pallas kernels: 12.3 us -> 18.4 us  [call(): pl.pallas_call(kernel, out_shape=[jax.ShapeDtypeStruct(shape, kind) for s...]
    slice x4 -> x0, local copies, waits for them, and re-layouts: 4.97 us -> none  [the longest x1 1.56 us: body(): low[0:9].reshape(w_spat2.shape)]
    convert_element_type x1 -> x0, other arithmetic: 1.82 us -> none  [body(): low = jnp.where(core[0] == 0, part, peer).astype(F32).reshape(12, CH, CH)]
  transfers between devices with their start and end apart: 7 -> 5, of which waited for: 5 -> 2; matrix products, arithmetic and copies ran while one was open for 0% -> 0% of each run, Pallas kernels for 4% -> 3%
where the time goes in v4:
time: 143 us; the launch traced here: 142 us
  blocking collectives  95.6 us (67%)
  Pallas kernels  18.4 us (13%)
  starting transfers between devices  17.3 us (12%)
  waiting for transfers between devices  8.96 us (6%)
    all_to_all x2, blocking collectives, gather_all(): return lax.all_to_all(copies, axes, 0, 0, tiled=True).reshape(-1, CH)  30.8 us
    all_to_all x1, blocking collectives, body(): both = lax.all_to_all(both, ('z', 'x'), 0, 0, tiled=True)  28.3 us
    all_to_all x1, blocking collectives, body(): lax.all_to_all(part.reshape(16, -1, CH), ('x', 'y'), 0, 0, tiled=True)  26.4 us
    pallas_call x8, Pallas kernels, call(): pl.pallas_call(kernel, out_shape=[jax.ShapeDtypeStruct(shape, kind) for s...  18.4 us
    ppermute x4, starting transfers between devices, swap_cores(): return lax.ppermute(values, 'core', [(0, 1), (1, 0)])  12 us
    all_to_all x1, blocking collectives, scatter_sum(): arrived = lax.all_to_all(parts, axes, 0, 0, tiled=True)  10.1 us
    all_to_all x1, waiting for transfers between devices, swap_frames(): return lax.all_to_all(blocks, ('z', 'x'), 0, 0, tiled=True).reshape(PIX, CH)  8.43 us
    all_to_all x1, starting transfers between devices, swap_frames(): return lax.all_to_all(blocks, ('z', 'x'), 0, 0, tiled=True).reshape(PIX, CH)  5.22 us
  transfers between devices with their start and end apart: 5, of which 2 were waited for; matrix products, arithmetic and copies ran while one was open for 0% of the time, Pallas kernels for 3%

profile of v4, /device:TPU:1, one launch (start us, length us, event | category | flops | bytes accessed | tf_op | source)
XLA Modules:
  0.0 142.4 jit_solution(8983988938483641861)
XLA Ops:
  0.6 5.4 %shard_map.101 = (bf16[32,32,256]{2,1,0:T(8,128)(2,1)}, f32[512,256]{1,0:T(8,128)}, f32[512,256]{1,0:T(8,128)}, bf16[512,256]{1,0:T(8,128)(2,1)}, bf16[512,256]{1,0:T(8,128)(2,1)}) custom-call(s32[1]{0:T(128)} %bitcast.pos, bf16[512,256]{1,0:T(8,128)(2,1)} %bitcast.39, bf16[32,16,256]{2,1,0:T(8,128)(2,1)} %bitcast.40, bf16[2304,256]{1,0:T(8,128)(2,1)} %bitcast.26, ...), custom_call_target="tpu_custom_call" | custom-call | flops 1207959552 | bytes 2883588 | tf_op jit(solution)/shard_map/pallas_call | solution.py:41
  6.1 28.3 %all_to_all.30.both_at = bf16[32,32,256]{2,1,0:T(8,128)(2,1)} all-to-all(bf16[32,32,256]{2,1,0:T(8,128)(2,1)} %get-tuple-element.28), channel_id=1, replica_groups=mesh['z'=8,'x'=4,'y'=4,'core'=2] {'z','x'}, dimensions={0} | all-to-all | bytes 1048576 | tf_op jit(solution)/shard_map/all_to_all | solution.py:303
  34.3 0.0 copy-start
  34.3 4.0 %shard_map.102 = (bf16[512,256]{1,0:T(8,128)(2,1)}, bf16[2,32,16,256]{3,2,1,0:T(8,128)(2,1)}, bf16[2,32,16,256]{3,2,1,0:T(8,128)(2,1)}) custom-call(s32[1]{0:T(128)} %bitcast.pos, bf16[32,32,256]{2,1,0:T(8,128)(2,1)} %all_to_all.30.both_at, bf16[768,256]{1,0:T(8,128)(2,1)} %bitcast.37, bf16[768,256]{1,0:T(8,128)(2,1)} %bitcast.38), custom_call_target="tpu_custom_call" | custom-call | flops 603979776 | bytes 1310724 | tf_op jit(solution)/shard_map/pallas_call | solution.py:41
  38.4 5.2 %all-to-all-start.1 = ((bf16[32,16,256]{2,1,0:T(8,128)(2,1)}), bf16[32,16,256]{2,1,0:T(8,128)(2,1)S(1)}, u32[]{:S(2)}, u32[]{:S(2)}) async-start(bf16[32,16,256]{2,1,0:T(8,128)(2,1)} %bitcast.36), calls=%async_computation.1 | async-start | bytes 524288 | tf_op jit(solution)/shard_map/all_to_all | solution.py:268
  43.6 1.9 %collective-permute-start.2 = (bf16[2,32,16,256]{3,2,1,0:T(8,128)(2,1)}, bf16[2,32,16,256]{3,2,1,0:T(8,128)(2,1)S(1)}, u32[]{:S(2)}, u32[]{:S(2)}) collective-permute-start(bf16[2,32,16,256]{3,2,1,0:T(8,128)(2,1)} %get-tuple-element.35), channel_id=1, source_target_pairs={{0,1},{1,0},{2,3},{3,2},{4,5},{5,4},{6,7},{7,6},{8,9},{9,8},{10,11... | collective-permute-start | bytes 1572872 | tf_op jit(solution)/shard_map/ppermute | solution.py:263
  45.5 0.1 collective-permute-start
  45.6 8.4 %all-to-all-done.1 = bf16[32,16,256]{2,1,0:T(8,128)(2,1)S(1)} async-done(((bf16[32,16,256]{2,1,0:T(8,128)(2,1)}), bf16[32,16,256]{2,1,0:T(8,128)(2,1)S(1)}, u32[]{:S(2)}, u32[]{:S(2)}) %all-to-all-start.1) | async-done | bytes 262176 | tf_op jit(solution)/shard_map/all_to_all | solution.py:268
  54.0 0.0 copy-done
  54.0 0.0 copy-done.1
  54.0 1.0 copy-done.2
  55.1 0.9 shard_map.103
  55.9 3.8 %collective-permute-start.1 = (bf16[512,256]{1,0:T(8,128)(2,1)S(1)}, bf16[512,256]{1,0:T(8,128)(2,1)S(1)}, u32[]{:S(2)}, u32[]{:S(2)}) collective-permute-start(bf16[512,256]{1,0:T(8,128)(2,1)S(1)} %get-tuple-element.33), channel_id=1, source_target_pairs={{0,1},{1,0},{2,3},{3,2},{4,5},{5,4},{6,7},{7,6},{8,9},{9,8},{10,11... | collective-permute-start | bytes 786440 | tf_op jit(solution)/shard_map/ppermute | solution.py:263
  59.8 0.0 collective-permute-done.2
  59.8 0.0 copy-done.4
  59.8 0.6 shard_map.104.time_part
  60.4 0.0 collective-permute-done.recv_x
  60.4 0.5 collective-permute-done.1.recv_g
  60.9 0.0 copy-done.5
  60.9 2.5 %shard_map.105 = bf16[3072,256]{1,0:T(8,128)(2,1)S(1)} custom-call(bf16[512,256]{1,0:T(8,128)(2,1)S(1)} %copy-done.5, bf16[512,256]{1,0:T(8,128)(2,1)} %collective-permute-done.recv_x, bf16[512,256]{1,0:T(8,128)(2,1)S(1)} %get-tuple-element.32.keep_g, bf16[512,256]{1,0:T(8,128)(2,1)S(1)} %collective-permute-done.1.recv_g, ...), custom_call_target="tpu_custom_call" | custom-call | flops 1207959552 | bytes 1441792 | tf_op jit(solution)/shard_map/pallas_call | solution.py:41
  63.4 26.4 %all_to_all.31 = bf16[16,192,256]{2,1,0:T(8,128)(2,1)S(1)} all-to-all(bf16[16,192,256]{2,1,0:T(8,128)(2,1)S(1)} %bitcast.22), channel_id=1, replica_groups=mesh['z'=8,'x'=4,'y'=4,'core'=2] {'x','y'}, dimensions={0} | all-to-all | bytes 3145728 | tf_op jit(solution)/shard_map/all_to_all | solution.py:333
  89.8 0.2 reduce_sum.24
  90.0 10.1 %all_to_all.32 = bf16[8,24,256]{2,1,0:T(8,128)(2,1)S(1)} all-to-all(bf16[8,24,256]{2,1,0:T(8,128)(2,1)S(1)} %bitcast.34), channel_id=1, replica_groups=mesh['z'=8,'x'=4,'y'=4,'core'=2] {'z'}, dimensions={0} | all-to-all | bytes 196608 | tf_op jit(solution)/shard_map/all_to_all | solution.py:273
  100.1 10.1 %all_to_all.33 = bf16[8,24,256]{2,1,0:T(8,128)(2,1)S(1)} all-to-all(bf16[8,24,256]{2,1,0:T(8,128)(2,1)S(1)} %broadcast_in_dim.6), channel_id=1, replica_groups=mesh['z'=8,'x'=4,'y'=4,'core'=2] {'z'}, dimensions={0} | all-to-all | bytes 196608 | tf_op jit(solution)/shard_map/all_to_all | solution.py:279
  110.2 0.1 broadcast_in_dim.15
  110.3 20.8 %all_to_all.34 = bf16[16,192,256]{2,1,0:T(8,128)(2,1)S(1)} all-to-all(bf16[16,192,256]{2,1,0:T(8,128)(2,1)S(1)} %broadcast_in_dim.15), channel_id=1, replica_groups=mesh['z'=8,'x'=4,'y'=4,'core'=2] {'x','y'}, dimensions={0} | all-to-all | bytes 3145728 | tf_op jit(solution)/shard_map/all_to_all | solution.py:279
  131.1 6.2 %collective-permute-start.3 = (bf16[3072,256]{1,0:T(8,128)(2,1)S(1)}, bf16[3072,256]{1,0:T(8,128)(2,1)S(1)}, u32[]{:S(2)}, u32[]{:S(2)}) collective-permute-start(bf16[3072,256]{1,0:T(8,128)(2,1)S(1)} %bitcast.20), channel_id=1, source_target_pairs={{0,1},{1,0},{2,3},{3,2},{4,5},{5,4},{6,7},{7,6},{8,9},{9,8},{10,11... | collective-permute-start | bytes 4718600 | tf_op jit(solution)/shard_map/ppermute | solution.py:263
  137.3 1.7 %shard_map.107 = (f32[2304,256]{1,0:T(8,128)}, f32[2304,256]{1,0:T(8,128)}, f32[768,256]{1,0:T(8,128)}, f32[768,256]{1,0:T(8,128)}) custom-call(s32[1]{0:T(128)} %bitcast.pos, bf16[3072,256]{1,0:T(8,128)(2,1)S(1)} %bitcast.21), custom_call_target="tpu_custom_call" | custom-call | bytes 1572868 | tf_op jit(solution)/shard_map/pallas_call | solution.py:41
  139.1 0.0 copy-done.3
  139.1 1.5 %shard_map.106 = bf16[512,256]{1,0:T(8,128)(2,1)} custom-call(bf16[512,256]{1,0:T(8,128)(2,1)S(1)} %get-tuple-element.37.first_grad, bf16[2304,256]{1,0:T(8,128)(2,1)S(1)} %bitcast.27), custom_call_target="tpu_custom_call" | custom-call | flops 603979776 | bytes 1441792 | tf_op jit(solution)/shard_map/pallas_call | solution.py:41
  140.6 0.0 collective-permute-done.3.half
  140.6 1.7 %shard_map.108 = (f32[2304,256]{1,0:T(8,128)}, f32[2304,256]{1,0:T(8,128)}, f32[768,256]{1,0:T(8,128)}, f32[768,256]{1,0:T(8,128)}) custom-call(s32[1]{0:T(128)} %bitcast.pos, bf16[3072,256]{1,0:T(8,128)(2,1)S(1)} %collective-permute-done.3.half, ...), custom_call_target="tpu_custom_call", output_to_operand_aliasing={{0}: (2, {}), {1}: (3, {}), {2}: (4, {}), {3}: (5, {})} | custom-call | bytes 7864324 | tf_op jit(solution)/shard_map/pallas_call | solution.py:41
  (7 shorter events, 0.0 us)
Async XLA Ops:
  34.3 19.7 %copy-start = (bf16[3,3,256,256]{3,2,1,0:T(8,128)(2,1)S(1)}, bf16[3,3,256,256]{3,2,1,0:T(8,128)(2,1)}, u32[]{:S(2)}) copy-start(bf16[3,3,256,256]{3,2,1,0:T(8,128)(2,1)} %param.9) | copy-start | bytes 3538948
  34.3 19.7 %copy-start.1 = (f32[512,256]{1,0:T(8,128)S(1)}, f32[512,256]{1,0:T(8,128)}, u32[]{:S(2)}) copy-start(f32[512,256]{1,0:T(8,128)} %get-tuple-element.30.slope1) | copy-start | bytes 1572868
  38.4 15.6 %all-to-all-start.1 = ((bf16[32,16,256]{2,1,0:T(8,128)(2,1)}), bf16[32,16,256]{2,1,0:T(8,128)(2,1)S(1)}, u32[]{:S(2)}, u32[]{:S(2)}) async-start(bf16[32,16,256]{2,1,0:T(8,128)(2,1)} %bitcast.36), calls=%async_computation.1 | async-start | bytes 524288 | tf_op jit(solution)/shard_map/all_to_all | solution.py:268
  43.6 16.2 %collective-permute-start.2 = (bf16[2,32,16,256]{3,2,1,0:T(8,128)(2,1)}, bf16[2,32,16,256]{3,2,1,0:T(8,128)(2,1)S(1)}, u32[]{:S(2)}, u32[]{:S(2)}) collective-permute-start(bf16[2,32,16,256]{3,2,1,0:T(8,128)(2,1)} %get-tuple-element.35), channel_id=1, source_target_pairs={{0,1},{1,0},{2,3},{3,2},{4,5},{5,4},{6,7},{7,6},{8,9},{9,8},{10,11... | collective-permute-start | bytes 1572872 | tf_op jit(solution)/shard_map/ppermute | solution.py:263
  45.5 14.9 %collective-permute-start = (bf16[512,256]{1,0:T(8,128)(2,1)}, bf16[512,256]{1,0:T(8,128)(2,1)}, u32[]{:S(2)}, u32[]{:S(2)}) collective-permute-start(bf16[512,256]{1,0:T(8,128)(2,1)} %get-tuple-element.27), channel_id=1, source_target_pairs={{0,1},{1,0},{2,3},{3,2},{4,5},{5,4},{6,7},{7,6},{8,9},{9,8},{10,11... | collective-permute-start | bytes 786440 | tf_op jit(solution)/shard_map/ppermute | solution.py:263
  54.0 1.0 copy-start.2
  55.1 4.7 %copy-start.4 = (bf16[2,32,16,256]{3,2,1,0:T(8,128)(2,1)S(1)}, bf16[2,32,16,256]{3,2,1,0:T(8,128)(2,1)}, u32[]{:S(2)}) copy-start(bf16[2,32,16,256]{3,2,1,0:T(8,128)(2,1)} %get-tuple-element.34) | copy-start | bytes 1572868
  55.1 5.9 %copy-start.5 = (bf16[512,256]{1,0:T(8,128)(2,1)S(1)}, bf16[512,256]{1,0:T(8,128)(2,1)}, u32[]{:S(2)}) copy-start(bf16[512,256]{1,0:T(8,128)(2,1)} %get-tuple-element.26.keep_x) | copy-start | bytes 786436
  55.9 5.0 %collective-permute-start.1 = (bf16[512,256]{1,0:T(8,128)(2,1)S(1)}, bf16[512,256]{1,0:T(8,128)(2,1)S(1)}, u32[]{:S(2)}, u32[]{:S(2)}) collective-permute-start(bf16[512,256]{1,0:T(8,128)(2,1)S(1)} %get-tuple-element.33), channel_id=1, source_target_pairs={{0,1},{1,0},{2,3},{3,2},{4,5},{5,4},{6,7},{7,6},{8,9},{9,8},{10,11... | collective-permute-start | bytes 786440 | tf_op jit(solution)/shard_map/ppermute | solution.py:263
  131.1 8.0 %copy-start.3 = (bf16[3,3,256,256]{3,2,1,0:T(8,128)(2,1)S(1)}, bf16[3,3,256,256]{3,2,1,0:T(8,128)(2,1)}, u32[]{:S(2)}) copy-start(bf16[3,3,256,256]{3,2,1,0:T(8,128)(2,1)} %param.8) | copy-start | bytes 3538948
  131.1 9.5 %collective-permute-start.3 = (bf16[3072,256]{1,0:T(8,128)(2,1)S(1)}, bf16[3072,256]{1,0:T(8,128)(2,1)S(1)}, u32[]{:S(2)}, u32[]{:S(2)}) collective-permute-start(bf16[3072,256]{1,0:T(8,128)(2,1)S(1)} %bitcast.20), channel_id=1, source_target_pairs={{0,1},{1,0},{2,3},{3,2},{4,5},{5,4},{6,7},{7,6},{8,9},{9,8},{10,11... | collective-permute-start | bytes 4718600 | tf_op jit(solution)/shard_map/ppermute | solution.py:263

commit v5 on v4

--- a/solution.py
+++ b/solution.py
@@ -13,6 +13,7 @@
 COLS = 16
 PIX = 512
 PAD = PIX + 2 * COLS
+FRAME_AXES = ("zh", "zl", "x")
 SCALE = 1.0 / math.sqrt(131072)
 BF = jnp.bfloat16
 F32 = jnp.float32
@@ -109,7 +110,7 @@
     return act, sigma * (1.0 + pre * (1.0 - sigma))
 
 
-def forward_kernel(pos, video_at, cot_at, w1_at, w2_at, both, slope1, slope2, keep, send, *rest):
+def forward_kernel(pos, video_at, cot_at, w1_at, w2_at, both, slopes, keep, send, *rest):
     video, first, w1, w2, wide, sems = rest
     rows = PIX // COLS
     loads = [
@@ -127,11 +128,11 @@
     first[...] = act.astype(BF)
     stores = [(first, video, keep), (video, first, send)]
     start_by_core(pos, sems, 4, stores)
-    slope1[...] = slope
+    slopes[0:PIX, :] = slope
     fill_windows(wide, first[...])
     loads[2].wait()
     act, slope = silu_pair(conv_from(wide, w2))
-    slope2[...] = slope
+    slopes[PIX : 2 * PIX, :] = slope
     both[:, 0:COLS, :] = act.astype(BF).reshape(rows, COLS, CH)
     loads[3].wait()
     wait_by_core(sems, 4, stores)
@@ -199,10 +200,10 @@
         out[step * CH : (step + 1) * CH, :] = (total * SCALE).astype(BF)
 
 
-def backward_kernel(pos, act_back, slope1, slope2, w2, first_grad, keep, send, wide):
-    second = (act_back[...].astype(F32) * slope2[...]).astype(BF)
+def backward_kernel(pos, act_back, slopes, w2, first_grad, keep, send, wide):
+    second = (act_back[...].astype(F32) * slopes[PIX : 2 * PIX, :]).astype(BF)
     fill_windows(wide, second)
-    first = (back_from(wide, w2) * slope1[...]).astype(BF)
+    first = (back_from(wide, w2) * slopes[0:PIX, :]).astype(BF)
     first_grad[...] = first
 
     @pl.when(pos[0] == 0)
@@ -265,7 +266,7 @@
 
 def swap_frames(values):
     blocks = values.reshape(PIX // COLS, COLS, CH)
-    return lax.all_to_all(blocks, ("z", "x"), 0, 0, tiled=True).reshape(PIX, CH)
+    return lax.all_to_all(blocks, FRAME_AXES, 0, 0, tiled=True).reshape(PIX, CH)
 
 
 def scatter_sum(values, axes, count):
@@ -283,24 +284,24 @@
     pos = lax.axis_index("core").astype(jnp.int32).reshape(1)
     w1, w2, wt1, wt2 = (w.reshape(-1, CH) for w in (w_spat1, w_spat2, w_time1, w_time2))
     rows = PIX // COLS
-    slab, slab32 = ((PIX, CH), BF), ((PIX, CH), F32)
+    slab = ((PIX, CH), BF)
     pair = ((2, rows, COLS, CH), BF)
     wide, tall = pltpu.VMEM((PAD, 3 * CH), BF), pltpu.VMEM((PAD, CH), BF)
     frame, lines = pltpu.VMEM((PIX, CH), BF), pltpu.VMEM((rows, COLS, CH), BF)
     space, time = pltpu.VMEM((9 * CH, CH), BF), pltpu.VMEM((3 * CH, CH), BF)
     conv_flops, time_flops = 2 * PIX * 9 * CH * CH, 2 * PIX * 3 * CH * CH
 
-    both, slope1, slope2, keep_x, send_x = call(
+    both, slopes, keep_x, send_x = call(
         forward_kernel,
-        [((rows, 2 * COLS, CH), BF), slab32, slab32, slab, slab],
+        [((rows, 2 * COLS, CH), BF), ((2 * PIX, CH), F32), slab, slab],
         (pos, video.reshape(PIX, CH), cotangent.reshape(rows, COLS, CH), w1, w2),
         [frame, frame, space, space, wide, pltpu.SemaphoreType.DMA((6,))],
         2 * conv_flops,
         (1, 2, 3, 4),
-        (3, 4),
-        vmem=62,
-    )
-    both = lax.all_to_all(both, ("z", "x"), 0, 0, tiled=True)
+        (2, 3),
+        vmem=60,
+    )
+    both = lax.all_to_all(both, FRAME_AXES, 0, 0, tiled=True)
     recv_x = swap_cores(send_x)
     act_back, keep_t, send_t = call(
         time_kernel,
@@ -310,7 +311,7 @@
         3 * time_flops,
         (1, 2, 3),
         (1, 2),
-        vmem=62,
+        vmem=60,
     )
     act_back = swap_frames(act_back)
     recv_t = swap_cores(send_t)
@@ -319,7 +320,7 @@
         time_weights_kernel, [((3 * CH, CH), BF)], (keep_t, recv_t), (), 2 * time_flops
     )
     first_grad, keep_g, send_g = call(
-        backward_kernel, [slab, slab, slab], (pos, act_back, slope1, slope2, w2), [wide], conv_flops
+        backward_kernel, [slab, slab, slab], (pos, act_back, slopes, w2), [wide], conv_flops
     )
     recv_g = swap_cores(send_g)
     (part,) = call(
@@ -330,11 +331,9 @@
         2 * conv_flops,
     )
 
-    part = lax.all_to_all(part.reshape(16, -1, CH), ("x", "y"), 0, 0, tiled=True)
-    part = jnp.sum(part.astype(F32), axis=0).astype(BF)
-    part = scatter_sum(part, "z", 8)
-    part = gather_all(part, "z", 8)
-    part = gather_all(part, ("x", "y"), 16)
+    part = scatter_sum(part, ("zl", "x", "y"), 32)
+    part = jnp.sum(gather_all(part, "zh", 4).reshape(4, -1, CH).astype(F32), axis=0).astype(BF)
+    part = gather_all(part, ("zl", "x", "y"), 32)
     peer = swap_cores(part)
     part, first_grad = lax.optimization_barrier((part, first_grad))
     (grad_input,) = call(input_kernel, [slab], (first_grad, w1), [wide], conv_flops)
@@ -363,8 +362,8 @@
 
 
 def solution(mesh):
-    fine = Mesh(mesh.devices.reshape(8, 4, 4, 2), ("z", "x", "y", "core"))
-    frames = P(("y", "core"), ("z", "x"), None, None, None)
+    fine = Mesh(mesh.devices.reshape(4, 2, 4, 4, 2), ("zh", "zl", "x", "y", "core"))
+    frames = P(("y", "core"), FRAME_AXES, None, None, None)
     return jax.shard_map(
         body,
         mesh=fine,

time: 143 us -> 133 us (0.930)
  blocking collectives: 95.6 us -> 88.1 us
    all_to_all x2 -> x1, blocking collectives: 54.7 us -> 28.3 us  [body(): both = lax.all_to_all(both, FRAME_AXES, 0, 0, tiled=True)]
    all_to_all x1, blocking collectives: 10.1 us -> 26.6 us  [scatter_sum(): arrived = lax.all_to_all(parts, axes, 0, 0, tiled=True)]
    all_to_all x2, blocking collectives: 30.8 us -> 33.3 us  [gather_all(): return lax.all_to_all(copies, axes, 0, 0, tiled=True).reshape(-1, CH)]
  transfers between devices with their start and end apart: 5 -> 5, of which waited for: 2 -> 2; matrix products, arithmetic and copies ran while one was open for 0% -> 0% of each run, Pallas kernels for 3% -> 4%
where the time goes in v5:
time: 133 us; the launch traced here: 132 us
  blocking collectives  88.1 us (66%)
  Pallas kernels  17.4 us (13%)
  starting transfers between devices  16.4 us (12%)
  waiting for transfers between devices  8.95 us (7%)
    all_to_all x2, blocking collectives, gather_all(): return lax.all_to_all(copies, axes, 0, 0, tiled=True).reshape(-1, CH)  33.3 us
    all_to_all x1, blocking collectives, body(): both = lax.all_to_all(both, FRAME_AXES, 0, 0, tiled=True)  28.3 us
    all_to_all x1, blocking collectives, scatter_sum(): arrived = lax.all_to_all(parts, axes, 0, 0, tiled=True)  26.6 us
    pallas_call x8, Pallas kernels, call(): pl.pallas_call(kernel, out_shape=[jax.ShapeDtypeStruct(shape, kind) for s...  17.4 us
    ppermute x4, starting transfers between devices, swap_cores(): return lax.ppermute(values, 'core', [(0, 1), (1, 0)])  11.2 us
    all_to_all x1, waiting for transfers between devices, swap_frames(): return lax.all_to_all(blocks, FRAME_AXES, 0, 0, tiled=True).reshape(PIX, CH)  8.43 us
    all_to_all x1, starting transfers between devices, swap_frames(): return lax.all_to_all(blocks, FRAME_AXES, 0, 0, tiled=True).reshape(PIX, CH)  5.22 us
  transfers between devices with their start and end apart: 5, of which 2 were waited for; matrix products, arithmetic and copies ran while one was open for 0% of the time, Pallas kernels for 4%

profile of v5, /device:TPU:1, one launch (start us, length us, event | category | flops | bytes accessed | tf_op | source)
XLA Modules:
  0.0 132.0 jit_solution(5375313452673418585)
XLA Ops:
  0.6 5.4 %shard_map.101 = (bf16[32,32,256]{2,1,0:T(8,128)(2,1)}, f32[1024,256]{1,0:T(8,128)}, bf16[512,256]{1,0:T(8,128)(2,1)}, bf16[512,256]{1,0:T(8,128)(2,1)}) custom-call(s32[1]{0:T(128)} %bitcast.pos, bf16[512,256]{1,0:T(8,128)(2,1)} %bitcast.35, bf16[32,16,256]{2,1,0:T(8,128)(2,1)} %bitcast.36, bf16[2304,256]{1,0:T(8,128)(2,1)} %bitcast.24, ...), custom_call_target="tpu_custom_call" | custom-call | flops 1207959552 | bytes 2883588 | tf_op jit(solution)/shard_map/pallas_call | solution.py:42
  6.1 28.3 %all_to_all.25.both_at = bf16[32,32,256]{2,1,0:T(8,128)(2,1)} all-to-all(bf16[32,32,256]{2,1,0:T(8,128)(2,1)} %get-tuple-element.27), channel_id=1, replica_groups=mesh['zh'=4,'zl'=2,'x'=4,'y'=4,'core'=2] {'zh','zl','x'}, dimensions={0} | all-to-all | bytes 1048576 | tf_op jit(solution)/shard_map/all_to_all | solution.py:304
  34.3 0.0 copy-start
  34.3 0.0 copy-start.1
  34.4 4.0 %shard_map.102 = (bf16[512,256]{1,0:T(8,128)(2,1)}, bf16[2,32,16,256]{3,2,1,0:T(8,128)(2,1)}, bf16[2,32,16,256]{3,2,1,0:T(8,128)(2,1)}) custom-call(s32[1]{0:T(128)} %bitcast.pos, bf16[32,32,256]{2,1,0:T(8,128)(2,1)} %all_to_all.25.both_at, bf16[768,256]{1,0:T(8,128)(2,1)} %bitcast.33, bf16[768,256]{1,0:T(8,128)(2,1)} %bitcast.34), custom_call_target="tpu_custom_call" | custom-call | flops 603979776 | bytes 1310724 | tf_op jit(solution)/shard_map/pallas_call | solution.py:42
  38.4 5.2 %all-to-all-start.1 = ((bf16[32,16,256]{2,1,0:T(8,128)(2,1)}), bf16[32,16,256]{2,1,0:T(8,128)(2,1)S(1)}, u32[]{:S(2)}, u32[]{:S(2)}) async-start(bf16[32,16,256]{2,1,0:T(8,128)(2,1)} %bitcast.32), calls=%async_computation.1 | async-start | bytes 524288 | tf_op jit(solution)/shard_map/all_to_all | solution.py:269
  43.6 1.9 %collective-permute-start.2 = (bf16[2,32,16,256]{3,2,1,0:T(8,128)(2,1)}, bf16[2,32,16,256]{3,2,1,0:T(8,128)(2,1)S(1)}, u32[]{:S(2)}, u32[]{:S(2)}) collective-permute-start(bf16[2,32,16,256]{3,2,1,0:T(8,128)(2,1)} %get-tuple-element.33), channel_id=1, source_target_pairs={{0,1},{1,0},{2,3},{3,2},{4,5},{5,4},{6,7},{7,6},{8,9},{9,8},{10,11... | collective-permute-start | bytes 1572872 | tf_op jit(solution)/shard_map/ppermute | solution.py:264
  45.5 0.1 collective-permute-start
  45.6 8.4 %all-to-all-done.1 = bf16[32,16,256]{2,1,0:T(8,128)(2,1)S(1)} async-done(((bf16[32,16,256]{2,1,0:T(8,128)(2,1)}), bf16[32,16,256]{2,1,0:T(8,128)(2,1)S(1)}, u32[]{:S(2)}, u32[]{:S(2)}) %all-to-all-start.1) | async-done | bytes 262176 | tf_op jit(solution)/shard_map/all_to_all | solution.py:269
  54.0 0.0 copy-done
  54.0 0.0 copy-done.1
  54.0 0.0 copy-start.4
  54.0 0.9 shard_map.103
  54.9 3.8 %collective-permute-start.1 = (bf16[512,256]{1,0:T(8,128)(2,1)S(1)}, bf16[512,256]{1,0:T(8,128)(2,1)S(1)}, u32[]{:S(2)}, u32[]{:S(2)}) collective-permute-start(bf16[512,256]{1,0:T(8,128)(2,1)S(1)} %get-tuple-element.31), channel_id=1, source_target_pairs={{0,1},{1,0},{2,3},{3,2},{4,5},{5,4},{6,7},{7,6},{8,9},{9,8},{10,11... | collective-permute-start | bytes 786440 | tf_op jit(solution)/shard_map/ppermute | solution.py:264
  58.7 0.0 collective-permute-done.2
  58.7 0.0 copy-done.3
  58.7 0.6 shard_map.104.time_part
  59.4 0.0 collective-permute-done.recv_x
  59.4 0.5 collective-permute-done.1.recv_g
  59.9 0.0 copy-done.4
  59.9 1.5 %shard_map.105 = bf16[3072,256]{1,0:T(8,128)(2,1)S(1)} custom-call(bf16[512,256]{1,0:T(8,128)(2,1)S(1)} %copy-done.4, bf16[512,256]{1,0:T(8,128)(2,1)S(1)} %collective-permute-done.recv_x, bf16[512,256]{1,0:T(8,128)(2,1)S(1)} %get-tuple-element.30.keep_g, bf16[512,256]{1,0:T(8,128)(2,1)S(1)} %collective-permute-done.1.recv_g, ...), custom_call_target="tpu_custom_call" | custom-call | flops 1207959552 | bytes 1441792 | tf_op jit(solution)/shard_map/pallas_call | solution.py:42
  61.4 26.6 %all_to_all.26 = bf16[32,96,256]{2,1,0:T(8,128)(2,1)S(1)} all-to-all(bf16[32,96,256]{2,1,0:T(8,128)(2,1)S(1)} %bitcast.20), channel_id=1, replica_groups=mesh['zh'=4,'zl'=2,'x'=4,'y'=4,'core'=2] {'zl','x','y'}, dimensions={0} | all-to-all | bytes 3145728 | tf_op jit(solution)/shard_map/all_to_all | solution.py:274
  87.9 0.2 reduce_sum.24
  88.2 11.0 %all_to_all.27 = bf16[4,96,256]{2,1,0:T(8,128)(2,1)S(1)} all-to-all(bf16[4,96,256]{2,1,0:T(8,128)(2,1)S(1)} %broadcast_in_dim.4), channel_id=1, replica_groups=mesh['zh'=4,'zl'=2,'x'=4,'y'=4,'core'=2] {'zh'}, dimensions={0} | all-to-all | bytes 393216 | tf_op jit(solution)/shard_map/all_to_all | solution.py:280
  99.3 0.2 broadcast_in_dim.5
  99.4 22.2 %all_to_all.28 = bf16[32,96,256]{2,1,0:T(8,128)(2,1)S(1)} all-to-all(bf16[32,96,256]{2,1,0:T(8,128)(2,1)S(1)} %broadcast_in_dim.5), channel_id=1, replica_groups=mesh['zh'=4,'zl'=2,'x'=4,'y'=4,'core'=2] {'zl','x','y'}, dimensions={0} | all-to-all | bytes 3145728 | tf_op jit(solution)/shard_map/all_to_all | solution.py:280
  121.7 5.4 %collective-permute-start.3 = (bf16[3072,256]{1,0:T(8,128)(2,1)S(1)}, bf16[3072,256]{1,0:T(8,128)(2,1)S(1)}, u32[]{:S(2)}, u32[]{:S(2)}) collective-permute-start(bf16[3072,256]{1,0:T(8,128)(2,1)S(1)} %bitcast.18), channel_id=1, source_target_pairs={{0,1},{1,0},{2,3},{3,2},{4,5},{5,4},{6,7},{7,6},{8,9},{9,8},{10,11... | collective-permute-start | bytes 4718600 | tf_op jit(solution)/shard_map/ppermute | solution.py:264
  127.0 1.7 %shard_map.107 = (f32[2304,256]{1,0:T(8,128)}, f32[2304,256]{1,0:T(8,128)}, f32[768,256]{1,0:T(8,128)}, f32[768,256]{1,0:T(8,128)}) custom-call(s32[1]{0:T(128)} %bitcast.pos, bf16[3072,256]{1,0:T(8,128)(2,1)S(1)} %bitcast.19), custom_call_target="tpu_custom_call" | custom-call | bytes 1572868 | tf_op jit(solution)/shard_map/pallas_call | solution.py:42
  128.8 0.0 copy-done.2
  128.8 1.5 %shard_map.106 = bf16[512,256]{1,0:T(8,128)(2,1)} custom-call(bf16[512,256]{1,0:T(8,128)(2,1)S(1)} %get-tuple-element.35.first_grad, bf16[2304,256]{1,0:T(8,128)(2,1)S(1)} %bitcast.25), custom_call_target="tpu_custom_call" | custom-call | flops 603979776 | bytes 1441792 | tf_op jit(solution)/shard_map/pallas_call | solution.py:42
  130.3 0.0 collective-permute-done.3.half
  130.3 1.7 %shard_map.108 = (f32[2304,256]{1,0:T(8,128)}, f32[2304,256]{1,0:T(8,128)}, f32[768,256]{1,0:T(8,128)}, f32[768,256]{1,0:T(8,128)}) custom-call(s32[1]{0:T(128)} %bitcast.pos, bf16[3072,256]{1,0:T(8,128)(2,1)S(1)} %collective-permute-done.3.half, ...), custom_call_target="tpu_custom_call", output_to_operand_aliasing={{0}: (2, {}), {1}: (3, {}), {2}: (4, {}), {3}: (5, {})} | custom-call | bytes 7864324 | tf_op jit(solution)/shard_map/pallas_call | solution.py:42
  (4 shorter events, 0.0 us)
Async XLA Ops:
  34.3 19.7 %copy-start = (bf16[3,3,256,256]{3,2,1,0:T(8,128)(2,1)S(1)}, bf16[3,3,256,256]{3,2,1,0:T(8,128)(2,1)}, u32[]{:S(2)}) copy-start(bf16[3,3,256,256]{3,2,1,0:T(8,128)(2,1)} %param.9) | copy-start | bytes 3538948
  34.3 19.7 %copy-start.1 = (f32[1024,256]{1,0:T(8,128)S(1)}, f32[1024,256]{1,0:T(8,128)}, u32[]{:S(2)}) copy-start(f32[1024,256]{1,0:T(8,128)} %get-tuple-element.29.slopes) | copy-start | bytes 3145732
  38.4 15.6 %all-to-all-start.1 = ((bf16[32,16,256]{2,1,0:T(8,128)(2,1)}), bf16[32,16,256]{2,1,0:T(8,128)(2,1)S(1)}, u32[]{:S(2)}, u32[]{:S(2)}) async-start(bf16[32,16,256]{2,1,0:T(8,128)(2,1)} %bitcast.32), calls=%async_computation.1 | async-start | bytes 524288 | tf_op jit(solution)/shard_map/all_to_all | solution.py:269
  43.6 15.1 %collective-permute-start.2 = (bf16[2,32,16,256]{3,2,1,0:T(8,128)(2,1)}, bf16[2,32,16,256]{3,2,1,0:T(8,128)(2,1)S(1)}, u32[]{:S(2)}, u32[]{:S(2)}) collective-permute-start(bf16[2,32,16,256]{3,2,1,0:T(8,128)(2,1)} %get-tuple-element.33), channel_id=1, source_target_pairs={{0,1},{1,0},{2,3},{3,2},{4,5},{5,4},{6,7},{7,6},{8,9},{9,8},{10,11... | collective-permute-start | bytes 1572872 | tf_op jit(solution)/shard_map/ppermute | solution.py:264
  45.5 13.9 %collective-permute-start = (bf16[512,256]{1,0:T(8,128)(2,1)}, bf16[512,256]{1,0:T(8,128)(2,1)S(1)}, u32[]{:S(2)}, u32[]{:S(2)}) collective-permute-start(bf16[512,256]{1,0:T(8,128)(2,1)} %get-tuple-element.26), channel_id=1, source_target_pairs={{0,1},{1,0},{2,3},{3,2},{4,5},{5,4},{6,7},{7,6},{8,9},{9,8},{10,11... | collective-permute-start | bytes 786440 | tf_op jit(solution)/shard_map/ppermute | solution.py:264
  54.0 4.7 %copy-start.3 = (bf16[2,32,16,256]{3,2,1,0:T(8,128)(2,1)S(1)}, bf16[2,32,16,256]{3,2,1,0:T(8,128)(2,1)}, u32[]{:S(2)}) copy-start(bf16[2,32,16,256]{3,2,1,0:T(8,128)(2,1)} %get-tuple-element.32) | copy-start | bytes 1572868
  54.0 5.9 %copy-start.4 = (bf16[512,256]{1,0:T(8,128)(2,1)S(1)}, bf16[512,256]{1,0:T(8,128)(2,1)}, u32[]{:S(2)}) copy-start(bf16[512,256]{1,0:T(8,128)(2,1)} %get-tuple-element.25.keep_x) | copy-start | bytes 786436
  54.9 5.0 %collective-permute-start.1 = (bf16[512,256]{1,0:T(8,128)(2,1)S(1)}, bf16[512,256]{1,0:T(8,128)(2,1)S(1)}, u32[]{:S(2)}, u32[]{:S(2)}) collective-permute-start(bf16[512,256]{1,0:T(8,128)(2,1)S(1)} %get-tuple-element.31), channel_id=1, source_target_pairs={{0,1},{1,0},{2,3},{3,2},{4,5},{5,4},{6,7},{7,6},{8,9},{9,8},{10,11... | collective-permute-start | bytes 786440 | tf_op jit(solution)/shard_map/ppermute | solution.py:264
  121.6 7.1 %copy-start.2 = (bf16[3,3,256,256]{3,2,1,0:T(8,128)(2,1)S(1)}, bf16[3,3,256,256]{3,2,1,0:T(8,128)(2,1)}, u32[]{:S(2)}) copy-start(bf16[3,3,256,256]{3,2,1,0:T(8,128)(2,1)} %param.8) | copy-start | bytes 3538948
  121.7 8.6 %collective-permute-start.3 = (bf16[3072,256]{1,0:T(8,128)(2,1)S(1)}, bf16[3072,256]{1,0:T(8,128)(2,1)S(1)}, u32[]{:S(2)}, u32[]{:S(2)}) collective-permute-start(bf16[3072,256]{1,0:T(8,128)(2,1)S(1)} %bitcast.18), channel_id=1, source_target_pairs={{0,1},{1,0},{2,3},{3,2},{4,5},{5,4},{6,7},{7,6},{8,9},{9,8},{10,11... | collective-permute-start | bytes 4718600 | tf_op jit(solution)/shard_map/ppermute | solution.py:264

commit v6 on v5

--- a/solution.py
+++ b/solution.py
@@ -81,9 +81,11 @@
     wide[COLS : COLS + PIX, 2 * CH : 3 * CH] = after.astype(BF)
 
 
-def conv_from(wide, weight):
+def conv_from(wide, weight, loads=(None, None, None)):
     total = None
-    for tap in range(3):
+    for tap, load in enumerate(loads):
+        if load is not None:
+            load.wait()
         term = dot_nn(
             wide[tap * COLS : tap * COLS + PIX, :], weight[tap * 3 * CH : (tap + 1) * 3 * CH, :]
         )
@@ -105,37 +107,45 @@
 
 
 def silu_pair(pre):
-    sigma = jax.nn.sigmoid(pre)
+    sigma = 0.5 + 0.5 * jnp.tanh(0.5 * pre)
     act = pre * sigma
     return act, sigma * (1.0 + pre * (1.0 - sigma))
 
 
-def forward_kernel(pos, video_at, cot_at, w1_at, w2_at, both, slopes, keep, send, *rest):
-    video, first, w1, w2, wide, sems = rest
-    rows = PIX // COLS
-    loads = [
+def forward_kernel(pos, video_at, cot_at, w1_at, w2_at, both_at, slopes_at, keep, send, *rest):
+    video, first, act2, slopes, w1, w2, wide, sems = rest
+    pieces = [(video_at, video)]
+    for source, target in ((w1_at, w1), (w2_at, w2)):
+        for tap in range(3):
+            part = pl.ds(tap * 3 * CH, 3 * CH)
+            pieces.append((source.at[part], target.at[part]))
+    pieces.append((cot_at, both_at.at[:, COLS : 2 * COLS, :]))
+    pieces.append((slopes.at[0], slopes_at.at[0]))
+    pieces.append((slopes.at[1], slopes_at.at[1]))
+    pieces.append((act2, both_at.at[:, 0:COLS, :]))
+    moves = [
         pltpu.make_async_copy(source, target, sems.at[at])
-        for at, (source, target) in enumerate(
-            [(video_at, video), (w1_at, w1), (w2_at, w2), (cot_at, both.at[:, COLS : 2 * COLS, :])]
-        )
+        for at, (source, target) in enumerate(pieces)
     ]
-    for load in loads:
-        load.start()
-    loads[0].wait()
+    for move in moves[0:8]:
+        move.start()
+    moves[0].wait()
     fill_windows(wide, video[...])
-    loads[1].wait()
-    act, slope = silu_pair(conv_from(wide, w1))
+    act, slope = silu_pair(conv_from(wide, w1, moves[1:4]))
     first[...] = act.astype(BF)
     stores = [(first, video, keep), (video, first, send)]
-    start_by_core(pos, sems, 4, stores)
-    slopes[0:PIX, :] = slope
+    start_by_core(pos, sems, 11, stores)
+    slopes[0] = slope.astype(BF)
+    moves[8].start()
     fill_windows(wide, first[...])
-    loads[2].wait()
-    act, slope = silu_pair(conv_from(wide, w2))
-    slopes[PIX : 2 * PIX, :] = slope
-    both[:, 0:COLS, :] = act.astype(BF).reshape(rows, COLS, CH)
-    loads[3].wait()
-    wait_by_core(sems, 4, stores)
+    act, slope = silu_pair(conv_from(wide, w2, moves[4:7]))
+    act2[...] = act.astype(BF).reshape(PIX // COLS, COLS, CH)
+    moves[10].start()
+    slopes[1] = slope.astype(BF)
+    moves[9].start()
+    for move in moves[7:11]:
+        move.wait()
+    wait_by_core(sems, 11, stores)
 
 
 def ahead_sum(padded, weight):
@@ -146,8 +156,8 @@
     return total
 
 
-def time_kernel(pos, both_at, wt1_at, wt2_at, act_back, keep, send, *rest):
-    act, cot, wt1, wt2, time_act, time_grad, behind, ahead, sems = rest
+def time_kernel(pos, both_at, wt1_at, wt2_at, back_at, keep, send, *rest):
+    act, cot, wt1, wt2, time_act, time_grad, act_back, behind, ahead, sems = rest
     loads = [
         pltpu.make_async_copy(source, target, sems.at[at])
         for at, (source, target) in enumerate(
@@ -189,7 +199,10 @@
     start_by_core(pos, sems, 4, stores)
     ahead[0:PIX, :] = grad
     act_back[...] = ahead_sum(ahead, wt1).astype(BF)
+    last = pltpu.make_async_copy(act_back, back_at, sems.at[8])
+    last.start()
     wait_by_core(sems, 4, stores)
+    last.wait()
 
 
 def time_weights_kernel(keep, recv, out):
@@ -201,9 +214,9 @@
 
 
 def backward_kernel(pos, act_back, slopes, w2, first_grad, keep, send, wide):
-    second = (act_back[...].astype(F32) * slopes[PIX : 2 * PIX, :]).astype(BF)
+    second = (act_back[...].astype(F32) * slopes[1].astype(F32)).astype(BF)
     fill_windows(wide, second)
-    first = (back_from(wide, w2) * slopes[0:PIX, :]).astype(BF)
+    first = (back_from(wide, w2) * slopes[0].astype(F32)).astype(BF)
     first_grad[...] = first
 
     @pl.when(pos[0] == 0)
@@ -269,12 +282,6 @@
     return lax.all_to_all(blocks, FRAME_AXES, 0, 0, tiled=True).reshape(PIX, CH)
 
 
-def scatter_sum(values, axes, count):
-    parts = values.reshape(count, -1, CH)
-    arrived = lax.all_to_all(parts, axes, 0, 0, tiled=True)
-    return jnp.sum(arrived.astype(F32), axis=0).astype(BF)
-
-
 def gather_all(values, axes, count):
     copies = jnp.broadcast_to(values[None], (count,) + values.shape)
     return lax.all_to_all(copies, axes, 0, 0, tiled=True).reshape(-1, CH)
@@ -288,17 +295,18 @@
     pair = ((2, rows, COLS, CH), BF)
     wide, tall = pltpu.VMEM((PAD, 3 * CH), BF), pltpu.VMEM((PAD, CH), BF)
     frame, lines = pltpu.VMEM((PIX, CH), BF), pltpu.VMEM((rows, COLS, CH), BF)
+    both_slopes = pltpu.VMEM((2, PIX, CH), BF)
     space, time = pltpu.VMEM((9 * CH, CH), BF), pltpu.VMEM((3 * CH, CH), BF)
     conv_flops, time_flops = 2 * PIX * 9 * CH * CH, 2 * PIX * 3 * CH * CH
 
     both, slopes, keep_x, send_x = call(
         forward_kernel,
-        [((rows, 2 * COLS, CH), BF), ((2 * PIX, CH), F32), slab, slab],
+        [((rows, 2 * COLS, CH), BF), ((2, PIX, CH), BF), slab, slab],
         (pos, video.reshape(PIX, CH), cotangent.reshape(rows, COLS, CH), w1, w2),
-        [frame, frame, space, space, wide, pltpu.SemaphoreType.DMA((6,))],
+        [frame, frame, lines, both_slopes, space, space, wide, pltpu.SemaphoreType.DMA((13,))],
         2 * conv_flops,
         (1, 2, 3, 4),
-        (2, 3),
+        (0, 1, 2, 3),
         vmem=60,
     )
     both = lax.all_to_all(both, FRAME_AXES, 0, 0, tiled=True)
@@ -307,10 +315,10 @@
         time_kernel,
         [slab, pair, pair],
         (pos, both, wt1, wt2),
-        [lines, lines, time, time, lines, lines, tall, tall, pltpu.SemaphoreType.DMA((8,))],
+        [lines, lines, time, time, lines, lines, frame, tall, tall, pltpu.SemaphoreType.DMA((9,))],
         3 * time_flops,
         (1, 2, 3),
-        (1, 2),
+        (0, 1, 2),
         vmem=60,
     )
     act_back = swap_frames(act_back)
@@ -331,12 +339,17 @@
         2 * conv_flops,
     )
 
-    part = scatter_sum(part, ("zl", "x", "y"), 32)
-    part = jnp.sum(gather_all(part, "zh", 4).reshape(4, -1, CH).astype(F32), axis=0).astype(BF)
+    (grad_input,) = call(input_kernel, [slab], (first_grad, w1), [wide], conv_flops)
+    part = lax.all_to_all(part.reshape(32, -1, CH), ("zl", "x", "y"), 0, 0, tiled=True)
+    part, grad_input = lax.optimization_barrier((part, grad_input))
+    part = jnp.sum(part.astype(F32), axis=0).astype(BF)
+    near, far, other = (
+        lax.ppermute(part, "zh", [(at, (at + step) % 4) for at in range(4)]).astype(F32)
+        for step in (1, 3, 2)
+    )
+    part = ((part.astype(F32) + other) + (near + far)).astype(BF)
     part = gather_all(part, ("zl", "x", "y"), 32)
     peer = swap_cores(part)
-    part, first_grad = lax.optimization_barrier((part, first_grad))
-    (grad_input,) = call(input_kernel, [slab], (first_grad, w1), [wide], conv_flops)
     grads = [((9 * CH, CH), F32)] * 2 + [((3 * CH, CH), F32)] * 2
     scratch = [pltpu.VMEM((12 * CH, CH), F32), pltpu.SemaphoreType.DMA((4,))]
     outs = call(

time: 133 us -> 137 us (1.030)
  blocking collectives: 88.1 us -> 54.2 us
  waiting for transfers between devices: 8.95 us -> 34.6 us
  starting transfers between devices: 16.4 us -> 24.8 us
  Pallas kernels: 17.4 us -> 21.8 us
    all_to_all x1 -> x0, blocking collectives: 26.6 us -> none  [scatter_sum(): arrived = lax.all_to_all(parts, axes, 0, 0, tiled=True)]
    all_to_all x0 -> x1, waiting for transfers between devices: none -> 18.8 us  [body(): lax.all_to_all(part.reshape(32, -1, CH), ('zl', 'x', 'y'), 0, 0, tiled=True)]
    all_to_all x2 -> x1, blocking collectives: 33.3 us -> 26 us  [gather_all(): return lax.all_to_all(copies, axes, 0, 0, tiled=True).reshape(-1, CH)]
    ppermute x0 -> x3, waiting for transfers between devices: none -> 5.7 us  [body(): lax.ppermute(part, 'zh', [(at, (at + step) % 4) for at in range(4)])]
    all_to_all x0 -> x1, starting transfers between devices: none -> 5.57 us  [body(): lax.all_to_all(part.reshape(32, -1, CH), ('zl', 'x', 'y'), 0, 0, tiled=True)]
    pallas_call x8, Pallas kernels: 17.4 us -> 21.8 us  [call(): pl.pallas_call(kernel, out_shape=[jax.ShapeDtypeStruct(shape, kind) for s...]
    ppermute x0 -> x3, starting transfers between devices: none -> 3.93 us  [body(): lax.ppermute(part, 'zh', [(at, (at + step) % 4) for at in range(4)])]
  transfers between devices with their start and end apart: 5 -> 9, of which waited for: 2 -> 7; matrix products, arithmetic and copies ran while one was open for 0% -> 0% of each run, Pallas kernels for 4% -> 3%
where the time goes in v6:
time: 137 us
  blocking collectives  54.2 us (40%)
  waiting for transfers between devices  34.6 us (25%)
  starting transfers between devices  24.8 us (18%)
  Pallas kernels  21.8 us (16%)
    all_to_all x1, blocking collectives, body(): both = lax.all_to_all(both, FRAME_AXES, 0, 0, tiled=True)  28.3 us
    all_to_all x1, blocking collectives, gather_all(): return lax.all_to_all(copies, axes, 0, 0, tiled=True).reshape(-1, CH)  26 us
    pallas_call x8, Pallas kernels, call(): pl.pallas_call(kernel, out_shape=[jax.ShapeDtypeStruct(shape, kind) for s...  21.8 us
    all_to_all x1, waiting for transfers between devices, body(): lax.all_to_all(part.reshape(32, -1, CH), ('zl', 'x', 'y'), 0, 0, tiled=True)  18.8 us
    ppermute x4, starting transfers between devices, swap_cores(): return lax.ppermute(values, 'core', [(0, 1), (1, 0)])  9.95 us
    all_to_all x1, waiting for transfers between devices, swap_frames(): return lax.all_to_all(blocks, FRAME_AXES, 0, 0, tiled=True).reshape(PIX, CH)  8.35 us
    ppermute x3, waiting for transfers between devices, body(): lax.ppermute(part, 'zh', [(at, (at + step) % 4) for at in range(4)])  5.7 us
    all_to_all x1, starting transfers between devices, body(): lax.all_to_all(part.reshape(32, -1, CH), ('zl', 'x', 'y'), 0, 0, tiled=True)  5.57 us
  transfers between devices with their start and end apart: 9, of which 7 were waited for; matrix products, arithmetic and copies ran while one was open for 0% of the time, Pallas kernels for 3%

profile of v6, /device:TPU:1, one launch (start us, length us, event | category | flops | bytes accessed | tf_op | source)
XLA Modules:
  0.0 136.7 jit_solution(14094092945036815435)
XLA Ops:
  0.6 9.2 %shard_map.101 = (bf16[32,32,256]{2,1,0:T(8,128)(2,1)}, bf16[2,512,256]{2,1,0:T(8,128)(2,1)}, bf16[512,256]{1,0:T(8,128)(2,1)}, bf16[512,256]{1,0:T(8,128)(2,1)}) custom-call(s32[1]{0:T(128)} %bitcast.pos, bf16[512,256]{1,0:T(8,128)(2,1)} %bitcast.34, bf16[32,16,256]{2,1,0:T(8,128)(2,1)} %bitcast.35, bf16[2304,256]{1,0:T(8,128)(2,1)} %bitcast.23, ...), custom_call_target="tpu_custom_call" | custom-call | flops 1207959552 | bytes 2883588 | tf_op jit(solution)/shard_map/pallas_call | solution.py:42
  9.8 28.3 %all_to_all.20.both_at = bf16[32,32,256]{2,1,0:T(8,128)(2,1)} all-to-all(bf16[32,32,256]{2,1,0:T(8,128)(2,1)} %get-tuple-element.27), channel_id=1, replica_groups=mesh['zh'=4,'zl'=2,'x'=4,'y'=4,'core'=2] {'zh','zl','x'}, dimensions={0} | all-to-all | bytes 1048576 | tf_op jit(solution)/shard_map/all_to_all | solution.py:312
  38.1 3.6 %shard_map.102 = (bf16[512,256]{1,0:T(8,128)(2,1)}, bf16[2,32,16,256]{3,2,1,0:T(8,128)(2,1)}, bf16[2,32,16,256]{3,2,1,0:T(8,128)(2,1)}) custom-call(s32[1]{0:T(128)} %bitcast.pos, bf16[32,32,256]{2,1,0:T(8,128)(2,1)} %all_to_all.20.both_at, bf16[768,256]{1,0:T(8,128)(2,1)} %bitcast.32, bf16[768,256]{1,0:T(8,128)(2,1)} %bitcast.33), custom_call_target="tpu_custom_call" | custom-call | flops 603979776 | bytes 1310724 | tf_op jit(solution)/shard_map/pallas_call | solution.py:42
  41.6 0.0 copy-start.2
  41.7 5.4 %all-to-all-start.1 = ((bf16[32,16,256]{2,1,0:T(8,128)(2,1)}), bf16[32,16,256]{2,1,0:T(8,128)(2,1)S(1)}, u32[]{:S(2)}, u32[]{:S(2)}) async-start(bf16[32,16,256]{2,1,0:T(8,128)(2,1)} %bitcast.31), calls=%async_computation.1 | async-start | bytes 524288 | tf_op jit(solution)/shard_map/all_to_all | solution.py:282
  47.0 2.0 %collective-permute-start.2 = (bf16[2,32,16,256]{3,2,1,0:T(8,128)(2,1)}, bf16[2,32,16,256]{3,2,1,0:T(8,128)(2,1)S(1)}, u32[]{:S(2)}, u32[]{:S(2)}) collective-permute-start(bf16[2,32,16,256]{3,2,1,0:T(8,128)(2,1)} %get-tuple-element.33), channel_id=1, source_target_pairs={{0,1},{1,0},{2,3},{3,2},{4,5},{5,4},{6,7},{7,6},{8,9},{9,8},{10,11... | collective-permute-start | bytes 1572872 | tf_op jit(solution)/shard_map/ppermute | solution.py:277
  49.0 0.1 collective-permute-start
  49.1 8.3 %all-to-all-done.1 = bf16[32,16,256]{2,1,0:T(8,128)(2,1)S(1)} async-done(((bf16[32,16,256]{2,1,0:T(8,128)(2,1)}), bf16[32,16,256]{2,1,0:T(8,128)(2,1)S(1)}, u32[]{:S(2)}, u32[]{:S(2)}) %all-to-all-start.1) | async-done | bytes 262176 | tf_op jit(solution)/shard_map/all_to_all | solution.py:282
  57.4 0.0 copy-done.3
  57.4 0.9 shard_map.103
  58.3 3.8 %collective-permute-start.1 = (bf16[512,256]{1,0:T(8,128)(2,1)S(1)}, bf16[512,256]{1,0:T(8,128)(2,1)S(1)}, u32[]{:S(2)}, u32[]{:S(2)}) collective-permute-start(bf16[512,256]{1,0:T(8,128)(2,1)S(1)} %get-tuple-element.31), channel_id=1, source_target_pairs={{0,1},{1,0},{2,3},{3,2},{4,5},{5,4},{6,7},{7,6},{8,9},{9,8},{10,11... | collective-permute-start | bytes 786440 | tf_op jit(solution)/shard_map/ppermute | solution.py:277
  62.1 0.0 collective-permute-done.2
  62.1 0.6 shard_map.104.time_part
  62.8 0.0 collective-permute-done.recv_x
  62.8 0.5 collective-permute-done.1.recv_g
  63.3 2.6 %shard_map.105 = bf16[3072,256]{1,0:T(8,128)(2,1)} custom-call(bf16[512,256]{1,0:T(8,128)(2,1)S(1)} %copy-done.4, bf16[512,256]{1,0:T(8,128)(2,1)S(1)} %collective-permute-done.recv_x, bf16[512,256]{1,0:T(8,128)(2,1)S(1)} %get-tuple-element.30.keep_g, bf16[512,256]{1,0:T(8,128)(2,1)S(1)} %collective-permute-done.1.recv_g, ...), custom_call_target="tpu_custom_call" | custom-call | flops 1207959552 | bytes 1441792 | tf_op jit(solution)/shard_map/pallas_call | solution.py:42
  65.9 5.6 %all-to-all-start.2 = ((bf16[32,96,256]{2,1,0:T(8,128)(2,1)}), bf16[32,96,256]{2,1,0:T(8,128)(2,1)S(1)}, u32[]{:S(2)}, u32[]{:S(2)}) async-start(bf16[32,96,256]{2,1,0:T(8,128)(2,1)} %bitcast.11), calls=%async_computation.2 | async-start | bytes 3145728 | tf_op jit(solution)/shard_map/all_to_all | solution.py:343
  71.5 1.5 %shard_map.106 = bf16[512,256]{1,0:T(8,128)(2,1)} custom-call(bf16[512,256]{1,0:T(8,128)(2,1)S(1)} %get-tuple-element.34.first_grad, bf16[2304,256]{1,0:T(8,128)(2,1)S(1)} %bitcast.24), custom_call_target="tpu_custom_call" | custom-call | flops 603979776 | bytes 1441792 | tf_op jit(solution)/shard_map/pallas_call | solution.py:42
  73.0 18.8 %all-to-all-done.2 = bf16[32,96,256]{2,1,0:T(8,128)(2,1)S(1)} async-done(((bf16[32,96,256]{2,1,0:T(8,128)(2,1)}), bf16[32,96,256]{2,1,0:T(8,128)(2,1)S(1)}, u32[]{:S(2)}, u32[]{:S(2)}) %all-to-all-start.2) | async-done | bytes 1572896 | tf_op jit(solution)/shard_map/all_to_all | solution.py:343
  91.8 0.2 reduce_sum.12
  92.0 0.7 collective-permute-start.5
  92.7 1.8 %collective-permute-start.4 = (bf16[96,256]{1,0:T(8,128)(2,1)S(1)}, bf16[96,256]{1,0:T(8,128)(2,1)S(1)}, u32[]{:S(2)}, u32[]{:S(2)}) collective-permute-start(bf16[96,256]{1,0:T(8,128)(2,1)S(1)} %reduce_sum.12), channel_id=1, source_target_pairs={{0,64},{64,128},{128,192},{192,0},{1,65},{65,129},{129,193},{193,1... | collective-permute-start | bytes 147464 | tf_op jit(solution)/shard_map/ppermute | solution.py:347
  94.5 1.5 %collective-permute-start.3 = (bf16[96,256]{1,0:T(8,128)(2,1)S(1)}, bf16[96,256]{1,0:T(8,128)(2,1)S(1)}, u32[]{:S(2)}, u32[]{:S(2)}) collective-permute-start(bf16[96,256]{1,0:T(8,128)(2,1)S(1)} %reduce_sum.12), channel_id=1, source_target_pairs={{0,128},{64,192},{128,0},{192,64},{1,129},{65,193},{129,1},{193,65... | collective-permute-start | bytes 147464 | tf_op jit(solution)/shard_map/ppermute | solution.py:347
  96.0 0.1 collective-permute-done.5
  96.1 2.3 %collective-permute-done.4 = bf16[96,256]{1,0:T(8,128)(2,1)S(1)} collective-permute-done((bf16[96,256]{1,0:T(8,128)(2,1)S(1)}, bf16[96,256]{1,0:T(8,128)(2,1)S(1)}, u32[]{:S(2)}, u32[]{:S(2)}) %collective-permute-start.4) | collective-permute-done | bytes 49184 | tf_op jit(solution)/shard_map/ppermute | solution.py:347
  98.4 3.3 %collective-permute-done.3 = bf16[96,256]{1,0:T(8,128)(2,1)S(1)} collective-permute-done((bf16[96,256]{1,0:T(8,128)(2,1)S(1)}, bf16[96,256]{1,0:T(8,128)(2,1)S(1)}, u32[]{:S(2)}, u32[]{:S(2)}) %collective-permute-start.3) | collective-permute-done | bytes 49184 | tf_op jit(solution)/shard_map/ppermute | solution.py:347
  101.7 0.2 broadcast_in_dim.2
  101.9 26.0 %all_to_all.21 = bf16[32,96,256]{2,1,0:T(8,128)(2,1)S(1)} all-to-all(bf16[32,96,256]{2,1,0:T(8,128)(2,1)S(1)} %broadcast_in_dim.2), channel_id=1, replica_groups=mesh['zh'=4,'zl'=2,'x'=4,'y'=4,'core'=2] {'zl','x','y'}, dimensions={0} | all-to-all | bytes 3145728 | tf_op jit(solution)/shard_map/all_to_all | solution.py:287
  127.8 4.1 %collective-permute-start.6 = (bf16[3072,256]{1,0:T(8,128)(2,1)S(1)}, bf16[3072,256]{1,0:T(8,128)(2,1)S(1)}, u32[]{:S(2)}, u32[]{:S(2)}) collective-permute-start(bf16[3072,256]{1,0:T(8,128)(2,1)S(1)} %bitcast.18), channel_id=1, source_target_pairs={{0,1},{1,0},{2,3},{3,2},{4,5},{5,4},{6,7},{7,6},{8,9},{9,8},{10,11... | collective-permute-start | bytes 4718600 | tf_op jit(solution)/shard_map/ppermute | solution.py:277
  131.9 1.7 %shard_map.107 = (f32[2304,256]{1,0:T(8,128)}, f32[2304,256]{1,0:T(8,128)}, f32[768,256]{1,0:T(8,128)}, f32[768,256]{1,0:T(8,128)}) custom-call(s32[1]{0:T(128)} %bitcast.pos, bf16[3072,256]{1,0:T(8,128)(2,1)S(1)} %bitcast.19), custom_call_target="tpu_custom_call" | custom-call | bytes 1572868 | tf_op jit(solution)/shard_map/pallas_call | solution.py:42
  133.7 1.3 collective-permute-done.6.half
  134.9 1.7 %shard_map.108 = (f32[2304,256]{1,0:T(8,128)}, f32[2304,256]{1,0:T(8,128)}, f32[768,256]{1,0:T(8,128)}, f32[768,256]{1,0:T(8,128)}) custom-call(s32[1]{0:T(128)} %bitcast.pos, bf16[3072,256]{1,0:T(8,128)(2,1)S(1)} %collective-permute-done.6.half, ...), custom_call_target="tpu_custom_call", output_to_operand_aliasing={{0}: (2, {}), {1}: (3, {}), {2}: (4, {}), {3}: (5, {})} | custom-call | bytes 7864324 | tf_op jit(solution)/shard_map/pallas_call | solution.py:42
  (9 shorter events, 0.0 us)
Async XLA Ops:
  38.1 19.4 %copy-start = (bf16[3,3,256,256]{3,2,1,0:T(8,128)(2,1)S(1)}, bf16[3,3,256,256]{3,2,1,0:T(8,128)(2,1)}, u32[]{:S(2)}) copy-start(bf16[3,3,256,256]{3,2,1,0:T(8,128)(2,1)} %param.9) | copy-start | bytes 3538948
  38.1 19.4 %copy-start.3 = (bf16[2,512,256]{2,1,0:T(8,128)(2,1)S(1)}, bf16[2,512,256]{2,1,0:T(8,128)(2,1)}, u32[]{:S(2)}) copy-start(bf16[2,512,256]{2,1,0:T(8,128)(2,1)} %get-tuple-element.29.slopes) | copy-start | bytes 1572868
  41.6 20.5 %copy-start.2 = (bf16[2,32,16,256]{3,2,1,0:T(8,128)(2,1)S(1)}, bf16[2,32,16,256]{3,2,1,0:T(8,128)(2,1)}, u32[]{:S(2)}) copy-start(bf16[2,32,16,256]{3,2,1,0:T(8,128)(2,1)} %get-tuple-element.32) | copy-start | bytes 1572868
  41.7 15.8 %all-to-all-start.1 = ((bf16[32,16,256]{2,1,0:T(8,128)(2,1)}), bf16[32,16,256]{2,1,0:T(8,128)(2,1)S(1)}, u32[]{:S(2)}, u32[]{:S(2)}) async-start(bf16[32,16,256]{2,1,0:T(8,128)(2,1)} %bitcast.31), calls=%async_computation.1 | async-start | bytes 524288 | tf_op jit(solution)/shard_map/all_to_all | solution.py:282
  47.0 15.1 %collective-permute-start.2 = (bf16[2,32,16,256]{3,2,1,0:T(8,128)(2,1)}, bf16[2,32,16,256]{3,2,1,0:T(8,128)(2,1)S(1)}, u32[]{:S(2)}, u32[]{:S(2)}) collective-permute-start(bf16[2,32,16,256]{3,2,1,0:T(8,128)(2,1)} %get-tuple-element.33), channel_id=1, source_target_pairs={{0,1},{1,0},{2,3},{3,2},{4,5},{5,4},{6,7},{7,6},{8,9},{9,8},{10,11... | collective-permute-start | bytes 1572872 | tf_op jit(solution)/shard_map/ppermute | solution.py:277
  49.0 13.8 %collective-permute-start = (bf16[512,256]{1,0:T(8,128)(2,1)}, bf16[512,256]{1,0:T(8,128)(2,1)S(1)}, u32[]{:S(2)}, u32[]{:S(2)}) collective-permute-start(bf16[512,256]{1,0:T(8,128)(2,1)} %get-tuple-element.26), channel_id=1, source_target_pairs={{0,1},{1,0},{2,3},{3,2},{4,5},{5,4},{6,7},{7,6},{8,9},{9,8},{10,11... | collective-permute-start | bytes 786440 | tf_op jit(solution)/shard_map/ppermute | solution.py:277
  57.4 5.9 %copy-start.4 = (bf16[512,256]{1,0:T(8,128)(2,1)S(1)}, bf16[512,256]{1,0:T(8,128)(2,1)}, u32[]{:S(2)}) copy-start(bf16[512,256]{1,0:T(8,128)(2,1)} %get-tuple-element.25.keep_x) | copy-start | bytes 786436
  58.3 5.0 %collective-permute-start.1 = (bf16[512,256]{1,0:T(8,128)(2,1)S(1)}, bf16[512,256]{1,0:T(8,128)(2,1)S(1)}, u32[]{:S(2)}, u32[]{:S(2)}) collective-permute-start(bf16[512,256]{1,0:T(8,128)(2,1)S(1)} %get-tuple-element.31), channel_id=1, source_target_pairs={{0,1},{1,0},{2,3},{3,2},{4,5},{5,4},{6,7},{7,6},{8,9},{9,8},{10,11... | collective-permute-start | bytes 786440 | tf_op jit(solution)/shard_map/ppermute | solution.py:277
  65.9 5.6 %copy-start.1 = (bf16[3,3,256,256]{3,2,1,0:T(8,128)(2,1)S(1)}, bf16[3,3,256,256]{3,2,1,0:T(8,128)(2,1)}, u32[]{:S(2)}) copy-start(bf16[3,3,256,256]{3,2,1,0:T(8,128)(2,1)} %param.8) | copy-start | bytes 3538948
  65.9 25.9 %all-to-all-start.2 = ((bf16[32,96,256]{2,1,0:T(8,128)(2,1)}), bf16[32,96,256]{2,1,0:T(8,128)(2,1)S(1)}, u32[]{:S(2)}, u32[]{:S(2)}) async-start(bf16[32,96,256]{2,1,0:T(8,128)(2,1)} %bitcast.11), calls=%async_computation.2 | async-start | bytes 3145728 | tf_op jit(solution)/shard_map/all_to_all | solution.py:343
  92.0 4.0 %collective-permute-start.5 = (bf16[96,256]{1,0:T(8,128)(2,1)S(1)}, bf16[96,256]{1,0:T(8,128)(2,1)S(1)}, u32[]{:S(2)}, u32[]{:S(2)}) collective-permute-start(bf16[96,256]{1,0:T(8,128)(2,1)S(1)} %reduce_sum.12), channel_id=1, source_target_pairs={{0,192},{64,0},{128,64},{192,128},{1,193},{65,1},{129,65},{193,129... | collective-permute-start | bytes 147464 | tf_op jit(solution)/shard_map/ppermute | solution.py:347
  92.7 5.7 %collective-permute-start.4 = (bf16[96,256]{1,0:T(8,128)(2,1)S(1)}, bf16[96,256]{1,0:T(8,128)(2,1)S(1)}, u32[]{:S(2)}, u32[]{:S(2)}) collective-permute-start(bf16[96,256]{1,0:T(8,128)(2,1)S(1)} %reduce_sum.12), channel_id=1, source_target_pairs={{0,64},{64,128},{128,192},{192,0},{1,65},{65,129},{129,193},{193,1... | collective-permute-start | bytes 147464 | tf_op jit(solution)/shard_map/ppermute | solution.py:347
  94.5 7.2 %collective-permute-start.3 = (bf16[96,256]{1,0:T(8,128)(2,1)S(1)}, bf16[96,256]{1,0:T(8,128)(2,1)S(1)}, u32[]{:S(2)}, u32[]{:S(2)}) collective-permute-start(bf16[96,256]{1,0:T(8,128)(2,1)S(1)} %reduce_sum.12), channel_id=1, source_target_pairs={{0,128},{64,192},{128,0},{192,64},{1,129},{65,193},{129,1},{193,65... | collective-permute-start | bytes 147464 | tf_op jit(solution)/shard_map/ppermute | solution.py:347
  127.8 7.1 %collective-permute-start.6 = (bf16[3072,256]{1,0:T(8,128)(2,1)S(1)}, bf16[3072,256]{1,0:T(8,128)(2,1)S(1)}, u32[]{:S(2)}, u32[]{:S(2)}) collective-permute-start(bf16[3072,256]{1,0:T(8,128)(2,1)S(1)} %bitcast.18), channel_id=1, source_target_pairs={{0,1},{1,0},{2,3},{3,2},{4,5},{5,4},{6,7},{7,6},{8,9},{9,8},{10,11... | collective-permute-start | bytes 4718600 | tf_op jit(solution)/shard_map/ppermute | solution.py:277

commit v7 on v6

--- a/solution.py
+++ b/solution.py
@@ -113,16 +113,16 @@
 
 
 def forward_kernel(pos, video_at, cot_at, w1_at, w2_at, both_at, slopes_at, keep, send, *rest):
-    video, first, act2, slopes, w1, w2, wide, sems = rest
+    video, first, both, slopes, w1, w2, wide, sems = rest
     pieces = [(video_at, video)]
     for source, target in ((w1_at, w1), (w2_at, w2)):
         for tap in range(3):
             part = pl.ds(tap * 3 * CH, 3 * CH)
             pieces.append((source.at[part], target.at[part]))
-    pieces.append((cot_at, both_at.at[:, COLS : 2 * COLS, :]))
+    pieces.append((cot_at, both.at[:, COLS : 2 * COLS, :]))
     pieces.append((slopes.at[0], slopes_at.at[0]))
     pieces.append((slopes.at[1], slopes_at.at[1]))
-    pieces.append((act2, both_at.at[:, 0:COLS, :]))
+    pieces.append((both, both_at))
     moves = [
         pltpu.make_async_copy(source, target, sems.at[at])
         for at, (source, target) in enumerate(pieces)
@@ -139,11 +139,12 @@
     moves[8].start()
     fill_windows(wide, first[...])
     act, slope = silu_pair(conv_from(wide, w2, moves[4:7]))
-    act2[...] = act.astype(BF).reshape(PIX // COLS, COLS, CH)
+    both[:, 0:COLS, :] = act.astype(BF).reshape(PIX // COLS, COLS, CH)
+    moves[7].wait()
     moves[10].start()
     slopes[1] = slope.astype(BF)
     moves[9].start()
-    for move in moves[7:11]:
+    for move in moves[8:11]:
         move.wait()
     wait_by_core(sems, 11, stores)
 
@@ -282,6 +283,12 @@
     return lax.all_to_all(blocks, FRAME_AXES, 0, 0, tiled=True).reshape(PIX, CH)
 
 
+def scatter_sum(values, axes, count):
+    parts = values.reshape(count, -1, CH)
+    arrived = lax.all_to_all(parts, axes, 0, 0, tiled=True)
+    return jnp.sum(arrived.astype(F32), axis=0).astype(BF)
+
+
 def gather_all(values, axes, count):
     copies = jnp.broadcast_to(values[None], (count,) + values.shape)
     return lax.all_to_all(copies, axes, 0, 0, tiled=True).reshape(-1, CH)
@@ -303,7 +310,7 @@
         forward_kernel,
         [((rows, 2 * COLS, CH), BF), ((2, PIX, CH), BF), slab, slab],
         (pos, video.reshape(PIX, CH), cotangent.reshape(rows, COLS, CH), w1, w2),
-        [frame, frame, lines, both_slopes, space, space, wide, pltpu.SemaphoreType.DMA((13,))],
+        [frame, frame, pltpu.VMEM((rows, 2 * COLS, CH), BF), both_slopes, space, space, wide, pltpu.SemaphoreType.DMA((13,))],
         2 * conv_flops,
         (1, 2, 3, 4),
         (0, 1, 2, 3),
@@ -339,17 +346,12 @@
         2 * conv_flops,
     )
 
-    (grad_input,) = call(input_kernel, [slab], (first_grad, w1), [wide], conv_flops)
-    part = lax.all_to_all(part.reshape(32, -1, CH), ("zl", "x", "y"), 0, 0, tiled=True)
-    part, grad_input = lax.optimization_barrier((part, grad_input))
-    part = jnp.sum(part.astype(F32), axis=0).astype(BF)
-    near, far, other = (
-        lax.ppermute(part, "zh", [(at, (at + step) % 4) for at in range(4)]).astype(F32)
-        for step in (1, 3, 2)
-    )
-    part = ((part.astype(F32) + other) + (near + far)).astype(BF)
+    part = scatter_sum(part, ("zl", "x", "y"), 32)
+    part = jnp.sum(gather_all(part, "zh", 4).reshape(4, -1, CH).astype(F32), axis=0).astype(BF)
     part = gather_all(part, ("zl", "x", "y"), 32)
     peer = swap_cores(part)
+    part, first_grad = lax.optimization_barrier((part, first_grad))
+    (grad_input,) = call(input_kernel, [slab], (first_grad, w1), [wide], conv_flops)
     grads = [((9 * CH, CH), F32)] * 2 + [((3 * CH, CH), F32)] * 2
     scratch = [pltpu.VMEM((12 * CH, CH), F32), pltpu.SemaphoreType.DMA((4,))]
     outs = call(

time: 137 us -> 132 us (0.964)
  blocking collectives: 54.2 us -> 88.1 us
  waiting for transfers between devices: 34.6 us -> 8.87 us
  starting transfers between devices: 24.8 us -> 16.6 us
  Pallas kernels: 21.8 us -> 16.8 us
    all_to_all x0 -> x1, blocking collectives: none -> 26.6 us  [scatter_sum(): arrived = lax.all_to_all(parts, axes, 0, 0, tiled=True)]
    all_to_all x1 -> x0, waiting for transfers between devices: 18.8 us -> none  [body(): lax.all_to_all(part.reshape(32, -1, CH), ('zl', 'x', 'y'), 0, 0, tiled=True)]
    all_to_all x1 -> x2, blocking collectives: 26 us -> 33.3 us  [gather_all(): return lax.all_to_all(copies, axes, 0, 0, tiled=True).reshape(-1, CH)]
    ppermute x3 -> x0, waiting for transfers between devices: 5.7 us -> none  [body(): lax.ppermute(part, 'zh', [(at, (at + step) % 4) for at in range(4)])]
    all_to_all x1 -> x0, starting transfers between devices: 5.57 us -> none  [body(): lax.all_to_all(part.reshape(32, -1, CH), ('zl', 'x', 'y'), 0, 0, tiled=True)]
    pallas_call x8, Pallas kernels: 21.8 us -> 16.8 us  [call(): pl.pallas_call(kernel, out_shape=[jax.ShapeDtypeStruct(shape, kind) for s...]
    ppermute x3 -> x0, starting transfers between devices: 3.93 us -> none  [body(): lax.ppermute(part, 'zh', [(at, (at + step) % 4) for at in range(4)])]
  transfers between devices with their start and end apart: 9 -> 5, of which waited for: 7 -> 2; matrix products, arithmetic and copies ran while one was open for 0% -> 0% of each run, Pallas kernels for 3% -> 4%
where the time goes in v7:
time: 132 us
  blocking collectives  88.1 us (67%)
  Pallas kernels  16.8 us (13%)
  starting transfers between devices  16.6 us (13%)
  waiting for transfers between devices  8.87 us (7%)
    all_to_all x2, blocking collectives, gather_all(): return lax.all_to_all(copies, axes, 0, 0, tiled=True).reshape(-1, CH)  33.3 us
    all_to_all x1, blocking collectives, body(): both = lax.all_to_all(both, FRAME_AXES, 0, 0, tiled=True)  28.3 us
    all_to_all x1, blocking collectives, scatter_sum(): arrived = lax.all_to_all(parts, axes, 0, 0, tiled=True)  26.6 us
    pallas_call x8, Pallas kernels, call(): pl.pallas_call(kernel, out_shape=[jax.ShapeDtypeStruct(shape, kind) for s...  16.8 us
    ppermute x4, starting transfers between devices, swap_cores(): return lax.ppermute(values, 'core', [(0, 1), (1, 0)])  11.2 us
    all_to_all x1, waiting for transfers between devices, swap_frames(): return lax.all_to_all(blocks, FRAME_AXES, 0, 0, tiled=True).reshape(PIX, CH)  8.35 us
    all_to_all x1, starting transfers between devices, swap_frames(): return lax.all_to_all(blocks, FRAME_AXES, 0, 0, tiled=True).reshape(PIX, CH)  5.35 us
  transfers between devices with their start and end apart: 5, of which 2 were waited for; matrix products, arithmetic and copies ran while one was open for 0% of the time, Pallas kernels for 4%

profile of v7, /device:TPU:1, one launch (start us, length us, event | category | flops | bytes accessed | tf_op | source)
XLA Modules:
  0.0 131.5 jit_solution(4293585666220072809)
XLA Ops:
  0.6 5.3 %shard_map.101 = (bf16[32,32,256]{2,1,0:T(8,128)(2,1)}, bf16[2,512,256]{2,1,0:T(8,128)(2,1)}, bf16[512,256]{1,0:T(8,128)(2,1)}, bf16[512,256]{1,0:T(8,128)(2,1)}) custom-call(s32[1]{0:T(128)} %bitcast.pos, bf16[512,256]{1,0:T(8,128)(2,1)} %bitcast.35, bf16[32,16,256]{2,1,0:T(8,128)(2,1)} %bitcast.36, bf16[2304,256]{1,0:T(8,128)(2,1)} %bitcast.24, ...), custom_call_target="tpu_custom_call" | custom-call | flops 1207959552 | bytes 2883588 | tf_op jit(solution)/shard_map/pallas_call | solution.py:42
  5.9 28.3 %all_to_all.25.both_at = bf16[32,32,256]{2,1,0:T(8,128)(2,1)} all-to-all(bf16[32,32,256]{2,1,0:T(8,128)(2,1)} %get-tuple-element.27), channel_id=1, replica_groups=mesh['zh'=4,'zl'=2,'x'=4,'y'=4,'core'=2] {'zh','zl','x'}, dimensions={0} | all-to-all | bytes 1048576 | tf_op jit(solution)/shard_map/all_to_all | solution.py:319
  34.2 0.0 copy-start
  34.2 0.0 copy-start.3
  34.2 3.6 %shard_map.102 = (bf16[512,256]{1,0:T(8,128)(2,1)}, bf16[2,32,16,256]{3,2,1,0:T(8,128)(2,1)}, bf16[2,32,16,256]{3,2,1,0:T(8,128)(2,1)}) custom-call(s32[1]{0:T(128)} %bitcast.pos, bf16[32,32,256]{2,1,0:T(8,128)(2,1)} %all_to_all.25.both_at, bf16[768,256]{1,0:T(8,128)(2,1)} %bitcast.33, bf16[768,256]{1,0:T(8,128)(2,1)} %bitcast.34), custom_call_target="tpu_custom_call" | custom-call | flops 603979776 | bytes 1310724 | tf_op jit(solution)/shard_map/pallas_call | solution.py:42
  37.7 0.0 copy-start.2
  37.7 5.4 %all-to-all-start.1 = ((bf16[32,16,256]{2,1,0:T(8,128)(2,1)}), bf16[32,16,256]{2,1,0:T(8,128)(2,1)S(1)}, u32[]{:S(2)}, u32[]{:S(2)}) async-start(bf16[32,16,256]{2,1,0:T(8,128)(2,1)} %bitcast.32), calls=%async_computation.1 | async-start | bytes 524288 | tf_op jit(solution)/shard_map/all_to_all | solution.py:283
  43.1 2.0 %collective-permute-start.2 = (bf16[2,32,16,256]{3,2,1,0:T(8,128)(2,1)}, bf16[2,32,16,256]{3,2,1,0:T(8,128)(2,1)S(1)}, u32[]{:S(2)}, u32[]{:S(2)}) collective-permute-start(bf16[2,32,16,256]{3,2,1,0:T(8,128)(2,1)} %get-tuple-element.33), channel_id=1, source_target_pairs={{0,1},{1,0},{2,3},{3,2},{4,5},{5,4},{6,7},{7,6},{8,9},{9,8},{10,11... | collective-permute-start | bytes 1572872 | tf_op jit(solution)/shard_map/ppermute | solution.py:278
  45.1 0.1 collective-permute-start
  45.2 8.3 %all-to-all-done.1 = bf16[32,16,256]{2,1,0:T(8,128)(2,1)S(1)} async-done(((bf16[32,16,256]{2,1,0:T(8,128)(2,1)}), bf16[32,16,256]{2,1,0:T(8,128)(2,1)S(1)}, u32[]{:S(2)}, u32[]{:S(2)}) %all-to-all-start.1) | async-done | bytes 262176 | tf_op jit(solution)/shard_map/all_to_all | solution.py:283
  53.5 0.0 copy-done
  53.5 0.0 copy-done.3
  53.5 0.9 shard_map.103
  54.4 3.8 %collective-permute-start.1 = (bf16[512,256]{1,0:T(8,128)(2,1)S(1)}, bf16[512,256]{1,0:T(8,128)(2,1)S(1)}, u32[]{:S(2)}, u32[]{:S(2)}) collective-permute-start(bf16[512,256]{1,0:T(8,128)(2,1)S(1)} %get-tuple-element.31), channel_id=1, source_target_pairs={{0,1},{1,0},{2,3},{3,2},{4,5},{5,4},{6,7},{7,6},{8,9},{9,8},{10,11... | collective-permute-start | bytes 786440 | tf_op jit(solution)/shard_map/ppermute | solution.py:278
  58.2 0.0 collective-permute-done.2
  58.2 0.0 copy-done.2
  58.2 0.6 shard_map.104.time_part
  58.8 0.0 collective-permute-done.recv_x
  58.9 0.5 collective-permute-done.1.recv_g
  59.4 0.0 copy-done.4
  59.4 1.5 %shard_map.105 = bf16[3072,256]{1,0:T(8,128)(2,1)S(1)} custom-call(bf16[512,256]{1,0:T(8,128)(2,1)S(1)} %copy-done.4, bf16[512,256]{1,0:T(8,128)(2,1)S(1)} %collective-permute-done.recv_x, bf16[512,256]{1,0:T(8,128)(2,1)S(1)} %get-tuple-element.30.keep_g, bf16[512,256]{1,0:T(8,128)(2,1)S(1)} %collective-permute-done.1.recv_g, ...), custom_call_target="tpu_custom_call" | custom-call | flops 1207959552 | bytes 1441792 | tf_op jit(solution)/shard_map/pallas_call | solution.py:42
  60.9 26.6 %all_to_all.26 = bf16[32,96,256]{2,1,0:T(8,128)(2,1)S(1)} all-to-all(bf16[32,96,256]{2,1,0:T(8,128)(2,1)S(1)} %bitcast.20), channel_id=1, replica_groups=mesh['zh'=4,'zl'=2,'x'=4,'y'=4,'core'=2] {'zl','x','y'}, dimensions={0} | all-to-all | bytes 3145728 | tf_op jit(solution)/shard_map/all_to_all | solution.py:288
  87.4 0.2 reduce_sum.24
  87.7 11.0 %all_to_all.27 = bf16[4,96,256]{2,1,0:T(8,128)(2,1)S(1)} all-to-all(bf16[4,96,256]{2,1,0:T(8,128)(2,1)S(1)} %broadcast_in_dim.4), channel_id=1, replica_groups=mesh['zh'=4,'zl'=2,'x'=4,'y'=4,'core'=2] {'zh'}, dimensions={0} | all-to-all | bytes 393216 | tf_op jit(solution)/shard_map/all_to_all | solution.py:294
  98.7 0.2 broadcast_in_dim.5
  98.9 22.3 %all_to_all.28 = bf16[32,96,256]{2,1,0:T(8,128)(2,1)S(1)} all-to-all(bf16[32,96,256]{2,1,0:T(8,128)(2,1)S(1)} %broadcast_in_dim.5), channel_id=1, replica_groups=mesh['zh'=4,'zl'=2,'x'=4,'y'=4,'core'=2] {'zl','x','y'}, dimensions={0} | all-to-all | bytes 3145728 | tf_op jit(solution)/shard_map/all_to_all | solution.py:294
  121.2 5.3 %collective-permute-start.3 = (bf16[3072,256]{1,0:T(8,128)(2,1)S(1)}, bf16[3072,256]{1,0:T(8,128)(2,1)S(1)}, u32[]{:S(2)}, u32[]{:S(2)}) collective-permute-start(bf16[3072,256]{1,0:T(8,128)(2,1)S(1)} %bitcast.18), channel_id=1, source_target_pairs={{0,1},{1,0},{2,3},{3,2},{4,5},{5,4},{6,7},{7,6},{8,9},{9,8},{10,11... | collective-permute-start | bytes 4718600 | tf_op jit(solution)/shard_map/ppermute | solution.py:278
  126.5 1.7 %shard_map.107 = (f32[2304,256]{1,0:T(8,128)}, f32[2304,256]{1,0:T(8,128)}, f32[768,256]{1,0:T(8,128)}, f32[768,256]{1,0:T(8,128)}) custom-call(s32[1]{0:T(128)} %bitcast.pos, bf16[3072,256]{1,0:T(8,128)(2,1)S(1)} %bitcast.19), custom_call_target="tpu_custom_call" | custom-call | bytes 1572868 | tf_op jit(solution)/shard_map/pallas_call | solution.py:42
  128.3 0.0 copy-done.1
  128.3 1.5 %shard_map.106 = bf16[512,256]{1,0:T(8,128)(2,1)} custom-call(bf16[512,256]{1,0:T(8,128)(2,1)S(1)} %get-tuple-element.35.first_grad, bf16[2304,256]{1,0:T(8,128)(2,1)S(1)} %bitcast.25), custom_call_target="tpu_custom_call" | custom-call | flops 603979776 | bytes 1441792 | tf_op jit(solution)/shard_map/pallas_call | solution.py:42
  129.8 0.0 collective-permute-done.3.half
  129.8 1.7 %shard_map.108 = (f32[2304,256]{1,0:T(8,128)}, f32[2304,256]{1,0:T(8,128)}, f32[768,256]{1,0:T(8,128)}, f32[768,256]{1,0:T(8,128)}) custom-call(s32[1]{0:T(128)} %bitcast.pos, bf16[3072,256]{1,0:T(8,128)(2,1)S(1)} %collective-permute-done.3.half, ...), custom_call_target="tpu_custom_call", output_to_operand_aliasing={{0}: (2, {}), {1}: (3, {}), {2}: (4, {}), {3}: (5, {})} | custom-call | bytes 7864324 | tf_op jit(solution)/shard_map/pallas_call | solution.py:42
  (4 shorter events, 0.0 us)
Async XLA Ops:
  34.2 19.3 %copy-start = (bf16[3,3,256,256]{3,2,1,0:T(8,128)(2,1)S(1)}, bf16[3,3,256,256]{3,2,1,0:T(8,128)(2,1)}, u32[]{:S(2)}) copy-start(bf16[3,3,256,256]{3,2,1,0:T(8,128)(2,1)} %param.9) | copy-start | bytes 3538948
  34.2 19.3 %copy-start.3 = (bf16[2,512,256]{2,1,0:T(8,128)(2,1)S(1)}, bf16[2,512,256]{2,1,0:T(8,128)(2,1)}, u32[]{:S(2)}) copy-start(bf16[2,512,256]{2,1,0:T(8,128)(2,1)} %get-tuple-element.29.slopes) | copy-start | bytes 1572868
  37.7 20.5 %copy-start.2 = (bf16[2,32,16,256]{3,2,1,0:T(8,128)(2,1)S(1)}, bf16[2,32,16,256]{3,2,1,0:T(8,128)(2,1)}, u32[]{:S(2)}) copy-start(bf16[2,32,16,256]{3,2,1,0:T(8,128)(2,1)} %get-tuple-element.32) | copy-start | bytes 1572868
  37.7 15.8 %all-to-all-start.1 = ((bf16[32,16,256]{2,1,0:T(8,128)(2,1)}), bf16[32,16,256]{2,1,0:T(8,128)(2,1)S(1)}, u32[]{:S(2)}, u32[]{:S(2)}) async-start(bf16[32,16,256]{2,1,0:T(8,128)(2,1)} %bitcast.32), calls=%async_computation.1 | async-start | bytes 524288 | tf_op jit(solution)/shard_map/all_to_all | solution.py:283
  43.1 15.1 %collective-permute-start.2 = (bf16[2,32,16,256]{3,2,1,0:T(8,128)(2,1)}, bf16[2,32,16,256]{3,2,1,0:T(8,128)(2,1)S(1)}, u32[]{:S(2)}, u32[]{:S(2)}) collective-permute-start(bf16[2,32,16,256]{3,2,1,0:T(8,128)(2,1)} %get-tuple-element.33), channel_id=1, source_target_pairs={{0,1},{1,0},{2,3},{3,2},{4,5},{5,4},{6,7},{7,6},{8,9},{9,8},{10,11... | collective-permute-start | bytes 1572872 | tf_op jit(solution)/shard_map/ppermute | solution.py:278
  45.1 13.8 %collective-permute-start = (bf16[512,256]{1,0:T(8,128)(2,1)}, bf16[512,256]{1,0:T(8,128)(2,1)S(1)}, u32[]{:S(2)}, u32[]{:S(2)}) collective-permute-start(bf16[512,256]{1,0:T(8,128)(2,1)} %get-tuple-element.26), channel_id=1, source_target_pairs={{0,1},{1,0},{2,3},{3,2},{4,5},{5,4},{6,7},{7,6},{8,9},{9,8},{10,11... | collective-permute-start | bytes 786440 | tf_op jit(solution)/shard_map/ppermute | solution.py:278
  53.5 5.9 %copy-start.4 = (bf16[512,256]{1,0:T(8,128)(2,1)S(1)}, bf16[512,256]{1,0:T(8,128)(2,1)}, u32[]{:S(2)}) copy-start(bf16[512,256]{1,0:T(8,128)(2,1)} %get-tuple-element.25.keep_x) | copy-start | bytes 786436
  54.4 5.0 %collective-permute-start.1 = (bf16[512,256]{1,0:T(8,128)(2,1)S(1)}, bf16[512,256]{1,0:T(8,128)(2,1)S(1)}, u32[]{:S(2)}, u32[]{:S(2)}) collective-permute-start(bf16[512,256]{1,0:T(8,128)(2,1)S(1)} %get-tuple-element.31), channel_id=1, source_target_pairs={{0,1},{1,0},{2,3},{3,2},{4,5},{5,4},{6,7},{7,6},{8,9},{9,8},{10,11... | collective-permute-start | bytes 786440 | tf_op jit(solution)/shard_map/ppermute | solution.py:278
  121.2 7.1 %copy-start.1 = (bf16[3,3,256,256]{3,2,1,0:T(8,128)(2,1)S(1)}, bf16[3,3,256,256]{3,2,1,0:T(8,128)(2,1)}, u32[]{:S(2)}) copy-start(bf16[3,3,256,256]{3,2,1,0:T(8,128)(2,1)} %param.8) | copy-start | bytes 3538948
  121.2 8.6 %collective-permute-start.3 = (bf16[3072,256]{1,0:T(8,128)(2,1)S(1)}, bf16[3072,256]{1,0:T(8,128)(2,1)S(1)}, u32[]{:S(2)}, u32[]{:S(2)}) collective-permute-start(bf16[3072,256]{1,0:T(8,128)(2,1)S(1)} %bitcast.18), channel_id=1, source_target_pairs={{0,1},{1,0},{2,3},{3,2},{4,5},{5,4},{6,7},{7,6},{8,9},{9,8},{10,11... | collective-permute-start | bytes 4718600 | tf_op jit(solution)/shard_map/ppermute | solution.py:278

commit v8 on v7

--- a/solution.py
+++ b/solution.py
@@ -12,6 +12,7 @@
 CH = 256
 COLS = 16
 PIX = 512
+HALF = PIX // 2
 PAD = PIX + 2 * COLS
 FRAME_AXES = ("zh", "zl", "x")
 SCALE = 1.0 / math.sqrt(131072)
@@ -81,14 +82,11 @@
     wide[COLS : COLS + PIX, 2 * CH : 3 * CH] = after.astype(BF)
 
 
-def conv_from(wide, weight, loads=(None, None, None)):
+def conv_half(wide, weight, half):
     total = None
-    for tap, load in enumerate(loads):
-        if load is not None:
-            load.wait()
-        term = dot_nn(
-            wide[tap * COLS : tap * COLS + PIX, :], weight[tap * 3 * CH : (tap + 1) * 3 * CH, :]
-        )
+    for tap in range(3):
+        at = tap * COLS + half * HALF
+        term = dot_nn(wide[at : at + HALF, :], weight[tap * 3 * CH : (tap + 1) * 3 * CH, :])
         total = term if total is None else total + term
     return total
 
@@ -121,8 +119,11 @@
             pieces.append((source.at[part], target.at[part]))
     pieces.append((cot_at, both.at[:, COLS : 2 * COLS, :]))
     pieces.append((slopes.at[0], slopes_at.at[0]))
-    pieces.append((slopes.at[1], slopes_at.at[1]))
-    pieces.append((both, both_at))
+    for half in range(2):
+        part = pl.ds(half * HALF, HALF)
+        pieces.append((slopes.at[1, part], slopes_at.at[1, part]))
+        part = pl.ds(half * (HALF // COLS), HALF // COLS)
+        pieces.append((both.at[part], both_at.at[part]))
     moves = [
         pltpu.make_async_copy(source, target, sems.at[at])
         for at, (source, target) in enumerate(pieces)
@@ -131,34 +132,43 @@
         move.start()
     moves[0].wait()
     fill_windows(wide, video[...])
-    act, slope = silu_pair(conv_from(wide, w1, moves[1:4]))
-    first[...] = act.astype(BF)
+    for move in moves[1:4]:
+        move.wait()
+    for half in range(2):
+        rows = slice(half * HALF, (half + 1) * HALF)
+        act, slope = silu_pair(conv_half(wide, w1, half))
+        first[rows, :] = act.astype(BF)
+        slopes[0, rows, :] = slope.astype(BF)
     stores = [(first, video, keep), (video, first, send)]
-    start_by_core(pos, sems, 11, stores)
-    slopes[0] = slope.astype(BF)
+    start_by_core(pos, sems, 13, stores)
     moves[8].start()
     fill_windows(wide, first[...])
-    act, slope = silu_pair(conv_from(wide, w2, moves[4:7]))
-    both[:, 0:COLS, :] = act.astype(BF).reshape(PIX // COLS, COLS, CH)
-    moves[7].wait()
-    moves[10].start()
-    slopes[1] = slope.astype(BF)
-    moves[9].start()
-    for move in moves[8:11]:
+    for move in moves[4:8]:
         move.wait()
-    wait_by_core(sems, 11, stores)
-
-
-def ahead_sum(padded, weight):
+    for half in range(2):
+        rows = slice(half * HALF, (half + 1) * HALF)
+        act, slope = silu_pair(conv_half(wide, w2, half))
+        lines = HALF // COLS
+        both[half * lines : (half + 1) * lines, 0:COLS, :] = act.astype(BF).reshape(lines, COLS, CH)
+        slopes[1, rows, :] = slope.astype(BF)
+    for move in moves[9:13]:
+        move.start()
+    for move in moves[8:13]:
+        move.wait()
+    wait_by_core(sems, 13, stores)
+
+
+def ahead_sum(padded, weight, half):
     total = None
     for step in range(3):
-        term = dot_nt(padded[step * COLS : step * COLS + PIX, :], weight[step * CH : (step + 1) * CH, :])
+        at = step * COLS + half * HALF
+        term = dot_nt(padded[at : at + HALF, :], weight[step * CH : (step + 1) * CH, :])
         total = term if total is None else total + term
     return total
 
 
 def time_kernel(pos, both_at, wt1_at, wt2_at, back_at, keep, send, *rest):
-    act, cot, wt1, wt2, time_act, time_grad, act_back, behind, ahead, sems = rest
+    act, cot, wt1, wt2, time_act, time_grad, act_back, behind, ahead, later, sems = rest
     loads = [
         pltpu.make_async_copy(source, target, sems.at[at])
         for at, (source, target) in enumerate(
@@ -176,21 +186,24 @@
     loads[0].wait()
     ahead[0:PIX, :] = cot[...].reshape(PIX, CH)
     ahead[PIX:PAD, :] = edge
-    loads[1].wait()
-    back = ahead_sum(ahead, wt2)
     loads[2].wait()
     behind[0 : 2 * COLS, :] = edge
     behind[2 * COLS : PAD, :] = act[...].reshape(PIX, CH)
+    loads[1].wait()
     loads[3].wait()
-    pre = None
-    for step in range(3):
-        at = (2 - step) * COLS
-        term = dot_nn(behind[at : at + PIX, :], wt1[step * CH : (step + 1) * CH, :])
-        pre = term if pre is None else pre + term
-    value, slope = silu_pair(pre)
-    grad = (back * slope).astype(BF)
-    time_act[...] = value.astype(BF).reshape(PIX // COLS, COLS, CH)
-    time_grad[...] = grad.reshape(PIX // COLS, COLS, CH)
+    for half in range(2):
+        pre = None
+        for step in range(3):
+            at = (2 - step) * COLS + half * HALF
+            term = dot_nn(behind[at : at + HALF, :], wt1[step * CH : (step + 1) * CH, :])
+            pre = term if pre is None else pre + term
+        value, slope = silu_pair(pre)
+        grad = (ahead_sum(ahead, wt2, half) * slope).astype(BF)
+        lines = slice(half * (HALF // COLS), (half + 1) * (HALF // COLS))
+        time_act[lines] = value.astype(BF).reshape(HALF // COLS, COLS, CH)
+        time_grad[lines] = grad.reshape(HALF // COLS, COLS, CH)
+        later[half * HALF : (half + 1) * HALF, :] = grad
+    later[PIX:PAD, :] = edge
     stores = [
         (act, time_act, keep.at[0]),
         (time_grad, cot, keep.at[1]),
@@ -198,12 +211,15 @@
         (cot, time_grad, send.at[1]),
     ]
     start_by_core(pos, sems, 4, stores)
-    ahead[0:PIX, :] = grad
-    act_back[...] = ahead_sum(ahead, wt1).astype(BF)
-    last = pltpu.make_async_copy(act_back, back_at, sems.at[8])
-    last.start()
+    tails = []
+    for half in range(2):
+        rows = pl.ds(half * HALF, HALF)
+        act_back[rows, :] = ahead_sum(later, wt1, half).astype(BF)
+        tails.append(pltpu.make_async_copy(act_back.at[rows], back_at.at[rows], sems.at[8 + half]))
+        tails[half].start()
     wait_by_core(sems, 4, stores)
-    last.wait()
+    for tail in tails:
+        tail.wait()
 
 
 def time_weights_kernel(keep, recv, out):
@@ -231,16 +247,24 @@
         send[...] = second
 
 
-def space_weights_kernel(keep_x, recv_x, keep_g, recv_g, time_part, out, wide, other):
+def own_weights_kernel(keep_x, keep_g, out, wide):
     fill_windows(wide, keep_x[...])
-    fill_windows(other, recv_x[...])
     for tap in range(3):
         for side in range(3):
             rows = slice(tap * COLS, tap * COLS + PIX)
             lanes = slice(side * CH, (side + 1) * CH)
-            total = dot_tn(wide[rows, lanes], keep_g[...])
-            total = total + dot_tn(other[rows, lanes], recv_g[...])
             at = (tap * 3 + side) * CH
+            out[at : at + CH, :] = dot_tn(wide[rows, lanes], keep_g[...])
+
+
+def space_weights_kernel(partial, recv_x, recv_g, time_part, out, wide):
+    fill_windows(wide, recv_x[...])
+    for tap in range(3):
+        for side in range(3):
+            rows = slice(tap * COLS, tap * COLS + PIX)
+            lanes = slice(side * CH, (side + 1) * CH)
+            at = (tap * 3 + side) * CH
+            total = partial[at : at + CH, :] + dot_tn(wide[rows, lanes], recv_g[...])
             out[at : at + CH, :] = (total * SCALE).astype(BF)
     out[9 * CH : 12 * CH, :] = time_part[...]
 
@@ -310,7 +334,7 @@
         forward_kernel,
         [((rows, 2 * COLS, CH), BF), ((2, PIX, CH), BF), slab, slab],
         (pos, video.reshape(PIX, CH), cotangent.reshape(rows, COLS, CH), w1, w2),
-        [frame, frame, pltpu.VMEM((rows, 2 * COLS, CH), BF), both_slopes, space, space, wide, pltpu.SemaphoreType.DMA((13,))],
+        [frame, frame, pltpu.VMEM((rows, 2 * COLS, CH), BF), both_slopes, space, space, wide, pltpu.SemaphoreType.DMA((15,))],
         2 * conv_flops,
         (1, 2, 3, 4),
         (0, 1, 2, 3),
@@ -322,7 +346,7 @@
         time_kernel,
         [slab, pair, pair],
         (pos, both, wt1, wt2),
-        [lines, lines, time, time, lines, lines, frame, tall, tall, pltpu.SemaphoreType.DMA((9,))],
+        [lines, lines, time, time, lines, lines, frame, tall, tall, tall, pltpu.SemaphoreType.DMA((10,))],
         3 * time_flops,
         (1, 2, 3),
         (0, 1, 2),
@@ -334,16 +358,20 @@
     (time_part,) = call(
         time_weights_kernel, [((3 * CH, CH), BF)], (keep_t, recv_t), (), 2 * time_flops
     )
+    act_back, time_part = lax.optimization_barrier((act_back, time_part))
     first_grad, keep_g, send_g = call(
         backward_kernel, [slab, slab, slab], (pos, act_back, slopes, w2), [wide], conv_flops
     )
     recv_g = swap_cores(send_g)
+    (partial,) = call(
+        own_weights_kernel, [((9 * CH, CH), F32)], (keep_x, keep_g), [wide], conv_flops
+    )
     (part,) = call(
         space_weights_kernel,
         [((12 * CH, CH), BF)],
-        (keep_x, recv_x, keep_g, recv_g, time_part),
-        [wide, wide],
-        2 * conv_flops,
+        (partial, recv_x, recv_g, time_part),
+        [wide],
+        conv_flops,
     )
 
     part = scatter_sum(part, ("zl", "x", "y"), 32)

time: 132 us -> 131 us (level)
  starting transfers between devices: 16.6 us -> 14.9 us
    pallas_call x8 -> x9, Pallas kernels: 16.8 us -> 15.5 us  [call(): pl.pallas_call(kernel, out_shape=[jax.ShapeDtypeStruct(shape, kind) for s...]
where the time goes in v8:
time: 131 us
  blocking collectives  88.2 us (67%)
  Pallas kernels  15.5 us (12%)
  starting transfers between devices  14.9 us (11%)
  waiting for transfers between devices  9.92 us (8%)
    all_to_all x2, blocking collectives, gather_all(): return lax.all_to_all(copies, axes, 0, 0, tiled=True).reshape(-1, CH)  33.3 us
    all_to_all x1, blocking collectives, body(): both = lax.all_to_all(both, FRAME_AXES, 0, 0, tiled=True)  28.3 us
    all_to_all x1, blocking collectives, scatter_sum(): arrived = lax.all_to_all(parts, axes, 0, 0, tiled=True)  26.7 us
    pallas_call x9, Pallas kernels, call(): pl.pallas_call(kernel, out_shape=[jax.ShapeDtypeStruct(shape, kind) for s...  15.5 us
    ppermute x4, starting transfers between devices, swap_cores(): return lax.ppermute(values, 'core', [(0, 1), (1, 0)])  10.5 us
    all_to_all x1, waiting for transfers between devices, swap_frames(): return lax.all_to_all(blocks, FRAME_AXES, 0, 0, tiled=True).reshape(PIX, CH)  9.63 us
    all_to_all x1, starting transfers between devices, swap_frames(): return lax.all_to_all(blocks, FRAME_AXES, 0, 0, tiled=True).reshape(PIX, CH)  4.41 us
  transfers between devices with their start and end apart: 5, of which 2 were waited for; matrix products, arithmetic and copies ran while one was open for 0% of the time, Pallas kernels for 4%

profile of v8, /device:TPU:1, one launch (start us, length us, event | category | flops | bytes accessed | tf_op | source)
XLA Modules:
  0.0 130.9 jit_solution(3262882446762532530)
XLA Ops:
  0.6 4.2 %shard_map.101 = (bf16[32,32,256]{2,1,0:T(8,128)(2,1)}, bf16[2,512,256]{2,1,0:T(8,128)(2,1)}, bf16[512,256]{1,0:T(8,128)(2,1)}, bf16[512,256]{1,0:T(8,128)(2,1)}) custom-call(s32[1]{0:T(128)} %bitcast.pos, bf16[512,256]{1,0:T(8,128)(2,1)} %bitcast.35, bf16[32,16,256]{2,1,0:T(8,128)(2,1)} %bitcast.36, bf16[2304,256]{1,0:T(8,128)(2,1)} %bitcast.24, ...), custom_call_target="tpu_custom_call" | custom-call | flops 1207959552 | bytes 2883588 | tf_op jit(solution)/shard_map/pallas_call | solution.py:43
  4.9 28.3 %all_to_all.25.both_at = bf16[32,32,256]{2,1,0:T(8,128)(2,1)} all-to-all(bf16[32,32,256]{2,1,0:T(8,128)(2,1)} %get-tuple-element.28), channel_id=1, replica_groups=mesh['zh'=4,'zl'=2,'x'=4,'y'=4,'core'=2] {'zh','zl','x'}, dimensions={0} | all-to-all | bytes 1048576 | tf_op jit(solution)/shard_map/all_to_all | solution.py:343
  33.1 0.0 copy-start.4
  33.1 3.1 %shard_map.102 = (bf16[512,256]{1,0:T(8,128)(2,1)}, bf16[2,32,16,256]{3,2,1,0:T(8,128)(2,1)}, bf16[2,32,16,256]{3,2,1,0:T(8,128)(2,1)}) custom-call(s32[1]{0:T(128)} %bitcast.pos, bf16[32,32,256]{2,1,0:T(8,128)(2,1)} %all_to_all.25.both_at, bf16[768,256]{1,0:T(8,128)(2,1)} %bitcast.33, bf16[768,256]{1,0:T(8,128)(2,1)} %bitcast.34), custom_call_target="tpu_custom_call" | custom-call | flops 603979776 | bytes 1310724 | tf_op jit(solution)/shard_map/pallas_call | solution.py:43
  36.2 0.0 copy-start.1
  36.2 2.4 %collective-permute-start = (bf16[2,32,16,256]{3,2,1,0:T(8,128)(2,1)}, bf16[2,32,16,256]{3,2,1,0:T(8,128)(2,1)S(1)}, u32[]{:S(2)}, u32[]{:S(2)}) collective-permute-start(bf16[2,32,16,256]{3,2,1,0:T(8,128)(2,1)} %get-tuple-element.31), channel_id=1, source_target_pairs={{0,1},{1,0},{2,3},{3,2},{4,5},{5,4},{6,7},{7,6},{8,9},{9,8},{10,11... | collective-permute-start | bytes 1572872 | tf_op jit(solution)/shard_map/ppermute | solution.py:302
  38.6 4.4 %all-to-all-start.1 = ((bf16[32,16,256]{2,1,0:T(8,128)(2,1)}), bf16[32,16,256]{2,1,0:T(8,128)(2,1)S(1)}, u32[]{:S(2)}, u32[]{:S(2)}) async-start(bf16[32,16,256]{2,1,0:T(8,128)(2,1)} %bitcast.32), calls=%async_computation.1 | async-start | bytes 524288 | tf_op jit(solution)/shard_map/all_to_all | solution.py:307
  43.1 0.5 collective-permute-start.1
  43.6 0.0 collective-permute-done
  43.6 1.0 copy-done.3
  44.6 0.6 shard_map.103.time_part
  45.3 9.6 %all-to-all-done.1 = bf16[32,16,256]{2,1,0:T(8,128)(2,1)S(1)} async-done(((bf16[32,16,256]{2,1,0:T(8,128)(2,1)}), bf16[32,16,256]{2,1,0:T(8,128)(2,1)S(1)}, u32[]{:S(2)}, u32[]{:S(2)}) %all-to-all-start.1) | async-done | bytes 262176 | tf_op jit(solution)/shard_map/all_to_all | solution.py:307
  54.9 0.0 copy-done.4
  54.9 0.0 copy-done.1
  54.9 0.9 shard_map.104
  55.8 2.2 %collective-permute-start.2 = (bf16[512,256]{1,0:T(8,128)(2,1)S(1)}, bf16[512,256]{1,0:T(8,128)(2,1)S(1)}, u32[]{:S(2)}, u32[]{:S(2)}) collective-permute-start(bf16[512,256]{1,0:T(8,128)(2,1)S(1)} %get-tuple-element.36), channel_id=1, source_target_pairs={{0,1},{1,0},{2,3},{3,2},{4,5},{5,4},{6,7},{7,6},{8,9},{9,8},{10,11... | collective-permute-start | bytes 786440 | tf_op jit(solution)/shard_map/ppermute | solution.py:302
  58.0 0.0 copy-done
  58.0 0.9 shard_map.105.partial
  58.9 0.0 collective-permute-done.1.recv_x
  58.9 0.3 collective-permute-done.2.recv_g
  59.1 0.8 shard_map.106
  60.0 26.7 %all_to_all.26 = bf16[32,96,256]{2,1,0:T(8,128)(2,1)S(1)} all-to-all(bf16[32,96,256]{2,1,0:T(8,128)(2,1)S(1)} %bitcast.20), channel_id=1, replica_groups=mesh['zh'=4,'zl'=2,'x'=4,'y'=4,'core'=2] {'zl','x','y'}, dimensions={0} | all-to-all | bytes 3145728 | tf_op jit(solution)/shard_map/all_to_all | solution.py:312
  86.7 0.2 reduce_sum.24
  86.9 11.1 %all_to_all.27 = bf16[4,96,256]{2,1,0:T(8,128)(2,1)S(1)} all-to-all(bf16[4,96,256]{2,1,0:T(8,128)(2,1)S(1)} %broadcast_in_dim.4), channel_id=1, replica_groups=mesh['zh'=4,'zl'=2,'x'=4,'y'=4,'core'=2] {'zh'}, dimensions={0} | all-to-all | bytes 393216 | tf_op jit(solution)/shard_map/all_to_all | solution.py:318
  98.1 0.2 broadcast_in_dim.5
  98.2 22.2 %all_to_all.28 = bf16[32,96,256]{2,1,0:T(8,128)(2,1)S(1)} all-to-all(bf16[32,96,256]{2,1,0:T(8,128)(2,1)S(1)} %broadcast_in_dim.5), channel_id=1, replica_groups=mesh['zh'=4,'zl'=2,'x'=4,'y'=4,'core'=2] {'zl','x','y'}, dimensions={0} | all-to-all | bytes 3145728 | tf_op jit(solution)/shard_map/all_to_all | solution.py:318
  120.5 5.4 %collective-permute-start.3 = (bf16[3072,256]{1,0:T(8,128)(2,1)S(1)}, bf16[3072,256]{1,0:T(8,128)(2,1)S(1)}, u32[]{:S(2)}, u32[]{:S(2)}) collective-permute-start(bf16[3072,256]{1,0:T(8,128)(2,1)S(1)} %bitcast.18), channel_id=1, source_target_pairs={{0,1},{1,0},{2,3},{3,2},{4,5},{5,4},{6,7},{7,6},{8,9},{9,8},{10,11... | collective-permute-start | bytes 4718600 | tf_op jit(solution)/shard_map/ppermute | solution.py:302
  125.8 1.7 %shard_map.108 = (f32[2304,256]{1,0:T(8,128)}, f32[2304,256]{1,0:T(8,128)}, f32[768,256]{1,0:T(8,128)}, f32[768,256]{1,0:T(8,128)}) custom-call(s32[1]{0:T(128)} %bitcast.pos, bf16[3072,256]{1,0:T(8,128)(2,1)S(1)} %bitcast.19), custom_call_target="tpu_custom_call" | custom-call | bytes 1572868 | tf_op jit(solution)/shard_map/pallas_call | solution.py:43
  127.6 0.0 copy-done.2
  127.6 1.5 %shard_map.107 = bf16[512,256]{1,0:T(8,128)(2,1)} custom-call(bf16[512,256]{1,0:T(8,128)(2,1)S(1)} %get-tuple-element.39.first_grad, bf16[2304,256]{1,0:T(8,128)(2,1)S(1)} %bitcast.25), custom_call_target="tpu_custom_call" | custom-call | flops 603979776 | bytes 1441792 | tf_op jit(solution)/shard_map/pallas_call | solution.py:43
  129.1 0.0 collective-permute-done.3.half
  129.1 1.7 %shard_map.109 = (f32[2304,256]{1,0:T(8,128)}, f32[2304,256]{1,0:T(8,128)}, f32[768,256]{1,0:T(8,128)}, f32[768,256]{1,0:T(8,128)}) custom-call(s32[1]{0:T(128)} %bitcast.pos, bf16[3072,256]{1,0:T(8,128)(2,1)S(1)} %collective-permute-done.3.half, ...), custom_call_target="tpu_custom_call", output_to_operand_aliasing={{0}: (2, {}), {1}: (3, {}), {2}: (4, {}), {3}: (5, {})} | custom-call | bytes 7864324 | tf_op jit(solution)/shard_map/pallas_call | solution.py:43
  (5 shorter events, 0.1 us)
Async XLA Ops:
  33.1 21.8 %copy-start.4 = (bf16[2,512,256]{2,1,0:T(8,128)(2,1)S(1)}, bf16[2,512,256]{2,1,0:T(8,128)(2,1)}, u32[]{:S(2)}) copy-start(bf16[2,512,256]{2,1,0:T(8,128)(2,1)} %get-tuple-element.33.slopes) | copy-start | bytes 1572868
  36.2 18.7 %copy-start.1 = (bf16[3,3,256,256]{3,2,1,0:T(8,128)(2,1)S(1)}, bf16[3,3,256,256]{3,2,1,0:T(8,128)(2,1)}, u32[]{:S(2)}) copy-start(bf16[3,3,256,256]{3,2,1,0:T(8,128)(2,1)} %param.9) | copy-start | bytes 3538948
  36.2 7.3 %collective-permute-start = (bf16[2,32,16,256]{3,2,1,0:T(8,128)(2,1)}, bf16[2,32,16,256]{3,2,1,0:T(8,128)(2,1)S(1)}, u32[]{:S(2)}, u32[]{:S(2)}) collective-permute-start(bf16[2,32,16,256]{3,2,1,0:T(8,128)(2,1)} %get-tuple-element.31), channel_id=1, source_target_pairs={{0,1},{1,0},{2,3},{3,2},{4,5},{5,4},{6,7},{7,6},{8,9},{9,8},{10,11... | collective-permute-start | bytes 1572872 | tf_op jit(solution)/shard_map/ppermute | solution.py:302
  38.6 16.2 %all-to-all-start.1 = ((bf16[32,16,256]{2,1,0:T(8,128)(2,1)}), bf16[32,16,256]{2,1,0:T(8,128)(2,1)S(1)}, u32[]{:S(2)}, u32[]{:S(2)}) async-start(bf16[32,16,256]{2,1,0:T(8,128)(2,1)} %bitcast.32), calls=%async_computation.1 | async-start | bytes 524288 | tf_op jit(solution)/shard_map/all_to_all | solution.py:307
  43.1 15.8 %collective-permute-start.1 = (bf16[512,256]{1,0:T(8,128)(2,1)}, bf16[512,256]{1,0:T(8,128)(2,1)S(1)}, u32[]{:S(2)}, u32[]{:S(2)}) collective-permute-start(bf16[512,256]{1,0:T(8,128)(2,1)} %get-tuple-element.35), channel_id=1, source_target_pairs={{0,1},{1,0},{2,3},{3,2},{4,5},{5,4},{6,7},{7,6},{8,9},{9,8},{10,11... | collective-permute-start | bytes 786440 | tf_op jit(solution)/shard_map/ppermute | solution.py:302
  43.6 1.0 copy-start.3
  44.6 13.4 %copy-start = (bf16[512,256]{1,0:T(8,128)(2,1)S(1)}, bf16[512,256]{1,0:T(8,128)(2,1)}, u32[]{:S(2)}) copy-start(bf16[512,256]{1,0:T(8,128)(2,1)} %get-tuple-element.27.keep_x) | copy-start | bytes 786436
  55.8 3.4 %collective-permute-start.2 = (bf16[512,256]{1,0:T(8,128)(2,1)S(1)}, bf16[512,256]{1,0:T(8,128)(2,1)S(1)}, u32[]{:S(2)}, u32[]{:S(2)}) collective-permute-start(bf16[512,256]{1,0:T(8,128)(2,1)S(1)} %get-tuple-element.36), channel_id=1, source_target_pairs={{0,1},{1,0},{2,3},{3,2},{4,5},{5,4},{6,7},{7,6},{8,9},{9,8},{10,11... | collective-permute-start | bytes 786440 | tf_op jit(solution)/shard_map/ppermute | solution.py:302
  120.5 7.1 %copy-start.2 = (bf16[3,3,256,256]{3,2,1,0:T(8,128)(2,1)S(1)}, bf16[3,3,256,256]{3,2,1,0:T(8,128)(2,1)}, u32[]{:S(2)}) copy-start(bf16[3,3,256,256]{3,2,1,0:T(8,128)(2,1)} %param.8) | copy-start | bytes 3538948
  120.5 8.7 %collective-permute-start.3 = (bf16[3072,256]{1,0:T(8,128)(2,1)S(1)}, bf16[3072,256]{1,0:T(8,128)(2,1)S(1)}, u32[]{:S(2)}, u32[]{:S(2)}) collective-permute-start(bf16[3072,256]{1,0:T(8,128)(2,1)S(1)} %bitcast.18), channel_id=1, source_target_pairs={{0,1},{1,0},{2,3},{3,2},{4,5},{5,4},{6,7},{7,6},{8,9},{9,8},{10,11... | collective-permute-start | bytes 4718600 | tf_op jit(solution)/shard_map/ppermute | solution.py:302

commit v9 on v8

--- a/solution.py
+++ b/solution.py
@@ -358,7 +358,6 @@
     (time_part,) = call(
         time_weights_kernel, [((3 * CH, CH), BF)], (keep_t, recv_t), (), 2 * time_flops
     )
-    act_back, time_part = lax.optimization_barrier((act_back, time_part))
     first_grad, keep_g, send_g = call(
         backward_kernel, [slab, slab, slab], (pos, act_back, slopes, w2), [wide], conv_flops
     )

time: 131 us -> 131 us (level)
  blocking collectives: 88.2 us -> 90.3 us
  waiting for transfers between devices: 9.92 us -> 8.42 us
    all_to_all x2, blocking collectives: 33.3 us -> 35.2 us  [gather_all(): return lax.all_to_all(copies, axes, 0, 0, tiled=True).reshape(-1, CH)]
  transfers between devices with their start and end apart: 5 -> 5, of which waited for: 2 -> 1; matrix products, arithmetic and copies ran while one was open for 0% -> 0% of each run, Pallas kernels for 4% -> 4%
where the time goes in v9:
time: 131 us
  blocking collectives  90.3 us (69%)
  Pallas kernels  15.6 us (12%)
  starting transfers between devices  15.2 us (12%)
  waiting for transfers between devices  8.42 us (6%)
    all_to_all x2, blocking collectives, gather_all(): return lax.all_to_all(copies, axes, 0, 0, tiled=True).reshape(-1, CH)  35.2 us
    all_to_all x1, blocking collectives, body(): both = lax.all_to_all(both, FRAME_AXES, 0, 0, tiled=True)  28.3 us
    all_to_all x1, blocking collectives, scatter_sum(): arrived = lax.all_to_all(parts, axes, 0, 0, tiled=True)  26.8 us
    pallas_call x9, Pallas kernels, call(): pl.pallas_call(kernel, out_shape=[jax.ShapeDtypeStruct(shape, kind) for s...  15.6 us
    ppermute x4, starting transfers between devices, swap_cores(): return lax.ppermute(values, 'core', [(0, 1), (1, 0)])  9.86 us
    all_to_all x1, waiting for transfers between devices, swap_frames(): return lax.all_to_all(blocks, FRAME_AXES, 0, 0, tiled=True).reshape(PIX, CH)  8.41 us
    all_to_all x1, starting transfers between devices, swap_frames(): return lax.all_to_all(blocks, FRAME_AXES, 0, 0, tiled=True).reshape(PIX, CH)  5.35 us
  transfers between devices with their start and end apart: 5, of which 1 were waited for; matrix products, arithmetic and copies ran while one was open for 0% of the time, Pallas kernels for 4%

profile of v9, /device:TPU:1, one launch (start us, length us, event | category | flops | bytes accessed | tf_op | source)
XLA Modules:
  0.0 130.7 jit_solution(10863111474562115623)
XLA Ops:
  0.6 4.2 %shard_map.101 = (bf16[32,32,256]{2,1,0:T(8,128)(2,1)}, bf16[2,512,256]{2,1,0:T(8,128)(2,1)}, bf16[512,256]{1,0:T(8,128)(2,1)}, bf16[512,256]{1,0:T(8,128)(2,1)}) custom-call(s32[1]{0:T(128)} %bitcast.pos, bf16[512,256]{1,0:T(8,128)(2,1)} %bitcast.35, bf16[32,16,256]{2,1,0:T(8,128)(2,1)} %bitcast.36, bf16[2304,256]{1,0:T(8,128)(2,1)} %bitcast.24, ...), custom_call_target="tpu_custom_call" | custom-call | flops 1207959552 | bytes 2883588 | tf_op jit(solution)/shard_map/pallas_call | solution.py:43
  4.9 28.3 %all_to_all.25.both_at = bf16[32,32,256]{2,1,0:T(8,128)(2,1)} all-to-all(bf16[32,32,256]{2,1,0:T(8,128)(2,1)} %get-tuple-element.26), channel_id=1, replica_groups=mesh['zh'=4,'zl'=2,'x'=4,'y'=4,'core'=2] {'zh','zl','x'}, dimensions={0} | all-to-all | bytes 1048576 | tf_op jit(solution)/shard_map/all_to_all | solution.py:343
  33.1 3.2 %shard_map.102 = (bf16[512,256]{1,0:T(8,128)(2,1)}, bf16[2,32,16,256]{3,2,1,0:T(8,128)(2,1)}, bf16[2,32,16,256]{3,2,1,0:T(8,128)(2,1)}) custom-call(s32[1]{0:T(128)} %bitcast.pos, bf16[32,32,256]{2,1,0:T(8,128)(2,1)} %all_to_all.25.both_at, bf16[768,256]{1,0:T(8,128)(2,1)} %bitcast.33, bf16[768,256]{1,0:T(8,128)(2,1)} %bitcast.34), custom_call_target="tpu_custom_call" | custom-call | flops 603979776 | bytes 1310724 | tf_op jit(solution)/shard_map/pallas_call | solution.py:43
  36.3 0.0 copy-start
  36.3 5.4 %all-to-all-start.1 = ((bf16[32,16,256]{2,1,0:T(8,128)(2,1)}), bf16[32,16,256]{2,1,0:T(8,128)(2,1)S(1)}, u32[]{:S(2)}, u32[]{:S(2)}) async-start(bf16[32,16,256]{2,1,0:T(8,128)(2,1)} %bitcast.32), calls=%async_computation.1 | async-start | bytes 524288 | tf_op jit(solution)/shard_map/all_to_all | solution.py:307
  41.7 1.9 %collective-permute-start.2 = (bf16[2,32,16,256]{3,2,1,0:T(8,128)(2,1)}, bf16[2,32,16,256]{3,2,1,0:T(8,128)(2,1)S(1)}, u32[]{:S(2)}, u32[]{:S(2)}) collective-permute-start(bf16[2,32,16,256]{3,2,1,0:T(8,128)(2,1)} %get-tuple-element.33), channel_id=1, source_target_pairs={{0,1},{1,0},{2,3},{3,2},{4,5},{5,4},{6,7},{7,6},{8,9},{9,8},{10,11... | collective-permute-start | bytes 1572872 | tf_op jit(solution)/shard_map/ppermute | solution.py:302
  43.6 0.0 copy-done.5
  43.6 0.1 collective-permute-start
  43.7 8.4 %all-to-all-done.1 = bf16[32,16,256]{2,1,0:T(8,128)(2,1)S(1)} async-done(((bf16[32,16,256]{2,1,0:T(8,128)(2,1)}), bf16[32,16,256]{2,1,0:T(8,128)(2,1)S(1)}, u32[]{:S(2)}, u32[]{:S(2)}) %all-to-all-start.1) | async-done | bytes 262176 | tf_op jit(solution)/shard_map/all_to_all | solution.py:307
  52.1 0.0 copy-done.1
  52.1 0.0 copy-done.4
  52.1 0.9 shard_map.103
  53.0 0.0 copy-start.3
  53.0 3.8 %collective-permute-start.1 = (bf16[512,256]{1,0:T(8,128)(2,1)S(1)}, bf16[512,256]{1,0:T(8,128)(2,1)S(1)}, u32[]{:S(2)}, u32[]{:S(2)}) collective-permute-start(bf16[512,256]{1,0:T(8,128)(2,1)S(1)} %get-tuple-element.31), channel_id=1, source_target_pairs={{0,1},{1,0},{2,3},{3,2},{4,5},{5,4},{6,7},{7,6},{8,9},{9,8},{10,11... | collective-permute-start | bytes 786440 | tf_op jit(solution)/shard_map/ppermute | solution.py:302
  56.8 0.0 copy-done
  56.8 0.8 shard_map.104.partial
  57.7 0.0 collective-permute-done.2
  57.7 0.6 shard_map.105.time_part
  58.3 0.0 collective-permute-done.recv_x
  58.3 0.0 collective-permute-done.1.recv_g
  58.3 0.9 shard_map.106
  59.2 26.8 %all_to_all.26 = bf16[32,96,256]{2,1,0:T(8,128)(2,1)S(1)} all-to-all(bf16[32,96,256]{2,1,0:T(8,128)(2,1)S(1)} %bitcast.20), channel_id=1, replica_groups=mesh['zh'=4,'zl'=2,'x'=4,'y'=4,'core'=2] {'zl','x','y'}, dimensions={0} | all-to-all | bytes 3145728 | tf_op jit(solution)/shard_map/all_to_all | solution.py:312
  86.0 0.2 reduce_sum.24
  86.2 10.9 %all_to_all.27 = bf16[4,96,256]{2,1,0:T(8,128)(2,1)S(1)} all-to-all(bf16[4,96,256]{2,1,0:T(8,128)(2,1)S(1)} %broadcast_in_dim.4), channel_id=1, replica_groups=mesh['zh'=4,'zl'=2,'x'=4,'y'=4,'core'=2] {'zh'}, dimensions={0} | all-to-all | bytes 393216 | tf_op jit(solution)/shard_map/all_to_all | solution.py:318
  97.1 0.2 broadcast_in_dim.5
  97.3 24.3 %all_to_all.28 = bf16[32,96,256]{2,1,0:T(8,128)(2,1)S(1)} all-to-all(bf16[32,96,256]{2,1,0:T(8,128)(2,1)S(1)} %broadcast_in_dim.5), channel_id=1, replica_groups=mesh['zh'=4,'zl'=2,'x'=4,'y'=4,'core'=2] {'zl','x','y'}, dimensions={0} | all-to-all | bytes 3145728 | tf_op jit(solution)/shard_map/all_to_all | solution.py:318
  121.6 4.0 %collective-permute-start.3 = (bf16[3072,256]{1,0:T(8,128)(2,1)S(1)}, bf16[3072,256]{1,0:T(8,128)(2,1)S(1)}, u32[]{:S(2)}, u32[]{:S(2)}) collective-permute-start(bf16[3072,256]{1,0:T(8,128)(2,1)S(1)} %bitcast.18), channel_id=1, source_target_pairs={{0,1},{1,0},{2,3},{3,2},{4,5},{5,4},{6,7},{7,6},{8,9},{9,8},{10,11... | collective-permute-start | bytes 4718600 | tf_op jit(solution)/shard_map/ppermute | solution.py:302
  125.7 1.7 %shard_map.108 = (f32[2304,256]{1,0:T(8,128)}, f32[2304,256]{1,0:T(8,128)}, f32[768,256]{1,0:T(8,128)}, f32[768,256]{1,0:T(8,128)}) custom-call(s32[1]{0:T(128)} %bitcast.pos, bf16[3072,256]{1,0:T(8,128)(2,1)S(1)} %bitcast.19), custom_call_target="tpu_custom_call" | custom-call | bytes 1572868 | tf_op jit(solution)/shard_map/pallas_call | solution.py:43
  127.4 0.0 copy-done.2
  127.4 1.5 %shard_map.107 = bf16[512,256]{1,0:T(8,128)(2,1)} custom-call(bf16[512,256]{1,0:T(8,128)(2,1)S(1)} %get-tuple-element.35.first_grad, bf16[2304,256]{1,0:T(8,128)(2,1)S(1)} %bitcast.25), custom_call_target="tpu_custom_call" | custom-call | flops 603979776 | bytes 1441792 | tf_op jit(solution)/shard_map/pallas_call | solution.py:43
  129.0 0.0 collective-permute-done.3.half
  129.0 1.7 %shard_map.109 = (f32[2304,256]{1,0:T(8,128)}, f32[2304,256]{1,0:T(8,128)}, f32[768,256]{1,0:T(8,128)}, f32[768,256]{1,0:T(8,128)}) custom-call(s32[1]{0:T(128)} %bitcast.pos, bf16[3072,256]{1,0:T(8,128)(2,1)S(1)} %collective-permute-done.3.half, ...), custom_call_target="tpu_custom_call", output_to_operand_aliasing={{0}: (2, {}), {1}: (3, {}), {2}: (4, {}), {3}: (5, {})} | custom-call | bytes 7864324 | tf_op jit(solution)/shard_map/pallas_call | solution.py:43
  (7 shorter events, 0.1 us)
Async XLA Ops:
  33.1 10.4 %copy-start.5 = (bf16[512,256]{1,0:T(8,128)(2,1)S(1)}, bf16[512,256]{1,0:T(8,128)(2,1)}, u32[]{:S(2)}) copy-start(bf16[512,256]{1,0:T(8,128)(2,1)} %get-tuple-element.30) | copy-start | bytes 786436
  33.1 18.9 %copy-start.1 = (bf16[3,3,256,256]{3,2,1,0:T(8,128)(2,1)S(1)}, bf16[3,3,256,256]{3,2,1,0:T(8,128)(2,1)}, u32[]{:S(2)}) copy-start(bf16[3,3,256,256]{3,2,1,0:T(8,128)(2,1)} %param.9) | copy-start | bytes 3538948
  33.1 18.9 %copy-start.4 = (bf16[2,512,256]{2,1,0:T(8,128)(2,1)S(1)}, bf16[2,512,256]{2,1,0:T(8,128)(2,1)}, u32[]{:S(2)}) copy-start(bf16[2,512,256]{2,1,0:T(8,128)(2,1)} %get-tuple-element.28.slopes) | copy-start | bytes 1572868
  36.3 20.5 %copy-start = (bf16[512,256]{1,0:T(8,128)(2,1)S(1)}, bf16[512,256]{1,0:T(8,128)(2,1)}, u32[]{:S(2)}) copy-start(bf16[512,256]{1,0:T(8,128)(2,1)} %get-tuple-element.25.keep_x) | copy-start | bytes 786436
  36.3 15.8 %all-to-all-start.1 = ((bf16[32,16,256]{2,1,0:T(8,128)(2,1)}), bf16[32,16,256]{2,1,0:T(8,128)(2,1)S(1)}, u32[]{:S(2)}, u32[]{:S(2)}) async-start(bf16[32,16,256]{2,1,0:T(8,128)(2,1)} %bitcast.32), calls=%async_computation.1 | async-start | bytes 524288 | tf_op jit(solution)/shard_map/all_to_all | solution.py:307
  41.7 16.0 %collective-permute-start.2 = (bf16[2,32,16,256]{3,2,1,0:T(8,128)(2,1)}, bf16[2,32,16,256]{3,2,1,0:T(8,128)(2,1)S(1)}, u32[]{:S(2)}, u32[]{:S(2)}) collective-permute-start(bf16[2,32,16,256]{3,2,1,0:T(8,128)(2,1)} %get-tuple-element.33), channel_id=1, source_target_pairs={{0,1},{1,0},{2,3},{3,2},{4,5},{5,4},{6,7},{7,6},{8,9},{9,8},{10,11... | collective-permute-start | bytes 1572872 | tf_op jit(solution)/shard_map/ppermute | solution.py:302
  43.6 14.7 %collective-permute-start = (bf16[512,256]{1,0:T(8,128)(2,1)S(1)}, bf16[512,256]{1,0:T(8,128)(2,1)S(1)}, u32[]{:S(2)}, u32[]{:S(2)}) collective-permute-start(bf16[512,256]{1,0:T(8,128)(2,1)S(1)} %copy-done.5), channel_id=1, source_target_pairs={{0,1},{1,0},{2,3},{3,2},{4,5},{5,4},{6,7},{7,6},{8,9},{9,8},{10,11... | collective-permute-start | bytes 786440 | tf_op jit(solution)/shard_map/ppermute | solution.py:302
  53.0 4.7 %copy-start.3 = (bf16[2,32,16,256]{3,2,1,0:T(8,128)(2,1)S(1)}, bf16[2,32,16,256]{3,2,1,0:T(8,128)(2,1)}, u32[]{:S(2)}) copy-start(bf16[2,32,16,256]{3,2,1,0:T(8,128)(2,1)} %get-tuple-element.32) | copy-start | bytes 1572868
  53.0 5.4 %collective-permute-start.1 = (bf16[512,256]{1,0:T(8,128)(2,1)S(1)}, bf16[512,256]{1,0:T(8,128)(2,1)S(1)}, u32[]{:S(2)}, u32[]{:S(2)}) collective-permute-start(bf16[512,256]{1,0:T(8,128)(2,1)S(1)} %get-tuple-element.31), channel_id=1, source_target_pairs={{0,1},{1,0},{2,3},{3,2},{4,5},{5,4},{6,7},{7,6},{8,9},{9,8},{10,11... | collective-permute-start | bytes 786440 | tf_op jit(solution)/shard_map/ppermute | solution.py:302
  121.6 5.8 %copy-start.2 = (bf16[3,3,256,256]{3,2,1,0:T(8,128)(2,1)S(1)}, bf16[3,3,256,256]{3,2,1,0:T(8,128)(2,1)}, u32[]{:S(2)}) copy-start(bf16[3,3,256,256]{3,2,1,0:T(8,128)(2,1)} %param.8) | copy-start | bytes 3538948
  121.6 7.3 %collective-permute-start.3 = (bf16[3072,256]{1,0:T(8,128)(2,1)S(1)}, bf16[3072,256]{1,0:T(8,128)(2,1)S(1)}, u32[]{:S(2)}, u32[]{:S(2)}) collective-permute-start(bf16[3072,256]{1,0:T(8,128)(2,1)S(1)} %bitcast.18), channel_id=1, source_target_pairs={{0,1},{1,0},{2,3},{3,2},{4,5},{5,4},{6,7},{7,6},{8,9},{9,8},{10,11... | collective-permute-start | bytes 4718600 | tf_op jit(solution)/shard_map/ppermute | solution.py:302

commit v10 on v9

--- a/solution.py
+++ b/solution.py
@@ -275,18 +275,18 @@
 
     def copies(at):
         space, time = targets[at]
-        rows = 3 * CH
-        for piece in range(3):
-            part = pl.ds(piece * rows, rows)
-            yield pltpu.make_async_copy(stage.at[part], space.at[part], sems.at[piece])
-        yield pltpu.make_async_copy(stage.at[pl.ds(3 * rows, rows)], time, sems.at[3])
+        for piece in range(12):
+            source = stage.at[pl.ds(piece * CH, CH)]
+            target = space if piece < 9 else time
+            part = pl.ds((piece if piece < 9 else piece - 9) * CH, CH)
+            yield pltpu.make_async_copy(source, target.at[part], sems.at[piece])
 
     for at in range(2):
 
         @pl.when((pos[0] ^ owner) == at)
         def _():
             for piece, copy in enumerate(copies(at)):
-                rows = slice(piece * 3 * CH, (piece + 1) * 3 * CH)
+                rows = slice(piece * CH, (piece + 1) * CH)
                 stage[rows, :] = half[rows, :].astype(F32)
                 copy.start()
             for copy in copies(at):
@@ -373,14 +373,14 @@
         conv_flops,
     )
 
-    part = scatter_sum(part, ("zl", "x", "y"), 32)
+    part = scatter_sum(part, ("y", "zl", "x"), 32)
     part = jnp.sum(gather_all(part, "zh", 4).reshape(4, -1, CH).astype(F32), axis=0).astype(BF)
-    part = gather_all(part, ("zl", "x", "y"), 32)
+    part = gather_all(part, ("y", "zl", "x"), 32)
     peer = swap_cores(part)
     part, first_grad = lax.optimization_barrier((part, first_grad))
     (grad_input,) = call(input_kernel, [slab], (first_grad, w1), [wide], conv_flops)
     grads = [((9 * CH, CH), F32)] * 2 + [((3 * CH, CH), F32)] * 2
-    scratch = [pltpu.VMEM((12 * CH, CH), F32), pltpu.SemaphoreType.DMA((4,))]
+    scratch = [pltpu.VMEM((12 * CH, CH), F32), pltpu.SemaphoreType.DMA((12,))]
     outs = call(
         functools.partial(spread_kernel, 0), grads, (pos, part), scratch, 0, (), (0, 1, 2, 3)
     )

time: 131 us -> 132 us (level)
  no operation moved by 1% of the time
where the time goes in v10:
time: 132 us; the launch traced here: 131 us
  blocking collectives  90.2 us (68%)
  starting transfers between devices  15.7 us (12%)
  Pallas kernels  15.6 us (12%)
  waiting for transfers between devices  8.42 us (6%)
    all_to_all x2, blocking collectives, gather_all(): return lax.all_to_all(copies, axes, 0, 0, tiled=True).reshape(-1, CH)  35 us
    all_to_all x1, blocking collectives, body(): both = lax.all_to_all(both, FRAME_AXES, 0, 0, tiled=True)  28.3 us
    all_to_all x1, blocking collectives, scatter_sum(): arrived = lax.all_to_all(parts, axes, 0, 0, tiled=True)  26.9 us
    pallas_call x9, Pallas kernels, call(): pl.pallas_call(kernel, out_shape=[jax.ShapeDtypeStruct(shape, kind) for s...  15.6 us
    ppermute x4, starting transfers between devices, swap_cores(): return lax.ppermute(values, 'core', [(0, 1), (1, 0)])  10.4 us
    all_to_all x1, waiting for transfers between devices, swap_frames(): return lax.all_to_all(blocks, FRAME_AXES, 0, 0, tiled=True).reshape(PIX, CH)  8.41 us
    all_to_all x1, starting transfers between devices, swap_frames(): return lax.all_to_all(blocks, FRAME_AXES, 0, 0, tiled=True).reshape(PIX, CH)  5.35 us
  transfers between devices with their start and end apart: 5, of which 1 were waited for; matrix products, arithmetic and copies ran while one was open for 0% of the time, Pallas kernels for 4%

profile of v10, /device:TPU:1, one launch (start us, length us, event | category | flops | bytes accessed | tf_op | source)
XLA Modules:
  0.0 131.3 jit_solution(1700367203799141115)
XLA Ops:
  0.6 4.2 %shard_map.101 = (bf16[32,32,256]{2,1,0:T(8,128)(2,1)}, bf16[2,512,256]{2,1,0:T(8,128)(2,1)}, bf16[512,256]{1,0:T(8,128)(2,1)}, bf16[512,256]{1,0:T(8,128)(2,1)}) custom-call(s32[1]{0:T(128)} %bitcast.pos, bf16[512,256]{1,0:T(8,128)(2,1)} %bitcast.35, bf16[32,16,256]{2,1,0:T(8,128)(2,1)} %bitcast.36, bf16[2304,256]{1,0:T(8,128)(2,1)} %bitcast.24, ...), custom_call_target="tpu_custom_call" | custom-call | flops 1207959552 | bytes 2883588 | tf_op jit(solution)/shard_map/pallas_call | solution.py:43
  4.9 28.3 %all_to_all.25.both_at = bf16[32,32,256]{2,1,0:T(8,128)(2,1)} all-to-all(bf16[32,32,256]{2,1,0:T(8,128)(2,1)} %get-tuple-element.26), channel_id=1, replica_groups=mesh['zh'=4,'zl'=2,'x'=4,'y'=4,'core'=2] {'zh','zl','x'}, dimensions={0} | all-to-all | bytes 1048576 | tf_op jit(solution)/shard_map/all_to_all | solution.py:343
  33.1 3.2 %shard_map.102 = (bf16[512,256]{1,0:T(8,128)(2,1)}, bf16[2,32,16,256]{3,2,1,0:T(8,128)(2,1)}, bf16[2,32,16,256]{3,2,1,0:T(8,128)(2,1)}) custom-call(s32[1]{0:T(128)} %bitcast.pos, bf16[32,32,256]{2,1,0:T(8,128)(2,1)} %all_to_all.25.both_at, bf16[768,256]{1,0:T(8,128)(2,1)} %bitcast.33, bf16[768,256]{1,0:T(8,128)(2,1)} %bitcast.34), custom_call_target="tpu_custom_call" | custom-call | flops 603979776 | bytes 1310724 | tf_op jit(solution)/shard_map/pallas_call | solution.py:43
  36.3 0.0 copy-start
  36.3 5.4 %all-to-all-start.1 = ((bf16[32,16,256]{2,1,0:T(8,128)(2,1)}), bf16[32,16,256]{2,1,0:T(8,128)(2,1)S(1)}, u32[]{:S(2)}, u32[]{:S(2)}) async-start(bf16[32,16,256]{2,1,0:T(8,128)(2,1)} %bitcast.32), calls=%async_computation.1 | async-start | bytes 524288 | tf_op jit(solution)/shard_map/all_to_all | solution.py:307
  41.7 1.9 %collective-permute-start.2 = (bf16[2,32,16,256]{3,2,1,0:T(8,128)(2,1)}, bf16[2,32,16,256]{3,2,1,0:T(8,128)(2,1)S(1)}, u32[]{:S(2)}, u32[]{:S(2)}) collective-permute-start(bf16[2,32,16,256]{3,2,1,0:T(8,128)(2,1)} %get-tuple-element.33), channel_id=1, source_target_pairs={{0,1},{1,0},{2,3},{3,2},{4,5},{5,4},{6,7},{7,6},{8,9},{9,8},{10,11... | collective-permute-start | bytes 1572872 | tf_op jit(solution)/shard_map/ppermute | solution.py:302
  43.6 0.0 copy-done.5
  43.6 0.1 collective-permute-start
  43.7 8.4 %all-to-all-done.1 = bf16[32,16,256]{2,1,0:T(8,128)(2,1)S(1)} async-done(((bf16[32,16,256]{2,1,0:T(8,128)(2,1)}), bf16[32,16,256]{2,1,0:T(8,128)(2,1)S(1)}, u32[]{:S(2)}, u32[]{:S(2)}) %all-to-all-start.1) | async-done | bytes 262176 | tf_op jit(solution)/shard_map/all_to_all | solution.py:307
  52.1 0.0 copy-done.1
  52.1 0.0 copy-done.4
  52.1 0.9 shard_map.103
  53.0 0.0 copy-start.3
  53.0 3.8 %collective-permute-start.1 = (bf16[512,256]{1,0:T(8,128)(2,1)S(1)}, bf16[512,256]{1,0:T(8,128)(2,1)S(1)}, u32[]{:S(2)}, u32[]{:S(2)}) collective-permute-start(bf16[512,256]{1,0:T(8,128)(2,1)S(1)} %get-tuple-element.31), channel_id=1, source_target_pairs={{0,1},{1,0},{2,3},{3,2},{4,5},{5,4},{6,7},{7,6},{8,9},{9,8},{10,11... | collective-permute-start | bytes 786440 | tf_op jit(solution)/shard_map/ppermute | solution.py:302
  56.8 0.0 copy-done
  56.8 0.8 shard_map.104.partial
  57.7 0.0 collective-permute-done.2
  57.7 0.0 copy-done.3
  57.7 0.6 shard_map.105.time_part
  58.3 0.0 collective-permute-done.recv_x
  58.3 0.0 collective-permute-done.1.recv_g
  58.3 0.9 shard_map.106
  59.2 26.9 %all_to_all.26 = bf16[32,96,256]{2,1,0:T(8,128)(2,1)S(1)} all-to-all(bf16[32,96,256]{2,1,0:T(8,128)(2,1)S(1)} %bitcast.20), channel_id=1, replica_groups=mesh['zh'=4,'zl'=2,'x'=4,'y'=4,'core'=2] {'y','zl','x'}, dimensions={0} | all-to-all | bytes 3145728 | tf_op jit(solution)/shard_map/all_to_all | solution.py:312
  86.1 0.2 reduce_sum.24
  86.4 10.6 %all_to_all.27 = bf16[4,96,256]{2,1,0:T(8,128)(2,1)S(1)} all-to-all(bf16[4,96,256]{2,1,0:T(8,128)(2,1)S(1)} %broadcast_in_dim.4), channel_id=1, replica_groups=mesh['zh'=4,'zl'=2,'x'=4,'y'=4,'core'=2] {'zh'}, dimensions={0} | all-to-all | bytes 393216 | tf_op jit(solution)/shard_map/all_to_all | solution.py:318
  97.0 0.2 broadcast_in_dim.5
  97.2 24.4 %all_to_all.28 = bf16[32,96,256]{2,1,0:T(8,128)(2,1)S(1)} all-to-all(bf16[32,96,256]{2,1,0:T(8,128)(2,1)S(1)} %broadcast_in_dim.5), channel_id=1, replica_groups=mesh['zh'=4,'zl'=2,'x'=4,'y'=4,'core'=2] {'y','zl','x'}, dimensions={0} | all-to-all | bytes 3145728 | tf_op jit(solution)/shard_map/all_to_all | solution.py:318
  121.6 4.6 %collective-permute-start.3 = (bf16[3072,256]{1,0:T(8,128)(2,1)S(1)}, bf16[3072,256]{1,0:T(8,128)(2,1)S(1)}, u32[]{:S(2)}, u32[]{:S(2)}) collective-permute-start(bf16[3072,256]{1,0:T(8,128)(2,1)S(1)} %bitcast.18), channel_id=1, source_target_pairs={{0,1},{1,0},{2,3},{3,2},{4,5},{5,4},{6,7},{7,6},{8,9},{9,8},{10,11... | collective-permute-start | bytes 4718600 | tf_op jit(solution)/shard_map/ppermute | solution.py:302
  126.2 1.8 %shard_map.108 = (f32[2304,256]{1,0:T(8,128)}, f32[2304,256]{1,0:T(8,128)}, f32[768,256]{1,0:T(8,128)}, f32[768,256]{1,0:T(8,128)}) custom-call(s32[1]{0:T(128)} %bitcast.pos, bf16[3072,256]{1,0:T(8,128)(2,1)S(1)} %bitcast.19), custom_call_target="tpu_custom_call" | custom-call | bytes 1572868 | tf_op jit(solution)/shard_map/pallas_call | solution.py:43
  128.0 1.5 %shard_map.107 = bf16[512,256]{1,0:T(8,128)(2,1)} custom-call(bf16[512,256]{1,0:T(8,128)(2,1)S(1)} %get-tuple-element.35.first_grad, bf16[2304,256]{1,0:T(8,128)(2,1)S(1)} %bitcast.25), custom_call_target="tpu_custom_call" | custom-call | flops 603979776 | bytes 1441792 | tf_op jit(solution)/shard_map/pallas_call | solution.py:43
  129.5 0.0 collective-permute-done.3.half
  129.5 1.8 %shard_map.109 = (f32[2304,256]{1,0:T(8,128)}, f32[2304,256]{1,0:T(8,128)}, f32[768,256]{1,0:T(8,128)}, f32[768,256]{1,0:T(8,128)}) custom-call(s32[1]{0:T(128)} %bitcast.pos, bf16[3072,256]{1,0:T(8,128)(2,1)S(1)} %collective-permute-done.3.half, ...), custom_call_target="tpu_custom_call", output_to_operand_aliasing={{0}: (2, {}), {1}: (3, {}), {2}: (4, {}), {3}: (5, {})} | custom-call | bytes 7864324 | tf_op jit(solution)/shard_map/pallas_call | solution.py:43
  (7 shorter events, 0.1 us)
Async XLA Ops:
  33.1 10.4 %copy-start.5 = (bf16[512,256]{1,0:T(8,128)(2,1)S(1)}, bf16[512,256]{1,0:T(8,128)(2,1)}, u32[]{:S(2)}) copy-start(bf16[512,256]{1,0:T(8,128)(2,1)} %get-tuple-element.30) | copy-start | bytes 786436
  33.1 18.9 %copy-start.1 = (bf16[3,3,256,256]{3,2,1,0:T(8,128)(2,1)S(1)}, bf16[3,3,256,256]{3,2,1,0:T(8,128)(2,1)}, u32[]{:S(2)}) copy-start(bf16[3,3,256,256]{3,2,1,0:T(8,128)(2,1)} %param.9) | copy-start | bytes 3538948
  33.1 18.9 %copy-start.4 = (bf16[2,512,256]{2,1,0:T(8,128)(2,1)S(1)}, bf16[2,512,256]{2,1,0:T(8,128)(2,1)}, u32[]{:S(2)}) copy-start(bf16[2,512,256]{2,1,0:T(8,128)(2,1)} %get-tuple-element.28.slopes) | copy-start | bytes 1572868
  36.3 20.5 %copy-start = (bf16[512,256]{1,0:T(8,128)(2,1)S(1)}, bf16[512,256]{1,0:T(8,128)(2,1)}, u32[]{:S(2)}) copy-start(bf16[512,256]{1,0:T(8,128)(2,1)} %get-tuple-element.25.keep_x) | copy-start | bytes 786436
  36.3 15.8 %all-to-all-start.1 = ((bf16[32,16,256]{2,1,0:T(8,128)(2,1)}), bf16[32,16,256]{2,1,0:T(8,128)(2,1)S(1)}, u32[]{:S(2)}, u32[]{:S(2)}) async-start(bf16[32,16,256]{2,1,0:T(8,128)(2,1)} %bitcast.32), calls=%async_computation.1 | async-start | bytes 524288 | tf_op jit(solution)/shard_map/all_to_all | solution.py:307
  41.7 16.0 %collective-permute-start.2 = (bf16[2,32,16,256]{3,2,1,0:T(8,128)(2,1)}, bf16[2,32,16,256]{3,2,1,0:T(8,128)(2,1)S(1)}, u32[]{:S(2)}, u32[]{:S(2)}) collective-permute-start(bf16[2,32,16,256]{3,2,1,0:T(8,128)(2,1)} %get-tuple-element.33), channel_id=1, source_target_pairs={{0,1},{1,0},{2,3},{3,2},{4,5},{5,4},{6,7},{7,6},{8,9},{9,8},{10,11... | collective-permute-start | bytes 1572872 | tf_op jit(solution)/shard_map/ppermute | solution.py:302
  43.6 14.7 %collective-permute-start = (bf16[512,256]{1,0:T(8,128)(2,1)S(1)}, bf16[512,256]{1,0:T(8,128)(2,1)S(1)}, u32[]{:S(2)}, u32[]{:S(2)}) collective-permute-start(bf16[512,256]{1,0:T(8,128)(2,1)S(1)} %copy-done.5), channel_id=1, source_target_pairs={{0,1},{1,0},{2,3},{3,2},{4,5},{5,4},{6,7},{7,6},{8,9},{9,8},{10,11... | collective-permute-start | bytes 786440 | tf_op jit(solution)/shard_map/ppermute | solution.py:302
  53.0 4.7 %copy-start.3 = (bf16[2,32,16,256]{3,2,1,0:T(8,128)(2,1)S(1)}, bf16[2,32,16,256]{3,2,1,0:T(8,128)(2,1)}, u32[]{:S(2)}) copy-start(bf16[2,32,16,256]{3,2,1,0:T(8,128)(2,1)} %get-tuple-element.32) | copy-start | bytes 1572868
  53.0 5.4 %collective-permute-start.1 = (bf16[512,256]{1,0:T(8,128)(2,1)S(1)}, bf16[512,256]{1,0:T(8,128)(2,1)S(1)}, u32[]{:S(2)}, u32[]{:S(2)}) collective-permute-start(bf16[512,256]{1,0:T(8,128)(2,1)S(1)} %get-tuple-element.31), channel_id=1, source_target_pairs={{0,1},{1,0},{2,3},{3,2},{4,5},{5,4},{6,7},{7,6},{8,9},{9,8},{10,11... | collective-permute-start | bytes 786440 | tf_op jit(solution)/shard_map/ppermute | solution.py:302
  121.6 6.3 %copy-start.2 = (bf16[3,3,256,256]{3,2,1,0:T(8,128)(2,1)S(1)}, bf16[3,3,256,256]{3,2,1,0:T(8,128)(2,1)}, u32[]{:S(2)}) copy-start(bf16[3,3,256,256]{3,2,1,0:T(8,128)(2,1)} %param.8) | copy-start | bytes 3538948
  121.6 7.9 %collective-permute-start.3 = (bf16[3072,256]{1,0:T(8,128)(2,1)S(1)}, bf16[3072,256]{1,0:T(8,128)(2,1)S(1)}, u32[]{:S(2)}, u32[]{:S(2)}) collective-permute-start(bf16[3072,256]{1,0:T(8,128)(2,1)S(1)} %bitcast.18), channel_id=1, source_target_pairs={{0,1},{1,0},{2,3},{3,2},{4,5},{5,4},{6,7},{7,6},{8,9},{9,8},{10,11... | collective-permute-start | bytes 4718600 | tf_op jit(solution)/shard_map/ppermute | solution.py:302

commit v11 on v9

--- a/solution.py
+++ b/solution.py
@@ -374,7 +374,9 @@
     )
 
     part = scatter_sum(part, ("zl", "x", "y"), 32)
-    part = jnp.sum(gather_all(part, "zh", 4).reshape(4, -1, CH).astype(F32), axis=0).astype(BF)
+    for pairs in (((0, 1), (1, 0), (2, 3), (3, 2)), ((0, 3), (3, 0), (1, 2), (2, 1))):
+        arrived = lax.ppermute(part, "zh", pairs)
+        part = (part.astype(F32) + arrived.astype(F32)).astype(BF)
     part = gather_all(part, ("zl", "x", "y"), 32)
     peer = swap_cores(part)
     part, first_grad = lax.optimization_barrier((part, first_grad))

time: 131 us -> 130 us (level)
  blocking collectives: 90.3 us -> 79.3 us
  waiting for transfers between devices: 8.42 us -> 16.3 us
  starting transfers between devices: 15.2 us -> 17.2 us
    all_to_all x2 -> x1, blocking collectives: 35.2 us -> 24.2 us  [gather_all(): return lax.all_to_all(copies, axes, 0, 0, tiled=True).reshape(-1, CH)]
    ppermute x0 -> x2, waiting for transfers between devices: none -> 7.85 us  [body(): arrived = lax.ppermute(part, 'zh', pairs)]
  transfers between devices with their start and end apart: 5 -> 7, of which waited for: 1 -> 3; matrix products, arithmetic and copies ran while one was open for 0% -> 0% of each run, Pallas kernels for 4% -> 4%
where the time goes in v11:
time: 130 us
  blocking collectives  79.3 us (61%)
  starting transfers between devices  17.2 us (13%)
  waiting for transfers between devices  16.3 us (13%)
  Pallas kernels  15.6 us (12%)
    all_to_all x1, blocking collectives, body(): both = lax.all_to_all(both, FRAME_AXES, 0, 0, tiled=True)  28.3 us
    all_to_all x1, blocking collectives, scatter_sum(): arrived = lax.all_to_all(parts, axes, 0, 0, tiled=True)  26.8 us
    all_to_all x1, blocking collectives, gather_all(): return lax.all_to_all(copies, axes, 0, 0, tiled=True).reshape(-1, CH)  24.2 us
    pallas_call x9, Pallas kernels, call(): pl.pallas_call(kernel, out_shape=[jax.ShapeDtypeStruct(shape, kind) for s...  15.6 us
    ppermute x4, starting transfers between devices, swap_cores(): return lax.ppermute(values, 'core', [(0, 1), (1, 0)])  10.5 us
    all_to_all x1, waiting for transfers between devices, swap_frames(): return lax.all_to_all(blocks, FRAME_AXES, 0, 0, tiled=True).reshape(PIX, CH)  8.41 us
    ppermute x2, waiting for transfers between devices, body(): arrived = lax.ppermute(part, 'zh', pairs)  7.85 us
    all_to_all x1, starting transfers between devices, swap_frames(): return lax.all_to_all(blocks, FRAME_AXES, 0, 0, tiled=True).reshape(PIX, CH)  5.35 us
  transfers between devices with their start and end apart: 7, of which 3 were waited for; matrix products, arithmetic and copies ran while one was open for 0% of the time, Pallas kernels for 4%

profile of v11, /device:TPU:1, one launch (start us, length us, event | category | flops | bytes accessed | tf_op | source)
XLA Modules:
  0.0 129.5 jit_solution(3800945290529265158)
XLA Ops:
  0.6 4.2 %shard_map.101 = (bf16[32,32,256]{2,1,0:T(8,128)(2,1)}, bf16[2,512,256]{2,1,0:T(8,128)(2,1)}, bf16[512,256]{1,0:T(8,128)(2,1)}, bf16[512,256]{1,0:T(8,128)(2,1)}) custom-call(s32[1]{0:T(128)} %bitcast.pos, bf16[512,256]{1,0:T(8,128)(2,1)} %bitcast.35, bf16[32,16,256]{2,1,0:T(8,128)(2,1)} %bitcast.36, bf16[2304,256]{1,0:T(8,128)(2,1)} %bitcast.24, ...), custom_call_target="tpu_custom_call" | custom-call | flops 1207959552 | bytes 2883588 | tf_op jit(solution)/shard_map/pallas_call | solution.py:43
  4.9 28.3 %all_to_all.20.both_at = bf16[32,32,256]{2,1,0:T(8,128)(2,1)} all-to-all(bf16[32,32,256]{2,1,0:T(8,128)(2,1)} %get-tuple-element.26), channel_id=1, replica_groups=mesh['zh'=4,'zl'=2,'x'=4,'y'=4,'core'=2] {'zh','zl','x'}, dimensions={0} | all-to-all | bytes 1048576 | tf_op jit(solution)/shard_map/all_to_all | solution.py:343
  33.1 3.2 %shard_map.102 = (bf16[512,256]{1,0:T(8,128)(2,1)}, bf16[2,32,16,256]{3,2,1,0:T(8,128)(2,1)}, bf16[2,32,16,256]{3,2,1,0:T(8,128)(2,1)}) custom-call(s32[1]{0:T(128)} %bitcast.pos, bf16[32,32,256]{2,1,0:T(8,128)(2,1)} %all_to_all.20.both_at, bf16[768,256]{1,0:T(8,128)(2,1)} %bitcast.33, bf16[768,256]{1,0:T(8,128)(2,1)} %bitcast.34), custom_call_target="tpu_custom_call" | custom-call | flops 603979776 | bytes 1310724 | tf_op jit(solution)/shard_map/pallas_call | solution.py:43
  36.3 0.0 copy-start
  36.3 5.4 %all-to-all-start.1 = ((bf16[32,16,256]{2,1,0:T(8,128)(2,1)}), bf16[32,16,256]{2,1,0:T(8,128)(2,1)S(1)}, u32[]{:S(2)}, u32[]{:S(2)}) async-start(bf16[32,16,256]{2,1,0:T(8,128)(2,1)} %bitcast.32), calls=%async_computation.1 | async-start | bytes 524288 | tf_op jit(solution)/shard_map/all_to_all | solution.py:307
  41.7 1.9 %collective-permute-start.2 = (bf16[2,32,16,256]{3,2,1,0:T(8,128)(2,1)}, bf16[2,32,16,256]{3,2,1,0:T(8,128)(2,1)S(1)}, u32[]{:S(2)}, u32[]{:S(2)}) collective-permute-start(bf16[2,32,16,256]{3,2,1,0:T(8,128)(2,1)} %get-tuple-element.33), channel_id=1, source_target_pairs={{0,1},{1,0},{2,3},{3,2},{4,5},{5,4},{6,7},{7,6},{8,9},{9,8},{10,11... | collective-permute-start | bytes 1572872 | tf_op jit(solution)/shard_map/ppermute | solution.py:302
  43.6 0.0 copy-done.5
  43.6 0.1 collective-permute-start
  43.7 8.4 %all-to-all-done.1 = bf16[32,16,256]{2,1,0:T(8,128)(2,1)S(1)} async-done(((bf16[32,16,256]{2,1,0:T(8,128)(2,1)}), bf16[32,16,256]{2,1,0:T(8,128)(2,1)S(1)}, u32[]{:S(2)}, u32[]{:S(2)}) %all-to-all-start.1) | async-done | bytes 262176 | tf_op jit(solution)/shard_map/all_to_all | solution.py:307
  52.1 0.0 copy-done.4
  52.1 0.9 shard_map.103
  53.0 0.0 copy-start.3
  53.0 3.8 %collective-permute-start.1 = (bf16[512,256]{1,0:T(8,128)(2,1)S(1)}, bf16[512,256]{1,0:T(8,128)(2,1)S(1)}, u32[]{:S(2)}, u32[]{:S(2)}) collective-permute-start(bf16[512,256]{1,0:T(8,128)(2,1)S(1)} %get-tuple-element.31), channel_id=1, source_target_pairs={{0,1},{1,0},{2,3},{3,2},{4,5},{5,4},{6,7},{7,6},{8,9},{9,8},{10,11... | collective-permute-start | bytes 786440 | tf_op jit(solution)/shard_map/ppermute | solution.py:302
  56.8 0.8 shard_map.104.partial
  57.7 0.0 collective-permute-done.2
  57.7 0.6 shard_map.105.time_part
  58.3 0.0 collective-permute-done.recv_x
  58.3 0.0 collective-permute-done.1.recv_g
  58.3 0.9 shard_map.106
  59.2 26.8 %all_to_all.21 = bf16[32,96,256]{2,1,0:T(8,128)(2,1)S(1)} all-to-all(bf16[32,96,256]{2,1,0:T(8,128)(2,1)S(1)} %bitcast.20), channel_id=1, replica_groups=mesh['zh'=4,'zl'=2,'x'=4,'y'=4,'core'=2] {'zl','x','y'}, dimensions={0} | all-to-all | bytes 3145728 | tf_op jit(solution)/shard_map/all_to_all | solution.py:312
  86.0 0.2 reduce_sum.12
  86.2 0.5 collective-permute-start.3
  86.7 3.4 %collective-permute-done.3 = bf16[96,256]{1,0:T(8,128)(2,1)S(1)} collective-permute-done((bf16[96,256]{1,0:T(8,128)(2,1)S(1)}, bf16[96,256]{1,0:T(8,128)(2,1)S(1)}, u32[]{:S(2)}, u32[]{:S(2)}) %collective-permute-start.3) | collective-permute-done | bytes 49184 | tf_op jit(solution)/shard_map/ppermute | solution.py:378
  90.2 0.8 collective-permute-start.4
  90.9 4.4 %collective-permute-done.4 = bf16[96,256]{1,0:T(8,128)(2,1)S(1)} collective-permute-done((bf16[96,256]{1,0:T(8,128)(2,1)S(1)}, bf16[96,256]{1,0:T(8,128)(2,1)S(1)}, u32[]{:S(2)}, u32[]{:S(2)}) %collective-permute-start.4) | collective-permute-done | bytes 49184 | tf_op jit(solution)/shard_map/ppermute | solution.py:378
  95.4 0.2 broadcast_in_dim.2
  95.6 24.2 %all_to_all.22 = bf16[32,96,256]{2,1,0:T(8,128)(2,1)S(1)} all-to-all(bf16[32,96,256]{2,1,0:T(8,128)(2,1)S(1)} %broadcast_in_dim.2), channel_id=1, replica_groups=mesh['zh'=4,'zl'=2,'x'=4,'y'=4,'core'=2] {'zl','x','y'}, dimensions={0} | all-to-all | bytes 3145728 | tf_op jit(solution)/shard_map/all_to_all | solution.py:318
  119.8 4.7 %collective-permute-start.5 = (bf16[3072,256]{1,0:T(8,128)(2,1)S(1)}, bf16[3072,256]{1,0:T(8,128)(2,1)S(1)}, u32[]{:S(2)}, u32[]{:S(2)}) collective-permute-start(bf16[3072,256]{1,0:T(8,128)(2,1)S(1)} %bitcast.18), channel_id=1, source_target_pairs={{0,1},{1,0},{2,3},{3,2},{4,5},{5,4},{6,7},{7,6},{8,9},{9,8},{10,11... | collective-permute-start | bytes 4718600 | tf_op jit(solution)/shard_map/ppermute | solution.py:302
  124.5 1.7 %shard_map.108 = (f32[2304,256]{1,0:T(8,128)}, f32[2304,256]{1,0:T(8,128)}, f32[768,256]{1,0:T(8,128)}, f32[768,256]{1,0:T(8,128)}) custom-call(s32[1]{0:T(128)} %bitcast.pos, bf16[3072,256]{1,0:T(8,128)(2,1)S(1)} %bitcast.19), custom_call_target="tpu_custom_call" | custom-call | bytes 1572868 | tf_op jit(solution)/shard_map/pallas_call | solution.py:43
  126.3 1.5 %shard_map.107 = bf16[512,256]{1,0:T(8,128)(2,1)} custom-call(bf16[512,256]{1,0:T(8,128)(2,1)S(1)} %get-tuple-element.35.first_grad, bf16[2304,256]{1,0:T(8,128)(2,1)S(1)} %bitcast.25), custom_call_target="tpu_custom_call" | custom-call | flops 603979776 | bytes 1441792 | tf_op jit(solution)/shard_map/pallas_call | solution.py:43
  127.8 0.0 collective-permute-done.5.half
  127.8 1.7 %shard_map.109 = (f32[2304,256]{1,0:T(8,128)}, f32[2304,256]{1,0:T(8,128)}, f32[768,256]{1,0:T(8,128)}, f32[768,256]{1,0:T(8,128)}) custom-call(s32[1]{0:T(128)} %bitcast.pos, bf16[3072,256]{1,0:T(8,128)(2,1)S(1)} %collective-permute-done.5.half, ...), custom_call_target="tpu_custom_call", output_to_operand_aliasing={{0}: (2, {}), {1}: (3, {}), {2}: (4, {}), {3}: (5, {})} | custom-call | bytes 7864324 | tf_op jit(solution)/shard_map/pallas_call | solution.py:43
  (10 shorter events, 0.0 us)
Async XLA Ops:
  33.1 10.4 %copy-start.5 = (bf16[512,256]{1,0:T(8,128)(2,1)S(1)}, bf16[512,256]{1,0:T(8,128)(2,1)}, u32[]{:S(2)}) copy-start(bf16[512,256]{1,0:T(8,128)(2,1)} %get-tuple-element.30) | copy-start | bytes 786436
  33.1 19.0 %copy-start.1 = (bf16[3,3,256,256]{3,2,1,0:T(8,128)(2,1)S(1)}, bf16[3,3,256,256]{3,2,1,0:T(8,128)(2,1)}, u32[]{:S(2)}) copy-start(bf16[3,3,256,256]{3,2,1,0:T(8,128)(2,1)} %param.9) | copy-start | bytes 3538948
  33.1 19.0 %copy-start.4 = (bf16[2,512,256]{2,1,0:T(8,128)(2,1)S(1)}, bf16[2,512,256]{2,1,0:T(8,128)(2,1)}, u32[]{:S(2)}) copy-start(bf16[2,512,256]{2,1,0:T(8,128)(2,1)} %get-tuple-element.28.slopes) | copy-start | bytes 1572868
  36.3 20.5 %copy-start = (bf16[512,256]{1,0:T(8,128)(2,1)S(1)}, bf16[512,256]{1,0:T(8,128)(2,1)}, u32[]{:S(2)}) copy-start(bf16[512,256]{1,0:T(8,128)(2,1)} %get-tuple-element.25.keep_x) | copy-start | bytes 786436
  36.3 15.8 %all-to-all-start.1 = ((bf16[32,16,256]{2,1,0:T(8,128)(2,1)}), bf16[32,16,256]{2,1,0:T(8,128)(2,1)S(1)}, u32[]{:S(2)}, u32[]{:S(2)}) async-start(bf16[32,16,256]{2,1,0:T(8,128)(2,1)} %bitcast.32), calls=%async_computation.1 | async-start | bytes 524288 | tf_op jit(solution)/shard_map/all_to_all | solution.py:307
  41.7 16.0 %collective-permute-start.2 = (bf16[2,32,16,256]{3,2,1,0:T(8,128)(2,1)}, bf16[2,32,16,256]{3,2,1,0:T(8,128)(2,1)S(1)}, u32[]{:S(2)}, u32[]{:S(2)}) collective-permute-start(bf16[2,32,16,256]{3,2,1,0:T(8,128)(2,1)} %get-tuple-element.33), channel_id=1, source_target_pairs={{0,1},{1,0},{2,3},{3,2},{4,5},{5,4},{6,7},{7,6},{8,9},{9,8},{10,11... | collective-permute-start | bytes 1572872 | tf_op jit(solution)/shard_map/ppermute | solution.py:302
  43.6 14.7 %collective-permute-start = (bf16[512,256]{1,0:T(8,128)(2,1)S(1)}, bf16[512,256]{1,0:T(8,128)(2,1)S(1)}, u32[]{:S(2)}, u32[]{:S(2)}) collective-permute-start(bf16[512,256]{1,0:T(8,128)(2,1)S(1)} %copy-done.5), channel_id=1, source_target_pairs={{0,1},{1,0},{2,3},{3,2},{4,5},{5,4},{6,7},{7,6},{8,9},{9,8},{10,11... | collective-permute-start | bytes 786440 | tf_op jit(solution)/shard_map/ppermute | solution.py:302
  53.0 4.7 %copy-start.3 = (bf16[2,32,16,256]{3,2,1,0:T(8,128)(2,1)S(1)}, bf16[2,32,16,256]{3,2,1,0:T(8,128)(2,1)}, u32[]{:S(2)}) copy-start(bf16[2,32,16,256]{3,2,1,0:T(8,128)(2,1)} %get-tuple-element.32) | copy-start | bytes 1572868
  53.0 5.3 %collective-permute-start.1 = (bf16[512,256]{1,0:T(8,128)(2,1)S(1)}, bf16[512,256]{1,0:T(8,128)(2,1)S(1)}, u32[]{:S(2)}, u32[]{:S(2)}) collective-permute-start(bf16[512,256]{1,0:T(8,128)(2,1)S(1)} %get-tuple-element.31), channel_id=1, source_target_pairs={{0,1},{1,0},{2,3},{3,2},{4,5},{5,4},{6,7},{7,6},{8,9},{9,8},{10,11... | collective-permute-start | bytes 786440 | tf_op jit(solution)/shard_map/ppermute | solution.py:302
  86.2 3.9 %collective-permute-start.3 = (bf16[96,256]{1,0:T(8,128)(2,1)S(1)}, bf16[96,256]{1,0:T(8,128)(2,1)S(1)}, u32[]{:S(2)}, u32[]{:S(2)}) collective-permute-start(bf16[96,256]{1,0:T(8,128)(2,1)S(1)} %reduce_sum.12), channel_id=1, source_target_pairs={{0,64},{64,0},{128,192},{192,128},{1,65},{65,1},{129,193},{193,129... | collective-permute-start | bytes 147464 | tf_op jit(solution)/shard_map/ppermute | solution.py:378
  90.2 5.2 %collective-permute-start.4 = (bf16[96,256]{1,0:T(8,128)(2,1)S(1)}, bf16[96,256]{1,0:T(8,128)(2,1)S(1)}, u32[]{:S(2)}, u32[]{:S(2)}) collective-permute-start(bf16[96,256]{1,0:T(8,128)(2,1)S(1)} %add_convert_fusion.1), channel_id=1, source_target_pairs={{0,192},{192,0},{64,128},{128,64},{1,193},{193,1},{65,129},{129,65... | collective-permute-start | bytes 147464 | tf_op jit(solution)/shard_map/ppermute | solution.py:378
  119.8 6.5 %copy-start.2 = (bf16[3,3,256,256]{3,2,1,0:T(8,128)(2,1)S(1)}, bf16[3,3,256,256]{3,2,1,0:T(8,128)(2,1)}, u32[]{:S(2)}) copy-start(bf16[3,3,256,256]{3,2,1,0:T(8,128)(2,1)} %param.8) | copy-start | bytes 3538948
  119.8 8.0 %collective-permute-start.5 = (bf16[3072,256]{1,0:T(8,128)(2,1)S(1)}, bf16[3072,256]{1,0:T(8,128)(2,1)S(1)}, u32[]{:S(2)}, u32[]{:S(2)}) collective-permute-start(bf16[3072,256]{1,0:T(8,128)(2,1)S(1)} %bitcast.18), channel_id=1, source_target_pairs={{0,1},{1,0},{2,3},{3,2},{4,5},{5,4},{6,7},{7,6},{8,9},{9,8},{10,11... | collective-permute-start | bytes 4718600 | tf_op jit(solution)/shard_map/ppermute | solution.py:302

commit v12 on v11

--- a/solution.py
+++ b/solution.py
@@ -269,25 +269,25 @@
     out[9 * CH : 12 * CH, :] = time_part[...]
 
 
-def spread_kernel(owner, pos, half, *refs):
+def spread_kernel(owner, pieces, pos, half, *refs):
     spat1, spat2, time1, time2, stage, sems = refs[-6:]
     targets = [(spat2, time1), (spat1, time2)]
+    rows = 3 * CH
 
     def copies(at):
         space, time = targets[at]
-        rows = 3 * CH
-        for piece in range(3):
-            part = pl.ds(piece * rows, rows)
-            yield pltpu.make_async_copy(stage.at[part], space.at[part], sems.at[piece])
-        yield pltpu.make_async_copy(stage.at[pl.ds(3 * rows, rows)], time, sems.at[3])
+        for slot, piece in enumerate(pieces):
+            target = space.at[pl.ds(piece * rows, rows)] if piece < 3 else time
+            source = stage.at[pl.ds(slot * rows, rows)]
+            yield pltpu.make_async_copy(source, target, sems.at[slot])
 
     for at in range(2):
 
         @pl.when((pos[0] ^ owner) == at)
         def _():
-            for piece, copy in enumerate(copies(at)):
-                rows = slice(piece * 3 * CH, (piece + 1) * 3 * CH)
-                stage[rows, :] = half[rows, :].astype(F32)
+            for slot, copy in enumerate(copies(at)):
+                part = slice(slot * rows, (slot + 1) * rows)
+                stage[part, :] = half[part, :].astype(F32)
                 copy.start()
             for copy in copies(at):
                 copy.wait()
@@ -374,28 +374,31 @@
     )
 
     part = scatter_sum(part, ("zl", "x", "y"), 32)
+    part, first_grad = lax.optimization_barrier((part, first_grad))
+    (grad_input,) = call(input_kernel, [slab], (first_grad, w1), [wide], conv_flops)
     for pairs in (((0, 1), (1, 0), (2, 3), (3, 2)), ((0, 3), (3, 0), (1, 2), (2, 1))):
         arrived = lax.ppermute(part, "zh", pairs)
+        arrived, grad_input = lax.optimization_barrier((arrived, grad_input))
         part = (part.astype(F32) + arrived.astype(F32)).astype(BF)
     part = gather_all(part, ("zl", "x", "y"), 32)
-    peer = swap_cores(part)
-    part, first_grad = lax.optimization_barrier((part, first_grad))
-    (grad_input,) = call(input_kernel, [slab], (first_grad, w1), [wide], conv_flops)
     grads = [((9 * CH, CH), F32)] * 2 + [((3 * CH, CH), F32)] * 2
-    scratch = [pltpu.VMEM((12 * CH, CH), F32), pltpu.SemaphoreType.DMA((4,))]
-    outs = call(
-        functools.partial(spread_kernel, 0), grads, (pos, part), scratch, 0, (), (0, 1, 2, 3)
-    )
-    outs = call(
-        functools.partial(spread_kernel, 1),
-        grads,
-        (pos, peer, *outs),
-        scratch,
-        0,
-        (2, 3, 4, 5),
-        (0, 1, 2, 3),
-        {2: 0, 3: 1, 4: 2, 5: 3},
-    )
+    outs = []
+    for owner, pieces in ((0, (0, 1, 2, 3)), (1, (0, 1)), (1, (2, 3))):
+        piece = part[pieces[0] * 3 * CH : (pieces[-1] + 1) * 3 * CH]
+        piece = swap_cores(piece) if owner else piece
+        outs = call(
+            functools.partial(spread_kernel, owner, pieces),
+            grads,
+            (pos, piece, *outs),
+            [
+                pltpu.VMEM((len(pieces) * 3 * CH, CH), F32),
+                pltpu.SemaphoreType.DMA((len(pieces),)),
+            ],
+            0,
+            (2, 3, 4, 5) if owner else (),
+            (0, 1, 2, 3),
+            {2: 0, 3: 1, 4: 2, 5: 3} if owner else None,
+        )
     return (
         grad_input.reshape(video.shape),
         outs[0].reshape(w_spat1.shape),

time: 130 us -> 130 us (level)
  waiting for transfers between devices: 16.3 us -> 14.8 us
    ppermute x2, waiting for transfers between devices: 7.85 us -> 6.32 us  [body(): arrived = lax.ppermute(part, 'zh', pairs)]
    pallas_call x9 -> x10, Pallas kernels: 15.6 us -> 16.2 us  [call(): pl.pallas_call(kernel, out_shape=[jax.ShapeDtypeStruct(shape, kind) for s...]
    ppermute x4 -> x5, starting transfers between devices: 10.5 us -> 10.7 us  [swap_cores(): return lax.ppermute(values, 'core', [(0, 1), (1, 0)])]
  transfers between devices with their start and end apart: 7 -> 8, of which waited for: 3 -> 4; matrix products, arithmetic and copies ran while one was open for 0% -> 0% of each run, Pallas kernels for 4% -> 5%
where the time goes in v12:
time: 130 us; the launch traced here: 129 us
  blocking collectives  79.6 us (61%)
  starting transfers between devices  17.2 us (13%)
  Pallas kernels  16.2 us (12%)
  waiting for transfers between devices  14.8 us (11%)
    all_to_all x1, blocking collectives, body(): both = lax.all_to_all(both, FRAME_AXES, 0, 0, tiled=True)  28.4 us
    all_to_all x1, blocking collectives, scatter_sum(): arrived = lax.all_to_all(parts, axes, 0, 0, tiled=True)  27 us
    all_to_all x1, blocking collectives, gather_all(): return lax.all_to_all(copies, axes, 0, 0, tiled=True).reshape(-1, CH)  24.1 us
    pallas_call x10, Pallas kernels, call(): pl.pallas_call(kernel, out_shape=[jax.ShapeDtypeStruct(shape, kind) for s...  16.2 us
    ppermute x5, starting transfers between devices, swap_cores(): return lax.ppermute(values, 'core', [(0, 1), (1, 0)])  10.7 us
    all_to_all x1, waiting for transfers between devices, swap_frames(): return lax.all_to_all(blocks, FRAME_AXES, 0, 0, tiled=True).reshape(PIX, CH)  8.41 us
    ppermute x2, waiting for transfers between devices, body(): arrived = lax.ppermute(part, 'zh', pairs)  6.32 us
    all_to_all x1, starting transfers between devices, swap_frames(): return lax.all_to_all(blocks, FRAME_AXES, 0, 0, tiled=True).reshape(PIX, CH)  5.22 us
  transfers between devices with their start and end apart: 8, of which 4 were waited for; matrix products, arithmetic and copies ran while one was open for 0% of the time, Pallas kernels for 5%

profile of v12, /device:TPU:1, one launch (start us, length us, event | category | flops | bytes accessed | tf_op | source)
XLA Modules:
  0.0 129.1 jit_solution(15211316935285081144)
XLA Ops:
  0.6 4.2 %shard_map.101 = (bf16[32,32,256]{2,1,0:T(8,128)(2,1)}, bf16[2,512,256]{2,1,0:T(8,128)(2,1)}, bf16[512,256]{1,0:T(8,128)(2,1)}, bf16[512,256]{1,0:T(8,128)(2,1)}) custom-call(s32[1]{0:T(128)} %bitcast.pos, bf16[512,256]{1,0:T(8,128)(2,1)} %bitcast.38, bf16[32,16,256]{2,1,0:T(8,128)(2,1)} %bitcast.39, bf16[2304,256]{1,0:T(8,128)(2,1)} %bitcast.25, ...), custom_call_target="tpu_custom_call" | custom-call | flops 1207959552 | bytes 2883588 | tf_op jit(solution)/shard_map/pallas_call | solution.py:43
  4.9 0.0 copy-start.5
  4.9 0.0 copy-start.1
  4.9 0.0 copy-start.4
  4.9 28.4 %all_to_all.20.both_at = bf16[32,32,256]{2,1,0:T(8,128)(2,1)} all-to-all(bf16[32,32,256]{2,1,0:T(8,128)(2,1)} %get-tuple-element.34), channel_id=1, replica_groups=mesh['zh'=4,'zl'=2,'x'=4,'y'=4,'core'=2] {'zh','zl','x'}, dimensions={0} | all-to-all | bytes 1048576 | tf_op jit(solution)/shard_map/all_to_all | solution.py:343
  33.3 3.1 %shard_map.102 = (bf16[512,256]{1,0:T(8,128)(2,1)}, bf16[2,32,16,256]{3,2,1,0:T(8,128)(2,1)}, bf16[2,32,16,256]{3,2,1,0:T(8,128)(2,1)}) custom-call(s32[1]{0:T(128)} %bitcast.pos, bf16[32,32,256]{2,1,0:T(8,128)(2,1)} %all_to_all.20.both_at, bf16[768,256]{1,0:T(8,128)(2,1)} %bitcast.36, bf16[768,256]{1,0:T(8,128)(2,1)} %bitcast.37), custom_call_target="tpu_custom_call" | custom-call | flops 603979776 | bytes 1310724 | tf_op jit(solution)/shard_map/pallas_call | solution.py:43
  36.4 5.2 %all-to-all-start.1 = ((bf16[32,16,256]{2,1,0:T(8,128)(2,1)}), bf16[32,16,256]{2,1,0:T(8,128)(2,1)S(1)}, u32[]{:S(2)}, u32[]{:S(2)}) async-start(bf16[32,16,256]{2,1,0:T(8,128)(2,1)} %bitcast.35), calls=%async_computation.1 | async-start | bytes 524288 | tf_op jit(solution)/shard_map/all_to_all | solution.py:307
  41.6 1.9 %collective-permute-start.2 = (bf16[2,32,16,256]{3,2,1,0:T(8,128)(2,1)}, bf16[2,32,16,256]{3,2,1,0:T(8,128)(2,1)S(1)}, u32[]{:S(2)}, u32[]{:S(2)}) collective-permute-start(bf16[2,32,16,256]{3,2,1,0:T(8,128)(2,1)} %get-tuple-element.41), channel_id=1, source_target_pairs={{0,1},{1,0},{2,3},{3,2},{4,5},{5,4},{6,7},{7,6},{8,9},{9,8},{10,11... | collective-permute-start | bytes 1572872 | tf_op jit(solution)/shard_map/ppermute | solution.py:302
  43.5 0.1 collective-permute-start
  43.6 8.4 %all-to-all-done.1 = bf16[32,16,256]{2,1,0:T(8,128)(2,1)S(1)} async-done(((bf16[32,16,256]{2,1,0:T(8,128)(2,1)}), bf16[32,16,256]{2,1,0:T(8,128)(2,1)S(1)}, u32[]{:S(2)}, u32[]{:S(2)}) %all-to-all-start.1) | async-done | bytes 262176 | tf_op jit(solution)/shard_map/all_to_all | solution.py:307
  52.0 0.9 shard_map.103
  52.9 3.8 %collective-permute-start.1 = (bf16[512,256]{1,0:T(8,128)(2,1)S(1)}, bf16[512,256]{1,0:T(8,128)(2,1)S(1)}, u32[]{:S(2)}, u32[]{:S(2)}) collective-permute-start(bf16[512,256]{1,0:T(8,128)(2,1)S(1)} %get-tuple-element.39), channel_id=1, source_target_pairs={{0,1},{1,0},{2,3},{3,2},{4,5},{5,4},{6,7},{7,6},{8,9},{9,8},{10,11... | collective-permute-start | bytes 786440 | tf_op jit(solution)/shard_map/ppermute | solution.py:302
  56.7 0.8 shard_map.104.partial
  57.6 0.6 shard_map.105.time_part
  58.2 0.9 shard_map.106
  59.1 0.0 copy-start.2
  59.1 27.0 %all_to_all.21 = bf16[32,96,256]{2,1,0:T(8,128)(2,1)S(1)} all-to-all(bf16[32,96,256]{2,1,0:T(8,128)(2,1)S(1)} %bitcast.21), channel_id=1, replica_groups=mesh['zh'=4,'zl'=2,'x'=4,'y'=4,'core'=2] {'zl','x','y'}, dimensions={0} | all-to-all | bytes 3145728 | tf_op jit(solution)/shard_map/all_to_all | solution.py:312
  86.2 0.2 reduce_sum.12
  86.4 0.5 collective-permute-start.3
  86.9 1.5 %shard_map.107 = bf16[512,256]{1,0:T(8,128)(2,1)} custom-call(bf16[512,256]{1,0:T(8,128)(2,1)S(1)} %get-tuple-element.44.first_grad, bf16[2304,256]{1,0:T(8,128)(2,1)S(1)} %bitcast.26), custom_call_target="tpu_custom_call" | custom-call | flops 603979776 | bytes 1441792 | tf_op jit(solution)/shard_map/pallas_call | solution.py:43
  88.4 1.9 %collective-permute-done.3 = bf16[96,256]{1,0:T(8,128)(2,1)S(1)} collective-permute-done((bf16[96,256]{1,0:T(8,128)(2,1)S(1)}, bf16[96,256]{1,0:T(8,128)(2,1)S(1)}, u32[]{:S(2)}, u32[]{:S(2)}) %collective-permute-start.3) | collective-permute-done | bytes 49184 | tf_op jit(solution)/shard_map/ppermute | solution.py:380
  90.3 0.8 collective-permute-start.4
  91.1 4.4 %collective-permute-done.4 = bf16[96,256]{1,0:T(8,128)(2,1)S(1)} collective-permute-done((bf16[96,256]{1,0:T(8,128)(2,1)S(1)}, bf16[96,256]{1,0:T(8,128)(2,1)S(1)}, u32[]{:S(2)}, u32[]{:S(2)}) %collective-permute-start.4) | collective-permute-done | bytes 49184 | tf_op jit(solution)/shard_map/ppermute | solution.py:380
  95.6 0.2 broadcast_in_dim.2
  95.8 24.1 %all_to_all.22 = bf16[32,96,256]{2,1,0:T(8,128)(2,1)S(1)} all-to-all(bf16[32,96,256]{2,1,0:T(8,128)(2,1)S(1)} %broadcast_in_dim.2), channel_id=1, replica_groups=mesh['zh'=4,'zl'=2,'x'=4,'y'=4,'core'=2] {'zl','x','y'}, dimensions={0} | all-to-all | bytes 3145728 | tf_op jit(solution)/shard_map/all_to_all | solution.py:318
  119.9 0.1 fusion
  120.0 4.8 %collective-permute-start.6 = (bf16[1536,256]{1,0:T(8,128)(2,1)S(1)}, bf16[1536,256]{1,0:T(8,128)(2,1)S(1)}, u32[]{:S(2)}, u32[]{:S(2)}) collective-permute-start(bf16[1536,256]{1,0:T(8,128)(2,1)S(1)} %bitcast.34), channel_id=1, source_target_pairs={{0,1},{1,0},{2,3},{3,2},{4,5},{5,4},{6,7},{7,6},{8,9},{9,8},{10,11... | collective-permute-start | bytes 2359304 | tf_op jit(solution)/shard_map/ppermute | solution.py:302
  124.8 0.1 collective-permute-start.5
  124.9 1.7 %shard_map.108 = (f32[2304,256]{1,0:T(8,128)}, f32[2304,256]{1,0:T(8,128)}, f32[768,256]{1,0:T(8,128)}, f32[768,256]{1,0:T(8,128)}) custom-call(s32[1]{0:T(128)} %bitcast.pos, bf16[3072,256]{1,0:T(8,128)(2,1)S(1)} %bitcast.20), custom_call_target="tpu_custom_call" | custom-call | bytes 1572868 | tf_op jit(solution)/shard_map/pallas_call | solution.py:43
  126.6 0.1 collective-permute-done.6.half
  126.7 1.2 shard_map.109
  127.9 1.2 shard_map.110
  (14 shorter events, 0.1 us)
Async XLA Ops:
  4.9 38.6 %copy-start.5 = (bf16[512,256]{1,0:T(8,128)(2,1)S(1)}, bf16[512,256]{1,0:T(8,128)(2,1)}, u32[]{:S(2)}) copy-start(bf16[512,256]{1,0:T(8,128)(2,1)} %get-tuple-element.38) | copy-start | bytes 786436
  4.9 47.1 %copy-start.1 = (bf16[3,3,256,256]{3,2,1,0:T(8,128)(2,1)S(1)}, bf16[3,3,256,256]{3,2,1,0:T(8,128)(2,1)}, u32[]{:S(2)}) copy-start(bf16[3,3,256,256]{3,2,1,0:T(8,128)(2,1)} %param.9) | copy-start | bytes 3538948
  4.9 47.1 %copy-start.4 = (bf16[2,512,256]{2,1,0:T(8,128)(2,1)S(1)}, bf16[2,512,256]{2,1,0:T(8,128)(2,1)}, u32[]{:S(2)}) copy-start(bf16[2,512,256]{2,1,0:T(8,128)(2,1)} %get-tuple-element.36.slopes) | copy-start | bytes 1572868
  33.3 23.4 %copy-start = (bf16[512,256]{1,0:T(8,128)(2,1)S(1)}, bf16[512,256]{1,0:T(8,128)(2,1)}, u32[]{:S(2)}) copy-start(bf16[512,256]{1,0:T(8,128)(2,1)} %get-tuple-element.33.keep_x) | copy-start | bytes 786436
  36.4 15.6 %all-to-all-start.1 = ((bf16[32,16,256]{2,1,0:T(8,128)(2,1)}), bf16[32,16,256]{2,1,0:T(8,128)(2,1)S(1)}, u32[]{:S(2)}, u32[]{:S(2)}) async-start(bf16[32,16,256]{2,1,0:T(8,128)(2,1)} %bitcast.35), calls=%async_computation.1 | async-start | bytes 524288 | tf_op jit(solution)/shard_map/all_to_all | solution.py:307
  41.6 16.0 %collective-permute-start.2 = (bf16[2,32,16,256]{3,2,1,0:T(8,128)(2,1)}, bf16[2,32,16,256]{3,2,1,0:T(8,128)(2,1)S(1)}, u32[]{:S(2)}, u32[]{:S(2)}) collective-permute-start(bf16[2,32,16,256]{3,2,1,0:T(8,128)(2,1)} %get-tuple-element.41), channel_id=1, source_target_pairs={{0,1},{1,0},{2,3},{3,2},{4,5},{5,4},{6,7},{7,6},{8,9},{9,8},{10,11... | collective-permute-start | bytes 1572872 | tf_op jit(solution)/shard_map/ppermute | solution.py:302
  43.5 14.7 %collective-permute-start = (bf16[512,256]{1,0:T(8,128)(2,1)S(1)}, bf16[512,256]{1,0:T(8,128)(2,1)S(1)}, u32[]{:S(2)}, u32[]{:S(2)}) collective-permute-start(bf16[512,256]{1,0:T(8,128)(2,1)S(1)} %copy-done.5), channel_id=1, source_target_pairs={{0,1},{1,0},{2,3},{3,2},{4,5},{5,4},{6,7},{7,6},{8,9},{9,8},{10,11... | collective-permute-start | bytes 786440 | tf_op jit(solution)/shard_map/ppermute | solution.py:302
  52.0 5.6 %copy-start.3 = (bf16[2,32,16,256]{3,2,1,0:T(8,128)(2,1)S(1)}, bf16[2,32,16,256]{3,2,1,0:T(8,128)(2,1)}, u32[]{:S(2)}) copy-start(bf16[2,32,16,256]{3,2,1,0:T(8,128)(2,1)} %get-tuple-element.40) | copy-start | bytes 1572868
  52.9 5.4 %collective-permute-start.1 = (bf16[512,256]{1,0:T(8,128)(2,1)S(1)}, bf16[512,256]{1,0:T(8,128)(2,1)S(1)}, u32[]{:S(2)}, u32[]{:S(2)}) collective-permute-start(bf16[512,256]{1,0:T(8,128)(2,1)S(1)} %get-tuple-element.39), channel_id=1, source_target_pairs={{0,1},{1,0},{2,3},{3,2},{4,5},{5,4},{6,7},{7,6},{8,9},{9,8},{10,11... | collective-permute-start | bytes 786440 | tf_op jit(solution)/shard_map/ppermute | solution.py:302
  59.1 27.8 %copy-start.2 = (bf16[3,3,256,256]{3,2,1,0:T(8,128)(2,1)S(1)}, bf16[3,3,256,256]{3,2,1,0:T(8,128)(2,1)}, u32[]{:S(2)}) copy-start(bf16[3,3,256,256]{3,2,1,0:T(8,128)(2,1)} %param.8) | copy-start | bytes 3538948
  86.4 3.9 %collective-permute-start.3 = (bf16[96,256]{1,0:T(8,128)(2,1)S(1)}, bf16[96,256]{1,0:T(8,128)(2,1)S(1)}, u32[]{:S(2)}, u32[]{:S(2)}) collective-permute-start(bf16[96,256]{1,0:T(8,128)(2,1)S(1)} %reduce_sum.12), channel_id=1, source_target_pairs={{0,64},{64,0},{128,192},{192,128},{1,65},{65,1},{129,193},{193,129... | collective-permute-start | bytes 147464 | tf_op jit(solution)/shard_map/ppermute | solution.py:380
  90.3 5.2 %collective-permute-start.4 = (bf16[96,256]{1,0:T(8,128)(2,1)S(1)}, bf16[96,256]{1,0:T(8,128)(2,1)S(1)}, u32[]{:S(2)}, u32[]{:S(2)}) collective-permute-start(bf16[96,256]{1,0:T(8,128)(2,1)S(1)} %add_convert_fusion.1), channel_id=1, source_target_pairs={{0,192},{192,0},{64,128},{128,64},{1,193},{193,1},{65,129},{129,65... | collective-permute-start | bytes 147464 | tf_op jit(solution)/shard_map/ppermute | solution.py:380
  120.0 6.7 %collective-permute-start.6 = (bf16[1536,256]{1,0:T(8,128)(2,1)S(1)}, bf16[1536,256]{1,0:T(8,128)(2,1)S(1)}, u32[]{:S(2)}, u32[]{:S(2)}) collective-permute-start(bf16[1536,256]{1,0:T(8,128)(2,1)S(1)} %bitcast.34), channel_id=1, source_target_pairs={{0,1},{1,0},{2,3},{3,2},{4,5},{5,4},{6,7},{7,6},{8,9},{9,8},{10,11... | collective-permute-start | bytes 2359304 | tf_op jit(solution)/shard_map/ppermute | solution.py:302
  124.8 3.1 %collective-permute-start.5 = (bf16[1536,256]{1,0:T(8,128)(2,1)S(1)}, bf16[1536,256]{1,0:T(8,128)(2,1)S(1)}, u32[]{:S(2)}, u32[]{:S(2)}) collective-permute-start(bf16[1536,256]{1,0:T(8,128)(2,1)S(1)} %bitcast.33), channel_id=1, source_target_pairs={{0,1},{1,0},{2,3},{3,2},{4,5},{5,4},{6,7},{7,6},{8,9},{9,8},{10,11... | collective-permute-start | bytes 2359304 | tf_op jit(solution)/shard_map/ppermute | solution.py:302

commit v13 on v12

--- a/solution.py
+++ b/solution.py
@@ -341,7 +341,6 @@
         vmem=60,
     )
     both = lax.all_to_all(both, FRAME_AXES, 0, 0, tiled=True)
-    recv_x = swap_cores(send_x)
     act_back, keep_t, send_t = call(
         time_kernel,
         [slab, pair, pair],
@@ -353,7 +352,8 @@
         vmem=60,
     )
     act_back = swap_frames(act_back)
-    recv_t = swap_cores(send_t)
+    act_back, send_t, send_x = lax.optimization_barrier((act_back, send_t, send_x))
+    recv_t, recv_x = swap_cores(send_t), swap_cores(send_x)
     keep_t, recv_t = keep_t.reshape(2, PIX, CH), recv_t.reshape(2, PIX, CH)
     (time_part,) = call(
         time_weights_kernel, [((3 * CH, CH), BF)], (keep_t, recv_t), (), 2 * time_flops

time: 130 us -> 130 us (level)
  blocking collectives: 79.6 us -> 95.1 us
  waiting for transfers between devices: 14.8 us -> 6.4 us
  starting transfers between devices: 17.2 us -> 10.6 us
    all_to_all x0 -> x1, blocking collectives: none -> 15.6 us  [swap_frames(): return lax.all_to_all(blocks, FRAME_AXES, 0, 0, tiled=True).reshape(PIX, CH)]
    all_to_all x1 -> x0, waiting for transfers between devices: 8.41 us -> none  [swap_frames(): return lax.all_to_all(blocks, FRAME_AXES, 0, 0, tiled=True).reshape(PIX, CH)]
    all_to_all x1 -> x0, starting transfers between devices: 5.22 us -> none  [swap_frames(): return lax.all_to_all(blocks, FRAME_AXES, 0, 0, tiled=True).reshape(PIX, CH)]
    ppermute x5, starting transfers between devices: 10.7 us -> 9.25 us  [swap_cores(): return lax.ppermute(values, 'core', [(0, 1), (1, 0)])]
  transfers between devices with their start and end apart: 8 -> 7, of which waited for: 4 -> 3; matrix products, arithmetic and copies ran while one was open for 0% -> 0% of each run, Pallas kernels for 5% -> 5%
where the time goes in v13:
time: 130 us
  blocking collectives  95.1 us (73%)
  Pallas kernels  16.2 us (12%)
  starting transfers between devices  10.6 us (8%)
  waiting for transfers between devices  6.4 us (5%)
    all_to_all x1, blocking collectives, body(): both = lax.all_to_all(both, FRAME_AXES, 0, 0, tiled=True)  28.4 us
    all_to_all x1, blocking collectives, scatter_sum(): arrived = lax.all_to_all(parts, axes, 0, 0, tiled=True)  26.9 us
    all_to_all x1, blocking collectives, gather_all(): return lax.all_to_all(copies, axes, 0, 0, tiled=True).reshape(-1, CH)  24.2 us
    pallas_call x10, Pallas kernels, call(): pl.pallas_call(kernel, out_shape=[jax.ShapeDtypeStruct(shape, kind) for s...  16.2 us
    all_to_all x1, blocking collectives, swap_frames(): return lax.all_to_all(blocks, FRAME_AXES, 0, 0, tiled=True).reshape(PIX, CH)  15.6 us
    ppermute x5, starting transfers between devices, swap_cores(): return lax.ppermute(values, 'core', [(0, 1), (1, 0)])  9.25 us
    ppermute x2, waiting for transfers between devices, body(): arrived = lax.ppermute(part, 'zh', pairs)  6.32 us
  transfers between devices with their start and end apart: 7, of which 3 were waited for; matrix products, arithmetic and copies ran while one was open for 0% of the time, Pallas kernels for 5%

profile of v13, /device:TPU:1, one launch (start us, length us, event | category | flops | bytes accessed | tf_op | source)
XLA Modules:
  0.0 129.7 jit_solution(14953489567146179543)
XLA Ops:
  0.6 4.2 %shard_map.101 = (bf16[32,32,256]{2,1,0:T(8,128)(2,1)}, bf16[2,512,256]{2,1,0:T(8,128)(2,1)}, bf16[512,256]{1,0:T(8,128)(2,1)}, bf16[512,256]{1,0:T(8,128)(2,1)}) custom-call(s32[1]{0:T(128)} %bitcast.pos, bf16[512,256]{1,0:T(8,128)(2,1)} %bitcast.38, bf16[32,16,256]{2,1,0:T(8,128)(2,1)} %bitcast.39, bf16[2304,256]{1,0:T(8,128)(2,1)} %bitcast.25, ...), custom_call_target="tpu_custom_call" | custom-call | flops 1207959552 | bytes 2883588 | tf_op jit(solution)/shard_map/pallas_call | solution.py:43
  4.9 0.0 copy-start.1
  4.9 0.0 copy-start.4
  4.9 28.4 %all_to_all.20.both_at = bf16[32,32,256]{2,1,0:T(8,128)(2,1)} all-to-all(bf16[32,32,256]{2,1,0:T(8,128)(2,1)} %get-tuple-element.37), channel_id=1, replica_groups=mesh['zh'=4,'zl'=2,'x'=4,'y'=4,'core'=2] {'zh','zl','x'}, dimensions={0} | all-to-all | bytes 1048576 | tf_op jit(solution)/shard_map/all_to_all | solution.py:343
  33.3 3.1 %shard_map.102 = (bf16[512,256]{1,0:T(8,128)(2,1)}, bf16[2,32,16,256]{3,2,1,0:T(8,128)(2,1)}, bf16[2,32,16,256]{3,2,1,0:T(8,128)(2,1)}) custom-call(s32[1]{0:T(128)} %bitcast.pos, bf16[32,32,256]{2,1,0:T(8,128)(2,1)} %all_to_all.20.both_at, bf16[768,256]{1,0:T(8,128)(2,1)} %bitcast.36, bf16[768,256]{1,0:T(8,128)(2,1)} %bitcast.37), custom_call_target="tpu_custom_call" | custom-call | flops 603979776 | bytes 1310724 | tf_op jit(solution)/shard_map/pallas_call | solution.py:43
  36.4 15.6 %all_to_all.21 = bf16[32,16,256]{2,1,0:T(8,128)(2,1)S(1)} all-to-all(bf16[32,16,256]{2,1,0:T(8,128)(2,1)} %bitcast.35), channel_id=1, replica_groups=mesh['zh'=4,'zl'=2,'x'=4,'y'=4,'core'=2] {'zh','zl','x'}, dimensions={0} | all-to-all | bytes 524288 | tf_op jit(solution)/shard_map/all_to_all | solution.py:307
  52.0 3.8 %collective-permute-start.2 = (bf16[2,32,16,256]{3,2,1,0:T(8,128)(2,1)}, bf16[2,32,16,256]{3,2,1,0:T(8,128)(2,1)S(1)}, u32[]{:S(2)}, u32[]{:S(2)}) collective-permute-start(bf16[2,32,16,256]{3,2,1,0:T(8,128)(2,1)} %get-tuple-element.47), channel_id=1, source_target_pairs={{0,1},{1,0},{2,3},{3,2},{4,5},{5,4},{6,7},{7,6},{8,9},{9,8},{10,11... | collective-permute-start | bytes 1572872 | tf_op jit(solution)/shard_map/ppermute | solution.py:302
  55.8 0.9 shard_map.103
  56.6 0.1 collective-permute-start.1
  56.8 0.5 collective-permute-start
  57.2 0.9 shard_map.104.partial
  58.1 0.6 shard_map.105.time_part
  58.8 0.0 collective-permute-done.1.recv_g
  58.8 0.9 shard_map.106
  59.6 0.0 copy-start.2
  59.7 26.9 %all_to_all.22 = bf16[32,96,256]{2,1,0:T(8,128)(2,1)S(1)} all-to-all(bf16[32,96,256]{2,1,0:T(8,128)(2,1)S(1)} %bitcast.21), channel_id=1, replica_groups=mesh['zh'=4,'zl'=2,'x'=4,'y'=4,'core'=2] {'zl','x','y'}, dimensions={0} | all-to-all | bytes 3145728 | tf_op jit(solution)/shard_map/all_to_all | solution.py:312
  86.6 0.2 reduce_sum.12
  86.8 0.5 collective-permute-start.3
  87.3 1.5 %shard_map.107 = bf16[512,256]{1,0:T(8,128)(2,1)} custom-call(bf16[512,256]{1,0:T(8,128)(2,1)S(1)} %get-tuple-element.50.first_grad, bf16[2304,256]{1,0:T(8,128)(2,1)S(1)} %bitcast.26), custom_call_target="tpu_custom_call" | custom-call | flops 603979776 | bytes 1441792 | tf_op jit(solution)/shard_map/pallas_call | solution.py:43
  88.8 1.9 %collective-permute-done.3 = bf16[96,256]{1,0:T(8,128)(2,1)S(1)} collective-permute-done((bf16[96,256]{1,0:T(8,128)(2,1)S(1)}, bf16[96,256]{1,0:T(8,128)(2,1)S(1)}, u32[]{:S(2)}, u32[]{:S(2)}) %collective-permute-start.3) | collective-permute-done | bytes 49184 | tf_op jit(solution)/shard_map/ppermute | solution.py:380
  90.7 0.8 collective-permute-start.4
  91.5 4.4 %collective-permute-done.4 = bf16[96,256]{1,0:T(8,128)(2,1)S(1)} collective-permute-done((bf16[96,256]{1,0:T(8,128)(2,1)S(1)}, bf16[96,256]{1,0:T(8,128)(2,1)S(1)}, u32[]{:S(2)}, u32[]{:S(2)}) %collective-permute-start.4) | collective-permute-done | bytes 49184 | tf_op jit(solution)/shard_map/ppermute | solution.py:380
  96.0 0.2 broadcast_in_dim.2
  96.2 24.2 %all_to_all.23 = bf16[32,96,256]{2,1,0:T(8,128)(2,1)S(1)} all-to-all(bf16[32,96,256]{2,1,0:T(8,128)(2,1)S(1)} %broadcast_in_dim.2), channel_id=1, replica_groups=mesh['zh'=4,'zl'=2,'x'=4,'y'=4,'core'=2] {'zl','x','y'}, dimensions={0} | all-to-all | bytes 3145728 | tf_op jit(solution)/shard_map/all_to_all | solution.py:318
  120.4 0.1 fusion
  120.5 4.8 %collective-permute-start.6 = (bf16[1536,256]{1,0:T(8,128)(2,1)S(1)}, bf16[1536,256]{1,0:T(8,128)(2,1)S(1)}, u32[]{:S(2)}, u32[]{:S(2)}) collective-permute-start(bf16[1536,256]{1,0:T(8,128)(2,1)S(1)} %bitcast.34), channel_id=1, source_target_pairs={{0,1},{1,0},{2,3},{3,2},{4,5},{5,4},{6,7},{7,6},{8,9},{9,8},{10,11... | collective-permute-start | bytes 2359304 | tf_op jit(solution)/shard_map/ppermute | solution.py:302
  125.3 0.1 collective-permute-start.5
  125.4 1.7 %shard_map.108 = (f32[2304,256]{1,0:T(8,128)}, f32[2304,256]{1,0:T(8,128)}, f32[768,256]{1,0:T(8,128)}, f32[768,256]{1,0:T(8,128)}) custom-call(s32[1]{0:T(128)} %bitcast.pos, bf16[3072,256]{1,0:T(8,128)(2,1)S(1)} %bitcast.20), custom_call_target="tpu_custom_call" | custom-call | bytes 1572868 | tf_op jit(solution)/shard_map/pallas_call | solution.py:43
  127.2 0.1 collective-permute-done.6.half
  127.2 1.2 shard_map.109
  128.4 0.0 collective-permute-done.5.half
  128.4 1.2 shard_map.110
  (13 shorter events, 0.1 us)
Async XLA Ops:
  4.9 50.9 %copy-start.1 = (bf16[3,3,256,256]{3,2,1,0:T(8,128)(2,1)S(1)}, bf16[3,3,256,256]{3,2,1,0:T(8,128)(2,1)}, u32[]{:S(2)}) copy-start(bf16[3,3,256,256]{3,2,1,0:T(8,128)(2,1)} %param.9) | copy-start | bytes 3538948
  4.9 50.9 %copy-start.4 = (bf16[2,512,256]{2,1,0:T(8,128)(2,1)S(1)}, bf16[2,512,256]{2,1,0:T(8,128)(2,1)}, u32[]{:S(2)}) copy-start(bf16[2,512,256]{2,1,0:T(8,128)(2,1)} %get-tuple-element.42.slopes) | copy-start | bytes 1572868
  33.3 23.5 %copy-start.5 = (bf16[512,256]{1,0:T(8,128)(2,1)S(1)}, bf16[512,256]{1,0:T(8,128)(2,1)}, u32[]{:S(2)}) copy-start(bf16[512,256]{1,0:T(8,128)(2,1)} %get-tuple-element.44) | copy-start | bytes 786436
  33.3 24.0 %copy-start = (bf16[512,256]{1,0:T(8,128)(2,1)S(1)}, bf16[512,256]{1,0:T(8,128)(2,1)}, u32[]{:S(2)}) copy-start(bf16[512,256]{1,0:T(8,128)(2,1)} %get-tuple-element.36.keep_x) | copy-start | bytes 786436
  52.0 6.1 %collective-permute-start.2 = (bf16[2,32,16,256]{3,2,1,0:T(8,128)(2,1)}, bf16[2,32,16,256]{3,2,1,0:T(8,128)(2,1)S(1)}, u32[]{:S(2)}, u32[]{:S(2)}) collective-permute-start(bf16[2,32,16,256]{3,2,1,0:T(8,128)(2,1)} %get-tuple-element.47), channel_id=1, source_target_pairs={{0,1},{1,0},{2,3},{3,2},{4,5},{5,4},{6,7},{7,6},{8,9},{9,8},{10,11... | collective-permute-start | bytes 1572872 | tf_op jit(solution)/shard_map/ppermute | solution.py:302
  55.8 2.3 %copy-start.3 = (bf16[2,32,16,256]{3,2,1,0:T(8,128)(2,1)S(1)}, bf16[2,32,16,256]{3,2,1,0:T(8,128)(2,1)}, u32[]{:S(2)}) copy-start(bf16[2,32,16,256]{3,2,1,0:T(8,128)(2,1)} %get-tuple-element.46) | copy-start | bytes 1572868
  56.6 2.1 %collective-permute-start.1 = (bf16[512,256]{1,0:T(8,128)(2,1)S(1)}, bf16[512,256]{1,0:T(8,128)(2,1)S(1)}, u32[]{:S(2)}, u32[]{:S(2)}) collective-permute-start(bf16[512,256]{1,0:T(8,128)(2,1)S(1)} %get-tuple-element.45), channel_id=1, source_target_pairs={{0,1},{1,0},{2,3},{3,2},{4,5},{5,4},{6,7},{7,6},{8,9},{9,8},{10,11... | collective-permute-start | bytes 786440 | tf_op jit(solution)/shard_map/ppermute | solution.py:302
  56.8 2.0 %collective-permute-start = (bf16[512,256]{1,0:T(8,128)(2,1)S(1)}, bf16[512,256]{1,0:T(8,128)(2,1)S(1)}, u32[]{:S(2)}, u32[]{:S(2)}) collective-permute-start(bf16[512,256]{1,0:T(8,128)(2,1)S(1)} %copy-done.5), channel_id=1, source_target_pairs={{0,1},{1,0},{2,3},{3,2},{4,5},{5,4},{6,7},{7,6},{8,9},{9,8},{10,11... | collective-permute-start | bytes 786440 | tf_op jit(solution)/shard_map/ppermute | solution.py:302
  59.6 27.7 %copy-start.2 = (bf16[3,3,256,256]{3,2,1,0:T(8,128)(2,1)S(1)}, bf16[3,3,256,256]{3,2,1,0:T(8,128)(2,1)}, u32[]{:S(2)}) copy-start(bf16[3,3,256,256]{3,2,1,0:T(8,128)(2,1)} %param.8) | copy-start | bytes 3538948
  86.8 3.9 %collective-permute-start.3 = (bf16[96,256]{1,0:T(8,128)(2,1)S(1)}, bf16[96,256]{1,0:T(8,128)(2,1)S(1)}, u32[]{:S(2)}, u32[]{:S(2)}) collective-permute-start(bf16[96,256]{1,0:T(8,128)(2,1)S(1)} %reduce_sum.12), channel_id=1, source_target_pairs={{0,64},{64,0},{128,192},{192,128},{1,65},{65,1},{129,193},{193,129... | collective-permute-start | bytes 147464 | tf_op jit(solution)/shard_map/ppermute | solution.py:380
  90.7 5.2 %collective-permute-start.4 = (bf16[96,256]{1,0:T(8,128)(2,1)S(1)}, bf16[96,256]{1,0:T(8,128)(2,1)S(1)}, u32[]{:S(2)}, u32[]{:S(2)}) collective-permute-start(bf16[96,256]{1,0:T(8,128)(2,1)S(1)} %add_convert_fusion.1), channel_id=1, source_target_pairs={{0,192},{192,0},{64,128},{128,64},{1,193},{193,1},{65,129},{129,65... | collective-permute-start | bytes 147464 | tf_op jit(solution)/shard_map/ppermute | solution.py:380
  120.5 6.7 %collective-permute-start.6 = (bf16[1536,256]{1,0:T(8,128)(2,1)S(1)}, bf16[1536,256]{1,0:T(8,128)(2,1)S(1)}, u32[]{:S(2)}, u32[]{:S(2)}) collective-permute-start(bf16[1536,256]{1,0:T(8,128)(2,1)S(1)} %bitcast.34), channel_id=1, source_target_pairs={{0,1},{1,0},{2,3},{3,2},{4,5},{5,4},{6,7},{7,6},{8,9},{9,8},{10,11... | collective-permute-start | bytes 2359304 | tf_op jit(solution)/shard_map/ppermute | solution.py:302
  125.3 3.1 %collective-permute-start.5 = (bf16[1536,256]{1,0:T(8,128)(2,1)S(1)}, bf16[1536,256]{1,0:T(8,128)(2,1)S(1)}, u32[]{:S(2)}, u32[]{:S(2)}) collective-permute-start(bf16[1536,256]{1,0:T(8,128)(2,1)S(1)} %bitcast.33), channel_id=1, source_target_pairs={{0,1},{1,0},{2,3},{3,2},{4,5},{5,4},{6,7},{7,6},{8,9},{9,8},{10,11... | collective-permute-start | bytes 2359304 | tf_op jit(solution)/shard_map/ppermute | solution.py:302

commit v14 on v12

--- a/solution.py
+++ b/solution.py
@@ -167,7 +167,7 @@
     return total
 
 
-def time_kernel(pos, both_at, wt1_at, wt2_at, back_at, keep, send, *rest):
+def time_kernel(both_at, wt1_at, wt2_at, back_at, own_at, *rest):
     act, cot, wt1, wt2, time_act, time_grad, act_back, behind, ahead, later, sems = rest
     loads = [
         pltpu.make_async_copy(source, target, sems.at[at])
@@ -205,29 +205,29 @@
         later[half * HALF : (half + 1) * HALF, :] = grad
     later[PIX:PAD, :] = edge
     stores = [
-        (act, time_act, keep.at[0]),
-        (time_grad, cot, keep.at[1]),
-        (time_act, act, send.at[0]),
-        (cot, time_grad, send.at[1]),
+        pltpu.make_async_copy(source, own_at.at[at], sems.at[4 + at])
+        for at, source in enumerate((act, time_grad, time_act, cot))
     ]
-    start_by_core(pos, sems, 4, stores)
+    for store in stores:
+        store.start()
     tails = []
     for half in range(2):
         rows = pl.ds(half * HALF, HALF)
         act_back[rows, :] = ahead_sum(later, wt1, half).astype(BF)
         tails.append(pltpu.make_async_copy(act_back.at[rows], back_at.at[rows], sems.at[8 + half]))
         tails[half].start()
-    wait_by_core(sems, 4, stores)
-    for tail in tails:
-        tail.wait()
-
-
-def time_weights_kernel(keep, recv, out):
+    for move in stores + tails:
+        move.wait()
+
+
+def time_weights_kernel(pos, own, keep, send):
     for step in range(3):
         rows = PIX - step * COLS
-        total = dot_tn(keep[0, 0:rows, :], keep[1, step * COLS : PIX, :])
-        total = total + dot_tn(recv[0, 0:rows, :], recv[1, step * COLS : PIX, :])
-        out[step * CH : (step + 1) * CH, :] = (total * SCALE).astype(BF)
+        first = dot_tn(own[0, 0:rows, :], own[1, step * COLS : PIX, :]) * SCALE
+        second = dot_tn(own[2, 0:rows, :], own[3, step * COLS : PIX, :]) * SCALE
+        part = slice(step * CH, (step + 1) * CH)
+        keep[part, :] = jnp.where(pos[0] == 0, first, second).astype(BF)
+        send[part, :] = jnp.where(pos[0] == 0, second, first).astype(BF)
 
 
 def backward_kernel(pos, act_back, slopes, w2, first_grad, keep, send, wide):
@@ -257,7 +257,7 @@
             out[at : at + CH, :] = dot_tn(wide[rows, lanes], keep_g[...])
 
 
-def space_weights_kernel(partial, recv_x, recv_g, time_part, out, wide):
+def space_weights_kernel(partial, recv_x, recv_g, keep_t, recv_t, out, wide):
     fill_windows(wide, recv_x[...])
     for tap in range(3):
         for side in range(3):
@@ -266,7 +266,7 @@
             at = (tap * 3 + side) * CH
             total = partial[at : at + CH, :] + dot_tn(wide[rows, lanes], recv_g[...])
             out[at : at + CH, :] = (total * SCALE).astype(BF)
-    out[9 * CH : 12 * CH, :] = time_part[...]
+    out[9 * CH : 12 * CH, :] = (keep_t[...].astype(F32) + recv_t[...].astype(F32)).astype(BF)
 
 
 def spread_kernel(owner, pieces, pos, half, *refs):
@@ -323,7 +323,6 @@
     w1, w2, wt1, wt2 = (w.reshape(-1, CH) for w in (w_spat1, w_spat2, w_time1, w_time2))
     rows = PIX // COLS
     slab = ((PIX, CH), BF)
-    pair = ((2, rows, COLS, CH), BF)
     wide, tall = pltpu.VMEM((PAD, 3 * CH), BF), pltpu.VMEM((PAD, CH), BF)
     frame, lines = pltpu.VMEM((PIX, CH), BF), pltpu.VMEM((rows, COLS, CH), BF)
     both_slopes = pltpu.VMEM((2, PIX, CH), BF)
@@ -342,22 +341,23 @@
     )
     both = lax.all_to_all(both, FRAME_AXES, 0, 0, tiled=True)
     recv_x = swap_cores(send_x)
-    act_back, keep_t, send_t = call(
+    act_back, own = call(
         time_kernel,
-        [slab, pair, pair],
-        (pos, both, wt1, wt2),
+        [slab, ((4, rows, COLS, CH), BF)],
+        (both, wt1, wt2),
         [lines, lines, time, time, lines, lines, frame, tall, tall, tall, pltpu.SemaphoreType.DMA((10,))],
         3 * time_flops,
-        (1, 2, 3),
         (0, 1, 2),
+        (0, 1),
         vmem=60,
     )
     act_back = swap_frames(act_back)
+    taps = ((3 * CH, CH), BF)
+    keep_t, send_t = call(
+        time_weights_kernel, [taps, taps], (pos, own.reshape(4, PIX, CH)), (), 2 * time_flops
+    )
+    act_back, send_t = lax.optimization_barrier((act_back, send_t))
     recv_t = swap_cores(send_t)
-    keep_t, recv_t = keep_t.reshape(2, PIX, CH), recv_t.reshape(2, PIX, CH)
-    (time_part,) = call(
-        time_weights_kernel, [((3 * CH, CH), BF)], (keep_t, recv_t), (), 2 * time_flops
-    )
     first_grad, keep_g, send_g = call(
         backward_kernel, [slab, slab, slab], (pos, act_back, slopes, w2), [wide], conv_flops
     )
@@ -368,7 +368,7 @@
     (part,) = call(
         space_weights_kernel,
         [((12 * CH, CH), BF)],
-        (partial, recv_x, recv_g, time_part),
+        (partial, recv_x, recv_g, keep_t, recv_t),
         [wide],
         conv_flops,
     )

time: 130 us -> 129 us (level)
  blocking collectives: 79.6 us -> 77.9 us
  transfers between devices with their start and end apart: 8 -> 8, of which waited for: 4 -> 5; matrix products, arithmetic and copies ran while one was open for 0% -> 0% of each run, Pallas kernels for 5% -> 5%
where the time goes in v14:
time: 129 us
  blocking collectives  77.9 us (60%)
  starting transfers between devices  16.7 us (13%)
  Pallas kernels  16.4 us (13%)
  waiting for transfers between devices  15.3 us (12%)
  local copies, waits for them, and re-layouts  1.51 us (1%)
    all_to_all x1, blocking collectives, body(): both = lax.all_to_all(both, FRAME_AXES, 0, 0, tiled=True)  28.3 us
    all_to_all x1, blocking collectives, scatter_sum(): arrived = lax.all_to_all(parts, axes, 0, 0, tiled=True)  26.7 us
    all_to_all x1, blocking collectives, gather_all(): return lax.all_to_all(copies, axes, 0, 0, tiled=True).reshape(-1, CH)  22.9 us
    pallas_call x10, Pallas kernels, call(): pl.pallas_call(kernel, out_shape=[jax.ShapeDtypeStruct(shape, kind) for s...  16.4 us
    ppermute x5, starting transfers between devices, swap_cores(): return lax.ppermute(values, 'core', [(0, 1), (1, 0)])  10.2 us
    all_to_all x1, waiting for transfers between devices, swap_frames(): return lax.all_to_all(blocks, FRAME_AXES, 0, 0, tiled=True).reshape(PIX, CH)  8.54 us
    ppermute x2, waiting for transfers between devices, body(): arrived = lax.ppermute(part, 'zh', pairs)  6.4 us
    all_to_all x1, starting transfers between devices, swap_frames(): return lax.all_to_all(blocks, FRAME_AXES, 0, 0, tiled=True).reshape(PIX, CH)  5.35 us
  transfers between devices with their start and end apart: 8, of which 5 were waited for; matrix products, arithmetic and copies ran while one was open for 0% of the time, Pallas kernels for 5%

profile of v14, /device:TPU:1, one launch (start us, length us, event | category | flops | bytes accessed | tf_op | source)
XLA Modules:
  0.0 128.8 jit_solution(10096531479215747900)
XLA Ops:
  0.6 4.2 %shard_map.101 = (bf16[32,32,256]{2,1,0:T(8,128)(2,1)}, bf16[2,512,256]{2,1,0:T(8,128)(2,1)}, bf16[512,256]{1,0:T(8,128)(2,1)}, bf16[512,256]{1,0:T(8,128)(2,1)}) custom-call(s32[1]{0:T(128)} %bitcast.pos, bf16[512,256]{1,0:T(8,128)(2,1)} %bitcast.36, bf16[32,16,256]{2,1,0:T(8,128)(2,1)} %bitcast.37, bf16[2304,256]{1,0:T(8,128)(2,1)} %bitcast.24, ...), custom_call_target="tpu_custom_call" | custom-call | flops 1207959552 | bytes 2883588 | tf_op jit(solution)/shard_map/pallas_call | solution.py:43
  4.9 28.3 %all_to_all.20.both_at = bf16[32,32,256]{2,1,0:T(8,128)(2,1)} all-to-all(bf16[32,32,256]{2,1,0:T(8,128)(2,1)} %get-tuple-element.37), channel_id=1, replica_groups=mesh['zh'=4,'zl'=2,'x'=4,'y'=4,'core'=2] {'zh','zl','x'}, dimensions={0} | all-to-all | bytes 1048576 | tf_op jit(solution)/shard_map/all_to_all | solution.py:342
  33.1 3.1 %shard_map.102 = (bf16[512,256]{1,0:T(8,128)(2,1)}, bf16[4,32,16,256]{3,2,1,0:T(8,128)(2,1)}) custom-call(bf16[32,32,256]{2,1,0:T(8,128)(2,1)} %all_to_all.20.both_at, bf16[768,256]{1,0:T(8,128)(2,1)} %bitcast.34, bf16[768,256]{1,0:T(8,128)(2,1)} %bitcast.35), custom_call_target="tpu_custom_call" | custom-call | flops 603979776 | bytes 1310720 | tf_op jit(solution)/shard_map/pallas_call | solution.py:43
  36.3 0.0 copy-start
  36.3 5.4 %all-to-all-start.1 = ((bf16[32,16,256]{2,1,0:T(8,128)(2,1)}), bf16[32,16,256]{2,1,0:T(8,128)(2,1)S(1)}, u32[]{:S(2)}, u32[]{:S(2)}) async-start(bf16[32,16,256]{2,1,0:T(8,128)(2,1)} %bitcast.33), calls=%async_computation.1 | async-start | bytes 524288 | tf_op jit(solution)/shard_map/all_to_all | solution.py:307
  41.6 0.0 copy-start.3
  41.6 1.2 copy-done.3
  42.9 0.6 shard_map.103
  43.5 8.5 %all-to-all-done.1 = bf16[32,16,256]{2,1,0:T(8,128)(2,1)S(1)} async-done(((bf16[32,16,256]{2,1,0:T(8,128)(2,1)}), bf16[32,16,256]{2,1,0:T(8,128)(2,1)S(1)}, u32[]{:S(2)}, u32[]{:S(2)}) %all-to-all-start.1) | async-done | bytes 262176 | tf_op jit(solution)/shard_map/all_to_all | solution.py:307
  52.0 3.8 %collective-permute-start.2 = (bf16[768,256]{1,0:T(8,128)(2,1)S(1)}, bf16[768,256]{1,0:T(8,128)(2,1)S(1)}, u32[]{:S(2)}, u32[]{:S(2)}) collective-permute-start(bf16[768,256]{1,0:T(8,128)(2,1)S(1)} %get-tuple-element.47), channel_id=1, source_target_pairs={{0,1},{1,0},{2,3},{3,2},{4,5},{5,4},{6,7},{7,6},{8,9},{9,8},{10,11... | collective-permute-start | bytes 1179656 | tf_op jit(solution)/shard_map/ppermute | solution.py:302
  55.8 0.9 shard_map.104
  56.7 0.6 collective-permute-start.1
  57.2 0.9 shard_map.105.partial
  58.1 0.3 collective-permute-done.1.recv_g
  58.4 1.0 shard_map.106
  59.4 0.0 copy-start.2
  59.4 26.7 %all_to_all.21 = bf16[32,96,256]{2,1,0:T(8,128)(2,1)S(1)} all-to-all(bf16[32,96,256]{2,1,0:T(8,128)(2,1)S(1)} %bitcast.20), channel_id=1, replica_groups=mesh['zh'=4,'zl'=2,'x'=4,'y'=4,'core'=2] {'zl','x','y'}, dimensions={0} | all-to-all | bytes 3145728 | tf_op jit(solution)/shard_map/all_to_all | solution.py:312
  86.2 0.2 reduce_sum.12
  86.4 0.5 collective-permute-start.3
  86.8 1.5 %shard_map.107 = bf16[512,256]{1,0:T(8,128)(2,1)} custom-call(bf16[512,256]{1,0:T(8,128)(2,1)S(1)} %get-tuple-element.50.first_grad, bf16[2304,256]{1,0:T(8,128)(2,1)S(1)} %bitcast.25), custom_call_target="tpu_custom_call" | custom-call | flops 603979776 | bytes 1441792 | tf_op jit(solution)/shard_map/pallas_call | solution.py:43
  88.4 1.9 %collective-permute-done.3 = bf16[96,256]{1,0:T(8,128)(2,1)S(1)} collective-permute-done((bf16[96,256]{1,0:T(8,128)(2,1)S(1)}, bf16[96,256]{1,0:T(8,128)(2,1)S(1)}, u32[]{:S(2)}, u32[]{:S(2)}) %collective-permute-start.3) | collective-permute-done | bytes 49184 | tf_op jit(solution)/shard_map/ppermute | solution.py:380
  90.3 0.7 collective-permute-start.4
  91.0 4.5 %collective-permute-done.4 = bf16[96,256]{1,0:T(8,128)(2,1)S(1)} collective-permute-done((bf16[96,256]{1,0:T(8,128)(2,1)S(1)}, bf16[96,256]{1,0:T(8,128)(2,1)S(1)}, u32[]{:S(2)}, u32[]{:S(2)}) %collective-permute-start.4) | collective-permute-done | bytes 49184 | tf_op jit(solution)/shard_map/ppermute | solution.py:380
  95.5 0.2 broadcast_in_dim.2
  95.7 22.9 %all_to_all.22 = bf16[32,96,256]{2,1,0:T(8,128)(2,1)S(1)} all-to-all(bf16[32,96,256]{2,1,0:T(8,128)(2,1)S(1)} %broadcast_in_dim.2), channel_id=1, replica_groups=mesh['zh'=4,'zl'=2,'x'=4,'y'=4,'core'=2] {'zl','x','y'}, dimensions={0} | all-to-all | bytes 3145728 | tf_op jit(solution)/shard_map/all_to_all | solution.py:318
  118.6 0.1 fusion
  118.7 5.8 %collective-permute-start.6 = (bf16[1536,256]{1,0:T(8,128)(2,1)S(1)}, bf16[1536,256]{1,0:T(8,128)(2,1)S(1)}, u32[]{:S(2)}, u32[]{:S(2)}) collective-permute-start(bf16[1536,256]{1,0:T(8,128)(2,1)S(1)} %bitcast.32), channel_id=1, source_target_pairs={{0,1},{1,0},{2,3},{3,2},{4,5},{5,4},{6,7},{7,6},{8,9},{9,8},{10,11... | collective-permute-start | bytes 2359304 | tf_op jit(solution)/shard_map/ppermute | solution.py:302
  124.5 0.1 collective-permute-start.5
  124.6 1.7 %shard_map.108 = (f32[2304,256]{1,0:T(8,128)}, f32[2304,256]{1,0:T(8,128)}, f32[768,256]{1,0:T(8,128)}, f32[768,256]{1,0:T(8,128)}) custom-call(s32[1]{0:T(128)} %bitcast.pos, bf16[3072,256]{1,0:T(8,128)(2,1)S(1)} %bitcast.19), custom_call_target="tpu_custom_call" | custom-call | bytes 1572868 | tf_op jit(solution)/shard_map/pallas_call | solution.py:43
  126.3 0.1 collective-permute-done.6.half
  126.4 1.2 shard_map.109
  127.6 1.2 shard_map.110
  (14 shorter events, 0.1 us)
Async XLA Ops:
  33.1 22.6 %copy-start.5 = (bf16[512,256]{1,0:T(8,128)(2,1)S(1)}, bf16[512,256]{1,0:T(8,128)(2,1)}, u32[]{:S(2)}) copy-start(bf16[512,256]{1,0:T(8,128)(2,1)} %get-tuple-element.44) | copy-start | bytes 786436
  33.1 22.7 %copy-start.1 = (bf16[3,3,256,256]{3,2,1,0:T(8,128)(2,1)S(1)}, bf16[3,3,256,256]{3,2,1,0:T(8,128)(2,1)}, u32[]{:S(2)}) copy-start(bf16[3,3,256,256]{3,2,1,0:T(8,128)(2,1)} %param.9) | copy-start | bytes 3538948
  33.1 22.7 %copy-start.4 = (bf16[2,512,256]{2,1,0:T(8,128)(2,1)S(1)}, bf16[2,512,256]{2,1,0:T(8,128)(2,1)}, u32[]{:S(2)}) copy-start(bf16[2,512,256]{2,1,0:T(8,128)(2,1)} %get-tuple-element.42.slopes) | copy-start | bytes 1572868
  36.3 21.0 %copy-start = (bf16[512,256]{1,0:T(8,128)(2,1)S(1)}, bf16[512,256]{1,0:T(8,128)(2,1)}, u32[]{:S(2)}) copy-start(bf16[512,256]{1,0:T(8,128)(2,1)} %get-tuple-element.36.keep_x) | copy-start | bytes 786436
  36.3 15.8 %all-to-all-start.1 = ((bf16[32,16,256]{2,1,0:T(8,128)(2,1)}), bf16[32,16,256]{2,1,0:T(8,128)(2,1)S(1)}, u32[]{:S(2)}, u32[]{:S(2)}) async-start(bf16[32,16,256]{2,1,0:T(8,128)(2,1)} %bitcast.33), calls=%async_computation.1 | async-start | bytes 524288 | tf_op jit(solution)/shard_map/all_to_all | solution.py:307
  41.6 1.2 copy-start.3
  52.0 6.4 %collective-permute-start.2 = (bf16[768,256]{1,0:T(8,128)(2,1)S(1)}, bf16[768,256]{1,0:T(8,128)(2,1)S(1)}, u32[]{:S(2)}, u32[]{:S(2)}) collective-permute-start(bf16[768,256]{1,0:T(8,128)(2,1)S(1)} %get-tuple-element.47), channel_id=1, source_target_pairs={{0,1},{1,0},{2,3},{3,2},{4,5},{5,4},{6,7},{7,6},{8,9},{9,8},{10,11... | collective-permute-start | bytes 1179656 | tf_op jit(solution)/shard_map/ppermute | solution.py:302
  55.8 2.3 %collective-permute-start = (bf16[512,256]{1,0:T(8,128)(2,1)S(1)}, bf16[512,256]{1,0:T(8,128)(2,1)S(1)}, u32[]{:S(2)}, u32[]{:S(2)}) collective-permute-start(bf16[512,256]{1,0:T(8,128)(2,1)S(1)} %copy-done.5), channel_id=1, source_target_pairs={{0,1},{1,0},{2,3},{3,2},{4,5},{5,4},{6,7},{7,6},{8,9},{9,8},{10,11... | collective-permute-start | bytes 786440 | tf_op jit(solution)/shard_map/ppermute | solution.py:302
  56.7 1.7 %collective-permute-start.1 = (bf16[512,256]{1,0:T(8,128)(2,1)S(1)}, bf16[512,256]{1,0:T(8,128)(2,1)S(1)}, u32[]{:S(2)}, u32[]{:S(2)}) collective-permute-start(bf16[512,256]{1,0:T(8,128)(2,1)S(1)} %get-tuple-element.45), channel_id=1, source_target_pairs={{0,1},{1,0},{2,3},{3,2},{4,5},{5,4},{6,7},{7,6},{8,9},{9,8},{10,11... | collective-permute-start | bytes 786440 | tf_op jit(solution)/shard_map/ppermute | solution.py:302
  59.4 27.4 %copy-start.2 = (bf16[3,3,256,256]{3,2,1,0:T(8,128)(2,1)S(1)}, bf16[3,3,256,256]{3,2,1,0:T(8,128)(2,1)}, u32[]{:S(2)}) copy-start(bf16[3,3,256,256]{3,2,1,0:T(8,128)(2,1)} %param.8) | copy-start | bytes 3538948
  86.4 3.9 %collective-permute-start.3 = (bf16[96,256]{1,0:T(8,128)(2,1)S(1)}, bf16[96,256]{1,0:T(8,128)(2,1)S(1)}, u32[]{:S(2)}, u32[]{:S(2)}) collective-permute-start(bf16[96,256]{1,0:T(8,128)(2,1)S(1)} %reduce_sum.12), channel_id=1, source_target_pairs={{0,64},{64,0},{128,192},{192,128},{1,65},{65,1},{129,193},{193,129... | collective-permute-start | bytes 147464 | tf_op jit(solution)/shard_map/ppermute | solution.py:380
  90.3 5.2 %collective-permute-start.4 = (bf16[96,256]{1,0:T(8,128)(2,1)S(1)}, bf16[96,256]{1,0:T(8,128)(2,1)S(1)}, u32[]{:S(2)}, u32[]{:S(2)}) collective-permute-start(bf16[96,256]{1,0:T(8,128)(2,1)S(1)} %add_convert_fusion.1), channel_id=1, source_target_pairs={{0,192},{192,0},{64,128},{128,64},{1,193},{193,1},{65,129},{129,65... | collective-permute-start | bytes 147464 | tf_op jit(solution)/shard_map/ppermute | solution.py:380
  118.7 7.7 %collective-permute-start.6 = (bf16[1536,256]{1,0:T(8,128)(2,1)S(1)}, bf16[1536,256]{1,0:T(8,128)(2,1)S(1)}, u32[]{:S(2)}, u32[]{:S(2)}) collective-permute-start(bf16[1536,256]{1,0:T(8,128)(2,1)S(1)} %bitcast.32), channel_id=1, source_target_pairs={{0,1},{1,0},{2,3},{3,2},{4,5},{5,4},{6,7},{7,6},{8,9},{9,8},{10,11... | collective-permute-start | bytes 2359304 | tf_op jit(solution)/shard_map/ppermute | solution.py:302
  124.5 3.1 %collective-permute-start.5 = (bf16[1536,256]{1,0:T(8,128)(2,1)S(1)}, bf16[1536,256]{1,0:T(8,128)(2,1)S(1)}, u32[]{:S(2)}, u32[]{:S(2)}) collective-permute-start(bf16[1536,256]{1,0:T(8,128)(2,1)S(1)} %bitcast.31), channel_id=1, source_target_pairs={{0,1},{1,0},{2,3},{3,2},{4,5},{5,4},{6,7},{7,6},{8,9},{9,8},{10,11... | collective-permute-start | bytes 2359304 | tf_op jit(solution)/shard_map/ppermute | solution.py:302

commit v15 on v14

--- a/solution.py
+++ b/solution.py
@@ -356,7 +356,7 @@
     keep_t, send_t = call(
         time_weights_kernel, [taps, taps], (pos, own.reshape(4, PIX, CH)), (), 2 * time_flops
     )
-    act_back, send_t = lax.optimization_barrier((act_back, send_t))
+    act_back, keep_t = lax.optimization_barrier((act_back, keep_t))
     recv_t = swap_cores(send_t)
     first_grad, keep_g, send_g = call(
         backward_kernel, [slab, slab, slab], (pos, act_back, slopes, w2), [wide], conv_flops

time: 129 us -> 130 us (level)
  waiting for transfers between devices: 15.3 us -> 13.2 us
  starting transfers between devices: 16.7 us -> 18.3 us
    all_to_all x1, waiting for transfers between devices: 8.54 us -> 6.48 us  [swap_frames(): return lax.all_to_all(blocks, FRAME_AXES, 0, 0, tiled=True).reshape(PIX, CH)]
    ppermute x5, starting transfers between devices: 10.2 us -> 11.8 us  [swap_cores(): return lax.ppermute(values, 'core', [(0, 1), (1, 0)])]
where the time goes in v15:
time: 130 us; the launch traced here: 129 us
  blocking collectives  77.9 us (60%)
  starting transfers between devices  18.3 us (14%)
  Pallas kernels  16.3 us (13%)
  waiting for transfers between devices  13.2 us (10%)
  local copies, waits for them, and re-layouts  2.55 us (2%)
    all_to_all x1, blocking collectives, body(): both = lax.all_to_all(both, FRAME_AXES, 0, 0, tiled=True)  28.3 us
    all_to_all x1, blocking collectives, scatter_sum(): arrived = lax.all_to_all(parts, axes, 0, 0, tiled=True)  26.7 us
    all_to_all x1, blocking collectives, gather_all(): return lax.all_to_all(copies, axes, 0, 0, tiled=True).reshape(-1, CH)  22.9 us
    pallas_call x10, Pallas kernels, call(): pl.pallas_call(kernel, out_shape=[jax.ShapeDtypeStruct(shape, kind) for s...  16.3 us
    ppermute x5, starting transfers between devices, swap_cores(): return lax.ppermute(values, 'core', [(0, 1), (1, 0)])  11.8 us
    all_to_all x1, waiting for transfers between devices, swap_frames(): return lax.all_to_all(blocks, FRAME_AXES, 0, 0, tiled=True).reshape(PIX, CH)  6.48 us
    ppermute x2, waiting for transfers between devices, body(): arrived = lax.ppermute(part, 'zh', pairs)  6.41 us
    all_to_all x1, starting transfers between devices, swap_frames(): return lax.all_to_all(blocks, FRAME_AXES, 0, 0, tiled=True).reshape(PIX, CH)  5.36 us
  transfers between devices with their start and end apart: 8, of which 5 were waited for; matrix products, arithmetic and copies ran while one was open for 0% of the time, Pallas kernels for 5%

profile of v15, /device:TPU:1, one launch (start us, length us, event | category | flops | bytes accessed | tf_op | source)
XLA Modules:
  0.0 129.3 jit_solution(14776934435257397000)
XLA Ops:
  0.6 4.2 %shard_map.101 = (bf16[32,32,256]{2,1,0:T(8,128)(2,1)}, bf16[2,512,256]{2,1,0:T(8,128)(2,1)}, bf16[512,256]{1,0:T(8,128)(2,1)}, bf16[512,256]{1,0:T(8,128)(2,1)}) custom-call(s32[1]{0:T(128)} %bitcast.pos, bf16[512,256]{1,0:T(8,128)(2,1)} %bitcast.36, bf16[32,16,256]{2,1,0:T(8,128)(2,1)} %bitcast.37, bf16[2304,256]{1,0:T(8,128)(2,1)} %bitcast.24, ...), custom_call_target="tpu_custom_call" | custom-call | flops 1207959552 | bytes 2883588 | tf_op jit(solution)/shard_map/pallas_call | solution.py:43
  4.9 28.3 %all_to_all.20.both_at = bf16[32,32,256]{2,1,0:T(8,128)(2,1)} all-to-all(bf16[32,32,256]{2,1,0:T(8,128)(2,1)} %get-tuple-element.37), channel_id=1, replica_groups=mesh['zh'=4,'zl'=2,'x'=4,'y'=4,'core'=2] {'zh','zl','x'}, dimensions={0} | all-to-all | bytes 1048576 | tf_op jit(solution)/shard_map/all_to_all | solution.py:342
  33.1 3.1 %shard_map.102 = (bf16[512,256]{1,0:T(8,128)(2,1)}, bf16[4,32,16,256]{3,2,1,0:T(8,128)(2,1)}) custom-call(bf16[32,32,256]{2,1,0:T(8,128)(2,1)} %all_to_all.20.both_at, bf16[768,256]{1,0:T(8,128)(2,1)} %bitcast.34, bf16[768,256]{1,0:T(8,128)(2,1)} %bitcast.35), custom_call_target="tpu_custom_call" | custom-call | flops 603979776 | bytes 1310720 | tf_op jit(solution)/shard_map/pallas_call | solution.py:43
  36.2 0.0 copy-start
  36.2 5.4 %all-to-all-start.1 = ((bf16[32,16,256]{2,1,0:T(8,128)(2,1)}), bf16[32,16,256]{2,1,0:T(8,128)(2,1)S(1)}, u32[]{:S(2)}, u32[]{:S(2)}) async-start(bf16[32,16,256]{2,1,0:T(8,128)(2,1)} %bitcast.33), calls=%async_computation.1 | async-start | bytes 524288 | tf_op jit(solution)/shard_map/all_to_all | solution.py:307
  41.6 1.2 copy-done.3
  42.8 0.6 shard_map.103
  43.4 2.0 %collective-permute-start.2 = (bf16[768,256]{1,0:T(8,128)(2,1)S(1)}, bf16[768,256]{1,0:T(8,128)(2,1)S(1)}, u32[]{:S(2)}, u32[]{:S(2)}) collective-permute-start(bf16[768,256]{1,0:T(8,128)(2,1)S(1)} %get-tuple-element.47), channel_id=1, source_target_pairs={{0,1},{1,0},{2,3},{3,2},{4,5},{5,4},{6,7},{7,6},{8,9},{9,8},{10,11... | collective-permute-start | bytes 1179656 | tf_op jit(solution)/shard_map/ppermute | solution.py:302
  45.4 0.1 collective-permute-start
  45.5 6.5 %all-to-all-done.1 = bf16[32,16,256]{2,1,0:T(8,128)(2,1)S(1)} async-done(((bf16[32,16,256]{2,1,0:T(8,128)(2,1)}), bf16[32,16,256]{2,1,0:T(8,128)(2,1)S(1)}, u32[]{:S(2)}, u32[]{:S(2)}) %all-to-all-start.1) | async-done | bytes 262176 | tf_op jit(solution)/shard_map/all_to_all | solution.py:307
  52.0 1.0 copy-done.4
  53.0 0.9 shard_map.104
  53.9 3.8 %collective-permute-start.1 = (bf16[512,256]{1,0:T(8,128)(2,1)S(1)}, bf16[512,256]{1,0:T(8,128)(2,1)S(1)}, u32[]{:S(2)}, u32[]{:S(2)}) collective-permute-start(bf16[512,256]{1,0:T(8,128)(2,1)S(1)} %get-tuple-element.45), channel_id=1, source_target_pairs={{0,1},{1,0},{2,3},{3,2},{4,5},{5,4},{6,7},{7,6},{8,9},{9,8},{10,11... | collective-permute-start | bytes 786440 | tf_op jit(solution)/shard_map/ppermute | solution.py:302
  57.7 0.9 shard_map.105.partial
  58.6 0.3 collective-permute-done.1.recv_g
  58.9 1.0 shard_map.106
  59.9 26.7 %all_to_all.21 = bf16[32,96,256]{2,1,0:T(8,128)(2,1)S(1)} all-to-all(bf16[32,96,256]{2,1,0:T(8,128)(2,1)S(1)} %bitcast.20), channel_id=1, replica_groups=mesh['zh'=4,'zl'=2,'x'=4,'y'=4,'core'=2] {'zl','x','y'}, dimensions={0} | all-to-all | bytes 3145728 | tf_op jit(solution)/shard_map/all_to_all | solution.py:312
  86.6 0.2 reduce_sum.12
  86.9 0.5 collective-permute-start.3
  87.3 1.5 %shard_map.107 = bf16[512,256]{1,0:T(8,128)(2,1)} custom-call(bf16[512,256]{1,0:T(8,128)(2,1)S(1)} %get-tuple-element.50.first_grad, bf16[2304,256]{1,0:T(8,128)(2,1)S(1)} %bitcast.25), custom_call_target="tpu_custom_call" | custom-call | flops 603979776 | bytes 1441792 | tf_op jit(solution)/shard_map/pallas_call | solution.py:43
  88.8 1.9 %collective-permute-done.3 = bf16[96,256]{1,0:T(8,128)(2,1)S(1)} collective-permute-done((bf16[96,256]{1,0:T(8,128)(2,1)S(1)}, bf16[96,256]{1,0:T(8,128)(2,1)S(1)}, u32[]{:S(2)}, u32[]{:S(2)}) %collective-permute-start.3) | collective-permute-done | bytes 49184 | tf_op jit(solution)/shard_map/ppermute | solution.py:380
  90.8 0.7 collective-permute-start.4
  91.5 4.5 %collective-permute-done.4 = bf16[96,256]{1,0:T(8,128)(2,1)S(1)} collective-permute-done((bf16[96,256]{1,0:T(8,128)(2,1)S(1)}, bf16[96,256]{1,0:T(8,128)(2,1)S(1)}, u32[]{:S(2)}, u32[]{:S(2)}) %collective-permute-start.4) | collective-permute-done | bytes 49184 | tf_op jit(solution)/shard_map/ppermute | solution.py:380
  96.0 0.2 broadcast_in_dim.2
  96.2 22.9 %all_to_all.22 = bf16[32,96,256]{2,1,0:T(8,128)(2,1)S(1)} all-to-all(bf16[32,96,256]{2,1,0:T(8,128)(2,1)S(1)} %broadcast_in_dim.2), channel_id=1, replica_groups=mesh['zh'=4,'zl'=2,'x'=4,'y'=4,'core'=2] {'zl','x','y'}, dimensions={0} | all-to-all | bytes 3145728 | tf_op jit(solution)/shard_map/all_to_all | solution.py:318
  119.1 0.1 fusion
  119.2 5.8 %collective-permute-start.6 = (bf16[1536,256]{1,0:T(8,128)(2,1)S(1)}, bf16[1536,256]{1,0:T(8,128)(2,1)S(1)}, u32[]{:S(2)}, u32[]{:S(2)}) collective-permute-start(bf16[1536,256]{1,0:T(8,128)(2,1)S(1)} %bitcast.32), channel_id=1, source_target_pairs={{0,1},{1,0},{2,3},{3,2},{4,5},{5,4},{6,7},{7,6},{8,9},{9,8},{10,11... | collective-permute-start | bytes 2359304 | tf_op jit(solution)/shard_map/ppermute | solution.py:302
  125.0 0.1 collective-permute-start.5
  125.1 1.7 %shard_map.108 = (f32[2304,256]{1,0:T(8,128)}, f32[2304,256]{1,0:T(8,128)}, f32[768,256]{1,0:T(8,128)}, f32[768,256]{1,0:T(8,128)}) custom-call(s32[1]{0:T(128)} %bitcast.pos, bf16[3072,256]{1,0:T(8,128)(2,1)S(1)} %bitcast.19), custom_call_target="tpu_custom_call" | custom-call | bytes 1572868 | tf_op jit(solution)/shard_map/pallas_call | solution.py:43
  126.8 0.1 collective-permute-done.6.half
  126.9 1.2 shard_map.109
  128.1 1.2 shard_map.110
  (12 shorter events, 0.1 us)
Async XLA Ops:
  33.1 18.8 %copy-start.1 = (bf16[3,3,256,256]{3,2,1,0:T(8,128)(2,1)S(1)}, bf16[3,3,256,256]{3,2,1,0:T(8,128)(2,1)}, u32[]{:S(2)}) copy-start(bf16[3,3,256,256]{3,2,1,0:T(8,128)(2,1)} %param.9) | copy-start | bytes 3538948
  36.2 21.5 %copy-start = (bf16[512,256]{1,0:T(8,128)(2,1)S(1)}, bf16[512,256]{1,0:T(8,128)(2,1)}, u32[]{:S(2)}) copy-start(bf16[512,256]{1,0:T(8,128)(2,1)} %get-tuple-element.36.keep_x) | copy-start | bytes 786436
  36.2 15.8 %all-to-all-start.1 = ((bf16[32,16,256]{2,1,0:T(8,128)(2,1)}), bf16[32,16,256]{2,1,0:T(8,128)(2,1)S(1)}, u32[]{:S(2)}, u32[]{:S(2)}) async-start(bf16[32,16,256]{2,1,0:T(8,128)(2,1)} %bitcast.33), calls=%async_computation.1 | async-start | bytes 524288 | tf_op jit(solution)/shard_map/all_to_all | solution.py:307
  41.6 1.2 copy-start.3
  43.4 15.2 %collective-permute-start.2 = (bf16[768,256]{1,0:T(8,128)(2,1)S(1)}, bf16[768,256]{1,0:T(8,128)(2,1)S(1)}, u32[]{:S(2)}, u32[]{:S(2)}) collective-permute-start(bf16[768,256]{1,0:T(8,128)(2,1)S(1)} %get-tuple-element.47), channel_id=1, source_target_pairs={{0,1},{1,0},{2,3},{3,2},{4,5},{5,4},{6,7},{7,6},{8,9},{9,8},{10,11... | collective-permute-start | bytes 1179656 | tf_op jit(solution)/shard_map/ppermute | solution.py:302
  45.4 13.2 %collective-permute-start = (bf16[512,256]{1,0:T(8,128)(2,1)}, bf16[512,256]{1,0:T(8,128)(2,1)S(1)}, u32[]{:S(2)}, u32[]{:S(2)}) collective-permute-start(bf16[512,256]{1,0:T(8,128)(2,1)} %get-tuple-element.44), channel_id=1, source_target_pairs={{0,1},{1,0},{2,3},{3,2},{4,5},{5,4},{6,7},{7,6},{8,9},{9,8},{10,11... | collective-permute-start | bytes 786440 | tf_op jit(solution)/shard_map/ppermute | solution.py:302
  52.0 1.0 copy-start.4
  53.9 5.0 %collective-permute-start.1 = (bf16[512,256]{1,0:T(8,128)(2,1)S(1)}, bf16[512,256]{1,0:T(8,128)(2,1)S(1)}, u32[]{:S(2)}, u32[]{:S(2)}) collective-permute-start(bf16[512,256]{1,0:T(8,128)(2,1)S(1)} %get-tuple-element.45), channel_id=1, source_target_pairs={{0,1},{1,0},{2,3},{3,2},{4,5},{5,4},{6,7},{7,6},{8,9},{9,8},{10,11... | collective-permute-start | bytes 786440 | tf_op jit(solution)/shard_map/ppermute | solution.py:302
  59.9 27.4 %copy-start.2 = (bf16[3,3,256,256]{3,2,1,0:T(8,128)(2,1)S(1)}, bf16[3,3,256,256]{3,2,1,0:T(8,128)(2,1)}, u32[]{:S(2)}) copy-start(bf16[3,3,256,256]{3,2,1,0:T(8,128)(2,1)} %param.8) | copy-start | bytes 3538948
  86.9 3.9 %collective-permute-start.3 = (bf16[96,256]{1,0:T(8,128)(2,1)S(1)}, bf16[96,256]{1,0:T(8,128)(2,1)S(1)}, u32[]{:S(2)}, u32[]{:S(2)}) collective-permute-start(bf16[96,256]{1,0:T(8,128)(2,1)S(1)} %reduce_sum.12), channel_id=1, source_target_pairs={{0,64},{64,0},{128,192},{192,128},{1,65},{65,1},{129,193},{193,129... | collective-permute-start | bytes 147464 | tf_op jit(solution)/shard_map/ppermute | solution.py:380
  90.8 5.2 %collective-permute-start.4 = (bf16[96,256]{1,0:T(8,128)(2,1)S(1)}, bf16[96,256]{1,0:T(8,128)(2,1)S(1)}, u32[]{:S(2)}, u32[]{:S(2)}) collective-permute-start(bf16[96,256]{1,0:T(8,128)(2,1)S(1)} %add_convert_fusion.1), channel_id=1, source_target_pairs={{0,192},{192,0},{64,128},{128,64},{1,193},{193,1},{65,129},{129,65... | collective-permute-start | bytes 147464 | tf_op jit(solution)/shard_map/ppermute | solution.py:380
  119.2 7.7 %collective-permute-start.6 = (bf16[1536,256]{1,0:T(8,128)(2,1)S(1)}, bf16[1536,256]{1,0:T(8,128)(2,1)S(1)}, u32[]{:S(2)}, u32[]{:S(2)}) collective-permute-start(bf16[1536,256]{1,0:T(8,128)(2,1)S(1)} %bitcast.32), channel_id=1, source_target_pairs={{0,1},{1,0},{2,3},{3,2},{4,5},{5,4},{6,7},{7,6},{8,9},{9,8},{10,11... | collective-permute-start | bytes 2359304 | tf_op jit(solution)/shard_map/ppermute | solution.py:302
  125.0 3.1 %collective-permute-start.5 = (bf16[1536,256]{1,0:T(8,128)(2,1)S(1)}, bf16[1536,256]{1,0:T(8,128)(2,1)S(1)}, u32[]{:S(2)}, u32[]{:S(2)}) collective-permute-start(bf16[1536,256]{1,0:T(8,128)(2,1)S(1)} %bitcast.31), channel_id=1, source_target_pairs={{0,1},{1,0},{2,3},{3,2},{4,5},{5,4},{6,7},{7,6},{8,9},{9,8},{10,11... | collective-permute-start | bytes 2359304 | tf_op jit(solution)/shard_map/ppermute | solution.py:302

commit v16 on v15

--- a/solution.py
+++ b/solution.py
@@ -356,7 +356,7 @@
     keep_t, send_t = call(
         time_weights_kernel, [taps, taps], (pos, own.reshape(4, PIX, CH)), (), 2 * time_flops
     )
-    act_back, keep_t = lax.optimization_barrier((act_back, keep_t))
+    act_back, send_t, recv_x = lax.optimization_barrier((act_back, send_t, recv_x))
     recv_t = swap_cores(send_t)
     first_grad, keep_g, send_g = call(
         backward_kernel, [slab, slab, slab], (pos, act_back, slopes, w2), [wide], conv_flops

time: 130 us -> 130 us (level)
  no operation moved by 1% of the time
where the time goes in v16:
time: 130 us; the launch traced here: 129 us
  blocking collectives  78.8 us (61%)
  starting transfers between devices  17.8 us (14%)
  Pallas kernels  16.4 us (13%)
  waiting for transfers between devices  13.7 us (11%)
  local copies, waits for them, and re-layouts  1.52 us (1%)
    all_to_all x1, blocking collectives, body(): both = lax.all_to_all(both, FRAME_AXES, 0, 0, tiled=True)  28.4 us
    all_to_all x1, blocking collectives, scatter_sum(): arrived = lax.all_to_all(parts, axes, 0, 0, tiled=True)  26.8 us
    all_to_all x1, blocking collectives, gather_all(): return lax.all_to_all(copies, axes, 0, 0, tiled=True).reshape(-1, CH)  23.6 us
    pallas_call x10, Pallas kernels, call(): pl.pallas_call(kernel, out_shape=[jax.ShapeDtypeStruct(shape, kind) for s...  16.4 us
    ppermute x5, starting transfers between devices, swap_cores(): return lax.ppermute(values, 'core', [(0, 1), (1, 0)])  11.2 us
    all_to_all x1, waiting for transfers between devices, swap_frames(): return lax.all_to_all(blocks, FRAME_AXES, 0, 0, tiled=True).reshape(PIX, CH)  6.57 us
    ppermute x2, waiting for transfers between devices, body(): arrived = lax.ppermute(part, 'zh', pairs)  6.4 us
    all_to_all x1, starting transfers between devices, swap_frames(): return lax.all_to_all(blocks, FRAME_AXES, 0, 0, tiled=True).reshape(PIX, CH)  5.35 us
  transfers between devices with their start and end apart: 8, of which 5 were waited for; matrix products, arithmetic and copies ran while one was open for 0% of the time, Pallas kernels for 5%

profile of v16, /device:TPU:1, one launch (start us, length us, event | category | flops | bytes accessed | tf_op | source)
XLA Modules:
  0.0 129.1 jit_solution(11744283078016309180)
XLA Ops:
  0.6 4.2 %shard_map.101 = (bf16[32,32,256]{2,1,0:T(8,128)(2,1)}, bf16[2,512,256]{2,1,0:T(8,128)(2,1)}, bf16[512,256]{1,0:T(8,128)(2,1)}, bf16[512,256]{1,0:T(8,128)(2,1)}) custom-call(s32[1]{0:T(128)} %bitcast.pos, bf16[512,256]{1,0:T(8,128)(2,1)} %bitcast.36, bf16[32,16,256]{2,1,0:T(8,128)(2,1)} %bitcast.37, bf16[2304,256]{1,0:T(8,128)(2,1)} %bitcast.24, ...), custom_call_target="tpu_custom_call" | custom-call | flops 1207959552 | bytes 2883588 | tf_op jit(solution)/shard_map/pallas_call | solution.py:43
  4.9 0.0 copy-start.5
  4.9 28.4 %all_to_all.20.both_at = bf16[32,32,256]{2,1,0:T(8,128)(2,1)} all-to-all(bf16[32,32,256]{2,1,0:T(8,128)(2,1)} %get-tuple-element.38), channel_id=1, replica_groups=mesh['zh'=4,'zl'=2,'x'=4,'y'=4,'core'=2] {'zh','zl','x'}, dimensions={0} | all-to-all | bytes 1048576 | tf_op jit(solution)/shard_map/all_to_all | solution.py:342
  33.3 3.1 %shard_map.102 = (bf16[512,256]{1,0:T(8,128)(2,1)}, bf16[4,32,16,256]{3,2,1,0:T(8,128)(2,1)}) custom-call(bf16[32,32,256]{2,1,0:T(8,128)(2,1)} %all_to_all.20.both_at, bf16[768,256]{1,0:T(8,128)(2,1)} %bitcast.34, bf16[768,256]{1,0:T(8,128)(2,1)} %bitcast.35), custom_call_target="tpu_custom_call" | custom-call | flops 603979776 | bytes 1310720 | tf_op jit(solution)/shard_map/pallas_call | solution.py:43
  36.4 0.0 copy-start
  36.4 5.4 %all-to-all-start.1 = ((bf16[32,16,256]{2,1,0:T(8,128)(2,1)}), bf16[32,16,256]{2,1,0:T(8,128)(2,1)S(1)}, u32[]{:S(2)}, u32[]{:S(2)}) async-start(bf16[32,16,256]{2,1,0:T(8,128)(2,1)} %bitcast.33), calls=%async_computation.1 | async-start | bytes 524288 | tf_op jit(solution)/shard_map/all_to_all | solution.py:307
  41.8 2.0 %collective-permute-start = (bf16[512,256]{1,0:T(8,128)(2,1)S(1)}, bf16[512,256]{1,0:T(8,128)(2,1)S(1)}, u32[]{:S(2)}, u32[]{:S(2)}) collective-permute-start(bf16[512,256]{1,0:T(8,128)(2,1)S(1)} %copy-done.5), channel_id=1, source_target_pairs={{0,1},{1,0},{2,3},{3,2},{4,5},{5,4},{6,7},{7,6},{8,9},{9,8},{10,11... | collective-permute-start | bytes 786440 | tf_op jit(solution)/shard_map/ppermute | solution.py:302
  43.7 1.2 copy-done.3
  44.9 0.6 shard_map.103
  45.6 6.6 %all-to-all-done.1 = bf16[32,16,256]{2,1,0:T(8,128)(2,1)S(1)} async-done(((bf16[32,16,256]{2,1,0:T(8,128)(2,1)}), bf16[32,16,256]{2,1,0:T(8,128)(2,1)S(1)}, u32[]{:S(2)}, u32[]{:S(2)}) %all-to-all-start.1) | async-done | bytes 262176 | tf_op jit(solution)/shard_map/all_to_all | solution.py:307
  52.2 3.8 %collective-permute-start.2 = (bf16[768,256]{1,0:T(8,128)(2,1)S(1)}, bf16[768,256]{1,0:T(8,128)(2,1)S(1)}, u32[]{:S(2)}, u32[]{:S(2)}) collective-permute-start(bf16[768,256]{1,0:T(8,128)(2,1)S(1)} %get-tuple-element.49), channel_id=1, source_target_pairs={{0,1},{1,0},{2,3},{3,2},{4,5},{5,4},{6,7},{7,6},{8,9},{9,8},{10,11... | collective-permute-start | bytes 1179656 | tf_op jit(solution)/shard_map/ppermute | solution.py:302
  55.9 0.9 shard_map.104
  56.8 0.1 collective-permute-start.1
  56.9 0.9 shard_map.105.partial
  57.8 0.6 collective-permute-done.1.recv_g
  58.4 1.0 shard_map.106
  59.4 26.8 %all_to_all.21 = bf16[32,96,256]{2,1,0:T(8,128)(2,1)S(1)} all-to-all(bf16[32,96,256]{2,1,0:T(8,128)(2,1)S(1)} %bitcast.20), channel_id=1, replica_groups=mesh['zh'=4,'zl'=2,'x'=4,'y'=4,'core'=2] {'zl','x','y'}, dimensions={0} | all-to-all | bytes 3145728 | tf_op jit(solution)/shard_map/all_to_all | solution.py:312
  86.2 0.2 reduce_sum.12
  86.5 0.5 collective-permute-start.3
  86.9 1.5 %shard_map.107 = bf16[512,256]{1,0:T(8,128)(2,1)} custom-call(bf16[512,256]{1,0:T(8,128)(2,1)S(1)} %get-tuple-element.52.first_grad, bf16[2304,256]{1,0:T(8,128)(2,1)S(1)} %bitcast.25), custom_call_target="tpu_custom_call" | custom-call | flops 603979776 | bytes 1441792 | tf_op jit(solution)/shard_map/pallas_call | solution.py:43
  88.5 1.9 %collective-permute-done.3 = bf16[96,256]{1,0:T(8,128)(2,1)S(1)} collective-permute-done((bf16[96,256]{1,0:T(8,128)(2,1)S(1)}, bf16[96,256]{1,0:T(8,128)(2,1)S(1)}, u32[]{:S(2)}, u32[]{:S(2)}) %collective-permute-start.3) | collective-permute-done | bytes 49184 | tf_op jit(solution)/shard_map/ppermute | solution.py:380
  90.4 0.7 collective-permute-start.4
  91.1 4.5 %collective-permute-done.4 = bf16[96,256]{1,0:T(8,128)(2,1)S(1)} collective-permute-done((bf16[96,256]{1,0:T(8,128)(2,1)S(1)}, bf16[96,256]{1,0:T(8,128)(2,1)S(1)}, u32[]{:S(2)}, u32[]{:S(2)}) %collective-permute-start.4) | collective-permute-done | bytes 49184 | tf_op jit(solution)/shard_map/ppermute | solution.py:380
  95.6 0.2 broadcast_in_dim.2
  95.8 23.6 %all_to_all.22 = bf16[32,96,256]{2,1,0:T(8,128)(2,1)S(1)} all-to-all(bf16[32,96,256]{2,1,0:T(8,128)(2,1)S(1)} %broadcast_in_dim.2), channel_id=1, replica_groups=mesh['zh'=4,'zl'=2,'x'=4,'y'=4,'core'=2] {'zl','x','y'}, dimensions={0} | all-to-all | bytes 3145728 | tf_op jit(solution)/shard_map/all_to_all | solution.py:318
  119.4 0.1 fusion
  119.5 5.3 %collective-permute-start.6 = (bf16[1536,256]{1,0:T(8,128)(2,1)S(1)}, bf16[1536,256]{1,0:T(8,128)(2,1)S(1)}, u32[]{:S(2)}, u32[]{:S(2)}) collective-permute-start(bf16[1536,256]{1,0:T(8,128)(2,1)S(1)} %bitcast.32), channel_id=1, source_target_pairs={{0,1},{1,0},{2,3},{3,2},{4,5},{5,4},{6,7},{7,6},{8,9},{9,8},{10,11... | collective-permute-start | bytes 2359304 | tf_op jit(solution)/shard_map/ppermute | solution.py:302
  124.8 0.1 collective-permute-start.5
  124.9 1.7 %shard_map.108 = (f32[2304,256]{1,0:T(8,128)}, f32[2304,256]{1,0:T(8,128)}, f32[768,256]{1,0:T(8,128)}, f32[768,256]{1,0:T(8,128)}) custom-call(s32[1]{0:T(128)} %bitcast.pos, bf16[3072,256]{1,0:T(8,128)(2,1)S(1)} %bitcast.19), custom_call_target="tpu_custom_call" | custom-call | bytes 1572868 | tf_op jit(solution)/shard_map/pallas_call | solution.py:43
  126.6 0.1 collective-permute-done.6.half
  126.7 1.2 shard_map.109
  127.9 1.2 shard_map.110
  (14 shorter events, 0.1 us)
Async XLA Ops:
  4.9 36.9 %copy-start.5 = (bf16[512,256]{1,0:T(8,128)(2,1)S(1)}, bf16[512,256]{1,0:T(8,128)(2,1)}, u32[]{:S(2)}) copy-start(bf16[512,256]{1,0:T(8,128)(2,1)} %get-tuple-element.42) | copy-start | bytes 786436
  33.3 22.6 %copy-start.1 = (bf16[3,3,256,256]{3,2,1,0:T(8,128)(2,1)S(1)}, bf16[3,3,256,256]{3,2,1,0:T(8,128)(2,1)}, u32[]{:S(2)}) copy-start(bf16[3,3,256,256]{3,2,1,0:T(8,128)(2,1)} %param.9) | copy-start | bytes 3538948
  33.3 22.6 %copy-start.4 = (bf16[2,512,256]{2,1,0:T(8,128)(2,1)S(1)}, bf16[2,512,256]{2,1,0:T(8,128)(2,1)}, u32[]{:S(2)}) copy-start(bf16[2,512,256]{2,1,0:T(8,128)(2,1)} %get-tuple-element.44.slopes) | copy-start | bytes 1572868
  36.4 20.5 %copy-start = (bf16[512,256]{1,0:T(8,128)(2,1)S(1)}, bf16[512,256]{1,0:T(8,128)(2,1)}, u32[]{:S(2)}) copy-start(bf16[512,256]{1,0:T(8,128)(2,1)} %get-tuple-element.37.keep_x) | copy-start | bytes 786436
  36.4 15.8 %all-to-all-start.1 = ((bf16[32,16,256]{2,1,0:T(8,128)(2,1)}), bf16[32,16,256]{2,1,0:T(8,128)(2,1)S(1)}, u32[]{:S(2)}, u32[]{:S(2)}) async-start(bf16[32,16,256]{2,1,0:T(8,128)(2,1)} %bitcast.33), calls=%async_computation.1 | async-start | bytes 524288 | tf_op jit(solution)/shard_map/all_to_all | solution.py:307
  41.8 3.8 %collective-permute-start = (bf16[512,256]{1,0:T(8,128)(2,1)S(1)}, bf16[512,256]{1,0:T(8,128)(2,1)S(1)}, u32[]{:S(2)}, u32[]{:S(2)}) collective-permute-start(bf16[512,256]{1,0:T(8,128)(2,1)S(1)} %copy-done.5), channel_id=1, source_target_pairs={{0,1},{1,0},{2,3},{3,2},{4,5},{5,4},{6,7},{7,6},{8,9},{9,8},{10,11... | collective-permute-start | bytes 786440 | tf_op jit(solution)/shard_map/ppermute | solution.py:302
  43.7 1.2 copy-start.3
  52.2 6.3 %collective-permute-start.2 = (bf16[768,256]{1,0:T(8,128)(2,1)S(1)}, bf16[768,256]{1,0:T(8,128)(2,1)S(1)}, u32[]{:S(2)}, u32[]{:S(2)}) collective-permute-start(bf16[768,256]{1,0:T(8,128)(2,1)S(1)} %get-tuple-element.49), channel_id=1, source_target_pairs={{0,1},{1,0},{2,3},{3,2},{4,5},{5,4},{6,7},{7,6},{8,9},{9,8},{10,11... | collective-permute-start | bytes 1179656 | tf_op jit(solution)/shard_map/ppermute | solution.py:302
  56.8 1.6 %collective-permute-start.1 = (bf16[512,256]{1,0:T(8,128)(2,1)S(1)}, bf16[512,256]{1,0:T(8,128)(2,1)S(1)}, u32[]{:S(2)}, u32[]{:S(2)}) collective-permute-start(bf16[512,256]{1,0:T(8,128)(2,1)S(1)} %get-tuple-element.47), channel_id=1, source_target_pairs={{0,1},{1,0},{2,3},{3,2},{4,5},{5,4},{6,7},{7,6},{8,9},{9,8},{10,11... | collective-permute-start | bytes 786440 | tf_op jit(solution)/shard_map/ppermute | solution.py:302
  59.4 27.5 %copy-start.2 = (bf16[3,3,256,256]{3,2,1,0:T(8,128)(2,1)S(1)}, bf16[3,3,256,256]{3,2,1,0:T(8,128)(2,1)}, u32[]{:S(2)}) copy-start(bf16[3,3,256,256]{3,2,1,0:T(8,128)(2,1)} %param.8) | copy-start | bytes 3538948
  86.5 3.9 %collective-permute-start.3 = (bf16[96,256]{1,0:T(8,128)(2,1)S(1)}, bf16[96,256]{1,0:T(8,128)(2,1)S(1)}, u32[]{:S(2)}, u32[]{:S(2)}) collective-permute-start(bf16[96,256]{1,0:T(8,128)(2,1)S(1)} %reduce_sum.12), channel_id=1, source_target_pairs={{0,64},{64,0},{128,192},{192,128},{1,65},{65,1},{129,193},{193,129... | collective-permute-start | bytes 147464 | tf_op jit(solution)/shard_map/ppermute | solution.py:380
  90.4 5.2 %collective-permute-start.4 = (bf16[96,256]{1,0:T(8,128)(2,1)S(1)}, bf16[96,256]{1,0:T(8,128)(2,1)S(1)}, u32[]{:S(2)}, u32[]{:S(2)}) collective-permute-start(bf16[96,256]{1,0:T(8,128)(2,1)S(1)} %add_convert_fusion.1), channel_id=1, source_target_pairs={{0,192},{192,0},{64,128},{128,64},{1,193},{193,1},{65,129},{129,65... | collective-permute-start | bytes 147464 | tf_op jit(solution)/shard_map/ppermute | solution.py:380
  119.5 7.2 %collective-permute-start.6 = (bf16[1536,256]{1,0:T(8,128)(2,1)S(1)}, bf16[1536,256]{1,0:T(8,128)(2,1)S(1)}, u32[]{:S(2)}, u32[]{:S(2)}) collective-permute-start(bf16[1536,256]{1,0:T(8,128)(2,1)S(1)} %bitcast.32), channel_id=1, source_target_pairs={{0,1},{1,0},{2,3},{3,2},{4,5},{5,4},{6,7},{7,6},{8,9},{9,8},{10,11... | collective-permute-start | bytes 2359304 | tf_op jit(solution)/shard_map/ppermute | solution.py:302
  124.8 3.1 %collective-permute-start.5 = (bf16[1536,256]{1,0:T(8,128)(2,1)S(1)}, bf16[1536,256]{1,0:T(8,128)(2,1)S(1)}, u32[]{:S(2)}, u32[]{:S(2)}) collective-permute-start(bf16[1536,256]{1,0:T(8,128)(2,1)S(1)} %bitcast.31), channel_id=1, source_target_pairs={{0,1},{1,0},{2,3},{3,2},{4,5},{5,4},{6,7},{7,6},{8,9},{9,8},{10,11... | collective-permute-start | bytes 2359304 | tf_op jit(solution)/shard_map/ppermute | solution.py:302
